TPU v7x, 32 devices: a whole 2x2x4 slice. The times are simulated.
32 devices in a mesh: seg: 8 (over y, x, core), coil: 4 (over z).
Axes of the slice: x: 2, y: 2, z: 4, core: 2. Of those that a mesh axis runs over, the one named last changes fastest.
Arguments:
- measured: float32 [16, 2, 32, 8, 512], P('seg', None, 'coil'), may hold values from -0.4 to 0.4
- forward_kernel: float32 [16, 2, 256, 128], P('seg', None, None, 'coil'), may hold values from -0.375 to 0.375
- backward_kernel: float32 [16, 2, 256, 128], P('seg', None, None, 'coil'), may hold values from -0.375 to 0.375
- line_offsets: int32 [16, 2, 4], P('seg'), may hold values from 0 to 7
Outputs:
- forward: float32 [16, 2, 32, 8, 512], P('seg', None, 'coil')
- result: float32 [16, 2, 32, 8, 512], P('seg', None, 'coil')
All inputs are finite; a program needn't handle non-finite values.
Results may differ from a plain program's by a relative error of at most 0.0003.
Values sent between devices are 32-bit elements; how exact they have to be, the bound alone decides.
No kernel may reach another device: no remote copies, remote signals or barrier semaphores. Data moves between devices by JAX's collectives and lax.ppermute only.
A program may use at most 128 MiB of HBM per device.

v0:
```python
import jax
import jax.numpy as jnp
from jax import lax
from jax.sharding import PartitionSpec as P

PRECISE = lax.Precision.HIGHEST


def shifted(block, axis, distance):
    devices = range(lax.axis_size(axis))
    route = [(i - distance, i) for i in devices if i - distance in devices]
    return lax.ppermute(block, axis, route)


def build_maps(kernel, offsets):
    blocks = kernel.shape[0]
    source_taps = offsets.shape[1]
    coil_count = kernel.shape[3] // source_taps
    line_count = kernel.shape[2] // coil_count
    line_picks = (
        offsets[:, :, None] == jnp.arange(line_count, dtype=jnp.int32)[None, None, :]
    ).astype(jnp.float32)
    kernel_parts = kernel.reshape(blocks, 2, coil_count * line_count, coil_count, source_taps)
    spread = jnp.einsum("srocj,sjl->srocl", kernel_parts, line_picks, precision=PRECISE)
    spread = spread.reshape(blocks, 2, coil_count * line_count, coil_count * line_count)
    upper_rows = jnp.concatenate([spread[:, 0], -spread[:, 1]], axis=2)
    lower_rows = jnp.concatenate([spread[:, 1], spread[:, 0]], axis=2)
    return jnp.concatenate([upper_rows, lower_rows], axis=1)


def apply_map(lines, matrix):
    return lax.dot_general(lines, matrix, (((1,), (1,)), ((), ())), precision=PRECISE)


def carry_in(composite, offset, backward):
    direction = -1 if backward else 1

    def relay(counter, incoming):
        return shifted(apply_map(incoming, composite) + offset, "seg", direction)

    incoming = lax.fori_loop(0, lax.axis_size("seg") - 1, relay, jnp.zeros_like(offset))
    return incoming


def sweep_block(seg_maps, sources, backward):
    seg_count = sources.shape[0]
    visit_order = list(range(seg_count))
    if backward:
        visit_order = visit_order[::-1]
    composite = jnp.eye(seg_maps.shape[1], dtype=jnp.float32)
    offset = jnp.zeros(sources.shape[1:], jnp.float32)
    for index in visit_order:
        composite = jnp.dot(seg_maps[index], composite, precision=PRECISE)
        offset = apply_map(offset, seg_maps[index]) + sources[index]
    current = carry_in(composite, offset, backward)
    states = [None] * seg_count
    for index in visit_order:
        current = apply_map(current, seg_maps[index]) + sources[index]
        states[index] = current
    return jnp.stack(states)


def shards(measured, forward_kernel, backward_kernel, line_offsets):
    forward_full, backward_full = (
        lax.all_gather(forward_kernel, "coil", axis=3, tiled=True),
        lax.all_gather(backward_kernel, "coil", axis=3, tiled=True),
    )
    forward_maps = build_maps(forward_full, line_offsets[:, 0])
    backward_maps = build_maps(backward_full, line_offsets[:, 1])
    columns = lax.all_to_all(measured, "coil", split_axis=4, concat_axis=2, tiled=True)
    layout = columns.shape
    state_size = layout[1] * layout[2] * layout[3]
    sources = jnp.swapaxes(columns.reshape(layout[0], state_size, layout[4]), 1, 2)
    forward = sweep_block(forward_maps, sources, False)
    result = sweep_block(backward_maps, forward, True)
    forward_cols = jnp.swapaxes(forward, 1, 2).reshape(layout)
    result_cols = jnp.swapaxes(result, 1, 2).reshape(layout)
    forward_out, result_out = (
        lax.all_to_all(forward_cols, "coil", split_axis=2, concat_axis=4, tiled=True),
        lax.all_to_all(result_cols, "coil", split_axis=2, concat_axis=4, tiled=True),
    )
    return (forward_out, result_out)


def solution(mesh):
    placed = (
        P("seg", None, "coil", None, None),
        P("seg", None, None, "coil"),
        P("seg", None, None, "coil"),
        P("seg", None, None),
    )
    return jax.shard_map(
        shards,
        mesh=mesh,
        in_specs=placed,
        out_specs=(P("seg", None, "coil", None, None), P("seg", None, "coil", None, None)),
        check_vma=False,
    )
```

profile of v0, /device:TPU:3, one launch (start us, length us, event | category | flops | bytes accessed | tf_op | source)
XLA Modules:
  0.0 286.8 jit_solution(951638632475838376)
XLA Ops:
  0.6 8.2 %copy.27 = f32[2,2,8,8,512]{3,2,1,0,4:T(8,128)} copy(f32[2,2,8,8,512]{4,3,2,1,0:T(8,128)} %param.8) | data formatting | bytes 1048576 | tf_op args[0]
  8.9 7.4 %reshape.37 = f32[4,1,32768]{2,1,0:T(1,128)} reshape(f32[512,2,2,8,8]{4,3,2,1,0:T(8,128)} %bitcast.129) | data formatting | bytes 1048576
  16.2 4.6 %all-to-all-start = ((f32[4,1,32768]{2,1,0:T(1,128)}), f32[4,1,32768]{2,1,0:T(1,128)S(1)}, u32[]{:S(2)}, u32[]{:S(2)}) async-start(f32[4,1,32768]{2,1,0:T(1,128)} %reshape.37), calls=%async_computation | async-start | bytes 1048576 | tf_op jit(solution)/shard_map/all_to_all | solution.py:70
  20.9 21.6 %all_gather.6 = f32[2,2,256,128]{2,3,1,0:T(8,128)S(1)} all-gather(f32[2,2,256,32]{2,3,1,0:T(8,128)S(1)} %copy-done.11), channel_id=1, replica_groups=mesh['seg'=8,'coil'=4] {'coil'}, dimensions={3}, use_global_device_ids=true | all-gather | bytes 655360 | tf_op jit(solution)/shard_map/all_gather | solution.py:65
  43.6 12.6 %all_gather.7 = f32[2,2,256,128]{2,3,1,0:T(8,128)S(1)} all-gather(f32[2,2,256,32]{2,3,1,0:T(8,128)S(1)} %copy-done.12), channel_id=1, replica_groups=mesh['seg'=8,'coil'=4] {'coil'}, dimensions={3}, use_global_device_ids=true | all-gather | bytes 655360 | tf_op jit(solution)/shard_map/all_gather | solution.py:66
  58.5 1.4 copy-done.2
  63.4 1.9 fusion.3
  65.4 1.9 fusion.4
  67.8 2.1 reduce
  70.0 8.2 %reshape.38 = f32[512,2,2,8,8]{4,3,2,1,0:T(8,128)} reshape(f32[4,32768]{1,0:T(4,128)S(1)} %reduce) | data formatting | bytes 1048576
  78.1 5.1 %copy.28 = f32[2,2,8,8,512]{4,3,2,1,0:T(8,128)S(1)} copy(f32[2,2,8,8,512]{3,2,1,0,4:T(8,128)} %bitcast.128) | data formatting | bytes 1048576 | tf_op jit(solution)/shard_map/all_to_all | solution.py:70
  83.5 2.1 convolution_add_fusion.9
  85.7 1.9 convolution_add_fusion.8
  87.6 73.3 %while.20 = (s32[]{:T(128)}, f32[128,512]{1,0:T(8,128)S(1)}, f32[512,512]{1,0:T(8,128)S(1)}, f32[128,512]{1,0:T(8,128)S(1)}, s32[]{:T(128)}) while((s32[]{:T(128)}, f32[128,512]{1,0:T(8,128)S(1)}, f32[512,512]{1,0:T(8,128)S(1)}, f32[128,512]{1,0:T(8,128)S(1)}, s32[]{:T(128)}) %tuple.38), condition=%wide.region_1.0_spmd, body=%wide.region_0.0_spmd.sunk | while | flops 402718720 | bytes 2883685 | solution.py:41
  87.7 1.2 convolution_add_fusion.12
  88.8 10.2 %collective-permute-start = (f32[128,512]{1,0:T(8,128)S(1)}, f32[128,512]{1,0:T(8,128)S(1)}, u32[]{:S(2)}, u32[]{:S(2)}) collective-permute-start(f32[128,512]{1,0:T(8,128)S(1)} %convolution_add_fusion.12), channel_id=1, source_target_pairs={{0,4},{4,8},{8,12},{12,16},{16,20},{20,24},{24,28},{1,5},{5,9},{9,... | collective-permute-start | bytes 786440 | tf_op jit(solution)/shard_map/while/body/eval_jaxpr/ppermute | solution.py:12
  99.0 3.3 %collective-permute-done = f32[128,512]{1,0:T(8,128)S(1)} collective-permute-done((f32[128,512]{1,0:T(8,128)S(1)}, f32[128,512]{1,0:T(8,128)S(1)}, u32[]{:S(2)}, u32[]{:S(2)}) %collective-permute-start) | collective-permute-done | bytes 262176 | tf_op jit(solution)/shard_map/while/body/eval_jaxpr/ppermute | solution.py:12
  102.3 1.2 convolution_add_fusion.12
  103.5 5.3 %collective-permute-start = (f32[128,512]{1,0:T(8,128)S(1)}, f32[128,512]{1,0:T(8,128)S(1)}, u32[]{:S(2)}, u32[]{:S(2)}) collective-permute-start(f32[128,512]{1,0:T(8,128)S(1)} %convolution_add_fusion.12), channel_id=1, source_target_pairs={{0,4},{4,8},{8,12},{12,16},{16,20},{20,24},{24,28},{1,5},{5,9},{9,... | collective-permute-start | bytes 786440 | tf_op jit(solution)/shard_map/while/body/eval_jaxpr/ppermute | solution.py:12
  108.8 3.3 %collective-permute-done = f32[128,512]{1,0:T(8,128)S(1)} collective-permute-done((f32[128,512]{1,0:T(8,128)S(1)}, f32[128,512]{1,0:T(8,128)S(1)}, u32[]{:S(2)}, u32[]{:S(2)}) %collective-permute-start) | collective-permute-done | bytes 262176 | tf_op jit(solution)/shard_map/while/body/eval_jaxpr/ppermute | solution.py:12
  112.1 1.2 convolution_add_fusion.12
  113.3 5.3 %collective-permute-start = (f32[128,512]{1,0:T(8,128)S(1)}, f32[128,512]{1,0:T(8,128)S(1)}, u32[]{:S(2)}, u32[]{:S(2)}) collective-permute-start(f32[128,512]{1,0:T(8,128)S(1)} %convolution_add_fusion.12), channel_id=1, source_target_pairs={{0,4},{4,8},{8,12},{12,16},{16,20},{20,24},{24,28},{1,5},{5,9},{9,... | collective-permute-start | bytes 786440 | tf_op jit(solution)/shard_map/while/body/eval_jaxpr/ppermute | solution.py:12
  118.6 3.3 %collective-permute-done = f32[128,512]{1,0:T(8,128)S(1)} collective-permute-done((f32[128,512]{1,0:T(8,128)S(1)}, f32[128,512]{1,0:T(8,128)S(1)}, u32[]{:S(2)}, u32[]{:S(2)}) %collective-permute-start) | collective-permute-done | bytes 262176 | tf_op jit(solution)/shard_map/while/body/eval_jaxpr/ppermute | solution.py:12
  121.9 1.2 convolution_add_fusion.12
  123.0 5.3 %collective-permute-start = (f32[128,512]{1,0:T(8,128)S(1)}, f32[128,512]{1,0:T(8,128)S(1)}, u32[]{:S(2)}, u32[]{:S(2)}) collective-permute-start(f32[128,512]{1,0:T(8,128)S(1)} %convolution_add_fusion.12), channel_id=1, source_target_pairs={{0,4},{4,8},{8,12},{12,16},{16,20},{20,24},{24,28},{1,5},{5,9},{9,... | collective-permute-start | bytes 786440 | tf_op jit(solution)/shard_map/while/body/eval_jaxpr/ppermute | solution.py:12
  128.3 3.3 %collective-permute-done = f32[128,512]{1,0:T(8,128)S(1)} collective-permute-done((f32[128,512]{1,0:T(8,128)S(1)}, f32[128,512]{1,0:T(8,128)S(1)}, u32[]{:S(2)}, u32[]{:S(2)}) %collective-permute-start) | collective-permute-done | bytes 262176 | tf_op jit(solution)/shard_map/while/body/eval_jaxpr/ppermute | solution.py:12
  131.6 1.2 convolution_add_fusion.12
  132.8 5.3 %collective-permute-start = (f32[128,512]{1,0:T(8,128)S(1)}, f32[128,512]{1,0:T(8,128)S(1)}, u32[]{:S(2)}, u32[]{:S(2)}) collective-permute-start(f32[128,512]{1,0:T(8,128)S(1)} %convolution_add_fusion.12), channel_id=1, source_target_pairs={{0,4},{4,8},{8,12},{12,16},{16,20},{20,24},{24,28},{1,5},{5,9},{9,... | collective-permute-start | bytes 786440 | tf_op jit(solution)/shard_map/while/body/eval_jaxpr/ppermute | solution.py:12
  138.1 3.3 %collective-permute-done = f32[128,512]{1,0:T(8,128)S(1)} collective-permute-done((f32[128,512]{1,0:T(8,128)S(1)}, f32[128,512]{1,0:T(8,128)S(1)}, u32[]{:S(2)}, u32[]{:S(2)}) %collective-permute-start) | collective-permute-done | bytes 262176 | tf_op jit(solution)/shard_map/while/body/eval_jaxpr/ppermute | solution.py:12
  142.6 5.3 %collective-permute-start = (f32[128,512]{1,0:T(8,128)S(1)}, f32[128,512]{1,0:T(8,128)S(1)}, u32[]{:S(2)}, u32[]{:S(2)}) collective-permute-start(f32[128,512]{1,0:T(8,128)S(1)} %convolution_add_fusion.12), channel_id=1, source_target_pairs={{0,4},{4,8},{8,12},{12,16},{16,20},{20,24},{24,28},{1,5},{5,9},{9,... | collective-permute-start | bytes 786440 | tf_op jit(solution)/shard_map/while/body/eval_jaxpr/ppermute | solution.py:12
  147.9 3.3 %collective-permute-done = f32[128,512]{1,0:T(8,128)S(1)} collective-permute-done((f32[128,512]{1,0:T(8,128)S(1)}, f32[128,512]{1,0:T(8,128)S(1)}, u32[]{:S(2)}, u32[]{:S(2)}) %collective-permute-start) | collective-permute-done | bytes 262176 | tf_op jit(solution)/shard_map/while/body/eval_jaxpr/ppermute | solution.py:12
  152.4 5.3 %collective-permute-start = (f32[128,512]{1,0:T(8,128)S(1)}, f32[128,512]{1,0:T(8,128)S(1)}, u32[]{:S(2)}, u32[]{:S(2)}) collective-permute-start(f32[128,512]{1,0:T(8,128)S(1)} %convolution_add_fusion.12), channel_id=1, source_target_pairs={{0,4},{4,8},{8,12},{12,16},{16,20},{20,24},{24,28},{1,5},{5,9},{9,... | collective-permute-start | bytes 786440 | tf_op jit(solution)/shard_map/while/body/eval_jaxpr/ppermute | solution.py:12
  157.7 3.3 %collective-permute-done = f32[128,512]{1,0:T(8,128)S(1)} collective-permute-done((f32[128,512]{1,0:T(8,128)S(1)}, f32[128,512]{1,0:T(8,128)S(1)}, u32[]{:S(2)}, u32[]{:S(2)}) %collective-permute-start) | collective-permute-done | bytes 262176 | tf_op jit(solution)/shard_map/while/body/eval_jaxpr/ppermute | solution.py:12
  161.0 2.1 convolution_add_fusion.7
  163.1 2.1 convolution_add_fusion.6
  165.9 1.4 convolution_add_fusion.4
  167.4 82.1 %while.21 = (s32[]{:T(128)}, f32[128,512]{1,0:T(8,128)S(1)}, f32[512,512]{1,0:T(8,128)S(1)}, f32[128,512]{1,0:T(8,128)}, s32[]{:T(128)}) while((s32[]{:T(128)}, f32[128,512]{1,0:T(8,128)S(1)}, f32[512,512]{1,0:T(8,128)S(1)}, f32[128,512]{1,0:T(8,128)}, s32[]{:T(128)}) %tuple.41), condition=%wide.region_3.0_spmd, body=%wide.region_2.0_spmd.sunk | while | flops 402718720 | bytes 2883685 | solution.py:41
  167.4 2.8 convolution_add_fusion.13
  170.2 1.9 collective-permute-start.1
  172.1 7.6 %collective-permute-done.1 = f32[128,512]{1,0:T(8,128)S(1)} collective-permute-done((f32[128,512]{1,0:T(8,128)}, f32[128,512]{1,0:T(8,128)S(1)}, u32[]{:S(2)}, u32[]{:S(2)}) %collective-permute-start.1) | collective-permute-done | bytes 262176 | tf_op jit(solution)/shard_map/while/body/eval_jaxpr/ppermute | solution.py:12
  179.8 2.8 convolution_add_fusion.13
  182.6 1.9 collective-permute-start.1
  184.5 6.9 %collective-permute-done.1 = f32[128,512]{1,0:T(8,128)S(1)} collective-permute-done((f32[128,512]{1,0:T(8,128)}, f32[128,512]{1,0:T(8,128)S(1)}, u32[]{:S(2)}, u32[]{:S(2)}) %collective-permute-start.1) | collective-permute-done | bytes 262176 | tf_op jit(solution)/shard_map/while/body/eval_jaxpr/ppermute | solution.py:12
  191.4 2.8 convolution_add_fusion.13
  194.2 1.9 collective-permute-start.1
  196.1 6.9 %collective-permute-done.1 = f32[128,512]{1,0:T(8,128)S(1)} collective-permute-done((f32[128,512]{1,0:T(8,128)}, f32[128,512]{1,0:T(8,128)S(1)}, u32[]{:S(2)}, u32[]{:S(2)}) %collective-permute-start.1) | collective-permute-done | bytes 262176 | tf_op jit(solution)/shard_map/while/body/eval_jaxpr/ppermute | solution.py:12
  203.0 2.8 convolution_add_fusion.13
  205.8 1.9 collective-permute-start.1
  207.8 6.9 %collective-permute-done.1 = f32[128,512]{1,0:T(8,128)S(1)} collective-permute-done((f32[128,512]{1,0:T(8,128)}, f32[128,512]{1,0:T(8,128)S(1)}, u32[]{:S(2)}, u32[]{:S(2)}) %collective-permute-start.1) | collective-permute-done | bytes 262176 | tf_op jit(solution)/shard_map/while/body/eval_jaxpr/ppermute | solution.py:12
  214.6 2.8 convolution_add_fusion.13
  217.5 1.9 collective-permute-start.1
  219.4 6.9 %collective-permute-done.1 = f32[128,512]{1,0:T(8,128)S(1)} collective-permute-done((f32[128,512]{1,0:T(8,128)}, f32[128,512]{1,0:T(8,128)S(1)}, u32[]{:S(2)}, u32[]{:S(2)}) %collective-permute-start.1) | collective-permute-done | bytes 262176 | tf_op jit(solution)/shard_map/while/body/eval_jaxpr/ppermute | solution.py:12
  226.2 2.8 convolution_add_fusion.13
  229.1 1.9 collective-permute-start.1
  231.0 6.9 %collective-permute-done.1 = f32[128,512]{1,0:T(8,128)S(1)} collective-permute-done((f32[128,512]{1,0:T(8,128)}, f32[128,512]{1,0:T(8,128)S(1)}, u32[]{:S(2)}, u32[]{:S(2)}) %collective-permute-start.1) | collective-permute-done | bytes 262176 | tf_op jit(solution)/shard_map/while/body/eval_jaxpr/ppermute | solution.py:12
  237.9 2.8 convolution_add_fusion.13
  240.7 1.9 collective-permute-start.1
  242.6 6.9 %collective-permute-done.1 = f32[128,512]{1,0:T(8,128)S(1)} collective-permute-done((f32[128,512]{1,0:T(8,128)}, f32[128,512]{1,0:T(8,128)S(1)}, u32[]{:S(2)}, u32[]{:S(2)}) %collective-permute-start.1) | collective-permute-done | bytes 262176 | tf_op jit(solution)/shard_map/while/body/eval_jaxpr/ppermute | solution.py:12
  249.5 1.7 convolution_add_fusion.3
  251.2 1.7 fusion
  254.0 4.6 %all-to-all-start.2 = ((f32[2,2,32,8,128]{4,3,1,0,2:T(8,128)}), f32[2,2,32,8,128]{4,3,1,0,2:T(8,128)S(1)}, u32[]{:S(2)}, u32[]{:S(2)}) async-start(f32[2,2,32,8,128]{4,3,1,0,2:T(8,128)} %copy.36), calls=%async_computation.2 | async-start | bytes 1048576 | tf_op jit(solution)/shard_map/all_to_all | solution.py:80
  259.7 9.2 %all-to-all-done.2 = f32[2,2,32,8,128]{4,3,1,0,2:T(8,128)S(1)} async-done(((f32[2,2,32,8,128]{4,3,1,0,2:T(8,128)}), f32[2,2,32,8,128]{4,3,1,0,2:T(8,128)S(1)}, u32[]{:S(2)}, u32[]{:S(2)}) %all-to-all-start.2) | async-done | bytes 524320 | tf_op jit(solution)/shard_map/all_to_all | solution.py:80
  268.9 3.5 %all-to-all-start.1 = ((f32[2,2,32,8,128]{4,3,1,0,2:T(8,128)}), f32[2,2,32,8,128]{4,3,1,0,2:T(8,128)S(1)}, u32[]{:S(2)}, u32[]{:S(2)}) async-start(f32[2,2,32,8,128]{4,3,1,0,2:T(8,128)} %copy.32), calls=%async_computation.1 | async-start | bytes 1048576 | tf_op jit(solution)/shard_map/all_to_all | solution.py:79
  273.3 12.6 %all-to-all-done.1 = f32[2,2,32,8,128]{4,3,1,0,2:T(8,128)S(1)} async-done(((f32[2,2,32,8,128]{4,3,1,0,2:T(8,128)}), f32[2,2,32,8,128]{4,3,1,0,2:T(8,128)S(1)}, u32[]{:S(2)}, u32[]{:S(2)}) %all-to-all-start.1) | async-done | bytes 524320 | tf_op jit(solution)/shard_map/all_to_all | solution.py:79
  (57 shorter events, 14.7 us)
Async XLA Ops:
  8.9 12.0 %copy-start.13 = (s32[2,2,4]{2,1,0:T(2,128)S(1)}, s32[2,2,4]{2,1,0:T(2,128)}, u32[]{:S(2)}) copy-start(s32[2,2,4]{2,1,0:T(2,128)} %param.11) | copy-start | bytes 196
  8.9 12.0 %copy-start.11 = (f32[2,2,256,32]{2,3,1,0:T(8,128)S(1)}, f32[2,2,256,32]{2,3,1,0:T(8,128)}, u32[]{:S(2)}) copy-start(f32[2,2,256,32]{2,3,1,0:T(8,128)} %param.9) | copy-start | bytes 393220
  16.2 51.0 %all-to-all-start = ((f32[4,1,32768]{2,1,0:T(1,128)}), f32[4,1,32768]{2,1,0:T(1,128)S(1)}, u32[]{:S(2)}, u32[]{:S(2)}) async-start(f32[4,1,32768]{2,1,0:T(1,128)} %reshape.37), calls=%async_computation | async-start | bytes 1048576 | tf_op jit(solution)/shard_map/all_to_all | solution.py:70
  42.6 0.9 copy-start.12
  58.5 1.4 copy-start.2
  59.9 1.1 copy-start.9
  59.9 1.2 copy-start.10
  61.1 2.3 copy-start.3
  61.4 4.0 %copy-start = (f32[2,512,512]{1,2,0:T(8,128)}, f32[2,512,512]{1,2,0:T(8,128)S(1)}, u32[]{:S(2)}) copy-start(f32[2,512,512]{1,2,0:T(8,128)S(1)} %maximum_maximum_fusion.1) | copy-start | bytes 6291460
  83.5 4.1 %copy-start.6 = (f32[2,512,128]{1,2,0:T(8,128)}, f32[2,512,128]{1,2,0:T(8,128)S(1)}, u32[]{:S(2)}) copy-start(f32[2,512,128]{1,2,0:T(8,128)S(1)} %copy.30) | copy-start | bytes 1572868
  88.8 13.5 %collective-permute-start = (f32[128,512]{1,0:T(8,128)S(1)}, f32[128,512]{1,0:T(8,128)S(1)}, u32[]{:S(2)}, u32[]{:S(2)}) collective-permute-start(f32[128,512]{1,0:T(8,128)S(1)} %convolution_add_fusion.12), channel_id=1, source_target_pairs={{0,4},{4,8},{8,12},{12,16},{16,20},{20,24},{24,28},{1,5},{5,9},{9,... | collective-permute-start | bytes 786440 | tf_op jit(solution)/shard_map/while/body/eval_jaxpr/ppermute | solution.py:12
  103.5 8.6 %collective-permute-start = (f32[128,512]{1,0:T(8,128)S(1)}, f32[128,512]{1,0:T(8,128)S(1)}, u32[]{:S(2)}, u32[]{:S(2)}) collective-permute-start(f32[128,512]{1,0:T(8,128)S(1)} %convolution_add_fusion.12), channel_id=1, source_target_pairs={{0,4},{4,8},{8,12},{12,16},{16,20},{20,24},{24,28},{1,5},{5,9},{9,... | collective-permute-start | bytes 786440 | tf_op jit(solution)/shard_map/while/body/eval_jaxpr/ppermute | solution.py:12
  113.3 8.6 %collective-permute-start = (f32[128,512]{1,0:T(8,128)S(1)}, f32[128,512]{1,0:T(8,128)S(1)}, u32[]{:S(2)}, u32[]{:S(2)}) collective-permute-start(f32[128,512]{1,0:T(8,128)S(1)} %convolution_add_fusion.12), channel_id=1, source_target_pairs={{0,4},{4,8},{8,12},{12,16},{16,20},{20,24},{24,28},{1,5},{5,9},{9,... | collective-permute-start | bytes 786440 | tf_op jit(solution)/shard_map/while/body/eval_jaxpr/ppermute | solution.py:12
  123.0 8.6 %collective-permute-start = (f32[128,512]{1,0:T(8,128)S(1)}, f32[128,512]{1,0:T(8,128)S(1)}, u32[]{:S(2)}, u32[]{:S(2)}) collective-permute-start(f32[128,512]{1,0:T(8,128)S(1)} %convolution_add_fusion.12), channel_id=1, source_target_pairs={{0,4},{4,8},{8,12},{12,16},{16,20},{20,24},{24,28},{1,5},{5,9},{9,... | collective-permute-start | bytes 786440 | tf_op jit(solution)/shard_map/while/body/eval_jaxpr/ppermute | solution.py:12
  132.8 8.6 %collective-permute-start = (f32[128,512]{1,0:T(8,128)S(1)}, f32[128,512]{1,0:T(8,128)S(1)}, u32[]{:S(2)}, u32[]{:S(2)}) collective-permute-start(f32[128,512]{1,0:T(8,128)S(1)} %convolution_add_fusion.12), channel_id=1, source_target_pairs={{0,4},{4,8},{8,12},{12,16},{16,20},{20,24},{24,28},{1,5},{5,9},{9,... | collective-permute-start | bytes 786440 | tf_op jit(solution)/shard_map/while/body/eval_jaxpr/ppermute | solution.py:12
  142.6 8.6 %collective-permute-start = (f32[128,512]{1,0:T(8,128)S(1)}, f32[128,512]{1,0:T(8,128)S(1)}, u32[]{:S(2)}, u32[]{:S(2)}) collective-permute-start(f32[128,512]{1,0:T(8,128)S(1)} %convolution_add_fusion.12), channel_id=1, source_target_pairs={{0,4},{4,8},{8,12},{12,16},{16,20},{20,24},{24,28},{1,5},{5,9},{9,... | collective-permute-start | bytes 786440 | tf_op jit(solution)/shard_map/while/body/eval_jaxpr/ppermute | solution.py:12
  152.4 8.6 %collective-permute-start = (f32[128,512]{1,0:T(8,128)S(1)}, f32[128,512]{1,0:T(8,128)S(1)}, u32[]{:S(2)}, u32[]{:S(2)}) collective-permute-start(f32[128,512]{1,0:T(8,128)S(1)} %convolution_add_fusion.12), channel_id=1, source_target_pairs={{0,4},{4,8},{8,12},{12,16},{16,20},{20,24},{24,28},{1,5},{5,9},{9,... | collective-permute-start | bytes 786440 | tf_op jit(solution)/shard_map/while/body/eval_jaxpr/ppermute | solution.py:12
  161.0 4.2 %copy-start.1 = (f32[2,512,512]{1,2,0:T(8,128)S(1)}, f32[2,512,512]{1,2,0:T(8,128)}, u32[]{:S(2)}) copy-start(f32[2,512,512]{1,2,0:T(8,128)} %copy-done) | copy-start | bytes 6291460
  163.1 4.2 %copy-start.4 = (f32[128,512]{1,0:T(8,128)}, f32[128,512]{1,0:T(8,128)S(1)}, u32[]{:S(2)}) copy-start(f32[128,512]{1,0:T(8,128)S(1)} %convolution_add_fusion.7) | copy-start | bytes 786436
  165.2 2.2 copy-start.7
  170.2 9.5 %collective-permute-start.1 = (f32[128,512]{1,0:T(8,128)}, f32[128,512]{1,0:T(8,128)S(1)}, u32[]{:S(2)}, u32[]{:S(2)}) collective-permute-start(f32[128,512]{1,0:T(8,128)} %convolution_add_fusion.13), channel_id=1, source_target_pairs={{4,0},{8,4},{12,8},{16,12},{20,16},{24,20},{28,24},{5,1},{9,5},{13... | collective-permute-start | bytes 786440 | tf_op jit(solution)/shard_map/while/body/eval_jaxpr/ppermute | solution.py:12
  182.6 8.8 %collective-permute-start.1 = (f32[128,512]{1,0:T(8,128)}, f32[128,512]{1,0:T(8,128)S(1)}, u32[]{:S(2)}, u32[]{:S(2)}) collective-permute-start(f32[128,512]{1,0:T(8,128)} %convolution_add_fusion.13), channel_id=1, source_target_pairs={{4,0},{8,4},{12,8},{16,12},{20,16},{24,20},{28,24},{5,1},{9,5},{13... | collective-permute-start | bytes 786440 | tf_op jit(solution)/shard_map/while/body/eval_jaxpr/ppermute | solution.py:12
  194.2 8.8 %collective-permute-start.1 = (f32[128,512]{1,0:T(8,128)}, f32[128,512]{1,0:T(8,128)S(1)}, u32[]{:S(2)}, u32[]{:S(2)}) collective-permute-start(f32[128,512]{1,0:T(8,128)} %convolution_add_fusion.13), channel_id=1, source_target_pairs={{4,0},{8,4},{12,8},{16,12},{20,16},{24,20},{28,24},{5,1},{9,5},{13... | collective-permute-start | bytes 786440 | tf_op jit(solution)/shard_map/while/body/eval_jaxpr/ppermute | solution.py:12
  205.8 8.8 %collective-permute-start.1 = (f32[128,512]{1,0:T(8,128)}, f32[128,512]{1,0:T(8,128)S(1)}, u32[]{:S(2)}, u32[]{:S(2)}) collective-permute-start(f32[128,512]{1,0:T(8,128)} %convolution_add_fusion.13), channel_id=1, source_target_pairs={{4,0},{8,4},{12,8},{16,12},{20,16},{24,20},{28,24},{5,1},{9,5},{13... | collective-permute-start | bytes 786440 | tf_op jit(solution)/shard_map/while/body/eval_jaxpr/ppermute | solution.py:12
  217.5 8.8 %collective-permute-start.1 = (f32[128,512]{1,0:T(8,128)}, f32[128,512]{1,0:T(8,128)S(1)}, u32[]{:S(2)}, u32[]{:S(2)}) collective-permute-start(f32[128,512]{1,0:T(8,128)} %convolution_add_fusion.13), channel_id=1, source_target_pairs={{4,0},{8,4},{12,8},{16,12},{20,16},{24,20},{28,24},{5,1},{9,5},{13... | collective-permute-start | bytes 786440 | tf_op jit(solution)/shard_map/while/body/eval_jaxpr/ppermute | solution.py:12
  229.1 8.8 %collective-permute-start.1 = (f32[128,512]{1,0:T(8,128)}, f32[128,512]{1,0:T(8,128)S(1)}, u32[]{:S(2)}, u32[]{:S(2)}) collective-permute-start(f32[128,512]{1,0:T(8,128)} %convolution_add_fusion.13), channel_id=1, source_target_pairs={{4,0},{8,4},{12,8},{16,12},{20,16},{24,20},{28,24},{5,1},{9,5},{13... | collective-permute-start | bytes 786440 | tf_op jit(solution)/shard_map/while/body/eval_jaxpr/ppermute | solution.py:12
  240.7 8.8 %collective-permute-start.1 = (f32[128,512]{1,0:T(8,128)}, f32[128,512]{1,0:T(8,128)S(1)}, u32[]{:S(2)}, u32[]{:S(2)}) collective-permute-start(f32[128,512]{1,0:T(8,128)} %convolution_add_fusion.13), channel_id=1, source_target_pairs={{4,0},{8,4},{12,8},{16,12},{20,16},{24,20},{28,24},{5,1},{9,5},{13... | collective-permute-start | bytes 786440 | tf_op jit(solution)/shard_map/while/body/eval_jaxpr/ppermute | solution.py:12
  252.8 5.8 %copy-start.5 = (f32[128,512]{1,0:T(8,128)S(1)}, f32[128,512]{1,0:T(8,128)}, u32[]{:S(2)}) copy-start(f32[128,512]{1,0:T(8,128)} %copy-done.4) | copy-start | bytes 786436
  252.8 5.7 %copy-start.8 = (f32[128,512]{1,0:T(8,128)S(1)}, f32[128,512]{1,0:T(8,128)}, u32[]{:S(2)}) copy-start(f32[128,512]{1,0:T(8,128)} %copy-done.7) | copy-start | bytes 786436
  254.0 15.0 %all-to-all-start.2 = ((f32[2,2,32,8,128]{4,3,1,0,2:T(8,128)}), f32[2,2,32,8,128]{4,3,1,0,2:T(8,128)S(1)}, u32[]{:S(2)}, u32[]{:S(2)}) async-start(f32[2,2,32,8,128]{4,3,1,0,2:T(8,128)} %copy.36), calls=%async_computation.2 | async-start | bytes 1048576 | tf_op jit(solution)/shard_map/all_to_all | solution.py:80
  268.9 17.0 %all-to-all-start.1 = ((f32[2,2,32,8,128]{4,3,1,0,2:T(8,128)}), f32[2,2,32,8,128]{4,3,1,0,2:T(8,128)S(1)}, u32[]{:S(2)}, u32[]{:S(2)}) async-start(f32[2,2,32,8,128]{4,3,1,0,2:T(8,128)} %copy.32), calls=%async_computation.1 | async-start | bytes 1048576 | tf_op jit(solution)/shard_map/all_to_all | solution.py:79
where the time goes:
time: 288 us; the launch traced here: 287 us
  waiting for transfers between devices  93.7 us (33%)
  starting transfers between devices  67.9 us (24%)
  matrix products  49.3 us (17%)
  local copies, waits for them, and re-layouts  37.5 us (13%)
  blocking collectives  34.2 us (12%)
    ppermute x14, waiting for transfers between devices, shifted(): return lax.ppermute(block, axis, route)  71.9 us
    ppermute x14, starting transfers between devices, shifted(): return lax.ppermute(block, axis, route)  55.2 us
    dot_general x22, matrix products, apply_map(): lax.dot_general(lines, matrix, (((1,), (1,)), ((), ())), precision=PRECISE)  41.8 us
    unnamed x31, local copies, waits for them, and re-layouts  26.3 us
    all_gather x1, blocking collectives, shards(): lax.all_gather(forward_kernel, 'coil', axis=3, tiled=True)  21.6 us
    all_to_all x1, waiting for transfers between devices, shards(): lax.all_to_all(forward_cols, 'coil', split_axis=2, concat_axis=4, tiled=T...  12.6 us
    all_gather x1, blocking collectives, shards(): lax.all_gather(backward_kernel, 'coil', axis=3, tiled=True)  12.6 us
    all_to_all x1, waiting for transfers between devices, shards(): lax.all_to_all(result_cols, 'coil', split_axis=2, concat_axis=4, tiled=True)  9.24 us
  transfers between devices with their start and end apart: 17, of which 16 were waited for; matrix products, arithmetic and copies ran while one was open for 4% of the time, Pallas kernels for 0%

commit v1 on v0

v1 whole, which is shorter than its diff:
```python
import functools

import jax
import jax.numpy as jnp
from jax import lax
from jax.experimental import pallas as pl
from jax.experimental.pallas import tpu as pltpu
from jax.sharding import PartitionSpec as P

F32 = jnp.float32
BF16 = jnp.bfloat16
VMEM = pl.BlockSpec(memory_space=pltpu.VMEM)
SMEM = pl.BlockSpec(memory_space=pltpu.SMEM)
ANY = pl.BlockSpec(memory_space=pl.ANY)
LANES = 128
PARAMS = pltpu.CompilerParams(vmem_limit_bytes=40 * 2**20)


def halves(a):
    high = a.astype(BF16)
    return high, (a - high.astype(F32)).astype(BF16)


def product(left, right):
    dot = functools.partial(jnp.dot, preferred_element_type=F32)
    high, low = left
    other_high, other_low = halves(right)
    return dot(high, other_high) + (dot(high, other_low) + dot(low, other_high))


def real_form(columns):
    size = columns.shape[0] // 2
    return jnp.concatenate([columns, jnp.concatenate([-columns[size:], columns[:size]], axis=0)], axis=1)


def spread(value):
    return [value[:, i : i + LANES] for i in range(0, value.shape[1], LANES)]


def pick(value, state, picked, offsets, row, coils, lines):
    taps = offsets.shape[1]
    chunks = spread(value)
    for i, chunk in enumerate(chunks):
        state[i] = chunk
        for part in range(2):
            for tap in range(taps):
                source = pl.ds(part * coils * lines + offsets[row, tap], coils, stride=lines)
                picked[i, pl.ds(part * coils * taps + tap, coils, stride=taps), :] = state[i, source, :]
    return jnp.concatenate([picked[i] for i in range(len(chunks))], axis=1)


def spot(ids, i):
    return lax.bitwise_xor(ids[0], i)


def pack(measured, kernels_f, kernels_b, ids):
    segs, parts, coils, lines, samples = measured.shape
    n = lax.axis_size("coil")
    width = samples // n
    cols, rows = kernels_f.shape[2:]

    def body(ids_ref, m_ref, f_ref, b_ref, k_out, *rest):
        outs, sems = rest[:n], rest[n]
        copies = [
            pltpu.make_async_copy(f_ref, k_out.at[pl.ds(0, segs)], sems.at[n]),
            pltpu.make_async_copy(b_ref, k_out.at[pl.ds(segs, segs)], sems.at[n + 1]),
        ]
        for i in range(n):
            start = pl.multiple_of(spot(ids_ref, i) * width, width)
            copies.append(pltpu.make_async_copy(m_ref.at[:, :, :, :, pl.ds(start, width)], outs[i], sems.at[i]))
        for c in copies:
            c.start()
        for c in copies:
            c.wait()

    return pl.pallas_call(
        body,
        out_shape=[jax.ShapeDtypeStruct((2 * segs, parts, cols, rows), F32)]
        + [jax.ShapeDtypeStruct((segs, parts, coils, lines, width), F32)] * n,
        in_specs=[SMEM, ANY, ANY, ANY],
        out_specs=[VMEM] * (n + 1),
        scratch_shapes=[pltpu.SemaphoreType.DMA((n + 2,))],
        compiler_params=PARAMS,
        name="pack",
    )(ids, measured, kernels_f, kernels_b)


def summary(ids, offsets, kernel_blocks, lines_blocks, taps):
    n = len(kernel_blocks)
    maps, _, block_cols, rows = kernel_blocks[0].shape
    own_coils = block_cols // taps
    coils = own_coils * n
    lines = rows // coils
    cols = block_cols * n
    segs, _, _, _, width = lines_blocks[0].shape
    size = 2 * cols

    def body(ids_ref, off_ref, *refs):
        k_refs, m_refs = refs[:n], refs[n : 2 * n]
        e_ref, hi_ref, lo_ref, m_ref = refs[2 * n : 2 * n + 4]
        kt, state, picked = refs[2 * n + 4 :]
        choose = functools.partial(pick, state=state, picked=picked, offsets=off_ref, coils=coils, lines=lines)
        for i in range(n):
            r = spot(ids_ref, i)
            m_ref[:, :, pl.ds(r * own_coils, own_coils)] = m_refs[i][...]
            kt[:, :, pl.ds(r, 1)] = k_refs[i][...][:, :, None]
        columns = []
        for k in range(maps):
            real, imag = (kt[k, part].reshape(cols, rows).T for part in range(2))
            columns.append(jnp.concatenate([real, imag], axis=0))
            hi_ref[k], lo_ref[k] = halves(real_form(columns[k]))
        m = [m_ref[s].reshape(2 * rows, width) for s in range(segs)]
        first = jnp.concatenate([columns[0], m[0]], axis=1)
        stepped = product((hi_ref[1], lo_ref[1]), choose(first, row=1))
        second = jnp.concatenate([stepped[:, :cols], stepped[:, cols:] + m[1]], axis=1)
        e_ref[:, : cols + width] = choose(second, row=4)
        third = jnp.concatenate([second, columns[3]], axis=1)
        stepped = product((hi_ref[2], lo_ref[2]), choose(third, row=2))
        last = jnp.concatenate([stepped[:, : cols + width] + first, stepped[:, cols + width :]], axis=1)
        e_ref[:, cols + width :] = choose(last, row=5)

    return pl.pallas_call(
        body,
        out_shape=[
            jax.ShapeDtypeStruct((size, 3 * cols + 2 * width), F32),
            jax.ShapeDtypeStruct((maps, 2 * rows, size), BF16),
            jax.ShapeDtypeStruct((maps, 2 * rows, size), BF16),
            jax.ShapeDtypeStruct((segs, 2, coils, lines, width), F32),
        ],
        in_specs=[SMEM, SMEM] + [VMEM] * (2 * n),
        out_specs=[VMEM] * 4,
        scratch_shapes=[
            pltpu.VMEM((maps, 2, n, block_cols, rows), F32),
            pltpu.VMEM(((2 * cols + width) // LANES, 2 * rows, LANES), F32),
            pltpu.VMEM(((2 * cols + width) // LANES, size, LANES), F32),
        ],
        compiler_params=PARAMS,
        name="summary",
    )(ids, offsets, *kernel_blocks, *lines_blocks)


def compose(ids, mine, other, cols):
    size, lanes = mine.shape
    width = (lanes - 3 * cols) // 2
    half = cols + width

    def body(ids_ref, a_ref, b_ref, out_ref, pair, whole):
        core = ids_ref[2]
        pair[pl.ds(core, 1)] = a_ref[...][None]
        pair[pl.ds(1 - core, 1)] = b_ref[...][None]
        a, b = pair[0], pair[1]
        forward = halves(real_form(b[:, :cols]))
        cross = halves(real_form(b[:, half : half + cols]))
        back = halves(real_form(a[:, 2 * half :]))
        head = product(forward, a[:, :half])
        inner = product(cross, a[:, :half])
        whole[:, :cols] = head[:, :cols]
        whole[:, cols:half] = head[:, cols:] + b[:, cols:half]
        right = jnp.concatenate([inner[:, :cols], inner[:, cols:] + b[:, half + cols : 2 * half], b[:, 2 * half :]], axis=1)
        tail = product(back, right)
        whole[:, half : 2 * half] = tail[:, :half] + a[:, half : 2 * half]
        whole[:, 2 * half :] = tail[:, half:]
        out_ref[...] = whole[pl.ds(pl.multiple_of(core * (size // 2), size // 2), size // 2), :]

    return pl.pallas_call(
        body,
        out_shape=jax.ShapeDtypeStruct((size // 2, lanes), F32),
        in_specs=[SMEM, VMEM, VMEM],
        out_specs=VMEM,
        scratch_shapes=[pltpu.VMEM((2, size, lanes), F32), pltpu.VMEM((size, lanes), F32)],
        compiler_params=PARAMS,
        name="compose",
    )(ids, mine, other)


def finish(ids, offsets, high, low, measured, mine, other, near, far):
    maps, state_size, size = high.shape
    segs, _, coils, lines, width = measured.shape
    cols = size // 2
    half = cols + width
    lanes = mine.shape[1]
    chips = len(near)
    n = lax.axis_size("coil")
    own_coils = coils // n

    def body(ids_ref, off_ref, hi_ref, lo_ref, m_ref, a_ref, b_ref, *refs):
        near_refs, far_refs = refs[:chips], refs[chips : 2 * chips]
        outs = refs[2 * chips : 2 * chips + n]
        pair, table, zs, ws, state, picked, states = refs[2 * chips + n :]
        chip, core = ids_ref[1], ids_ref[2]
        pair[pl.ds(core, 1)] = a_ref[...][None]
        pair[pl.ds(1 - core, 1)] = b_ref[...][None]
        for i in range(chips):
            e = lax.bitwise_xor(chip, i)
            table[pl.ds(e * 2 + core, 1)] = near_refs[i][...][None]
            table[pl.ds(e * 2 + 1 - core, 1)] = far_refs[i][...][None]

        def block(e, start, stop):
            return jnp.concatenate([table[2 * e, :, start:stop], table[2 * e + 1, :, start:stop]], axis=0)

        def matrix(columns):
            return halves(real_form(columns))

        zs[0] = jnp.zeros((size, width), F32)
        z = None
        for e in range(chips - 1):
            incoming = block(e, cols, half)
            z = incoming if z is None else product(matrix(block(e, 0, cols)), z) + incoming
            zs[e + 1] = z
        ws[chips - 1] = jnp.zeros((size, width), F32)
        w = None
        for e in range(chips - 1, 0, -1):
            local = product(matrix(block(e, half, half + cols)), zs[e]) + block(e, half + cols, 2 * half)
            w = local if w is None else product(matrix(block(e, 2 * half, lanes)), w) + local
            ws[e - 1] = w
        zc, wc = zs[chip], ws[chip]
        z_mid = product(matrix(pair[0, :, :cols]), zc) + pair[0, :, cols:half]
        w_mid = (
            product(matrix(pair[1, :, 2 * half :]), wc)
            + product(matrix(pair[1, :, half : half + cols]), z_mid)
            + pair[1, :, half + cols : 2 * half]
        )
        first_core = core == 0
        z = jnp.where(first_core, zc, z_mid)
        w = jnp.where(first_core, w_mid, wc)
        m = [m_ref[s].reshape(state_size, width) for s in range(segs)]
        f0 = product((hi_ref[0], lo_ref[0]), z) + m[0]
        choose = functools.partial(pick, state=state, picked=picked, offsets=off_ref, coils=coils, lines=lines)
        f1 = product((hi_ref[1], lo_ref[1]), choose(f0, row=1)) + m[1]
        r1 = product((hi_ref[3], lo_ref[3]), w) + f1
        r0 = product((hi_ref[2], lo_ref[2]), choose(r1, row=2)) + f0
        for i, value in enumerate((f0, f1, r0, r1)):
            states[i // segs, i % segs] = value.reshape(2, coils, lines, width)
        for i in range(n):
            outs[i][...] = states[:, :, :, pl.ds(spot(ids_ref, i) * own_coils, own_coils)]

    return pl.pallas_call(
        body,
        out_shape=[jax.ShapeDtypeStruct((2, segs, 2, own_coils, lines, width), F32)] * n,
        in_specs=[SMEM, SMEM] + [VMEM] * (5 + 2 * chips),
        out_specs=[VMEM] * n,
        scratch_shapes=[
            pltpu.VMEM((2, size, lanes), F32),
            pltpu.VMEM((2 * chips, size // 2, lanes), F32),
            pltpu.VMEM((chips, size, width), F32),
            pltpu.VMEM((chips, size, width), F32),
            pltpu.VMEM((width // LANES, state_size, LANES), F32),
            pltpu.VMEM((width // LANES, size, LANES), F32),
            pltpu.VMEM((2, segs, 2, coils, lines, width), F32),
        ],
        compiler_params=PARAMS,
        name="finish",
    )(ids, offsets, high, low, measured, mine, other, *near, *far)


def unpack(blocks, ids):
    n = len(blocks)
    _, segs, parts, coils, lines, width = blocks[0].shape

    def body(ids_ref, *refs):
        ins, outs, sems = refs[:n], refs[n : n + 2], refs[n + 2]
        copies = []
        for i in range(n):
            start = pl.multiple_of(spot(ids_ref, i) * width, width)
            for o in range(2):
                copies.append(pltpu.make_async_copy(ins[i].at[o], outs[o].at[:, :, :, :, pl.ds(start, width)], sems.at[i, o]))
        for c in copies:
            c.start()
        for c in copies:
            c.wait()

    return pl.pallas_call(
        body,
        out_shape=[jax.ShapeDtypeStruct((segs, parts, coils, lines, n * width), F32)] * 2,
        in_specs=[SMEM] + [VMEM] * n,
        out_specs=[ANY] * 2,
        scratch_shapes=[pltpu.SemaphoreType.DMA((n, 2))],
        compiler_params=PARAMS,
        name="unpack",
    )(ids, *blocks)


def swap(block, axis, distance):
    return lax.ppermute(block, axis, [(i, i ^ distance) for i in range(lax.axis_size(axis))])


def shards(measured, forward_kernel, backward_kernel, line_offsets):
    n = lax.axis_size("coil")
    places = lax.axis_size("seg")
    coil, seg = lax.axis_index("coil"), lax.axis_index("seg")
    chips = places // 2
    taps = line_offsets.shape[2]
    width = measured.shape[4] // n
    cols = forward_kernel.shape[3] * n
    ids = jnp.stack([coil, seg // 2, seg % 2]).astype(jnp.int32)
    after = lax.ppermute(line_offsets[0, 0], "seg", [(i + 1, i) for i in range(places - 1)])
    before = lax.ppermute(line_offsets[-1, 1], "seg", [(i, i + 1) for i in range(places - 1)])
    offsets = jnp.concatenate([line_offsets[:, 0], line_offsets[:, 1], after[None], before[None]])
    kernels_f, kernels_b = (jnp.swapaxes(k, 2, 3) for k in (forward_kernel, backward_kernel))
    if width % LANES == 0 and (cols // taps // n) % 8 == 0:
        packed = pack(measured, kernels_f, kernels_b, ids)
        own, pieces = packed[0], packed[1:]
        kernel_blocks = {0: own}
        distance = n // 2
        while distance:
            held = sorted(kernel_blocks)
            received = swap(jnp.stack([kernel_blocks[i] for i in held]), "coil", distance)
            for at, i in enumerate(held):
                kernel_blocks[i ^ distance] = received[at]
            distance //= 2
        kernel_blocks = [kernel_blocks[i] for i in range(n)]
        lines_blocks = [pieces[0]] + [swap(pieces[i], "coil", i) for i in range(1, n)]
        order = ids
    else:
        whole = lax.all_gather(jnp.concatenate([kernels_f, kernels_b]), "coil")
        kernel_blocks = [whole[i] for i in range(n)]
        split = lax.all_to_all(measured, "coil", split_axis=4, concat_axis=2, tiled=True)
        split = jnp.pad(split, [(0, 0)] * 4 + [(0, -width % LANES)])
        coils = measured.shape[2]
        lines_blocks = [split[:, :, i * coils : (i + 1) * coils] for i in range(n)]
        order = ids * jnp.array([0, 1, 1], jnp.int32)
    mine, high, low, lines = summary(order, offsets, kernel_blocks, lines_blocks, taps)
    other = swap(mine, "seg", 1)
    half = compose(ids, mine, other, cols)
    near = [half] + [swap(half, "seg", 2 * i) for i in range(1, chips)]
    far = [swap(part, "seg", 1) for part in near]
    blocks = finish(order, offsets, high, low, lines, mine, other, near, far)
    if order is ids:
        blocks = [blocks[0]] + [swap(blocks[i], "coil", i) for i in range(1, n)]
        return tuple(unpack(blocks, ids))
    states = lax.all_to_all(jnp.stack(blocks), "coil", split_axis=0, concat_axis=0)[..., :width]
    states = jnp.moveaxis(states, 0, 5)
    states = states.reshape(states.shape[:5] + (n * width,))
    return states[0], states[1]


def solution(mesh):
    placed = (
        P("seg", None, "coil", None, None),
        P("seg", None, None, "coil"),
        P("seg", None, None, "coil"),
        P("seg", None, None),
    )
    return jax.shard_map(
        shards,
        mesh=mesh,
        in_specs=placed,
        out_specs=(P("seg", None, "coil", None, None), P("seg", None, "coil", None, None)),
        check_vma=False,
    )
```

time: 288 us -> 101 us (0.35)
  the two profiles are of different devices: /device:TPU:3 before, /device:TPU:8 now
where the time goes in v1:
time: 101 us; the launch traced here: 100 us
  waiting for transfers between devices  64.4 us (64%)
  starting transfers between devices  21.5 us (21%)
  Pallas kernels  10.6 us (10%)
  local copies, waits for them, and re-layouts  2.9 us (3%)
    ppermute x16, waiting for transfers between devices, swap(): lax.ppermute(block, axis, [(i, i ^ distance) for i in range(lax.axis_size...  64.4 us
    ppermute x16, starting transfers between devices, swap(): lax.ppermute(block, axis, [(i, i ^ distance) for i in range(lax.axis_size...  17.2 us
    pallas_call x1, Pallas kernels, finish(): pl.pallas_call(body, out_shape=[jax.ShapeDtypeStruct((2, segs, 2, own_coi...  4.05 us
    ppermute x1, starting transfers between devices, shards(): lax.ppermute(line_offsets[-1, 1], 'seg', [(i, i + 1) for i in range(place...  3.03 us
    unnamed x8, local copies, waits for them, and re-layouts  2.86 us
    pallas_call x1, Pallas kernels, summary(): pl.pallas_call(body, out_shape=[jax.ShapeDtypeStruct((size, 3 * cols + 2...  2.65 us
  transfers between devices with their start and end apart: 18, of which 14 were waited for; matrix products, arithmetic and copies ran while one was open for 0% of the time, Pallas kernels for 0%

profile of v1, /device:TPU:8, one launch (start us, length us, event | category | flops | bytes accessed | tf_op | source)
XLA Modules:
  0.0 100.3 jit_solution(9037870387788721249)
XLA Ops:
  0.6 0.1 pad_add_fusion.1.ids_ref
  0.7 0.0 copy-start
  0.7 1.0 %copy-done = f32[2,2,8,8,512]{4,3,2,1,0:T(8,128)S(1)} copy-done((f32[2,2,8,8,512]{4,3,2,1,0:T(8,128)S(1)}, f32[2,2,8,8,512]{4,3,2,1,0:T(8,128)}, u32[]{:S(2)}) %copy-start) | copy-done | bytes 524312
  1.8 0.0 copy-start.1
  1.8 0.9 copy-done.1
  2.7 0.0 copy-start.2
  2.7 0.9 copy-done.2
  3.6 1.0 %pack.1 = (f32[4,2,32,256]{3,2,1,0:T(8,128)S(1)}, f32[2,2,8,8,128]{4,3,2,1,0:T(8,128)S(1)}, f32[2,2,8,8,128]{4,3,2,1,0:T(8,128)S(1)}, f32[2,2,8,8,128]{4,3,2,1,0:T(8,128)S(1)}, f32[2,2,8,8,128]{4,3,2,1,0:T(8,128)S(1)}) custom-call(s32[3]{0:T(128)S(1)} %pad_add_fusion.1.ids_ref, f32[2,2,8,8,512]{4,3,2,1,0:T(8,128)S(1)} %copy-done, ...), custom_call_target="tpu_custom_call" | custom-call | tf_op jit(solution)/shard_map/pack/pallas_call | solution.py:76
  4.6 0.0 copy-start.3
  4.6 2.7 %collective-permute-start.2 = (f32[1,4,2,32,256]{4,3,2,1,0:T(8,128)S(1)}, f32[1,4,2,32,256]{4,3,2,1,0:T(8,128)S(1)}, u32[]{:S(2)}, u32[]{:S(2)}) collective-permute-start(f32[1,4,2,32,256]{4,3,2,1,0:T(8,128)S(1)} %bitcast.19), channel_id=1, source_target_pairs={{0,2},{1,3},{2,0},{3,1},{4,6},{5,7},{6,4},{7,5},{8,10},{9,11},{10,... | collective-permute-start | bytes 786440 | tf_op jit(solution)/shard_map/ppermute | solution.py:284
  7.3 11.1 %collective-permute-done.2 = f32[1,4,2,32,256]{4,3,2,1,0:T(8,128)S(1)} collective-permute-done((f32[1,4,2,32,256]{4,3,2,1,0:T(8,128)S(1)}, f32[1,4,2,32,256]{4,3,2,1,0:T(8,128)S(1)}, u32[]{:S(2)}, u32[]{:S(2)}) %collective-permute-start.2) | collective-permute-done | bytes 262176 | tf_op jit(solution)/shard_map/ppermute | solution.py:284
  18.4 1.4 %collective-permute-start.3 = (f32[2,4,2,32,256]{4,3,2,1,0:T(8,128)S(1)}, f32[2,4,2,32,256]{4,3,2,1,0:T(8,128)S(1)}, u32[]{:S(2)}, u32[]{:S(2)}) collective-permute-start(f32[2,4,2,32,256]{4,3,2,1,0:T(8,128)S(1)} %pad_maximum_fusion), channel_id=1, source_target_pairs={{0,1},{1,0},{2,3},{3,2},{4,5},{5,4},{6,7},{7,6},{8,9},{9,8},{10,11... | collective-permute-start | bytes 1572872 | tf_op jit(solution)/shard_map/ppermute | solution.py:284
  19.8 0.0 copy-done.3
  19.8 1.3 %collective-permute-start = (s32[4]{0:T(128)S(1)}, s32[4]{0:T(128)S(1)}, u32[]{:S(2)}, u32[]{:S(2)}) collective-permute-start(s32[4]{0:T(128)S(1)} %get-tuple-element.32), channel_id=1, source_target_pairs={{4,0},{8,4},{12,8},{16,12},{20,16},{24,20},{28,24},{5,1},{9,5},{13... | collective-permute-start | bytes 56 | tf_op jit(solution)/shard_map/ppermute | solution.py:296
  21.0 3.0 %collective-permute-start.1 = (s32[4]{0:T(128)S(1)}, s32[4]{0:T(128)S(1)}, u32[]{:S(2)}, u32[]{:S(2)}) collective-permute-start(s32[4]{0:T(128)S(1)} %get-tuple-element.33), channel_id=1, source_target_pairs={{0,4},{4,8},{8,12},{12,16},{16,20},{20,24},{24,28},{1,5},{5,9},{9,... | collective-permute-start | bytes 56 | tf_op jit(solution)/shard_map/ppermute | solution.py:297
  24.1 0.8 collective-permute-start.4
  24.9 3.4 %collective-permute-start.5 = (f32[2,2,8,8,128]{4,3,2,1,0:T(8,128)S(1)}, f32[2,2,8,8,128]{4,3,2,1,0:T(8,128)S(1)}, u32[]{:S(2)}, u32[]{:S(2)}) collective-permute-start(f32[2,2,8,8,128]{4,3,2,1,0:T(8,128)S(1)} %get-tuple-element.18), channel_id=1, source_target_pairs={{0,2},{1,3},{2,0},{3,1},{4,6},{5,7},{6,4},{7,5},{8,10},{9,11},{10,... | collective-permute-start | bytes 393224 | tf_op jit(solution)/shard_map/ppermute | solution.py:284
  28.3 0.0 collective-permute-done
  28.3 0.0 collective-permute-start.6
  28.3 0.0 collective-permute-done.1
  28.3 6.3 %collective-permute-done.3 = f32[2,4,2,32,256]{4,3,2,1,0:T(8,128)S(1)} collective-permute-done((f32[2,4,2,32,256]{4,3,2,1,0:T(8,128)S(1)}, f32[2,4,2,32,256]{4,3,2,1,0:T(8,128)S(1)}, u32[]{:S(2)}, u32[]{:S(2)}) %collective-permute-start.3) | collective-permute-done | bytes 524320 | tf_op jit(solution)/shard_map/ppermute | solution.py:284
  34.6 1.4 %collective-permute-done.4.refs_5_ = f32[2,2,8,8,128]{4,3,2,1,0:T(8,128)S(1)} collective-permute-done((f32[2,2,8,8,128]{4,3,2,1,0:T(8,128)S(1)}, f32[2,2,8,8,128]{4,3,2,1,0:T(8,128)S(1)}, u32[]{:S(2)}, u32[]{:S(2)}) %collective-permute-start.4) | collective-permute-done | bytes 131104 | tf_op jit(solution)/shard_map/ppermute | solution.py:284
  36.0 4.1 %collective-permute-done.5.refs_6_ = f32[2,2,8,8,128]{4,3,2,1,0:T(8,128)S(1)} collective-permute-done((f32[2,2,8,8,128]{4,3,2,1,0:T(8,128)S(1)}, f32[2,2,8,8,128]{4,3,2,1,0:T(8,128)S(1)}, u32[]{:S(2)}, u32[]{:S(2)}) %collective-permute-start.5) | collective-permute-done | bytes 131104 | tf_op jit(solution)/shard_map/ppermute | solution.py:284
  40.2 0.3 collective-permute-done.6.refs_7_
  40.5 2.6 %summary.1 = (f32[256,640]{1,0:T(8,128)S(1)}, bf16[4,512,256]{2,1,0:T(8,128)(2,1)S(1)}, bf16[4,512,256]{2,1,0:T(8,128)(2,1)S(1)}, f32[2,2,32,8,128]{4,3,2,1,0:T(8,128)S(1)}) custom-call(s32[3]{0:T(128)S(1)} %pad_add_fusion.1.ids_ref, s32[6,4]{1,0:T(8,128)S(1)} %pad_add_fusion.off_ref, f32[4,2,32,256]{3,2,1,0:T(8,128)S(1)} %get-tuple-element.15.refs_0_, ...), custom_call_target="tpu_custom_call" | custom-call | tf_op jit(solution)/shard_map/summary/pallas_call | solution.py:122
  43.1 0.1 collective-permute-start.7
  43.2 2.1 %collective-permute-done.7.b_ref = f32[256,640]{1,0:T(8,128)S(1)} collective-permute-done((f32[256,640]{1,0:T(8,128)S(1)}, f32[256,640]{1,0:T(8,128)S(1)}, u32[]{:S(2)}, u32[]{:S(2)}) %collective-permute-start.7) | collective-permute-done | bytes 655392 | tf_op jit(solution)/shard_map/ppermute | solution.py:284
  45.3 1.3 %compose.1.refs_0_ = f32[128,640]{1,0:T(8,128)S(1)} custom-call(s32[3]{0:T(128)S(1)} %pad_add_fusion.1.ids_ref, f32[256,640]{1,0:T(8,128)S(1)} %get-tuple-element.23.a_ref, f32[256,640]{1,0:T(8,128)S(1)} %collective-permute-done.7.b_ref), custom_call_target="tpu_custom_call" | custom-call | tf_op jit(solution)/shard_map/compose/pallas_call | solution.py:165
  46.7 2.2 %collective-permute-start.10 = (f32[128,640]{1,0:T(8,128)S(1)}, f32[128,640]{1,0:T(8,128)S(1)}, u32[]{:S(2)}, u32[]{:S(2)}) collective-permute-start(f32[128,640]{1,0:T(8,128)S(1)} %compose.1.refs_0_), channel_id=1, source_target_pairs={{0,24},{4,28},{8,16},{12,20},{16,8},{20,12},{24,0},{28,4},{1,25},{... | collective-permute-start | bytes 983048 | tf_op jit(solution)/shard_map/ppermute | solution.py:284
  48.9 0.7 collective-permute-start.9
  49.6 0.6 collective-permute-start.8
  50.2 0.0 collective-permute-start.11
  50.2 8.0 %collective-permute-done.10.refs_3_ = f32[128,640]{1,0:T(8,128)S(1)} collective-permute-done((f32[128,640]{1,0:T(8,128)S(1)}, f32[128,640]{1,0:T(8,128)S(1)}, u32[]{:S(2)}, u32[]{:S(2)}) %collective-permute-start.10) | collective-permute-done | bytes 327712 | tf_op jit(solution)/shard_map/ppermute | solution.py:284
  58.2 0.0 collective-permute-start.14
  58.2 6.2 %collective-permute-done.9.refs_2_ = f32[128,640]{1,0:T(8,128)S(1)} collective-permute-done((f32[128,640]{1,0:T(8,128)S(1)}, f32[128,640]{1,0:T(8,128)S(1)}, u32[]{:S(2)}, u32[]{:S(2)}) %collective-permute-start.9) | collective-permute-done | bytes 327712 | tf_op jit(solution)/shard_map/ppermute | solution.py:284
  64.4 0.0 collective-permute-start.13
  64.4 0.1 collective-permute-done.8.refs_1_
  64.5 0.4 collective-permute-start.12
  64.9 0.0 collective-permute-done.11.refs_4_
  64.9 0.0 collective-permute-done.14.refs_7_
  64.9 1.1 %collective-permute-done.13.refs_6_ = f32[128,640]{1,0:T(8,128)S(1)} collective-permute-done((f32[128,640]{1,0:T(8,128)S(1)}, f32[128,640]{1,0:T(8,128)S(1)}, u32[]{:S(2)}, u32[]{:S(2)}) %collective-permute-start.13) | collective-permute-done | bytes 327712 | tf_op jit(solution)/shard_map/ppermute | solution.py:284
  66.0 0.5 collective-permute-done.12.refs_5_
  66.5 4.1 %finish.1 = (f32[2,2,2,8,8,128]{5,4,3,2,1,0:T(8,128)S(1)}, f32[2,2,2,8,8,128]{5,4,3,2,1,0:T(8,128)S(1)}, f32[2,2,2,8,8,128]{5,4,3,2,1,0:T(8,128)S(1)}, f32[2,2,2,8,8,128]{5,4,3,2,1,0:T(8,128)S(1)}) custom-call(s32[3]{0:T(128)S(1)} %pad_add_fusion.1.ids_ref, s32[6,4]{1,0:T(8,128)S(1)} %pad_add_fusion.off_ref, ...), custom_call_target="tpu_custom_call" | custom-call | tf_op jit(solution)/shard_map/finish/pallas_call | solution.py:237
  70.5 3.4 %collective-permute-start.15 = (f32[2,2,2,8,8,128]{5,4,3,2,1,0:T(8,128)S(1)}, f32[2,2,2,8,8,128]{5,4,3,2,1,0:T(8,128)S(1)}, u32[]{:S(2)}, u32[]{:S(2)}) collective-permute-start(f32[2,2,2,8,8,128]{5,4,3,2,1,0:T(8,128)S(1)} %get-tuple-element.25), channel_id=1, source_target_pairs={{0,1},{1,0},{2,3},{3,2},{4,5},{5,4},{6,7},{7,6},{8,9},{9,8},{10,11... | collective-permute-start | bytes 786440 | tf_op jit(solution)/shard_map/ppermute | solution.py:284
  74.0 0.6 collective-permute-start.16
  74.6 0.9 collective-permute-start.17
  75.5 9.1 %collective-permute-done.15.refs_1_ = f32[2,2,2,8,8,128]{5,4,3,2,1,0:T(8,128)S(1)} collective-permute-done((f32[2,2,2,8,8,128]{5,4,3,2,1,0:T(8,128)S(1)}, f32[2,2,2,8,8,128]{5,4,3,2,1,0:T(8,128)S(1)}, u32[]{:S(2)}, u32[]{:S(2)}) %collective-permute-start.15) | collective-permute-done | bytes 262176 | tf_op jit(solution)/shard_map/ppermute | solution.py:284
  84.5 8.0 %collective-permute-done.16.refs_2_ = f32[2,2,2,8,8,128]{5,4,3,2,1,0:T(8,128)S(1)} collective-permute-done((f32[2,2,2,8,8,128]{5,4,3,2,1,0:T(8,128)S(1)}, f32[2,2,2,8,8,128]{5,4,3,2,1,0:T(8,128)S(1)}, u32[]{:S(2)}, u32[]{:S(2)}) %collective-permute-start.16) | collective-permute-done | bytes 262176 | tf_op jit(solution)/shard_map/ppermute | solution.py:284
  92.5 6.2 %collective-permute-done.17.refs_3_ = f32[2,2,2,8,8,128]{5,4,3,2,1,0:T(8,128)S(1)} collective-permute-done((f32[2,2,2,8,8,128]{5,4,3,2,1,0:T(8,128)S(1)}, f32[2,2,2,8,8,128]{5,4,3,2,1,0:T(8,128)S(1)}, u32[]{:S(2)}, u32[]{:S(2)}) %collective-permute-start.17) | collective-permute-done | bytes 262176 | tf_op jit(solution)/shard_map/ppermute | solution.py:284
  98.7 1.6 %unpack.1 = (f32[2,2,8,8,512]{4,3,2,1,0:T(8,128)}, f32[2,2,8,8,512]{4,3,2,1,0:T(8,128)}) custom-call(s32[3]{0:T(128)S(1)} %pad_add_fusion.1.ids_ref, f32[2,2,2,8,8,128]{5,4,3,2,1,0:T(8,128)S(1)} %get-tuple-element.24.refs_0_, f32[2,2,2,8,8,128]{5,4,3,2,1,0:T(8,128)S(1)} %collective-permute-done.15.refs_1_, ...), custom_call_target="tpu_custom_call" | custom-call | tf_op jit(solution)/shard_map/unpack/pallas_call | solution.py:272
  (5 shorter events, 0.1 us)
Async XLA Ops:
  0.7 1.0 %copy-start = (f32[2,2,8,8,512]{4,3,2,1,0:T(8,128)S(1)}, f32[2,2,8,8,512]{4,3,2,1,0:T(8,128)}, u32[]{:S(2)}) copy-start(f32[2,2,8,8,512]{4,3,2,1,0:T(8,128)} %m_ref.1) | copy-start | bytes 1572868
  1.8 0.9 copy-start.1
  2.7 0.9 copy-start.2
  4.6 15.1 %copy-start.3 = (s32[2,2,4]{2,1,0:T(2,128)S(1)}, s32[2,2,4]{2,1,0:T(2,128)}, u32[]{:S(2)}) copy-start(s32[2,2,4]{2,1,0:T(2,128)} %param.7) | copy-start | bytes 196
  4.6 13.7 %collective-permute-start.2 = (f32[1,4,2,32,256]{4,3,2,1,0:T(8,128)S(1)}, f32[1,4,2,32,256]{4,3,2,1,0:T(8,128)S(1)}, u32[]{:S(2)}, u32[]{:S(2)}) collective-permute-start(f32[1,4,2,32,256]{4,3,2,1,0:T(8,128)S(1)} %bitcast.19), channel_id=1, source_target_pairs={{0,2},{1,3},{2,0},{3,1},{4,6},{5,7},{6,4},{7,5},{8,10},{9,11},{10,... | collective-permute-start | bytes 786440 | tf_op jit(solution)/shard_map/ppermute | solution.py:284
  18.4 16.2 %collective-permute-start.3 = (f32[2,4,2,32,256]{4,3,2,1,0:T(8,128)S(1)}, f32[2,4,2,32,256]{4,3,2,1,0:T(8,128)S(1)}, u32[]{:S(2)}, u32[]{:S(2)}) collective-permute-start(f32[2,4,2,32,256]{4,3,2,1,0:T(8,128)S(1)} %pad_maximum_fusion), channel_id=1, source_target_pairs={{0,1},{1,0},{2,3},{3,2},{4,5},{5,4},{6,7},{7,6},{8,9},{9,8},{10,11... | collective-permute-start | bytes 1572872 | tf_op jit(solution)/shard_map/ppermute | solution.py:284
  19.8 8.5 %collective-permute-start = (s32[4]{0:T(128)S(1)}, s32[4]{0:T(128)S(1)}, u32[]{:S(2)}, u32[]{:S(2)}) collective-permute-start(s32[4]{0:T(128)S(1)} %get-tuple-element.32), channel_id=1, source_target_pairs={{4,0},{8,4},{12,8},{16,12},{20,16},{24,20},{28,24},{5,1},{9,5},{13... | collective-permute-start | bytes 56 | tf_op jit(solution)/shard_map/ppermute | solution.py:296
  21.0 7.2 %collective-permute-start.1 = (s32[4]{0:T(128)S(1)}, s32[4]{0:T(128)S(1)}, u32[]{:S(2)}, u32[]{:S(2)}) collective-permute-start(s32[4]{0:T(128)S(1)} %get-tuple-element.33), channel_id=1, source_target_pairs={{0,4},{4,8},{8,12},{12,16},{16,20},{20,24},{24,28},{1,5},{5,9},{9,... | collective-permute-start | bytes 56 | tf_op jit(solution)/shard_map/ppermute | solution.py:297
  24.1 12.0 %collective-permute-start.4 = (f32[2,2,8,8,128]{4,3,2,1,0:T(8,128)S(1)}, f32[2,2,8,8,128]{4,3,2,1,0:T(8,128)S(1)}, u32[]{:S(2)}, u32[]{:S(2)}) collective-permute-start(f32[2,2,8,8,128]{4,3,2,1,0:T(8,128)S(1)} %get-tuple-element.17), channel_id=1, source_target_pairs={{0,1},{1,0},{2,3},{3,2},{4,5},{5,4},{6,7},{7,6},{8,9},{9,8},{10,11... | collective-permute-start | bytes 393224 | tf_op jit(solution)/shard_map/ppermute | solution.py:284
  24.9 15.3 %collective-permute-start.5 = (f32[2,2,8,8,128]{4,3,2,1,0:T(8,128)S(1)}, f32[2,2,8,8,128]{4,3,2,1,0:T(8,128)S(1)}, u32[]{:S(2)}, u32[]{:S(2)}) collective-permute-start(f32[2,2,8,8,128]{4,3,2,1,0:T(8,128)S(1)} %get-tuple-element.18), channel_id=1, source_target_pairs={{0,2},{1,3},{2,0},{3,1},{4,6},{5,7},{6,4},{7,5},{8,10},{9,11},{10,... | collective-permute-start | bytes 393224 | tf_op jit(solution)/shard_map/ppermute | solution.py:284
  28.3 12.2 %collective-permute-start.6 = (f32[2,2,8,8,128]{4,3,2,1,0:T(8,128)S(1)}, f32[2,2,8,8,128]{4,3,2,1,0:T(8,128)S(1)}, u32[]{:S(2)}, u32[]{:S(2)}) collective-permute-start(f32[2,2,8,8,128]{4,3,2,1,0:T(8,128)S(1)} %get-tuple-element.19), channel_id=1, source_target_pairs={{0,3},{1,2},{2,1},{3,0},{4,7},{5,6},{6,5},{7,4},{8,11},{9,10},{10,... | collective-permute-start | bytes 393224 | tf_op jit(solution)/shard_map/ppermute | solution.py:284
  43.1 2.2 %collective-permute-start.7 = (f32[256,640]{1,0:T(8,128)S(1)}, f32[256,640]{1,0:T(8,128)S(1)}, u32[]{:S(2)}, u32[]{:S(2)}) collective-permute-start(f32[256,640]{1,0:T(8,128)S(1)} %get-tuple-element.23.a_ref), channel_id=1, source_target_pairs={{0,4},{4,0},{8,12},{12,8},{16,20},{20,16},{24,28},{28,24},{1,5},{5... | collective-permute-start | bytes 1966088 | tf_op jit(solution)/shard_map/ppermute | solution.py:284
  46.7 11.6 %collective-permute-start.10 = (f32[128,640]{1,0:T(8,128)S(1)}, f32[128,640]{1,0:T(8,128)S(1)}, u32[]{:S(2)}, u32[]{:S(2)}) collective-permute-start(f32[128,640]{1,0:T(8,128)S(1)} %compose.1.refs_0_), channel_id=1, source_target_pairs={{0,24},{4,28},{8,16},{12,20},{16,8},{20,12},{24,0},{28,4},{1,25},{... | collective-permute-start | bytes 983048 | tf_op jit(solution)/shard_map/ppermute | solution.py:284
  48.9 15.5 %collective-permute-start.9 = (f32[128,640]{1,0:T(8,128)S(1)}, f32[128,640]{1,0:T(8,128)S(1)}, u32[]{:S(2)}, u32[]{:S(2)}) collective-permute-start(f32[128,640]{1,0:T(8,128)S(1)} %compose.1.refs_0_), channel_id=1, source_target_pairs={{0,16},{4,20},{8,24},{12,28},{16,0},{20,4},{24,8},{28,12},{1,17},{... | collective-permute-start | bytes 983048 | tf_op jit(solution)/shard_map/ppermute | solution.py:284
  49.6 14.9 %collective-permute-start.8 = (f32[128,640]{1,0:T(8,128)S(1)}, f32[128,640]{1,0:T(8,128)S(1)}, u32[]{:S(2)}, u32[]{:S(2)}) collective-permute-start(f32[128,640]{1,0:T(8,128)S(1)} %compose.1.refs_0_), channel_id=1, source_target_pairs={{0,8},{4,12},{8,0},{12,4},{16,24},{20,28},{24,16},{28,20},{1,9},{5... | collective-permute-start | bytes 983048 | tf_op jit(solution)/shard_map/ppermute | solution.py:284
  50.2 14.7 %collective-permute-start.11 = (f32[128,640]{1,0:T(8,128)S(1)}, f32[128,640]{1,0:T(8,128)S(1)}, u32[]{:S(2)}, u32[]{:S(2)}) collective-permute-start(f32[128,640]{1,0:T(8,128)S(1)} %compose.1.refs_0_), channel_id=1, source_target_pairs={{0,4},{4,0},{8,12},{12,8},{16,20},{20,16},{24,28},{28,24},{1,5},{5... | collective-permute-start | bytes 983048 | tf_op jit(solution)/shard_map/ppermute | solution.py:284
  58.2 6.7 %collective-permute-start.14 = (f32[128,640]{1,0:T(8,128)S(1)}, f32[128,640]{1,0:T(8,128)S(1)}, u32[]{:S(2)}, u32[]{:S(2)}) collective-permute-start(f32[128,640]{1,0:T(8,128)S(1)} %collective-permute-done.10.refs_3_), channel_id=1, source_target_pairs={{0,4},{4,0},{8,12},{12,8},{16,20},{20,16},{24,28},{28,24},{1,5},{5... | collective-permute-start | bytes 983048 | tf_op jit(solution)/shard_map/ppermute | solution.py:284
  64.4 1.6 %collective-permute-start.13 = (f32[128,640]{1,0:T(8,128)S(1)}, f32[128,640]{1,0:T(8,128)S(1)}, u32[]{:S(2)}, u32[]{:S(2)}) collective-permute-start(f32[128,640]{1,0:T(8,128)S(1)} %collective-permute-done.9.refs_2_), channel_id=1, source_target_pairs={{0,4},{4,0},{8,12},{12,8},{16,20},{20,16},{24,28},{28,24},{1,5},{5... | collective-permute-start | bytes 983048 | tf_op jit(solution)/shard_map/ppermute | solution.py:284
  64.5 2.0 %collective-permute-start.12 = (f32[128,640]{1,0:T(8,128)S(1)}, f32[128,640]{1,0:T(8,128)S(1)}, u32[]{:S(2)}, u32[]{:S(2)}) collective-permute-start(f32[128,640]{1,0:T(8,128)S(1)} %collective-permute-done.8.refs_1_), channel_id=1, source_target_pairs={{0,4},{4,0},{8,12},{12,8},{16,20},{20,16},{24,28},{28,24},{1,5},{5... | collective-permute-start | bytes 983048 | tf_op jit(solution)/shard_map/ppermute | solution.py:284
  70.5 14.0 %collective-permute-start.15 = (f32[2,2,2,8,8,128]{5,4,3,2,1,0:T(8,128)S(1)}, f32[2,2,2,8,8,128]{5,4,3,2,1,0:T(8,128)S(1)}, u32[]{:S(2)}, u32[]{:S(2)}) collective-permute-start(f32[2,2,2,8,8,128]{5,4,3,2,1,0:T(8,128)S(1)} %get-tuple-element.25), channel_id=1, source_target_pairs={{0,1},{1,0},{2,3},{3,2},{4,5},{5,4},{6,7},{7,6},{8,9},{9,8},{10,11... | collective-permute-start | bytes 786440 | tf_op jit(solution)/shard_map/ppermute | solution.py:284
  74.0 18.6 %collective-permute-start.16 = (f32[2,2,2,8,8,128]{5,4,3,2,1,0:T(8,128)S(1)}, f32[2,2,2,8,8,128]{5,4,3,2,1,0:T(8,128)S(1)}, u32[]{:S(2)}, u32[]{:S(2)}) collective-permute-start(f32[2,2,2,8,8,128]{5,4,3,2,1,0:T(8,128)S(1)} %get-tuple-element.26), channel_id=1, source_target_pairs={{0,2},{1,3},{2,0},{3,1},{4,6},{5,7},{6,4},{7,5},{8,10},{9,11},{10,... | collective-permute-start | bytes 786440 | tf_op jit(solution)/shard_map/ppermute | solution.py:284
  74.6 24.2 %collective-permute-start.17 = (f32[2,2,2,8,8,128]{5,4,3,2,1,0:T(8,128)S(1)}, f32[2,2,2,8,8,128]{5,4,3,2,1,0:T(8,128)S(1)}, u32[]{:S(2)}, u32[]{:S(2)}) collective-permute-start(f32[2,2,2,8,8,128]{5,4,3,2,1,0:T(8,128)S(1)} %get-tuple-element.27), channel_id=1, source_target_pairs={{0,3},{1,2},{2,1},{3,0},{4,7},{5,6},{6,5},{7,4},{8,11},{9,10},{10,... | collective-permute-start | bytes 786440 | tf_op jit(solution)/shard_map/ppermute | solution.py:284

commit v2 on v0

v2 whole, which is shorter than its diff:
```python
import functools

import jax
import jax.numpy as jnp
from jax import lax
from jax.experimental import pallas as pl
from jax.experimental.pallas import tpu as pltpu
from jax.sharding import PartitionSpec as P

F32 = jnp.float32
BF16 = jnp.bfloat16
VMEM = pl.BlockSpec(memory_space=pltpu.VMEM)
SMEM = pl.BlockSpec(memory_space=pltpu.SMEM)
ANY = pl.BlockSpec(memory_space=pl.ANY)
HBM = pl.BlockSpec(memory_space=pltpu.HBM)
LANES = 128
PARAMS = pltpu.CompilerParams(vmem_limit_bytes=40 * 2**20)


def call(body, name, out_shape, in_specs, scratch=(), out_specs=None):
    return pl.pallas_call(
        body,
        out_shape=[jax.ShapeDtypeStruct(shape, dtype) for shape, dtype in out_shape],
        in_specs=in_specs,
        out_specs=out_specs or [VMEM] * len(out_shape),
        scratch_shapes=list(scratch),
        compiler_params=PARAMS,
        name=name,
    )


def halves(a):
    high = a.astype(BF16)
    return high, (a - high.astype(F32)).astype(BF16)


def product(left, right):
    dot = functools.partial(jnp.dot, preferred_element_type=F32)
    high, low = left
    other_high, other_low = halves(right)
    return dot(high, other_high) + (dot(high, other_low) + dot(low, other_high))


def real_form(columns):
    size = columns.shape[0] // 2
    return jnp.concatenate([columns, jnp.concatenate([-columns[size:], columns[:size]], axis=0)], axis=1)


def pick(value, state, picked, offsets, row):
    taps = offsets.shape[1]
    size, lines = picked.shape[1], state.shape[1] * taps // picked.shape[1]
    coils = size // 2 // taps
    chunks = value.shape[1] // LANES
    for i in range(chunks):
        state[i] = value[:, i * LANES : (i + 1) * LANES]
        for part in range(2):
            for tap in range(taps):
                source = pl.ds(part * coils * lines + offsets[row, tap], coils, stride=lines)
                picked[i, pl.ds(part * coils * taps + tap, coils, stride=taps), :] = state[i, source, :]
    return jnp.concatenate([picked[i] for i in range(chunks)], axis=1)


def pick_scratch(lanes, state, size):
    return [pltpu.VMEM((lanes // LANES, state, LANES), F32), pltpu.VMEM((lanes // LANES, size, LANES), F32)]


def visits(segs, backward):
    if backward:
        return [(s, segs + s - 1 if s else 2 * segs + 1) for s in reversed(range(segs))]
    return [(s, s + 1 if s < segs - 1 else 2 * segs) for s in range(segs)]


def through(maps, sources, choose, backward):
    state = None
    for s, row in visits(len(sources), backward):
        state = sources[s] if state is None else product(maps(s), carried) + sources[s]
        carried = choose(state, row=row)
    return carried


def spot(ids, i):
    return lax.bitwise_xor(ids[0], i)


def pack(measured, ids):
    segs, parts, coils, lines, samples = measured.shape
    n = lax.axis_size("coil")
    width = samples // n

    def body(ids_ref, m_ref, *rest):
        outs, sems = rest[:n], rest[n]
        copies = []
        for i in range(n):
            start = pl.multiple_of(spot(ids_ref, i) * width, width)
            copies.append(pltpu.make_async_copy(m_ref.at[:, :, :, :, pl.ds(start, width)], outs[i], sems.at[i]))
        for c in copies:
            c.start()
        for c in copies:
            c.wait()

    out = ((segs, parts, coils, lines, width), F32)
    return call(body, "pack", [out] * n, [SMEM, HBM], [pltpu.SemaphoreType.DMA((n,))])(ids, measured)


def hold(first, kernels, offsets):
    def body(_, k_ref, o_ref, k_out, f_out, b_out):
        k_out[...] = k_ref[...]
        f_out[...] = o_ref[:1, 0]
        b_out[...] = o_ref[-1:, 1]

    edge = ((1, offsets.shape[2]), jnp.int32)
    return call(body, "hold", [(kernels.shape, F32), edge, edge], [ANY, VMEM, VMEM])(first, kernels, offsets)


def gather(ids, blocks):
    n = len(blocks)
    segs, parts, coils, lines, width = blocks[0].shape

    def body(ids_ref, *refs):
        for i in range(n):
            refs[n][:, :, pl.ds(spot(ids_ref, i) * coils, coils)] = refs[i][...]

    out = ((segs, parts, n * coils, lines, width), F32)
    return call(body, "gather", [out], [SMEM] + [VMEM] * n)(ids, *blocks)[0]


def prepare(ids, offsets, blocks, backward):
    n = len(blocks)
    segs, _, block_cols, rows = blocks[0].shape
    cols = block_cols * n
    size = 2 * cols

    def body(ids_ref, off_ref, *refs):
        hi_ref, lo_ref, c_ref, kt, state, picked = refs[n:]
        choose = functools.partial(pick, state=state, picked=picked, offsets=off_ref)
        for i in range(n):
            kt[:, :, pl.ds(spot(ids_ref, i), 1)] = refs[i][...][:, :, None]
        columns = []
        for s in range(segs):
            real, imag = (kt[s, part].reshape(cols, rows).T for part in range(2))
            columns.append(jnp.concatenate([real, imag], axis=0))
            hi_ref[s], lo_ref[s] = halves(real_form(columns[s]))
        first = visits(segs, backward)[0][0]
        sources = [columns[s] if s == first else jnp.zeros_like(columns[s]) for s in range(segs)]
        c_ref[...] = through(lambda s: (hi_ref[s], lo_ref[s]), sources, choose, backward)

    return call(
        body,
        "prepare_backward" if backward else "prepare_forward",
        [((segs, 2 * rows, size), BF16)] * 2 + [((size, cols), F32)],
        [SMEM, SMEM] + [VMEM] * n,
        [pltpu.VMEM((segs, 2, n, block_cols, rows), F32)] + pick_scratch(cols, 2 * rows, size),
    )(ids, offsets, *blocks)


def summary(offsets, maps, measured):
    high, low, columns = maps
    size, cols = columns.shape
    segs, parts, coils, lines, width = measured.shape
    rows = parts * coils * lines

    def body(off_ref, hi_ref, lo_ref, c_ref, m_ref, e_ref, state, picked):
        choose = functools.partial(pick, state=state, picked=picked, offsets=off_ref)
        e_ref[:, :cols] = c_ref[...]
        sources = [m_ref[s].reshape(rows, width) for s in range(segs)]
        e_ref[:, cols:] = through(lambda s: (hi_ref[s], lo_ref[s]), sources, choose, False)
    return call(
        body,
        "summary",
        [((size, cols + width), F32)],
        [SMEM] + [VMEM] * 4,
        pick_scratch(width, rows, size),
    )(offsets, high, low, columns, measured)[0]


def compose(ids, mine, other, cols, backward):
    size, lanes = mine.shape

    def body(ids_ref, a_ref, b_ref, out_ref, pair, whole):
        core = ids_ref[2]
        pair[pl.ds(core, 1)] = a_ref[...][None]
        pair[pl.ds(1 - core, 1)] = b_ref[...][None]
        near, far = (pair[1], pair[0]) if backward else (pair[0], pair[1])
        both = product(halves(real_form(far[:, :cols])), near)
        whole[:, :cols] = both[:, :cols]
        whole[:, cols:] = both[:, cols:] + far[:, cols:]
        out_ref[...] = whole[pl.ds(pl.multiple_of(core * (size // 2), size // 2), size // 2), :]

    return call(
        body,
        "compose_backward" if backward else "compose_forward",
        [((size // 2, lanes), F32)],
        [SMEM, VMEM, VMEM],
        [pltpu.VMEM((2, size, lanes), F32), pltpu.VMEM((size, lanes), F32)],
    )(ids, mine, other)[0]


def finish(ids, offsets, maps, sources, mine, other, near, far, backward, following=None, arrived=()):
    high, low, _ = maps
    segs, _, coils, lines, width = sources.shape
    _, rows, size = high.shape
    cols = size // 2
    lanes = mine.shape[1]
    chips = len(near)
    n = lax.axis_size("coil")
    own_coils = coils // n
    extra = list(following) if following else []
    homes = len(arrived)

    def body(ids_ref, off_ref, hi_ref, lo_ref, m_ref, a_ref, b_ref, *refs):
        near_refs, far_refs, refs = refs[:chips], refs[chips : 2 * chips], refs[2 * chips :]
        home_refs, refs = refs[:homes], refs[homes:]
        extra_refs, outs, refs = refs[: len(extra)], refs[len(extra) : len(extra) + n + 1], refs[len(extra) + n + 1 :]
        if extra:
            e_ref, refs = refs[0], refs[1:]
        if homes:
            home_out, refs = refs[0], refs[1:]
        pair, table, carried, state, picked = refs[:5]
        copies = unpack_copies(ids_ref, home_refs, home_out, refs[5]) if homes else []
        for c in copies:
            c.start()
        choose = functools.partial(pick, state=state, picked=picked, offsets=off_ref)
        chip, core = ids_ref[1], ids_ref[2]
        pair[pl.ds(core, 1)] = a_ref[...][None]
        pair[pl.ds(1 - core, 1)] = b_ref[...][None]
        for i in range(chips):
            e = lax.bitwise_xor(chip, i)
            table[pl.ds(e * 2 + core, 1)] = near_refs[i][...][None]
            table[pl.ds(e * 2 + 1 - core, 1)] = far_refs[i][...][None]

        def step(block, value):
            return product(halves(real_form(block[:, :cols])), value) + block[:, cols:]

        order = list(range(chips))[:: -1 if backward else 1]
        value = jnp.zeros((size, width), F32)
        carried[order[0]] = value
        for at, e in enumerate(order[:-1]):
            block = jnp.concatenate([table[2 * e], table[2 * e + 1]], axis=0)
            value = step(block, value) if at else block[:, cols:]
            carried[order[at + 1]] = value
        value = carried[chip]
        leading = 1 if backward else 0
        value = jnp.where(core == leading, value, step(pair[leading], value))
        states = [None] * segs
        for at, (s, row) in enumerate(visits(segs, backward)):
            states[s] = product((hi_ref[s], lo_ref[s]), value) + m_ref[s].reshape(rows, width)
            if at < segs - 1:
                value = choose(states[s], row=row)
        for s in range(segs):
            outs[n][s] = states[s].reshape(2, coils, lines, width)
        for i in range(n):
            outs[i][...] = outs[n][:, :, pl.ds(spot(ids_ref, i) * own_coils, own_coils)]
        if extra:
            next_hi, next_lo, next_columns = extra_refs
            e_ref[:, :cols] = next_columns[...]
            e_ref[:, cols:] = through(lambda s: (next_hi[s], next_lo[s]), states, choose, not backward)
        for c in copies:
            c.wait()

    out_shape = [((segs, 2, own_coils, lines, width), F32)] * n + [((segs, 2, coils, lines, width), F32)]
    if extra:
        out_shape.append(((size, lanes), F32))
    out_specs = [VMEM] * len(out_shape)
    if homes:
        out_shape.append(((segs, 2, own_coils, lines, n * width), F32))
        out_specs.append(ANY)
    return call(
        body,
        "finish_backward" if backward else "finish_forward",
        out_shape,
        [SMEM, SMEM] + [VMEM] * (5 + 2 * chips + homes + len(extra)),
        [
            pltpu.VMEM((2, size, lanes), F32),
            pltpu.VMEM((2 * chips, size // 2, lanes), F32),
            pltpu.VMEM((chips, size, width), F32),
        ]
        + pick_scratch(width, rows, size)
        + [pltpu.SemaphoreType.DMA((n,))] * bool(homes),
        out_specs,
    )(ids, offsets, high, low, sources, mine, other, *near, *far, *arrived, *extra)


def unpack_copies(ids, ins, out, sems):
    width = ins[0].shape[-1]
    copies = []
    for i, block in enumerate(ins):
        start = pl.multiple_of(spot(ids, i) * width, width)
        copies.append(pltpu.make_async_copy(block, out.at[:, :, :, :, pl.ds(start, width)], sems.at[i]))
    return copies


def unpack(blocks, ids):
    n = len(blocks)
    segs, parts, coils, lines, width = blocks[0].shape

    def body(ids_ref, *refs):
        copies = unpack_copies(ids_ref, refs[:n], refs[n], refs[n + 1])
        for c in copies:
            c.start()
        for c in copies:
            c.wait()

    return call(
        body,
        "unpack",
        [((segs, parts, coils, lines, n * width), F32)],
        [SMEM] + [VMEM] * n,
        [pltpu.SemaphoreType.DMA((n,))],
        [ANY],
    )(ids, *blocks)[0]


def swap(block, axis, distance):
    return lax.ppermute(block, axis, [(i, i ^ distance) for i in range(lax.axis_size(axis))])


def spread_kernels(own):
    n = lax.axis_size("coil")
    blocks = {0: own}
    distance = n // 2
    while distance:
        for i in sorted(blocks):
            blocks[i ^ distance] = swap(blocks[i], "coil", distance)
        distance //= 2
    return [blocks[i] for i in range(n)]


def spread_summary(ids, mine, cols, backward):
    chips = lax.axis_size("seg") // 2
    other = swap(mine, "seg", 1)
    half = compose(ids, mine, other, cols, backward)
    near = [half] + [swap(half, "seg", 2 * i) for i in range(1, chips)]
    far = [swap(part, "seg", 1) for part in near]
    return mine, other, near, far


def shards(measured, forward_kernel, backward_kernel, line_offsets):
    n = lax.axis_size("coil")
    places = lax.axis_size("seg")
    coil, seg = lax.axis_index("coil"), lax.axis_index("seg")
    taps = line_offsets.shape[2]
    width = measured.shape[4] // n
    cols = forward_kernel.shape[3] * n
    ids = jnp.stack([coil, seg // 2, seg % 2]).astype(jnp.int32)
    kernels_f, kernels_b = (jnp.swapaxes(k, 2, 3) for k in (forward_kernel, backward_kernel))
    aligned = width % LANES == 0 and (cols // taps // n) % 8 == 0
    if aligned:
        order = ids
        forward_blocks = spread_kernels(kernels_f)
        pieces = pack(measured, ids)
        lines_blocks = [pieces[0]] + [swap(pieces[i], "coil", i) for i in range(1, n)]
    else:
        order = ids * jnp.array([0, 1, 1], jnp.int32)
        forward_blocks = list(lax.all_gather(kernels_f, "coil"))
        split = lax.all_to_all(measured, "coil", split_axis=4, concat_axis=2, tiled=True)
        split = jnp.pad(split, [(0, 0)] * 4 + [(0, -width % LANES)])
        lines_blocks = jnp.split(split, n, axis=2)
    kernels_b, first, last = hold(lines_blocks[1], kernels_b, line_offsets)
    after = lax.ppermute(first, "seg", [(i + 1, i) for i in range(places - 1)])
    before = lax.ppermute(last, "seg", [(i, i + 1) for i in range(places - 1)])
    offsets = jnp.concatenate([line_offsets[:, 0], line_offsets[:, 1], after, before])
    lines = gather(order, lines_blocks)
    forward_maps = prepare(order, offsets, forward_blocks, False)
    mine = summary(offsets, forward_maps, lines)
    backward_blocks = spread_kernels(kernels_b) if aligned else list(lax.all_gather(kernels_b, "coil"))
    backward_maps = prepare(order, offsets, backward_blocks, True)
    shared = spread_summary(ids, mine, cols, False)
    *forward_out, forward, mine = finish(order, offsets, forward_maps, lines, *shared, False, backward_maps)
    shared = spread_summary(ids, mine, cols, True)

    def home(blocks):
        return [blocks[0]] + [swap(blocks[i], "coil", i) for i in range(1, n)]

    if aligned:
        *result_out, _, forward = finish(order, offsets, backward_maps, forward, *shared, True, arrived=home(forward_out))
        return forward, unpack(home(result_out), ids)
    *result_out, _ = finish(order, offsets, backward_maps, forward, *shared, True)

    def rejoin(blocks):
        states = lax.all_to_all(jnp.stack(blocks), "coil", split_axis=0, concat_axis=0)[..., :width]
        states = jnp.moveaxis(states, 0, 4)
        return states.reshape(states.shape[:4] + (n * width,))

    return rejoin(forward_out), rejoin(result_out)


def solution(mesh):
    placed = (
        P("seg", None, "coil", None, None),
        P("seg", None, None, "coil"),
        P("seg", None, None, "coil"),
        P("seg", None, None),
    )
    return jax.shard_map(
        shards,
        mesh=mesh,
        in_specs=placed,
        out_specs=(P("seg", None, "coil", None, None), P("seg", None, "coil", None, None)),
        check_vma=False,
    )
```

time: 288 us -> 81.3 us (0.28)
  the two profiles are of different devices: /device:TPU:3 before, /device:TPU:0 now
where the time goes in v2:
time: 81.3 us; the launch traced here: 81 us
  starting transfers between devices  37.6 us (46%)
  waiting for transfers between devices  26.8 us (33%)
  Pallas kernels  14.5 us (18%)
  local copies, waits for them, and re-layouts  1.15 us (1%)
  between operations  0.85 us (1%)
    ppermute x31, starting transfers between devices, swap(): lax.ppermute(block, axis, [(i, i ^ distance) for i in range(lax.axis_size...  34.4 us
    ppermute x31, waiting for transfers between devices, swap(): lax.ppermute(block, axis, [(i, i ^ distance) for i in range(lax.axis_size...  26.6 us
    pallas_call x2, Pallas kernels, finish(): call(body, 'finish_backward' if backward else 'finish_forward', out_shape...  6.68 us
    pallas_call x2, Pallas kernels, prepare(): call(body, 'prepare_backward' if backward else 'prepare_forward', [((segs...  2.47 us
    ppermute x1, starting transfers between devices, shards(): before = lax.ppermute(last, 'seg', [(i, i + 1) for i in range(places - 1)])  1.86 us
    pallas_call x2, Pallas kernels, compose(): call(body, 'compose_backward' if backward else 'compose_forward', [((size...  1.71 us
  transfers between devices with their start and end apart: 33, of which 14 were waited for; matrix products, arithmetic and copies ran while one was open for 0% of the time, Pallas kernels for 5%

profile of v2, /device:TPU:0, one launch (start us, length us, event | category | flops | bytes accessed | tf_op | source)
XLA Modules:
  0.0 81.0 jit_solution(16312407512267621843)
XLA Ops:
  0.6 4.1 %collective-permute-start.7 = (f32[2,2,32,256]{3,2,1,0:T(8,128)}, f32[2,2,32,256]{3,2,1,0:T(8,128)S(1)}, u32[]{:S(2)}, u32[]{:S(2)}) collective-permute-start(f32[2,2,32,256]{3,2,1,0:T(8,128)} %bitcast.7), channel_id=1, source_target_pairs={{0,2},{1,3},{2,0},{3,1},{4,6},{5,7},{6,4},{7,5},{8,10},{9,11},{10,... | collective-permute-start | bytes 393224 | tf_op jit(solution)/shard_map/ppermute | solution.py:314
  4.7 1.6 %collective-permute-start.6 = (f32[2,2,32,256]{3,2,1,0:T(8,128)}, f32[2,2,32,256]{3,2,1,0:T(8,128)S(1)}, u32[]{:S(2)}, u32[]{:S(2)}) collective-permute-start(f32[2,2,32,256]{3,2,1,0:T(8,128)} %bitcast.8), channel_id=1, source_target_pairs={{0,1},{1,0},{2,3},{3,2},{4,5},{5,4},{6,7},{7,6},{8,9},{9,8},{10,11... | collective-permute-start | bytes 393224 | tf_op jit(solution)/shard_map/ppermute | solution.py:314
  6.3 0.1 pad_add_fusion.1.ids_ref
  6.4 1.0 %copy-done = f32[2,2,8,8,512]{4,3,2,1,0:T(8,128)S(1)} copy-done((f32[2,2,8,8,512]{4,3,2,1,0:T(8,128)S(1)}, f32[2,2,8,8,512]{4,3,2,1,0:T(8,128)}, u32[]{:S(2)}) %copy-start) | copy-done | bytes 524312
  7.4 0.7 pack.1
  8.1 0.0 copy-start.3
  8.1 0.5 collective-permute-start
  8.6 0.1 collective-permute-start.9
  8.7 3.9 %collective-permute-start.10 = (f32[2,2,8,8,128]{4,3,2,1,0:T(8,128)S(1)}, f32[2,2,8,8,128]{4,3,2,1,0:T(8,128)S(1)}, u32[]{:S(2)}, u32[]{:S(2)}) collective-permute-start(f32[2,2,8,8,128]{4,3,2,1,0:T(8,128)S(1)} %get-tuple-element.36), channel_id=1, source_target_pairs={{0,3},{1,2},{2,1},{3,0},{4,7},{5,6},{6,5},{7,4},{8,11},{9,10},{10,... | collective-permute-start | bytes 393224 | tf_op jit(solution)/shard_map/ppermute | solution.py:314
  12.6 0.0 collective-permute-done.7.refs_2_
  12.6 0.0 collective-permute-start.8
  12.6 5.4 %collective-permute-done._.refs_1_ = f32[2,2,8,8,128]{4,3,2,1,0:T(8,128)S(1)} collective-permute-done((f32[2,2,8,8,128]{4,3,2,1,0:T(8,128)S(1)}, f32[2,2,8,8,128]{4,3,2,1,0:T(8,128)S(1)}, u32[]{:S(2)}, u32[]{:S(2)}) %collective-permute-start) | collective-permute-done | bytes 131104 | tf_op jit(solution)/shard_map/ppermute | solution.py:314
  18.0 1.3 %collective-permute-start.1 = (s32[1,4]{1,0:T(1,128)S(1)}, s32[1,4]{1,0:T(1,128)S(1)}, u32[]{:S(2)}, u32[]{:S(2)}) collective-permute-start(s32[1,4]{1,0:T(1,128)S(1)} %get-tuple-element.27), channel_id=1, source_target_pairs={{4,0},{8,4},{12,8},{16,12},{20,16},{24,20},{28,24},{5,1},{9,5},{13... | collective-permute-start | bytes 56 | tf_op jit(solution)/shard_map/ppermute | solution.py:359
  19.3 1.2 %collective-permute-done.9.refs_2_ = f32[2,2,8,8,128]{4,3,2,1,0:T(8,128)S(1)} collective-permute-done((f32[2,2,8,8,128]{4,3,2,1,0:T(8,128)S(1)}, f32[2,2,8,8,128]{4,3,2,1,0:T(8,128)S(1)}, u32[]{:S(2)}, u32[]{:S(2)}) %collective-permute-start.9) | collective-permute-done | bytes 131104 | tf_op jit(solution)/shard_map/ppermute | solution.py:314
  20.5 1.9 %collective-permute-start.2 = (s32[1,4]{1,0:T(1,128)S(1)}, s32[1,4]{1,0:T(1,128)S(1)}, u32[]{:S(2)}, u32[]{:S(2)}) collective-permute-start(s32[1,4]{1,0:T(1,128)S(1)} %get-tuple-element.28), channel_id=1, source_target_pairs={{0,4},{4,8},{8,12},{12,16},{16,20},{20,24},{24,28},{1,5},{5,9},{9,... | collective-permute-start | bytes 56 | tf_op jit(solution)/shard_map/ppermute | solution.py:360
  22.3 0.0 collective-permute-done.10.refs_3_
  22.3 0.0 copy-start.1
  22.4 0.6 gather.1.m_ref
  23.0 0.2 collective-permute-done.2
  23.1 0.0 collective-permute-done.6.refs_1_
  23.2 0.1 copy-done.1
  23.2 1.2 %prepare_forward.1 = (bf16[2,512,256]{2,1,0:T(8,128)(2,1)S(1)}, bf16[2,512,256]{2,1,0:T(8,128)(2,1)S(1)}, f32[256,128]{1,0:T(8,128)S(1)}) custom-call(s32[3]{0:T(128)S(1)} %pad_add_fusion.1.ids_ref, s32[6,4]{1,0:T(8,128)S(1)} %pad_add_fusion.off_ref, f32[2,2,32,256]{3,2,1,0:T(8,128)S(1)} %bitcast.9, f32[2,2,32,256]{3,2,1,0:T(8,128)S(1)} %collective-permute-done.6.refs_1_, ...), custom_call_target="tpu_custom_call" | custom-call | tf_op jit(solution)/shard_map/prepare_forward/pallas_call | solution.py:147
  24.5 1.1 %summary.1.a_ref = f32[256,256]{1,0:T(8,128)S(1)} custom-call(s32[6,4]{1,0:T(8,128)S(1)} %pad_add_fusion.off_ref, bf16[2,512,256]{2,1,0:T(8,128)(2,1)S(1)} %get-tuple-element.32.hi_ref, bf16[2,512,256]{2,1,0:T(8,128)(2,1)S(1)} %get-tuple-element.33.lo_ref, f32[256,128]{1,0:T(8,128)S(1)} %get-tuple-element.37.c_ref, f32[2,2,32,8,128]{4,3,2,1,0:T(8,128)S(1)} %gather.1.m_ref), custom_call_target="tpu_custom_call" | custom-call | tf_op jit(solution)/shard_map/summary/pallas_call | solution.py:167
  25.6 1.8 %collective-permute-start.11 = (f32[256,256]{1,0:T(8,128)S(1)}, f32[256,256]{1,0:T(8,128)S(1)}, u32[]{:S(2)}, u32[]{:S(2)}) collective-permute-start(f32[256,256]{1,0:T(8,128)S(1)} %summary.1.a_ref), channel_id=1, source_target_pairs={{0,4},{4,0},{8,12},{12,8},{16,20},{20,16},{24,28},{28,24},{1,5},{5... | collective-permute-start | bytes 786440 | tf_op jit(solution)/shard_map/ppermute | solution.py:314
  27.4 1.2 %collective-permute-start.4 = (f32[2,2,32,256]{3,2,1,0:T(8,128)S(1)}, f32[2,2,32,256]{3,2,1,0:T(8,128)S(1)}, u32[]{:S(2)}, u32[]{:S(2)}) collective-permute-start(f32[2,2,32,256]{3,2,1,0:T(8,128)S(1)} %get-tuple-element.29.refs_0_), channel_id=1, source_target_pairs={{0,2},{1,3},{2,0},{3,1},{4,6},{5,7},{6,4},{7,5},{8,10},{9,11},{10,... | collective-permute-start | bytes 393224 | tf_op jit(solution)/shard_map/ppermute | solution.py:314
  28.5 3.6 %collective-permute-start.3 = (f32[2,2,32,256]{3,2,1,0:T(8,128)S(1)}, f32[2,2,32,256]{3,2,1,0:T(8,128)S(1)}, u32[]{:S(2)}, u32[]{:S(2)}) collective-permute-start(f32[2,2,32,256]{3,2,1,0:T(8,128)S(1)} %get-tuple-element.29.refs_0_), channel_id=1, source_target_pairs={{0,1},{1,0},{2,3},{3,2},{4,5},{5,4},{6,7},{7,6},{8,9},{9,8},{10,11... | collective-permute-start | bytes 393224 | tf_op jit(solution)/shard_map/ppermute | solution.py:314
  32.1 0.0 collective-permute-done.11.b_ref
  32.1 0.9 %compose_forward.1.refs_0_ = f32[128,256]{1,0:T(8,128)S(1)} custom-call(s32[3]{0:T(128)S(1)} %pad_add_fusion.1.ids_ref, f32[256,256]{1,0:T(8,128)S(1)} %summary.1.a_ref, f32[256,256]{1,0:T(8,128)S(1)} %collective-permute-done.11.b_ref), custom_call_target="tpu_custom_call" | custom-call | tf_op jit(solution)/shard_map/compose_forward/pallas_call | solution.py:189
  33.0 3.1 %collective-permute-start.14 = (f32[128,256]{1,0:T(8,128)S(1)}, f32[128,256]{1,0:T(8,128)S(1)}, u32[]{:S(2)}, u32[]{:S(2)}) collective-permute-start(f32[128,256]{1,0:T(8,128)S(1)} %compose_forward.1.refs_0_), channel_id=1, source_target_pairs={{0,24},{4,28},{8,16},{12,20},{16,8},{20,12},{24,0},{28,4},{1,25},{... | collective-permute-start | bytes 393224 | tf_op jit(solution)/shard_map/ppermute | solution.py:314
  36.0 0.5 collective-permute-start.13
  36.5 0.9 %collective-permute-start.12 = (f32[128,256]{1,0:T(8,128)S(1)}, f32[128,256]{1,0:T(8,128)S(1)}, u32[]{:S(2)}, u32[]{:S(2)}) collective-permute-start(f32[128,256]{1,0:T(8,128)S(1)} %compose_forward.1.refs_0_), channel_id=1, source_target_pairs={{0,8},{4,12},{8,0},{12,4},{16,24},{20,28},{24,16},{28,20},{1,9},{5... | collective-permute-start | bytes 393224 | tf_op jit(solution)/shard_map/ppermute | solution.py:314
  37.5 0.0 collective-permute-start.5
  37.5 0.0 collective-permute-done.3.refs_1_
  37.5 0.1 collective-permute-start.15
  37.5 2.4 %collective-permute-done.14.refs_3_ = f32[128,256]{1,0:T(8,128)S(1)} collective-permute-done((f32[128,256]{1,0:T(8,128)S(1)}, f32[128,256]{1,0:T(8,128)S(1)}, u32[]{:S(2)}, u32[]{:S(2)}) %collective-permute-start.14) | collective-permute-done | bytes 131104 | tf_op jit(solution)/shard_map/ppermute | solution.py:314
  39.9 0.0 collective-permute-start.18
  39.9 2.5 %collective-permute-done.13.refs_2_ = f32[128,256]{1,0:T(8,128)S(1)} collective-permute-done((f32[128,256]{1,0:T(8,128)S(1)}, f32[128,256]{1,0:T(8,128)S(1)}, u32[]{:S(2)}, u32[]{:S(2)}) %collective-permute-start.13) | collective-permute-done | bytes 131104 | tf_op jit(solution)/shard_map/ppermute | solution.py:314
  42.4 0.0 collective-permute-start.17
  42.4 1.2 %collective-permute-done.12.refs_1_ = f32[128,256]{1,0:T(8,128)S(1)} collective-permute-done((f32[128,256]{1,0:T(8,128)S(1)}, f32[128,256]{1,0:T(8,128)S(1)}, u32[]{:S(2)}, u32[]{:S(2)}) %collective-permute-start.12) | collective-permute-done | bytes 131104 | tf_op jit(solution)/shard_map/ppermute | solution.py:314
  43.6 1.2 %prepare_backward.1 = (bf16[2,512,256]{2,1,0:T(8,128)(2,1)S(1)}, bf16[2,512,256]{2,1,0:T(8,128)(2,1)S(1)}, f32[256,128]{1,0:T(8,128)S(1)}) custom-call(s32[3]{0:T(128)S(1)} %pad_add_fusion.1.ids_ref, s32[6,4]{1,0:T(8,128)S(1)} %pad_add_fusion.off_ref, f32[2,2,32,256]{3,2,1,0:T(8,128)S(1)} %get-tuple-element.29.refs_0_, ...), custom_call_target="tpu_custom_call" | custom-call | tf_op jit(solution)/shard_map/prepare_backward/pallas_call | solution.py:147
  44.8 0.1 collective-permute-done.16.refs_5_
  44.9 3.0 %finish_forward.1 = (f32[2,2,8,8,128]{4,3,2,1,0:T(8,128)S(1)}, f32[2,2,8,8,128]{4,3,2,1,0:T(8,128)S(1)}, f32[2,2,8,8,128]{4,3,2,1,0:T(8,128)S(1)}, f32[2,2,8,8,1...) custom-call(s32[3]{0:T(128)S(1)} %pad_add_fusion.1.ids_ref, ...), custom_call_target="tpu_custom_call" | custom-call | tf_op jit(solution)/shard_map/finish_forward/pallas_call | solution.py:267
  47.9 0.5 collective-permute-start.19
  48.4 0.3 collective-permute-start.27
  48.7 1.4 %collective-permute-start.28 = (f32[2,2,8,8,128]{4,3,2,1,0:T(8,128)S(1)}, f32[2,2,8,8,128]{4,3,2,1,0:T(8,128)S(1)}, u32[]{:S(2)}, u32[]{:S(2)}) collective-permute-start(f32[2,2,8,8,128]{4,3,2,1,0:T(8,128)S(1)} %get-tuple-element.43), channel_id=1, source_target_pairs={{0,2},{1,3},{2,0},{3,1},{4,6},{5,7},{6,4},{7,5},{8,10},{9,11},{10,... | collective-permute-start | bytes 393224 | tf_op jit(solution)/shard_map/ppermute | solution.py:314
  50.1 0.9 %compose_backward.1.refs_0_ = f32[128,256]{1,0:T(8,128)S(1)} custom-call(s32[3]{0:T(128)S(1)} %pad_add_fusion.1.ids_ref, f32[256,256]{1,0:T(8,128)S(1)} %get-tuple-element.40.a_ref, f32[256,256]{1,0:T(8,128)S(1)} %collective-permute-done.19.b_ref), custom_call_target="tpu_custom_call" | custom-call | tf_op jit(solution)/shard_map/compose_backward/pallas_call | solution.py:189
  51.0 2.4 %collective-permute-start.22 = (f32[128,256]{1,0:T(8,128)S(1)}, f32[128,256]{1,0:T(8,128)S(1)}, u32[]{:S(2)}, u32[]{:S(2)}) collective-permute-start(f32[128,256]{1,0:T(8,128)S(1)} %compose_backward.1.refs_0_), channel_id=1, source_target_pairs={{0,24},{4,28},{8,16},{12,20},{16,8},{20,12},{24,0},{28,4},{1,25},{... | collective-permute-start | bytes 393224 | tf_op jit(solution)/shard_map/ppermute | solution.py:314
  53.4 0.5 collective-permute-start.21
  53.9 0.9 %collective-permute-start.20 = (f32[128,256]{1,0:T(8,128)S(1)}, f32[128,256]{1,0:T(8,128)S(1)}, u32[]{:S(2)}, u32[]{:S(2)}) collective-permute-start(f32[128,256]{1,0:T(8,128)S(1)} %compose_backward.1.refs_0_), channel_id=1, source_target_pairs={{0,8},{4,12},{8,0},{12,4},{16,24},{20,28},{24,16},{28,20},{1,9},{5... | collective-permute-start | bytes 393224 | tf_op jit(solution)/shard_map/ppermute | solution.py:314
  54.8 0.7 collective-permute-done.27.refs_9_
  55.5 2.1 %collective-permute-start.29 = (f32[2,2,8,8,128]{4,3,2,1,0:T(8,128)S(1)}, f32[2,2,8,8,128]{4,3,2,1,0:T(8,128)S(1)}, u32[]{:S(2)}, u32[]{:S(2)}) collective-permute-start(f32[2,2,8,8,128]{4,3,2,1,0:T(8,128)S(1)} %get-tuple-element.44), channel_id=1, source_target_pairs={{0,3},{1,2},{2,1},{3,0},{4,7},{5,6},{6,5},{7,4},{8,11},{9,10},{10,... | collective-permute-start | bytes 393224 | tf_op jit(solution)/shard_map/ppermute | solution.py:314
  57.6 1.2 %collective-permute-done.28.refs_10_ = f32[2,2,8,8,128]{4,3,2,1,0:T(8,128)S(1)} collective-permute-done((f32[2,2,8,8,128]{4,3,2,1,0:T(8,128)S(1)}, f32[2,2,8,8,128]{4,3,2,1,0:T(8,128)S(1)}, u32[]{:S(2)}, u32[]{:S(2)}) %collective-permute-start.28) | collective-permute-done | bytes 131104 | tf_op jit(solution)/shard_map/ppermute | solution.py:314
  58.8 0.5 collective-permute-start.26
  59.3 0.7 collective-permute-done.21.refs_2_
  60.0 0.0 collective-permute-start.25
  60.0 0.9 %collective-permute-done.20.refs_1_ = f32[128,256]{1,0:T(8,128)S(1)} collective-permute-done((f32[128,256]{1,0:T(8,128)S(1)}, f32[128,256]{1,0:T(8,128)S(1)}, u32[]{:S(2)}, u32[]{:S(2)}) %collective-permute-start.20) | collective-permute-done | bytes 131104 | tf_op jit(solution)/shard_map/ppermute | solution.py:314
  60.9 1.4 %collective-permute-done.29.refs_11_ = f32[2,2,8,8,128]{4,3,2,1,0:T(8,128)S(1)} collective-permute-done((f32[2,2,8,8,128]{4,3,2,1,0:T(8,128)S(1)}, f32[2,2,8,8,128]{4,3,2,1,0:T(8,128)S(1)}, u32[]{:S(2)}, u32[]{:S(2)}) %collective-permute-start.29) | collective-permute-done | bytes 131104 | tf_op jit(solution)/shard_map/ppermute | solution.py:314
  62.3 3.7 %finish_backward.1 = (f32[2,2,8,8,128]{4,3,2,1,0:T(8,128)S(1)}, f32[2,2,8,8,128]{4,3,2,1,0:T(8,128)S(1)}, f32[2,2,8,8,128]{4,3,2,1,0:T(8,128)S(1)}, f32[2,2,8,8,...) custom-call(s32[3]{0:T(128)S(1)} %pad_add_fusion.1.ids_ref, ...), custom_call_target="tpu_custom_call" | custom-call | tf_op jit(solution)/shard_map/finish_backward/pallas_call | solution.py:267
  66.1 1.7 %collective-permute-start.30 = (f32[2,2,8,8,128]{4,3,2,1,0:T(8,128)S(1)}, f32[2,2,8,8,128]{4,3,2,1,0:T(8,128)S(1)}, u32[]{:S(2)}, u32[]{:S(2)}) collective-permute-start(f32[2,2,8,8,128]{4,3,2,1,0:T(8,128)S(1)} %get-tuple-element.47), channel_id=1, source_target_pairs={{0,1},{1,0},{2,3},{3,2},{4,5},{5,4},{6,7},{7,6},{8,9},{9,8},{10,11... | collective-permute-start | bytes 393224 | tf_op jit(solution)/shard_map/ppermute | solution.py:314
  67.7 1.2 %collective-permute-start.31 = (f32[2,2,8,8,128]{4,3,2,1,0:T(8,128)S(1)}, f32[2,2,8,8,128]{4,3,2,1,0:T(8,128)S(1)}, u32[]{:S(2)}, u32[]{:S(2)}) collective-permute-start(f32[2,2,8,8,128]{4,3,2,1,0:T(8,128)S(1)} %get-tuple-element.48), channel_id=1, source_target_pairs={{0,2},{1,3},{2,0},{3,1},{4,6},{5,7},{6,4},{7,5},{8,10},{9,11},{10,... | collective-permute-start | bytes 393224 | tf_op jit(solution)/shard_map/ppermute | solution.py:314
  68.9 1.6 %collective-permute-start.32 = (f32[2,2,8,8,128]{4,3,2,1,0:T(8,128)S(1)}, f32[2,2,8,8,128]{4,3,2,1,0:T(8,128)S(1)}, u32[]{:S(2)}, u32[]{:S(2)}) collective-permute-start(f32[2,2,8,8,128]{4,3,2,1,0:T(8,128)S(1)} %get-tuple-element.49), channel_id=1, source_target_pairs={{0,3},{1,2},{2,1},{3,0},{4,7},{5,6},{6,5},{7,4},{8,11},{9,10},{10,... | collective-permute-start | bytes 393224 | tf_op jit(solution)/shard_map/ppermute | solution.py:314
  70.5 2.7 %collective-permute-done.30.refs_1_ = f32[2,2,8,8,128]{4,3,2,1,0:T(8,128)S(1)} collective-permute-done((f32[2,2,8,8,128]{4,3,2,1,0:T(8,128)S(1)}, f32[2,2,8,8,128]{4,3,2,1,0:T(8,128)S(1)}, u32[]{:S(2)}, u32[]{:S(2)}) %collective-permute-start.30) | collective-permute-done | bytes 131104 | tf_op jit(solution)/shard_map/ppermute | solution.py:314
  73.3 6.4 %collective-permute-done.31.refs_2_ = f32[2,2,8,8,128]{4,3,2,1,0:T(8,128)S(1)} collective-permute-done((f32[2,2,8,8,128]{4,3,2,1,0:T(8,128)S(1)}, f32[2,2,8,8,128]{4,3,2,1,0:T(8,128)S(1)}, u32[]{:S(2)}, u32[]{:S(2)}) %collective-permute-start.31) | collective-permute-done | bytes 131104 | tf_op jit(solution)/shard_map/ppermute | solution.py:314
  79.7 1.4 %unpack.1 = f32[2,2,8,8,512]{4,3,2,1,0:T(8,128)} custom-call(s32[3]{0:T(128)S(1)} %pad_add_fusion.1.ids_ref, f32[2,2,8,8,128]{4,3,2,1,0:T(8,128)S(1)} %get-tuple-element.46.refs_0_, f32[2,2,8,8,128]{4,3,2,1,0:T(8,128)S(1)} %collective-permute-done.30.refs_1_, f32[2,2,8,8,128]{4,3,2,1,0:T(8,128)S(1)} %collective-permute-done.31.refs_2_, ...), custom_call_target="tpu_custom_call" | custom-call | tf_op jit(solution)/shard_map/unpack/pallas_call | solution.py:303
  (24 shorter events, 0.1 us)
Async XLA Ops:
  0.6 11.9 %collective-permute-start.7 = (f32[2,2,32,256]{3,2,1,0:T(8,128)}, f32[2,2,32,256]{3,2,1,0:T(8,128)S(1)}, u32[]{:S(2)}, u32[]{:S(2)}) collective-permute-start(f32[2,2,32,256]{3,2,1,0:T(8,128)} %bitcast.7), channel_id=1, source_target_pairs={{0,2},{1,3},{2,0},{3,1},{4,6},{5,7},{6,4},{7,5},{8,10},{9,11},{10,... | collective-permute-start | bytes 393224 | tf_op jit(solution)/shard_map/ppermute | solution.py:314
  4.7 18.4 %collective-permute-start.6 = (f32[2,2,32,256]{3,2,1,0:T(8,128)}, f32[2,2,32,256]{3,2,1,0:T(8,128)S(1)}, u32[]{:S(2)}, u32[]{:S(2)}) collective-permute-start(f32[2,2,32,256]{3,2,1,0:T(8,128)} %bitcast.8), channel_id=1, source_target_pairs={{0,1},{1,0},{2,3},{3,2},{4,5},{5,4},{6,7},{7,6},{8,9},{9,8},{10,11... | collective-permute-start | bytes 393224 | tf_op jit(solution)/shard_map/ppermute | solution.py:314
  6.4 1.0 %copy-start = (f32[2,2,8,8,512]{4,3,2,1,0:T(8,128)S(1)}, f32[2,2,8,8,512]{4,3,2,1,0:T(8,128)}, u32[]{:S(2)}) copy-start(f32[2,2,8,8,512]{4,3,2,1,0:T(8,128)} %m_ref.1) | copy-start | bytes 1572868
  7.4 10.5 %copy-start.2 = (f32[2,2,256,32]{2,3,1,0:T(8,128)S(1)}, f32[2,2,256,32]{2,3,1,0:T(8,128)}, u32[]{:S(2)}) copy-start(f32[2,2,256,32]{2,3,1,0:T(8,128)} %param.6) | copy-start | bytes 393220
  8.1 4.5 %copy-start.3 = (s32[2,2,4]{2,1,0:T(2,128)S(1)}, s32[2,2,4]{2,1,0:T(2,128)}, u32[]{:S(2)}) copy-start(s32[2,2,4]{2,1,0:T(2,128)} %o_ref.1) | copy-start | bytes 196
  8.1 9.8 %collective-permute-start = (f32[2,2,8,8,128]{4,3,2,1,0:T(8,128)S(1)}, f32[2,2,8,8,128]{4,3,2,1,0:T(8,128)S(1)}, u32[]{:S(2)}, u32[]{:S(2)}) collective-permute-start(f32[2,2,8,8,128]{4,3,2,1,0:T(8,128)S(1)} %get-tuple-element.26), channel_id=1, source_target_pairs={{0,1},{1,0},{2,3},{3,2},{4,5},{5,4},{6,7},{7,6},{8,9},{9,8},{10,11... | collective-permute-start | bytes 393224 | tf_op jit(solution)/shard_map/ppermute | solution.py:314
  8.6 11.8 %collective-permute-start.9 = (f32[2,2,8,8,128]{4,3,2,1,0:T(8,128)S(1)}, f32[2,2,8,8,128]{4,3,2,1,0:T(8,128)S(1)}, u32[]{:S(2)}, u32[]{:S(2)}) collective-permute-start(f32[2,2,8,8,128]{4,3,2,1,0:T(8,128)S(1)} %get-tuple-element.35), channel_id=1, source_target_pairs={{0,2},{1,3},{2,0},{3,1},{4,6},{5,7},{6,4},{7,5},{8,10},{9,11},{10,... | collective-permute-start | bytes 393224 | tf_op jit(solution)/shard_map/ppermute | solution.py:314
  8.7 13.6 %collective-permute-start.10 = (f32[2,2,8,8,128]{4,3,2,1,0:T(8,128)S(1)}, f32[2,2,8,8,128]{4,3,2,1,0:T(8,128)S(1)}, u32[]{:S(2)}, u32[]{:S(2)}) collective-permute-start(f32[2,2,8,8,128]{4,3,2,1,0:T(8,128)S(1)} %get-tuple-element.36), channel_id=1, source_target_pairs={{0,3},{1,2},{2,1},{3,0},{4,7},{5,6},{6,5},{7,4},{8,11},{9,10},{10,... | collective-permute-start | bytes 393224 | tf_op jit(solution)/shard_map/ppermute | solution.py:314
  12.6 10.6 %collective-permute-start.8 = (f32[2,2,32,256]{3,2,1,0:T(8,128)S(1)}, f32[2,2,32,256]{3,2,1,0:T(8,128)S(1)}, u32[]{:S(2)}, u32[]{:S(2)}) collective-permute-start(f32[2,2,32,256]{3,2,1,0:T(8,128)S(1)} %collective-permute-done.7.refs_2_), channel_id=1, source_target_pairs={{0,1},{1,0},{2,3},{3,2},{4,5},{5,4},{6,7},{7,6},{8,9},{9,8},{10,11... | collective-permute-start | bytes 393224 | tf_op jit(solution)/shard_map/ppermute | solution.py:314
  18.0 5.0 %collective-permute-start.1 = (s32[1,4]{1,0:T(1,128)S(1)}, s32[1,4]{1,0:T(1,128)S(1)}, u32[]{:S(2)}, u32[]{:S(2)}) collective-permute-start(s32[1,4]{1,0:T(1,128)S(1)} %get-tuple-element.27), channel_id=1, source_target_pairs={{4,0},{8,4},{12,8},{16,12},{20,16},{24,20},{28,24},{5,1},{9,5},{13... | collective-permute-start | bytes 56 | tf_op jit(solution)/shard_map/ppermute | solution.py:359
  20.5 2.7 %collective-permute-start.2 = (s32[1,4]{1,0:T(1,128)S(1)}, s32[1,4]{1,0:T(1,128)S(1)}, u32[]{:S(2)}, u32[]{:S(2)}) collective-permute-start(s32[1,4]{1,0:T(1,128)S(1)} %get-tuple-element.28), channel_id=1, source_target_pairs={{0,4},{4,8},{8,12},{12,16},{16,20},{20,24},{24,28},{1,5},{5,9},{9,... | collective-permute-start | bytes 56 | tf_op jit(solution)/shard_map/ppermute | solution.py:360
  22.3 0.9 %copy-start.1 = (f32[2,2,256,32]{2,3,1,0:T(8,128)S(1)}, f32[2,2,256,32]{2,3,1,0:T(8,128)}, u32[]{:S(2)}) copy-start(f32[2,2,256,32]{2,3,1,0:T(8,128)} %param.5) | copy-start | bytes 393220
  25.6 6.5 %collective-permute-start.11 = (f32[256,256]{1,0:T(8,128)S(1)}, f32[256,256]{1,0:T(8,128)S(1)}, u32[]{:S(2)}, u32[]{:S(2)}) collective-permute-start(f32[256,256]{1,0:T(8,128)S(1)} %summary.1.a_ref), channel_id=1, source_target_pairs={{0,4},{4,0},{8,12},{12,8},{16,20},{20,16},{24,28},{28,24},{1,5},{5... | collective-permute-start | bytes 786440 | tf_op jit(solution)/shard_map/ppermute | solution.py:314
  27.4 10.1 %collective-permute-start.4 = (f32[2,2,32,256]{3,2,1,0:T(8,128)S(1)}, f32[2,2,32,256]{3,2,1,0:T(8,128)S(1)}, u32[]{:S(2)}, u32[]{:S(2)}) collective-permute-start(f32[2,2,32,256]{3,2,1,0:T(8,128)S(1)} %get-tuple-element.29.refs_0_), channel_id=1, source_target_pairs={{0,2},{1,3},{2,0},{3,1},{4,6},{5,7},{6,4},{7,5},{8,10},{9,11},{10,... | collective-permute-start | bytes 393224 | tf_op jit(solution)/shard_map/ppermute | solution.py:314
  28.5 8.9 %collective-permute-start.3 = (f32[2,2,32,256]{3,2,1,0:T(8,128)S(1)}, f32[2,2,32,256]{3,2,1,0:T(8,128)S(1)}, u32[]{:S(2)}, u32[]{:S(2)}) collective-permute-start(f32[2,2,32,256]{3,2,1,0:T(8,128)S(1)} %get-tuple-element.29.refs_0_), channel_id=1, source_target_pairs={{0,1},{1,0},{2,3},{3,2},{4,5},{5,4},{6,7},{7,6},{8,9},{9,8},{10,11... | collective-permute-start | bytes 393224 | tf_op jit(solution)/shard_map/ppermute | solution.py:314
  33.0 7.0 %collective-permute-start.14 = (f32[128,256]{1,0:T(8,128)S(1)}, f32[128,256]{1,0:T(8,128)S(1)}, u32[]{:S(2)}, u32[]{:S(2)}) collective-permute-start(f32[128,256]{1,0:T(8,128)S(1)} %compose_forward.1.refs_0_), channel_id=1, source_target_pairs={{0,24},{4,28},{8,16},{12,20},{16,8},{20,12},{24,0},{28,4},{1,25},{... | collective-permute-start | bytes 393224 | tf_op jit(solution)/shard_map/ppermute | solution.py:314
  36.0 6.4 %collective-permute-start.13 = (f32[128,256]{1,0:T(8,128)S(1)}, f32[128,256]{1,0:T(8,128)S(1)}, u32[]{:S(2)}, u32[]{:S(2)}) collective-permute-start(f32[128,256]{1,0:T(8,128)S(1)} %compose_forward.1.refs_0_), channel_id=1, source_target_pairs={{0,16},{4,20},{8,24},{12,28},{16,0},{20,4},{24,8},{28,12},{1,17},{... | collective-permute-start | bytes 393224 | tf_op jit(solution)/shard_map/ppermute | solution.py:314
  36.5 7.0 %collective-permute-start.12 = (f32[128,256]{1,0:T(8,128)S(1)}, f32[128,256]{1,0:T(8,128)S(1)}, u32[]{:S(2)}, u32[]{:S(2)}) collective-permute-start(f32[128,256]{1,0:T(8,128)S(1)} %compose_forward.1.refs_0_), channel_id=1, source_target_pairs={{0,8},{4,12},{8,0},{12,4},{16,24},{20,28},{24,16},{28,20},{1,9},{5... | collective-permute-start | bytes 393224 | tf_op jit(solution)/shard_map/ppermute | solution.py:314
  37.5 6.1 %collective-permute-start.5 = (f32[2,2,32,256]{3,2,1,0:T(8,128)S(1)}, f32[2,2,32,256]{3,2,1,0:T(8,128)S(1)}, u32[]{:S(2)}, u32[]{:S(2)}) collective-permute-start(f32[2,2,32,256]{3,2,1,0:T(8,128)S(1)} %collective-permute-done.4.refs_2_), channel_id=1, source_target_pairs={{0,1},{1,0},{2,3},{3,2},{4,5},{5,4},{6,7},{7,6},{8,9},{9,8},{10,11... | collective-permute-start | bytes 393224 | tf_op jit(solution)/shard_map/ppermute | solution.py:314
  37.5 7.3 %collective-permute-start.15 = (f32[128,256]{1,0:T(8,128)S(1)}, f32[128,256]{1,0:T(8,128)S(1)}, u32[]{:S(2)}, u32[]{:S(2)}) collective-permute-start(f32[128,256]{1,0:T(8,128)S(1)} %compose_forward.1.refs_0_), channel_id=1, source_target_pairs={{0,4},{4,0},{8,12},{12,8},{16,20},{20,16},{24,28},{28,24},{1,5},{5... | collective-permute-start | bytes 393224 | tf_op jit(solution)/shard_map/ppermute | solution.py:314
  39.9 4.9 %collective-permute-start.18 = (f32[128,256]{1,0:T(8,128)S(1)}, f32[128,256]{1,0:T(8,128)S(1)}, u32[]{:S(2)}, u32[]{:S(2)}) collective-permute-start(f32[128,256]{1,0:T(8,128)S(1)} %collective-permute-done.14.refs_3_), channel_id=1, source_target_pairs={{0,4},{4,0},{8,12},{12,8},{16,20},{20,16},{24,28},{28,24},{1,5},{5... | collective-permute-start | bytes 393224 | tf_op jit(solution)/shard_map/ppermute | solution.py:314
  42.4 2.5 %collective-permute-start.17 = (f32[128,256]{1,0:T(8,128)S(1)}, f32[128,256]{1,0:T(8,128)S(1)}, u32[]{:S(2)}, u32[]{:S(2)}) collective-permute-start(f32[128,256]{1,0:T(8,128)S(1)} %collective-permute-done.13.refs_2_), channel_id=1, source_target_pairs={{0,4},{4,0},{8,12},{12,8},{16,20},{20,16},{24,28},{28,24},{1,5},{5... | collective-permute-start | bytes 393224 | tf_op jit(solution)/shard_map/ppermute | solution.py:314
  43.6 1.3 %collective-permute-start.16 = (f32[128,256]{1,0:T(8,128)S(1)}, f32[128,256]{1,0:T(8,128)S(1)}, u32[]{:S(2)}, u32[]{:S(2)}) collective-permute-start(f32[128,256]{1,0:T(8,128)S(1)} %collective-permute-done.12.refs_1_), channel_id=1, source_target_pairs={{0,4},{4,0},{8,12},{12,8},{16,20},{20,16},{24,28},{28,24},{1,5},{5... | collective-permute-start | bytes 393224 | tf_op jit(solution)/shard_map/ppermute | solution.py:314
  47.9 2.2 %collective-permute-start.19 = (f32[256,256]{1,0:T(8,128)S(1)}, f32[256,256]{1,0:T(8,128)S(1)}, u32[]{:S(2)}, u32[]{:S(2)}) collective-permute-start(f32[256,256]{1,0:T(8,128)S(1)} %get-tuple-element.40.a_ref), channel_id=1, source_target_pairs={{0,4},{4,0},{8,12},{12,8},{16,20},{20,16},{24,28},{28,24},{1,5},{5... | collective-permute-start | bytes 786440 | tf_op jit(solution)/shard_map/ppermute | solution.py:314
  48.4 7.1 %collective-permute-start.27 = (f32[2,2,8,8,128]{4,3,2,1,0:T(8,128)S(1)}, f32[2,2,8,8,128]{4,3,2,1,0:T(8,128)S(1)}, u32[]{:S(2)}, u32[]{:S(2)}) collective-permute-start(f32[2,2,8,8,128]{4,3,2,1,0:T(8,128)S(1)} %get-tuple-element.42), channel_id=1, source_target_pairs={{0,1},{1,0},{2,3},{3,2},{4,5},{5,4},{6,7},{7,6},{8,9},{9,8},{10,11... | collective-permute-start | bytes 393224 | tf_op jit(solution)/shard_map/ppermute | solution.py:314
  48.7 10.1 %collective-permute-start.28 = (f32[2,2,8,8,128]{4,3,2,1,0:T(8,128)S(1)}, f32[2,2,8,8,128]{4,3,2,1,0:T(8,128)S(1)}, u32[]{:S(2)}, u32[]{:S(2)}) collective-permute-start(f32[2,2,8,8,128]{4,3,2,1,0:T(8,128)S(1)} %get-tuple-element.43), channel_id=1, source_target_pairs={{0,2},{1,3},{2,0},{3,1},{4,6},{5,7},{6,4},{7,5},{8,10},{9,11},{10,... | collective-permute-start | bytes 393224 | tf_op jit(solution)/shard_map/ppermute | solution.py:314
  51.0 7.8 %collective-permute-start.22 = (f32[128,256]{1,0:T(8,128)S(1)}, f32[128,256]{1,0:T(8,128)S(1)}, u32[]{:S(2)}, u32[]{:S(2)}) collective-permute-start(f32[128,256]{1,0:T(8,128)S(1)} %compose_backward.1.refs_0_), channel_id=1, source_target_pairs={{0,24},{4,28},{8,16},{12,20},{16,8},{20,12},{24,0},{28,4},{1,25},{... | collective-permute-start | bytes 393224 | tf_op jit(solution)/shard_map/ppermute | solution.py:314
  53.4 6.6 %collective-permute-start.21 = (f32[128,256]{1,0:T(8,128)S(1)}, f32[128,256]{1,0:T(8,128)S(1)}, u32[]{:S(2)}, u32[]{:S(2)}) collective-permute-start(f32[128,256]{1,0:T(8,128)S(1)} %compose_backward.1.refs_0_), channel_id=1, source_target_pairs={{0,16},{4,20},{8,24},{12,28},{16,0},{20,4},{24,8},{28,12},{1,17},{... | collective-permute-start | bytes 393224 | tf_op jit(solution)/shard_map/ppermute | solution.py:314
  53.9 7.0 %collective-permute-start.20 = (f32[128,256]{1,0:T(8,128)S(1)}, f32[128,256]{1,0:T(8,128)S(1)}, u32[]{:S(2)}, u32[]{:S(2)}) collective-permute-start(f32[128,256]{1,0:T(8,128)S(1)} %compose_backward.1.refs_0_), channel_id=1, source_target_pairs={{0,8},{4,12},{8,0},{12,4},{16,24},{20,28},{24,16},{28,20},{1,9},{5... | collective-permute-start | bytes 393224 | tf_op jit(solution)/shard_map/ppermute | solution.py:314
  55.5 6.8 %collective-permute-start.29 = (f32[2,2,8,8,128]{4,3,2,1,0:T(8,128)S(1)}, f32[2,2,8,8,128]{4,3,2,1,0:T(8,128)S(1)}, u32[]{:S(2)}, u32[]{:S(2)}) collective-permute-start(f32[2,2,8,8,128]{4,3,2,1,0:T(8,128)S(1)} %get-tuple-element.44), channel_id=1, source_target_pairs={{0,3},{1,2},{2,1},{3,0},{4,7},{5,6},{6,5},{7,4},{8,11},{9,10},{10,... | collective-permute-start | bytes 393224 | tf_op jit(solution)/shard_map/ppermute | solution.py:314
  58.8 3.5 %collective-permute-start.23 = (f32[128,256]{1,0:T(8,128)S(1)}, f32[128,256]{1,0:T(8,128)S(1)}, u32[]{:S(2)}, u32[]{:S(2)}) collective-permute-start(f32[128,256]{1,0:T(8,128)S(1)} %compose_backward.1.refs_0_), channel_id=1, source_target_pairs={{0,4},{4,0},{8,12},{12,8},{16,20},{20,16},{24,28},{28,24},{1,5},{5... | collective-permute-start | bytes 393224 | tf_op jit(solution)/shard_map/ppermute | solution.py:314
  58.8 3.5 %collective-permute-start.26 = (f32[128,256]{1,0:T(8,128)S(1)}, f32[128,256]{1,0:T(8,128)S(1)}, u32[]{:S(2)}, u32[]{:S(2)}) collective-permute-start(f32[128,256]{1,0:T(8,128)S(1)} %collective-permute-done.22.refs_3_), channel_id=1, source_target_pairs={{0,4},{4,0},{8,12},{12,8},{16,20},{20,16},{24,28},{28,24},{1,5},{5... | collective-permute-start | bytes 393224 | tf_op jit(solution)/shard_map/ppermute | solution.py:314
  60.0 2.3 %collective-permute-start.25 = (f32[128,256]{1,0:T(8,128)S(1)}, f32[128,256]{1,0:T(8,128)S(1)}, u32[]{:S(2)}, u32[]{:S(2)}) collective-permute-start(f32[128,256]{1,0:T(8,128)S(1)} %collective-permute-done.21.refs_2_), channel_id=1, source_target_pairs={{0,4},{4,0},{8,12},{12,8},{16,20},{20,16},{24,28},{28,24},{1,5},{5... | collective-permute-start | bytes 393224 | tf_op jit(solution)/shard_map/ppermute | solution.py:314
  60.9 1.4 %collective-permute-start.24 = (f32[128,256]{1,0:T(8,128)S(1)}, f32[128,256]{1,0:T(8,128)S(1)}, u32[]{:S(2)}, u32[]{:S(2)}) collective-permute-start(f32[128,256]{1,0:T(8,128)S(1)} %collective-permute-done.20.refs_1_), channel_id=1, source_target_pairs={{0,4},{4,0},{8,12},{12,8},{16,20},{20,16},{24,28},{28,24},{1,5},{5... | collective-permute-start | bytes 393224 | tf_op jit(solution)/shard_map/ppermute | solution.py:314
  66.1 7.2 %collective-permute-start.30 = (f32[2,2,8,8,128]{4,3,2,1,0:T(8,128)S(1)}, f32[2,2,8,8,128]{4,3,2,1,0:T(8,128)S(1)}, u32[]{:S(2)}, u32[]{:S(2)}) collective-permute-start(f32[2,2,8,8,128]{4,3,2,1,0:T(8,128)S(1)} %get-tuple-element.47), channel_id=1, source_target_pairs={{0,1},{1,0},{2,3},{3,2},{4,5},{5,4},{6,7},{7,6},{8,9},{9,8},{10,11... | collective-permute-start | bytes 393224 | tf_op jit(solution)/shard_map/ppermute | solution.py:314
  67.7 11.9 %collective-permute-start.31 = (f32[2,2,8,8,128]{4,3,2,1,0:T(8,128)S(1)}, f32[2,2,8,8,128]{4,3,2,1,0:T(8,128)S(1)}, u32[]{:S(2)}, u32[]{:S(2)}) collective-permute-start(f32[2,2,8,8,128]{4,3,2,1,0:T(8,128)S(1)} %get-tuple-element.48), channel_id=1, source_target_pairs={{0,2},{1,3},{2,0},{3,1},{4,6},{5,7},{6,4},{7,5},{8,10},{9,11},{10,... | collective-permute-start | bytes 393224 | tf_op jit(solution)/shard_map/ppermute | solution.py:314
  68.9 10.8 %collective-permute-start.32 = (f32[2,2,8,8,128]{4,3,2,1,0:T(8,128)S(1)}, f32[2,2,8,8,128]{4,3,2,1,0:T(8,128)S(1)}, u32[]{:S(2)}, u32[]{:S(2)}) collective-permute-start(f32[2,2,8,8,128]{4,3,2,1,0:T(8,128)S(1)} %get-tuple-element.49), channel_id=1, source_target_pairs={{0,3},{1,2},{2,1},{3,0},{4,7},{5,6},{6,5},{7,4},{8,11},{9,10},{10,... | collective-permute-start | bytes 393224 | tf_op jit(solution)/shard_map/ppermute | solution.py:314

commit v3 on v2

v3 whole, which is shorter than its diff:
```python
import functools

import jax
import jax.numpy as jnp
from jax import lax
from jax.experimental import pallas as pl
from jax.experimental.pallas import tpu as pltpu
from jax.sharding import PartitionSpec as P

F32 = jnp.float32
BF16 = jnp.bfloat16
VMEM = pl.BlockSpec(memory_space=pltpu.VMEM)
ANY = pl.BlockSpec(memory_space=pl.ANY)
HBM = pl.BlockSpec(memory_space=pltpu.HBM)
LANES = 128
PARAMS = pltpu.CompilerParams(vmem_limit_bytes=40 * 2**20)


def call(body, name, out_shape, in_specs, scratch=(), out_specs=None, after=()):
    def whole(*refs):
        body(*refs[len(after) :])

    kernel = pl.pallas_call(
        whole,
        out_shape=[jax.ShapeDtypeStruct(shape, dtype) for shape, dtype in out_shape],
        in_specs=[ANY] * len(after) + in_specs,
        out_specs=out_specs or [VMEM] * len(out_shape),
        scratch_shapes=list(scratch),
        compiler_params=PARAMS,
        name=name,
    )
    return functools.partial(kernel, *after)


def halves(a):
    high = a.astype(BF16)
    return high, (a - high.astype(F32)).astype(BF16)


def product(left, right):
    dot = functools.partial(jnp.dot, preferred_element_type=F32)
    high, low = left
    other_high, other_low = halves(right)
    width = right.shape[1]
    if width > LANES:
        return dot(high, other_high) + (dot(high, other_low) + dot(low, other_high))
    both = dot(high, jnp.concatenate([other_high, other_low], axis=1))
    return both[:, :width] + (both[:, width:] + dot(low, other_high))


def real_form(columns):
    size = columns.shape[0] // 2
    return jnp.concatenate([columns, jnp.concatenate([-columns[size:], columns[:size]], axis=0)], axis=1)


def pick(value, state, picked, offsets, coils, row):
    taps, lines = picked.shape[1] // 2 // coils, state.shape[1] // 2 // coils
    chunks = value.shape[1] // LANES
    for i in range(chunks):
        state[i] = value[:, i * LANES : (i + 1) * LANES]
        for part in range(2):
            for tap in range(taps):
                source = pl.ds(part * coils * lines + offsets[row, tap], coils, stride=lines)
                picked[i, pl.ds(part * coils * taps + tap, coils, stride=taps), :] = state[i, source, :]
    return jnp.concatenate([picked[i] for i in range(chunks)], axis=1)


def pick_scratch(lanes, state, size):
    return [pltpu.VMEM((lanes // LANES, state, LANES), F32), pltpu.VMEM((lanes // LANES, size, LANES), F32)]


def offset_scratch(offsets):
    return [pltpu.SMEM(offsets.shape, jnp.int32), pltpu.SemaphoreType.DMA]


def visits(segs, backward):
    if backward:
        return [(s, segs + s - 1 if s else 2 * segs + 1) for s in reversed(range(segs))]
    return [(s, s + 1 if s < segs - 1 else 2 * segs) for s in range(segs)]


def walk(maps, carried, sources, choose, backward):
    states = list(sources)
    for s, row in visits(len(sources), backward):
        if carried is not None:
            states[s] = product(maps(s), carried) + sources[s]
        carried = choose(states[s], row=row)
    return states, carried


def response(high, low, states, choose, backward):
    size = high.shape[2]
    first = visits(len(states), backward)[0][0]
    columns = high[first, :, : size // 2].astype(F32) + low[first, :, : size // 2].astype(F32)
    blank = jnp.zeros_like(columns)
    sources = [jnp.concatenate([columns if s == first else blank, state], axis=1) for s, state in enumerate(states)]
    return walk(lambda s: (high[s], low[s]), None, sources, choose, backward)[1]


def spot(near, i):
    return lax.bitwise_xor(lax.axis_index("coil"), i) if near else i


def my_chip():
    seg = lax.axis_index("seg")
    return lax.shift_right_logical(seg, 1), lax.bitwise_and(seg, 1)


def pack(measured):
    segs, parts, coils, lines, samples = measured.shape
    n = lax.axis_size("coil")
    width = samples // n

    def body(m_ref, *rest):
        outs, sems = rest[:n], rest[n]
        copies = []
        for i in range(n):
            start = pl.multiple_of(spot(True, i) * width, width)
            copies.append(pltpu.make_async_copy(m_ref.at[:, :, :, :, pl.ds(start, width)], outs[i], sems.at[i]))
        for c in copies:
            c.start()
        for c in copies:
            c.wait()

    out = ((segs, parts, coils, lines, width), F32)
    return call(body, "pack", [out] * n, [HBM], [pltpu.SemaphoreType.DMA((n,))])(measured)


def hold(first, *values):
    def body(_, *refs):
        for i in range(len(values)):
            refs[len(values) + i][...] = refs[i][...]

    out_shape = [(v.shape, v.dtype) for v in values]
    return call(body, "hold", out_shape, [ANY] + [VMEM] * len(values))(first, *values)


def gather(near, blocks, after):
    n = len(blocks)
    segs, parts, coils, lines, width = blocks[0].shape

    def body(*refs):
        for i in range(n):
            refs[n][:, :, pl.ds(spot(near, i) * coils, coils)] = refs[i][...]

    out = ((segs, parts, n * coils, lines, width), F32)
    return call(body, "gather", [out], [VMEM] * n, after=after)(*blocks)[0]


def prepare(near, blocks, backward):
    n = len(blocks)
    segs, _, block_cols, rows = blocks[0].shape
    cols = block_cols * n
    size = 2 * cols

    def body(*refs):
        hi_ref, lo_ref, kt = refs[n:]
        for i in range(n):
            kt[:, :, pl.ds(spot(near, i), 1)] = refs[i][...][:, :, None]
        for s in range(segs):
            real, imag = (kt[s, part].reshape(cols, rows).T for part in range(2))
            hi_ref[s], lo_ref[s] = halves(real_form(jnp.concatenate([real, imag], axis=0)))

    return call(
        body,
        "prepare_backward" if backward else "prepare_forward",
        [((segs, 2 * rows, size), BF16)] * 2,
        [VMEM] * n,
        [pltpu.VMEM((segs, 2, n, block_cols, rows), F32)],
    )(*blocks)


def summary(offsets, maps, measured):
    high, low = maps
    _, rows, size = high.shape
    segs, _, coils, _, width = measured.shape
    lanes = size // 2 + width

    def body(off_ref, hi_ref, lo_ref, m_ref, e_ref, state, picked, off, sem):
        fetch = pltpu.make_async_copy(off_ref, off, sem)
        fetch.start()
        fetch.wait()
        choose = functools.partial(pick, state=state, picked=picked, offsets=off, coils=coils)
        e_ref[...] = response(hi_ref, lo_ref, [m_ref[s].reshape(rows, width) for s in range(segs)], choose, False)

    return call(
        body,
        "summary",
        [((size, lanes), F32)],
        [VMEM] * 4,
        pick_scratch(lanes, rows, size) + offset_scratch(offsets),
    )(offsets, high, low, measured)[0]


def compose(mine, other, cols, backward):
    size, lanes = mine.shape

    def body(a_ref, b_ref, whole, out_ref, pair):
        _, core = my_chip()
        pair[pl.ds(core, 1)] = a_ref[...][None]
        pair[pl.ds(1 - core, 1)] = b_ref[...][None]
        near, far = (pair[1], pair[0]) if backward else (pair[0], pair[1])
        both = product(halves(real_form(far[:, :cols])), near)
        whole[:, :cols] = both[:, :cols]
        whole[:, cols:] = both[:, cols:] + far[:, cols:]
        out_ref[...] = whole[pl.ds(pl.multiple_of(core * (size // 2), size // 2), size // 2), :]

    return call(
        body,
        "compose_backward" if backward else "compose_forward",
        [((size, lanes), F32), ((size // 2, lanes), F32)],
        [VMEM, VMEM],
        [pltpu.VMEM((2, size, lanes), F32)],
    )(mine, other)


def incoming(own, parts, table, carried, backward):
    chips, _, cols, _ = table.shape
    chip, core = my_chip()
    table[pl.ds(chip, 1)] = own[...].reshape((1,) + table.shape[1:])
    for i in range(1, chips):
        e = lax.bitwise_xor(chip, i)
        table[pl.ds(e, 1), pl.ds(core, 1)] = parts[2 * i - 2][...][None, None]
        table[pl.ds(e, 1), pl.ds(1 - core, 1)] = parts[2 * i - 1][...][None, None]
    order = list(range(chips))[:: -1 if backward else 1]
    carried[order[0]] = jnp.zeros(carried.shape[1:], F32)
    value = None
    for at, e in enumerate(order[:-1]):
        block = table[e].reshape(2 * cols, -1)
        if value is None:
            value = block[:, cols:]
        else:
            value = product(halves(real_form(block[:, :cols])), value) + block[:, cols:]
        carried[order[at + 1]] = value
    return carried[chip]


def incoming_scratch(chips, size, lanes):
    return [pltpu.VMEM((chips, 2, size // 2, lanes), F32), pltpu.VMEM((chips, size, lanes - size // 2), F32)]


def finish(near, offsets, maps, sources, mine, other, blocks, backward, following=(), joined=None, after=()):
    high, low = maps
    segs, _, coils, lines, width = sources.shape
    _, rows, size = high.shape
    cols, lanes = size // 2, mine.shape[1]
    chips = (len(blocks) + 1) // 2
    n = lax.axis_size("coil")
    own_coils = coils // n
    extra = list(following) + ([] if joined is None else [joined])

    def body(off_ref, hi_ref, lo_ref, m_ref, a_ref, b_ref, own, *refs):
        at = 2 * chips - 2
        rest, extra_refs, refs = refs[:at], refs[at : at + len(extra)], refs[at + len(extra) :]
        outs, refs = refs[:n], refs[n:]
        if following:
            e_ref, refs = refs[0], refs[1:]
        whole, table, carried, state, picked, off, sem = refs
        fetch = pltpu.make_async_copy(off_ref, off, sem)
        fetch.start()
        choose = functools.partial(pick, state=state, picked=picked, offsets=off, coils=coils)
        value = incoming(own, rest, table, carried, backward)
        moved = product(halves(real_form(b_ref[:, :cols])), value) + b_ref[:, cols:]
        value = jnp.where(my_chip()[1] == (1 if backward else 0), value, moved)
        fetch.wait()
        source = [m_ref[s].reshape(rows, width) for s in range(segs)]
        states, _ = walk(lambda s: (hi_ref[s], lo_ref[s]), value, source, choose, backward)
        if following:
            e_ref[...] = response(extra_refs[0], extra_refs[1], states, choose, not backward)
        for s in range(segs):
            whole[s] = states[s].reshape(2, coils, lines, width)
        for i in range(n):
            cut = whole[:, :, pl.ds(spot(near, i) * own_coils, own_coils)]
            if joined is not None and i == 1:
                outs[i][0] = extra_refs[-1][...]
                outs[i][1] = cut
            else:
                outs[i][...] = cut

    block = (segs, 2, own_coils, lines, width)
    out_shape = [((2, *block) if joined is not None and i == 1 else block, F32) for i in range(n)]
    scratch = [pltpu.VMEM(sources.shape, F32)]
    if following:
        out_shape += [((size, lanes), F32), (sources.shape, F32)]
        scratch = []
    return call(
        body,
        "finish_backward" if backward else "finish_forward",
        out_shape,
        [VMEM] * (6 + len(blocks) + len(extra)),
        scratch
        + incoming_scratch(chips, size, lanes)
        + pick_scratch(lanes if following else width, rows, size)
        + offset_scratch(offsets),
        after=after,
    )(offsets, high, low, sources, mine, other, *blocks, *extra)


def unpack(forward, result, joined):
    n = len(forward)
    segs, parts, coils, lines, width = forward[0].shape
    sent = [forward[0], result[0], joined] + [b for i in range(2, n) for b in (forward[i], result[i])]

    def body(*refs):
        ins, outs, sems = refs[: len(sent)], refs[len(sent) : len(sent) + 2], refs[len(sent) + 2]
        copies = []
        for i in range(n):
            start = pl.multiple_of(spot(True, i) * width, width)
            for o in range(2):
                source = ins[2].at[o] if i == 1 else ins[o if i == 0 else 2 * i - 1 + o]
                copies.append(pltpu.make_async_copy(source, outs[o].at[:, :, :, :, pl.ds(start, width)], sems.at[i, o]))
        for c in copies:
            c.start()
        for c in copies:
            c.wait()

    return call(
        body,
        "unpack",
        [((segs, parts, coils, lines, n * width), F32)] * 2,
        [VMEM] * len(sent),
        [pltpu.SemaphoreType.DMA((n, 2))],
        [ANY] * 2,
    )(*sent)


def swap(block, axis, distance):
    return lax.ppermute(block, axis, [(i, i ^ distance) for i in range(lax.axis_size(axis))])


def spread_kernels(own):
    n = lax.axis_size("coil")
    blocks = {0: own}
    distance = n // 2
    while distance:
        blocks.update({i ^ distance: swap(blocks[i], "coil", distance) for i in sorted(blocks)})
        distance //= 2
    return [blocks[i] for i in range(n)]


def exchange(whole, half, first=None):
    chips = lax.axis_size("seg") // 2
    blocks = [whole]
    for i in range(1, chips):
        block = swap(half, "seg", 2 * i)
        if i == min(2, chips - 1) and first is not None:
            (block,) = hold(first, block)
        blocks += [block, swap(block, "seg", 1)]
    return blocks


def shards(measured, forward_kernel, backward_kernel, line_offsets):
    n = lax.axis_size("coil")
    places = lax.axis_size("seg")
    taps = line_offsets.shape[2]
    width = measured.shape[4] // n
    cols = forward_kernel.shape[3] * n
    first, last = line_offsets[0, 0], line_offsets[-1, 1]
    kernels_f, kernels_b = (jnp.swapaxes(k, 2, 3) for k in (forward_kernel, backward_kernel))
    aligned = width % LANES == 0 and (cols // taps // n) % 8 == 0
    if aligned:
        forward_blocks = spread_kernels(kernels_f)
        backward_blocks = spread_kernels(kernels_b)
        pieces = pack(measured)
        lines_blocks = [pieces[0]] + [swap(pieces[i], "coil", i) for i in range(1, n)]
        first, last = hold(forward_blocks[1], first, last)
    else:
        forward_blocks = list(lax.all_gather(kernels_f, "coil"))
        backward_blocks = list(lax.all_gather(kernels_b, "coil"))
        split = lax.all_to_all(measured, "coil", split_axis=4, concat_axis=2, tiled=True)
        split = jnp.pad(split, [(0, 0)] * 4 + [(0, -width % LANES)])
        lines_blocks = jnp.split(split, n, axis=2)
    after = lax.ppermute(first, "seg", [(i + 1, i) for i in range(places - 1)])[None]
    before = lax.ppermute(last, "seg", [(i, i + 1) for i in range(places - 1)])[None]
    offsets = jnp.concatenate([line_offsets[:, 0], line_offsets[:, 1], after, before])
    offsets = jnp.pad(offsets, [(0, -offsets.shape[0] % 8), (0, LANES - taps)])

    forward_maps = prepare(aligned, forward_blocks, False)
    lines = gather(aligned, lines_blocks, forward_maps[:1])
    backward_maps = prepare(aligned, backward_blocks, True)
    mine = summary(offsets, forward_maps, lines)
    other = swap(mine, "seg", 1)
    blocks = exchange(*compose(mine, other, cols, False))
    *forward_out, mine, forward = finish(aligned, offsets, forward_maps, lines, mine, other, blocks, False, backward_maps)
    other = swap(mine, "seg", 1)
    whole, half = compose(mine, other, cols, True)
    if aligned:
        home = dict(enumerate(forward_out[:2])) | {i: swap(forward_out[i], "coil", i) for i in range(2, n)}
        blocks = exchange(whole, half, home[n - 1] if n > 2 else None)
        result_out = finish(
            aligned,
            offsets,
            backward_maps,
            forward,
            mine,
            other,
            blocks,
            True,
            joined=forward_out[1],
            after=[home[i] for i in range(2, n - 1)],
        )
        result_home = [result_out[0]] + [swap(result_out[i], "coil", i) for i in range(1, n)]
        return tuple(unpack(home, result_home, result_home[1]))
    blocks = exchange(whole, half)
    result_out = finish(aligned, offsets, backward_maps, forward, mine, other, blocks, True)

    def rejoin(blocks):
        states = lax.all_to_all(jnp.stack(blocks), "coil", split_axis=0, concat_axis=0)[..., :width]
        states = jnp.moveaxis(states, 0, 4)
        return states.reshape(states.shape[:4] + (n * width,))

    return rejoin(forward_out), rejoin(result_out)


def solution(mesh):
    placed = (
        P("seg", None, "coil", None, None),
        P("seg", None, None, "coil"),
        P("seg", None, None, "coil"),
        P("seg", None, None),
    )
    return jax.shard_map(
        shards,
        mesh=mesh,
        in_specs=placed,
        out_specs=(P("seg", None, "coil", None, None), P("seg", None, "coil", None, None)),
        check_vma=False,
    )
```

time: 81.3 us -> 74.3 us (0.914)
  Pallas kernels: 14.5 us -> 7.56 us
  waiting for transfers between devices: 26.8 us -> 29.8 us
  starting transfers between devices: 37.6 us -> 34.8 us
    ppermute x31 -> x28, starting transfers between devices: 34.4 us -> 29.5 us  [swap(): lax.ppermute(block, axis, [(i, i ^ distance) for i in range(lax.axis_size...]
    pallas_call x2, Pallas kernels: 6.68 us -> 3.9 us  [finish(): call(body, 'finish_backward' if backward else 'finish_forward', out_shape...]
    ppermute x2, waiting for transfers between devices: 0.18 us -> 2.52 us  [the longest x1 1.72 us: shards(): lax.ppermute(first, 'seg', [(i + 1, i) for i in range(places - 1)])[None]]
    ppermute x2, starting transfers between devices: 3.15 us -> 5.25 us  [the longest x1 3.97 us: shards(): lax.ppermute(last, 'seg', [(i, i + 1) for i in range(places - 1)])[None]]
    pallas_call x2, Pallas kernels: 2.47 us -> 0.51 us  [prepare(): call(body, 'prepare_backward' if backward else 'prepare_forward', [((segs...]
    pallas_call x5 -> x6, Pallas kernels: 3.68 us -> 2.43 us  [the longest x1 1.23 us: summary(): call(body, 'summary', [((size, lanes), F32)], [VMEM] * 4, pick_scratch(la...]
    pallas_call x2, Pallas kernels: 1.71 us -> 0.72 us  [compose(): call(body, 'compose_backward' if backward else 'compose_forward', [((size...]
    ppermute x31 -> x28, waiting for transfers between devices: 26.6 us -> 27.3 us  [swap(): lax.ppermute(block, axis, [(i, i ^ distance) for i in range(lax.axis_size...]
  transfers between devices with their start and end apart: 33 -> 30, of which waited for: 14 -> 15; matrix products, arithmetic and copies ran while one was open for 0% -> 0% of each run, Pallas kernels for 5% -> 2%
where the time goes in v3:
time: 74.3 us; the launch traced here: 74.1 us
  starting transfers between devices  34.8 us (47%)
  waiting for transfers between devices  29.8 us (40%)
  Pallas kernels  7.56 us (10%)
  local copies, waits for them, and re-layouts  1.07 us (1%)
  between operations  0.85 us (1%)
    ppermute x28, starting transfers between devices, swap(): lax.ppermute(block, axis, [(i, i ^ distance) for i in range(lax.axis_size...  29.5 us
    ppermute x28, waiting for transfers between devices, swap(): lax.ppermute(block, axis, [(i, i ^ distance) for i in range(lax.axis_size...  27.3 us
    ppermute x1, starting transfers between devices, shards(): lax.ppermute(last, 'seg', [(i, i + 1) for i in range(places - 1)])[None]  3.97 us
    pallas_call x2, Pallas kernels, finish(): call(body, 'finish_backward' if backward else 'finish_forward', out_shape...  3.9 us
    ppermute x1, waiting for transfers between devices, shards(): lax.ppermute(first, 'seg', [(i + 1, i) for i in range(places - 1)])[None]  1.72 us
  transfers between devices with their start and end apart: 30, of which 15 were waited for; matrix products, arithmetic and copies ran while one was open for 0% of the time, Pallas kernels for 2%

profile of v3, /device:TPU:0, one launch (start us, length us, event | category | flops | bytes accessed | tf_op | source)
XLA Modules:
  0.0 74.1 jit_solution(6181646693012770720)
XLA Ops:
  0.6 4.1 %collective-permute-start.3 = (f32[2,2,32,256]{3,2,1,0:T(8,128)}, f32[2,2,32,256]{3,2,1,0:T(8,128)S(1)}, u32[]{:S(2)}, u32[]{:S(2)}) collective-permute-start(f32[2,2,32,256]{3,2,1,0:T(8,128)} %bitcast.10), channel_id=1, source_target_pairs={{0,2},{1,3},{2,0},{3,1},{4,6},{5,7},{6,4},{7,5},{8,10},{9,11},{10,... | collective-permute-start | bytes 393224 | tf_op jit(solution)/shard_map/ppermute | solution.py:328
  4.7 1.6 %collective-permute-start = (f32[2,2,32,256]{3,2,1,0:T(8,128)}, f32[2,2,32,256]{3,2,1,0:T(8,128)S(1)}, u32[]{:S(2)}, u32[]{:S(2)}) collective-permute-start(f32[2,2,32,256]{3,2,1,0:T(8,128)} %bitcast.11), channel_id=1, source_target_pairs={{0,1},{1,0},{2,3},{3,2},{4,5},{5,4},{6,7},{7,6},{8,9},{9,8},{10,11... | collective-permute-start | bytes 393224 | tf_op jit(solution)/shard_map/ppermute | solution.py:328
  6.3 1.0 %copy-done = f32[2,2,8,8,512]{4,3,2,1,0:T(8,128)S(1)} copy-done((f32[2,2,8,8,512]{4,3,2,1,0:T(8,128)S(1)}, f32[2,2,8,8,512]{4,3,2,1,0:T(8,128)}, u32[]{:S(2)}) %copy-start) | copy-done | bytes 524312
  7.4 0.1 pack.1
  7.5 0.0 copy-start.1
  7.5 0.5 collective-permute-start.5
  8.0 0.1 collective-permute-start.6
  8.1 3.9 %collective-permute-start.7 = (f32[2,2,8,8,128]{4,3,2,1,0:T(8,128)S(1)}, f32[2,2,8,8,128]{4,3,2,1,0:T(8,128)S(1)}, u32[]{:S(2)}, u32[]{:S(2)}) collective-permute-start(f32[2,2,8,8,128]{4,3,2,1,0:T(8,128)S(1)} %get-tuple-element.33), channel_id=1, source_target_pairs={{0,3},{1,2},{2,1},{3,0},{4,7},{5,6},{6,5},{7,4},{8,11},{9,10},{10,... | collective-permute-start | bytes 393224 | tf_op jit(solution)/shard_map/ppermute | solution.py:328
  11.9 0.0 collective-permute-done.3.refs_2_
  12.0 0.3 collective-permute-start.4
  12.2 2.6 %collective-permute-done.refs_0_.refs_1_ = f32[2,2,32,256]{3,2,1,0:T(8,128)S(1)} collective-permute-done((f32[2,2,32,256]{3,2,1,0:T(8,128)}, f32[2,2,32,256]{3,2,1,0:T(8,128)S(1)}, u32[]{:S(2)}, u32[]{:S(2)}) %collective-permute-start) | collective-permute-done | bytes 131104 | tf_op jit(solution)/shard_map/ppermute | solution.py:328
  14.9 1.3 %collective-permute-start.1 = (s32[4]{0:T(128)S(1)}, s32[4]{0:T(128)S(1)}, u32[]{:S(2)}, u32[]{:S(2)}) collective-permute-start(s32[4]{0:T(128)S(1)} %get-tuple-element.26), channel_id=1, source_target_pairs={{4,0},{8,4},{12,8},{16,12},{20,16},{24,20},{28,24},{5,1},{9,5},{13... | collective-permute-start | bytes 56 | tf_op jit(solution)/shard_map/ppermute | solution.py:373
  16.2 1.7 %collective-permute-done.1 = s32[4]{0:T(128)S(1)} collective-permute-done((s32[4]{0:T(128)S(1)}, s32[4]{0:T(128)S(1)}, u32[]{:S(2)}, u32[]{:S(2)}) %collective-permute-start.1) | collective-permute-done | bytes 48 | tf_op jit(solution)/shard_map/ppermute | solution.py:373
  17.9 4.0 %collective-permute-start.2 = (s32[4]{0:T(128)S(1)}, s32[4]{0:T(128)S(1)}, u32[]{:S(2)}, u32[]{:S(2)}) collective-permute-start(s32[4]{0:T(128)S(1)} %get-tuple-element.27), channel_id=1, source_target_pairs={{0,4},{4,8},{8,12},{12,16},{16,20},{20,24},{24,28},{1,5},{5,9},{9,... | collective-permute-start | bytes 56 | tf_op jit(solution)/shard_map/ppermute | solution.py:374
  21.8 0.8 %collective-permute-done.2 = s32[4]{0:T(128)S(1)} collective-permute-done((s32[4]{0:T(128)S(1)}, s32[4]{0:T(128)S(1)}, u32[]{:S(2)}, u32[]{:S(2)}) %collective-permute-start.2) | collective-permute-done | bytes 48 | tf_op jit(solution)/shard_map/ppermute | solution.py:374
  22.7 0.1 collective-permute-done.4.refs_3_
  22.8 0.3 prepare_forward.1
  23.1 0.0 collective-permute-done.5.refs_2_
  23.1 0.0 collective-permute-done.6.refs_3_
  23.1 0.0 collective-permute-done.7.refs_4_
  23.1 0.0 copy-start.2
  23.2 1.2 %summary.1.refs_0_.refs_4_ = f32[256,256]{1,0:T(8,128)S(1)} custom-call(s32[8,128]{1,0:T(8,128)S(1)} %pad.4.refs_0_.refs_1_, bf16[2,512,256]{2,1,0:T(8,128)(2,1)S(1)} %get-tuple-element.28.refs_0_.refs_1_, bf16[2,512,256]{2,1,0:T(8,128)(2,1)S(1)} %get-tuple-element.29.refs_2_, f32[2,2,32,8,128]{4,3,2,1,0:T(8,128)S(1)} %gather.1.refs_3_), custom_call_target="tpu_custom_call" | custom-call | tf_op jit(solution)/shard_map/summary/pallas_call | solution.py:186
  24.4 0.3 collective-permute-start.8
  24.7 2.0 %collective-permute-start.16 = (f32[2,2,32,256]{3,2,1,0:T(8,128)S(1)}, f32[2,2,32,256]{3,2,1,0:T(8,128)S(1)}, u32[]{:S(2)}, u32[]{:S(2)}) collective-permute-start(f32[2,2,32,256]{3,2,1,0:T(8,128)S(1)} %bitcast.13), channel_id=1, source_target_pairs={{0,2},{1,3},{2,0},{3,1},{4,6},{5,7},{6,4},{7,5},{8,10},{9,11},{10,... | collective-permute-start | bytes 393224 | tf_op jit(solution)/shard_map/ppermute | solution.py:328
  26.6 0.0 collective-permute-done.8.refs_1_.refs_5_
  26.6 0.4 compose_forward.1
  27.0 2.5 %collective-permute-start.13 = (f32[128,256]{1,0:T(8,128)S(1)}, f32[128,256]{1,0:T(8,128)S(1)}, u32[]{:S(2)}, u32[]{:S(2)}) collective-permute-start(f32[128,256]{1,0:T(8,128)S(1)} %get-tuple-element.35), channel_id=1, source_target_pairs={{0,24},{4,28},{8,16},{12,20},{16,8},{20,12},{24,0},{28,4},{1,25},{... | collective-permute-start | bytes 393224 | tf_op jit(solution)/shard_map/ppermute | solution.py:328
  29.5 0.5 collective-permute-start.11
  30.0 0.8 %collective-permute-start.9 = (f32[128,256]{1,0:T(8,128)S(1)}, f32[128,256]{1,0:T(8,128)S(1)}, u32[]{:S(2)}, u32[]{:S(2)}) collective-permute-start(f32[128,256]{1,0:T(8,128)S(1)} %get-tuple-element.35), channel_id=1, source_target_pairs={{0,8},{4,12},{8,0},{12,4},{16,24},{20,28},{24,16},{28,20},{1,9},{5... | collective-permute-start | bytes 393224 | tf_op jit(solution)/shard_map/ppermute | solution.py:328
  30.8 1.9 %collective-permute-start.15 = (f32[2,2,32,256]{3,2,1,0:T(8,128)S(1)}, f32[2,2,32,256]{3,2,1,0:T(8,128)S(1)}, u32[]{:S(2)}, u32[]{:S(2)}) collective-permute-start(f32[2,2,32,256]{3,2,1,0:T(8,128)S(1)} %bitcast.14), channel_id=1, source_target_pairs={{0,1},{1,0},{2,3},{3,2},{4,5},{5,4},{6,7},{7,6},{8,9},{9,8},{10,11... | collective-permute-start | bytes 393224 | tf_op jit(solution)/shard_map/ppermute | solution.py:328
  32.7 1.5 %collective-permute-done.16.refs_2_ = f32[2,2,32,256]{3,2,1,0:T(8,128)S(1)} collective-permute-done((f32[2,2,32,256]{3,2,1,0:T(8,128)S(1)}, f32[2,2,32,256]{3,2,1,0:T(8,128)S(1)}, u32[]{:S(2)}, u32[]{:S(2)}) %collective-permute-start.16) | collective-permute-done | bytes 131104 | tf_op jit(solution)/shard_map/ppermute | solution.py:328
  34.2 0.0 collective-permute-start.17
  34.2 2.1 %collective-permute-done.11.refs_9_ = f32[128,256]{1,0:T(8,128)S(1)} collective-permute-done((f32[128,256]{1,0:T(8,128)S(1)}, f32[128,256]{1,0:T(8,128)S(1)}, u32[]{:S(2)}, u32[]{:S(2)}) %collective-permute-start.11) | collective-permute-done | bytes 131104 | tf_op jit(solution)/shard_map/ppermute | solution.py:328
  36.3 0.0 collective-permute-start.12
  36.4 0.8 %collective-permute-done.9.refs_7_ = f32[128,256]{1,0:T(8,128)S(1)} collective-permute-done((f32[128,256]{1,0:T(8,128)S(1)}, f32[128,256]{1,0:T(8,128)S(1)}, u32[]{:S(2)}, u32[]{:S(2)}) %collective-permute-start.9) | collective-permute-done | bytes 131104 | tf_op jit(solution)/shard_map/ppermute | solution.py:328
  37.1 2.6 %collective-permute-done.17.refs_3_ = f32[2,2,32,256]{3,2,1,0:T(8,128)S(1)} collective-permute-done((f32[2,2,32,256]{3,2,1,0:T(8,128)S(1)}, f32[2,2,32,256]{3,2,1,0:T(8,128)S(1)}, u32[]{:S(2)}, u32[]{:S(2)}) %collective-permute-start.17) | collective-permute-done | bytes 131104 | tf_op jit(solution)/shard_map/ppermute | solution.py:328
  39.7 0.3 prepare_backward.1
  40.0 0.0 collective-permute-done.14.refs_12_
  40.0 0.0 collective-permute-done.12.refs_10_
  40.0 2.4 %finish_forward.1 = (f32[2,2,8,8,128]{4,3,2,1,0:T(8,128)S(1)}, f32[2,2,8,8,128]{4,3,2,1,0:T(8,128)S(1)}, f32[2,2,8,8,128]{4,3,2,1,0:T(8,128)S(1)}, f32[2,2,8,8,1...) custom-call(s32[8,128]{1,0:T(8,128)S(1)} %pad.4.refs_0_.refs_1_, ...), custom_call_target="tpu_custom_call" | custom-call | tf_op jit(solution)/shard_map/finish_forward/pallas_call | solution.py:286
  42.4 0.1 collective-permute-start.19
  42.5 2.8 %collective-permute-start.22 = (f32[2,2,8,8,128]{4,3,2,1,0:T(8,128)S(1)}, f32[2,2,8,8,128]{4,3,2,1,0:T(8,128)S(1)}, u32[]{:S(2)}, u32[]{:S(2)}) collective-permute-start(f32[2,2,8,8,128]{4,3,2,1,0:T(8,128)S(1)} %get-tuple-element.44), channel_id=1, source_target_pairs={{0,3},{1,2},{2,1},{3,0},{4,7},{5,6},{6,5},{7,4},{8,11},{9,10},{10,... | collective-permute-start | bytes 393224 | tf_op jit(solution)/shard_map/ppermute | solution.py:328
  45.3 0.0 collective-permute-done.19.refs_1_.refs_6_
  45.3 0.4 compose_backward.1
  45.7 2.2 %collective-permute-start.23 = (f32[128,256]{1,0:T(8,128)S(1)}, f32[128,256]{1,0:T(8,128)S(1)}, u32[]{:S(2)}, u32[]{:S(2)}) collective-permute-start(f32[128,256]{1,0:T(8,128)S(1)} %get-tuple-element.43), channel_id=1, source_target_pairs={{0,16},{4,20},{8,24},{12,28},{16,0},{20,4},{24,8},{28,12},{1,17},{... | collective-permute-start | bytes 393224 | tf_op jit(solution)/shard_map/ppermute | solution.py:328
  47.8 1.1 %collective-permute-start.25 = (f32[128,256]{1,0:T(8,128)S(1)}, f32[128,256]{1,0:T(8,128)S(1)}, u32[]{:S(2)}, u32[]{:S(2)}) collective-permute-start(f32[128,256]{1,0:T(8,128)S(1)} %get-tuple-element.43), channel_id=1, source_target_pairs={{0,24},{4,28},{8,16},{12,20},{16,8},{20,12},{24,0},{28,4},{1,25},{... | collective-permute-start | bytes 393224 | tf_op jit(solution)/shard_map/ppermute | solution.py:328
  49.0 0.4 collective-permute-start.20
  49.4 0.1 collective-permute-start.18
  49.5 0.8 %collective-permute-done.22.refs_0_.refs_5_ = f32[2,2,8,8,128]{4,3,2,1,0:T(8,128)S(1)} collective-permute-done((f32[2,2,8,8,128]{4,3,2,1,0:T(8,128)S(1)}, f32[2,2,8,8,128]{4,3,2,1,0:T(8,128)S(1)}, u32[]{:S(2)}, u32[]{:S(2)}) %collective-permute-start.22) | collective-permute-done | bytes 131104 | tf_op jit(solution)/shard_map/ppermute | solution.py:328
  50.3 3.5 %collective-permute-done.23.refs_1_ = f32[128,256]{1,0:T(8,128)S(1)} collective-permute-done((f32[128,256]{1,0:T(8,128)S(1)}, f32[128,256]{1,0:T(8,128)S(1)}, u32[]{:S(2)}, u32[]{:S(2)}) %collective-permute-start.23) | collective-permute-done | bytes 131104 | tf_op jit(solution)/shard_map/ppermute | solution.py:328
  53.8 0.1 collective-permute-start.24
  53.9 1.2 %collective-permute-done.25.refs_12_ = f32[128,256]{1,0:T(8,128)S(1)} collective-permute-done((f32[128,256]{1,0:T(8,128)S(1)}, f32[128,256]{1,0:T(8,128)S(1)}, u32[]{:S(2)}, u32[]{:S(2)}) %collective-permute-start.25) | collective-permute-done | bytes 131104 | tf_op jit(solution)/shard_map/ppermute | solution.py:328
  55.1 0.7 collective-permute-done.20.refs_8_
  55.8 1.6 %collective-permute-done.18.refs_0_.refs_3_ = f32[2,2,8,8,128]{4,3,2,1,0:T(8,128)S(1)} collective-permute-done((f32[2,2,8,8,128]{4,3,2,1,0:T(8,128)S(1)}, f32[2,2,8,8,128]{4,3,2,1,0:T(8,128)S(1)}, u32[]{:S(2)}, u32[]{:S(2)}) %collective-permute-start.18) | collective-permute-done | bytes 131104 | tf_op jit(solution)/shard_map/ppermute | solution.py:328
  57.3 0.0 collective-permute-done.26.refs_13_
  57.3 0.0 collective-permute-done.24.refs_11_
  57.4 1.5 %finish_backward.1 = (f32[2,2,8,8,128]{4,3,2,1,0:T(8,128)S(1)}, f32[2,2,2,8,8,128]{5,4,3,2,1,0:T(8,128)S(1)}, f32[2,2,8,8,128]{4,3,2,1,0:T(8,128)S(1)}, f32[2,2,8,8,128]{4,3,2,1,0:T(8,128)S(1)}) custom-call(f32[2,2,8,8,128]{4,3,2,1,0:T(8,128)S(1)} %collective-permute-done.18.refs_0_.refs_3_, s32[8,128]{1,0:T(8,128)S(1)} %pad.4.refs_0_.refs_1_, ...), custom_call_target="tpu_custom_call" | custom-call | tf_op jit(solution)/shard_map/finish_backward/pallas_call | solution.py:286
  58.8 0.1 collective-permute-start.27
  58.9 2.5 %collective-permute-start.28 = (f32[2,2,8,8,128]{4,3,2,1,0:T(8,128)S(1)}, f32[2,2,8,8,128]{4,3,2,1,0:T(8,128)S(1)}, u32[]{:S(2)}, u32[]{:S(2)}) collective-permute-start(f32[2,2,8,8,128]{4,3,2,1,0:T(8,128)S(1)} %get-tuple-element.48), channel_id=1, source_target_pairs={{0,2},{1,3},{2,0},{3,1},{4,6},{5,7},{6,4},{7,5},{8,10},{9,11},{10,... | collective-permute-start | bytes 393224 | tf_op jit(solution)/shard_map/ppermute | solution.py:328
  61.4 1.9 %collective-permute-start.29 = (f32[2,2,8,8,128]{4,3,2,1,0:T(8,128)S(1)}, f32[2,2,8,8,128]{4,3,2,1,0:T(8,128)S(1)}, u32[]{:S(2)}, u32[]{:S(2)}) collective-permute-start(f32[2,2,8,8,128]{4,3,2,1,0:T(8,128)S(1)} %get-tuple-element.49), channel_id=1, source_target_pairs={{0,3},{1,2},{2,1},{3,0},{4,7},{5,6},{6,5},{7,4},{8,11},{9,10},{10,... | collective-permute-start | bytes 393224 | tf_op jit(solution)/shard_map/ppermute | solution.py:328
  63.3 5.1 %collective-permute-done.28.refs_4_ = f32[2,2,8,8,128]{4,3,2,1,0:T(8,128)S(1)} collective-permute-done((f32[2,2,8,8,128]{4,3,2,1,0:T(8,128)S(1)}, f32[2,2,8,8,128]{4,3,2,1,0:T(8,128)S(1)}, u32[]{:S(2)}, u32[]{:S(2)}) %collective-permute-start.28) | collective-permute-done | bytes 131104 | tf_op jit(solution)/shard_map/ppermute | solution.py:328
  68.4 4.7 %collective-permute-done.29.refs_6_ = f32[2,2,8,8,128]{4,3,2,1,0:T(8,128)S(1)} collective-permute-done((f32[2,2,8,8,128]{4,3,2,1,0:T(8,128)S(1)}, f32[2,2,8,8,128]{4,3,2,1,0:T(8,128)S(1)}, u32[]{:S(2)}, u32[]{:S(2)}) %collective-permute-start.29) | collective-permute-done | bytes 131104 | tf_op jit(solution)/shard_map/ppermute | solution.py:328
  73.1 0.0 collective-permute-done.27.refs_2_
  73.1 1.0 %unpack.1 = (f32[2,2,8,8,512]{4,3,2,1,0:T(8,128)}, f32[2,2,8,8,512]{4,3,2,1,0:T(8,128)}) custom-call(f32[2,2,8,8,128]{4,3,2,1,0:T(8,128)S(1)} %get-tuple-element.38.refs_0_, f32[2,2,8,8,128]{4,3,2,1,0:T(8,128)S(1)} %get-tuple-element.46.refs_1_, f32[2,2,2,8,8,128]{5,4,3,2,1,0:T(8,128)S(1)} %collective-permute-done.27.refs_2_, ...), custom_call_target="tpu_custom_call" | custom-call | tf_op jit(solution)/shard_map/unpack/pallas_call | solution.py:317
  (20 shorter events, 0.1 us)
Async XLA Ops:
  0.6 11.3 %collective-permute-start.3 = (f32[2,2,32,256]{3,2,1,0:T(8,128)}, f32[2,2,32,256]{3,2,1,0:T(8,128)S(1)}, u32[]{:S(2)}, u32[]{:S(2)}) collective-permute-start(f32[2,2,32,256]{3,2,1,0:T(8,128)} %bitcast.10), channel_id=1, source_target_pairs={{0,2},{1,3},{2,0},{3,1},{4,6},{5,7},{6,4},{7,5},{8,10},{9,11},{10,... | collective-permute-start | bytes 393224 | tf_op jit(solution)/shard_map/ppermute | solution.py:328
  4.7 10.1 %collective-permute-start = (f32[2,2,32,256]{3,2,1,0:T(8,128)}, f32[2,2,32,256]{3,2,1,0:T(8,128)S(1)}, u32[]{:S(2)}, u32[]{:S(2)}) collective-permute-start(f32[2,2,32,256]{3,2,1,0:T(8,128)} %bitcast.11), channel_id=1, source_target_pairs={{0,1},{1,0},{2,3},{3,2},{4,5},{5,4},{6,7},{7,6},{8,9},{9,8},{10,11... | collective-permute-start | bytes 393224 | tf_op jit(solution)/shard_map/ppermute | solution.py:328
  6.3 1.0 %copy-start = (f32[2,2,8,8,512]{4,3,2,1,0:T(8,128)S(1)}, f32[2,2,8,8,512]{4,3,2,1,0:T(8,128)}, u32[]{:S(2)}) copy-start(f32[2,2,8,8,512]{4,3,2,1,0:T(8,128)} %refs_0_.1) | copy-start | bytes 1572868
  7.3 4.6 %copy-start.3 = (s32[2,2,4]{2,1,0:T(2,128)S(1)}, s32[2,2,4]{2,1,0:T(2,128)}, u32[]{:S(2)}) copy-start(s32[2,2,4]{2,1,0:T(2,128)} %param.7) | copy-start | bytes 196
  7.5 15.3 %copy-start.1 = (f32[2,2,256,32]{2,3,1,0:T(8,128)S(1)}, f32[2,2,256,32]{2,3,1,0:T(8,128)}, u32[]{:S(2)}) copy-start(f32[2,2,256,32]{2,3,1,0:T(8,128)} %param.5) | copy-start | bytes 393220
  7.5 15.6 %collective-permute-start.5 = (f32[2,2,8,8,128]{4,3,2,1,0:T(8,128)S(1)}, f32[2,2,8,8,128]{4,3,2,1,0:T(8,128)S(1)}, u32[]{:S(2)}, u32[]{:S(2)}) collective-permute-start(f32[2,2,8,8,128]{4,3,2,1,0:T(8,128)S(1)} %get-tuple-element.31), channel_id=1, source_target_pairs={{0,1},{1,0},{2,3},{3,2},{4,5},{5,4},{6,7},{7,6},{8,9},{9,8},{10,11... | collective-permute-start | bytes 393224 | tf_op jit(solution)/shard_map/ppermute | solution.py:328
  8.0 15.1 %collective-permute-start.6 = (f32[2,2,8,8,128]{4,3,2,1,0:T(8,128)S(1)}, f32[2,2,8,8,128]{4,3,2,1,0:T(8,128)S(1)}, u32[]{:S(2)}, u32[]{:S(2)}) collective-permute-start(f32[2,2,8,8,128]{4,3,2,1,0:T(8,128)S(1)} %get-tuple-element.32), channel_id=1, source_target_pairs={{0,2},{1,3},{2,0},{3,1},{4,6},{5,7},{6,4},{7,5},{8,10},{9,11},{10,... | collective-permute-start | bytes 393224 | tf_op jit(solution)/shard_map/ppermute | solution.py:328
  8.1 15.0 %collective-permute-start.7 = (f32[2,2,8,8,128]{4,3,2,1,0:T(8,128)S(1)}, f32[2,2,8,8,128]{4,3,2,1,0:T(8,128)S(1)}, u32[]{:S(2)}, u32[]{:S(2)}) collective-permute-start(f32[2,2,8,8,128]{4,3,2,1,0:T(8,128)S(1)} %get-tuple-element.33), channel_id=1, source_target_pairs={{0,3},{1,2},{2,1},{3,0},{4,7},{5,6},{6,5},{7,4},{8,11},{9,10},{10,... | collective-permute-start | bytes 393224 | tf_op jit(solution)/shard_map/ppermute | solution.py:328
  12.0 10.8 %collective-permute-start.4 = (f32[2,2,32,256]{3,2,1,0:T(8,128)S(1)}, f32[2,2,32,256]{3,2,1,0:T(8,128)S(1)}, u32[]{:S(2)}, u32[]{:S(2)}) collective-permute-start(f32[2,2,32,256]{3,2,1,0:T(8,128)S(1)} %collective-permute-done.3.refs_2_), channel_id=1, source_target_pairs={{0,1},{1,0},{2,3},{3,2},{4,5},{5,4},{6,7},{7,6},{8,9},{9,8},{10,11... | collective-permute-start | bytes 393224 | tf_op jit(solution)/shard_map/ppermute | solution.py:328
  14.9 3.0 %collective-permute-start.1 = (s32[4]{0:T(128)S(1)}, s32[4]{0:T(128)S(1)}, u32[]{:S(2)}, u32[]{:S(2)}) collective-permute-start(s32[4]{0:T(128)S(1)} %get-tuple-element.26), channel_id=1, source_target_pairs={{4,0},{8,4},{12,8},{16,12},{20,16},{24,20},{28,24},{5,1},{9,5},{13... | collective-permute-start | bytes 56 | tf_op jit(solution)/shard_map/ppermute | solution.py:373
  17.9 4.8 %collective-permute-start.2 = (s32[4]{0:T(128)S(1)}, s32[4]{0:T(128)S(1)}, u32[]{:S(2)}, u32[]{:S(2)}) collective-permute-start(s32[4]{0:T(128)S(1)} %get-tuple-element.27), channel_id=1, source_target_pairs={{0,4},{4,8},{8,12},{12,16},{16,20},{20,24},{24,28},{1,5},{5,9},{9,... | collective-permute-start | bytes 56 | tf_op jit(solution)/shard_map/ppermute | solution.py:374
  23.1 1.5 %copy-start.2 = (f32[2,2,256,32]{2,3,1,0:T(8,128)S(1)}, f32[2,2,256,32]{2,3,1,0:T(8,128)}, u32[]{:S(2)}) copy-start(f32[2,2,256,32]{2,3,1,0:T(8,128)} %param.6) | copy-start | bytes 393220
  24.4 2.2 %collective-permute-start.8 = (f32[256,256]{1,0:T(8,128)S(1)}, f32[256,256]{1,0:T(8,128)S(1)}, u32[]{:S(2)}, u32[]{:S(2)}) collective-permute-start(f32[256,256]{1,0:T(8,128)S(1)} %summary.1.refs_0_.refs_4_), channel_id=1, source_target_pairs={{0,4},{4,0},{8,12},{12,8},{16,20},{20,16},{24,28},{28,24},{1,5},{5... | collective-permute-start | bytes 786440 | tf_op jit(solution)/shard_map/ppermute | solution.py:328
  24.7 9.5 %collective-permute-start.16 = (f32[2,2,32,256]{3,2,1,0:T(8,128)S(1)}, f32[2,2,32,256]{3,2,1,0:T(8,128)S(1)}, u32[]{:S(2)}, u32[]{:S(2)}) collective-permute-start(f32[2,2,32,256]{3,2,1,0:T(8,128)S(1)} %bitcast.13), channel_id=1, source_target_pairs={{0,2},{1,3},{2,0},{3,1},{4,6},{5,7},{6,4},{7,5},{8,10},{9,11},{10,... | collective-permute-start | bytes 393224 | tf_op jit(solution)/shard_map/ppermute | solution.py:328
  27.0 7.2 %collective-permute-start.13 = (f32[128,256]{1,0:T(8,128)S(1)}, f32[128,256]{1,0:T(8,128)S(1)}, u32[]{:S(2)}, u32[]{:S(2)}) collective-permute-start(f32[128,256]{1,0:T(8,128)S(1)} %get-tuple-element.35), channel_id=1, source_target_pairs={{0,24},{4,28},{8,16},{12,20},{16,8},{20,12},{24,0},{28,4},{1,25},{... | collective-permute-start | bytes 393224 | tf_op jit(solution)/shard_map/ppermute | solution.py:328
  29.5 6.8 %collective-permute-start.11 = (f32[128,256]{1,0:T(8,128)S(1)}, f32[128,256]{1,0:T(8,128)S(1)}, u32[]{:S(2)}, u32[]{:S(2)}) collective-permute-start(f32[128,256]{1,0:T(8,128)S(1)} %get-tuple-element.35), channel_id=1, source_target_pairs={{0,16},{4,20},{8,24},{12,28},{16,0},{20,4},{24,8},{28,12},{1,17},{... | collective-permute-start | bytes 393224 | tf_op jit(solution)/shard_map/ppermute | solution.py:328
  30.0 7.1 %collective-permute-start.9 = (f32[128,256]{1,0:T(8,128)S(1)}, f32[128,256]{1,0:T(8,128)S(1)}, u32[]{:S(2)}, u32[]{:S(2)}) collective-permute-start(f32[128,256]{1,0:T(8,128)S(1)} %get-tuple-element.35), channel_id=1, source_target_pairs={{0,8},{4,12},{8,0},{12,4},{16,24},{20,28},{24,16},{28,20},{1,9},{5... | collective-permute-start | bytes 393224 | tf_op jit(solution)/shard_map/ppermute | solution.py:328
  30.8 6.4 %collective-permute-start.15 = (f32[2,2,32,256]{3,2,1,0:T(8,128)S(1)}, f32[2,2,32,256]{3,2,1,0:T(8,128)S(1)}, u32[]{:S(2)}, u32[]{:S(2)}) collective-permute-start(f32[2,2,32,256]{3,2,1,0:T(8,128)S(1)} %bitcast.14), channel_id=1, source_target_pairs={{0,1},{1,0},{2,3},{3,2},{4,5},{5,4},{6,7},{7,6},{8,9},{9,8},{10,11... | collective-permute-start | bytes 393224 | tf_op jit(solution)/shard_map/ppermute | solution.py:328
  34.2 5.5 %collective-permute-start.17 = (f32[2,2,32,256]{3,2,1,0:T(8,128)S(1)}, f32[2,2,32,256]{3,2,1,0:T(8,128)S(1)}, u32[]{:S(2)}, u32[]{:S(2)}) collective-permute-start(f32[2,2,32,256]{3,2,1,0:T(8,128)S(1)} %collective-permute-done.16.refs_2_), channel_id=1, source_target_pairs={{0,1},{1,0},{2,3},{3,2},{4,5},{5,4},{6,7},{7,6},{8,9},{9,8},{10,11... | collective-permute-start | bytes 393224 | tf_op jit(solution)/shard_map/ppermute | solution.py:328
  34.2 5.8 %collective-permute-start.14 = (f32[128,256]{1,0:T(8,128)S(1)}, f32[128,256]{1,0:T(8,128)S(1)}, u32[]{:S(2)}, u32[]{:S(2)}) collective-permute-start(f32[128,256]{1,0:T(8,128)S(1)} %collective-permute-done.13.refs_11_), channel_id=1, source_target_pairs={{0,4},{4,0},{8,12},{12,8},{16,20},{20,16},{24,28},{28,24},{1,5},{5... | collective-permute-start | bytes 393224 | tf_op jit(solution)/shard_map/ppermute | solution.py:328
  36.3 3.6 %collective-permute-start.12 = (f32[128,256]{1,0:T(8,128)S(1)}, f32[128,256]{1,0:T(8,128)S(1)}, u32[]{:S(2)}, u32[]{:S(2)}) collective-permute-start(f32[128,256]{1,0:T(8,128)S(1)} %collective-permute-done.11.refs_9_), channel_id=1, source_target_pairs={{0,4},{4,0},{8,12},{12,8},{16,20},{20,16},{24,28},{28,24},{1,5},{5... | collective-permute-start | bytes 393224 | tf_op jit(solution)/shard_map/ppermute | solution.py:328
  37.1 2.8 %collective-permute-start.10 = (f32[128,256]{1,0:T(8,128)S(1)}, f32[128,256]{1,0:T(8,128)S(1)}, u32[]{:S(2)}, u32[]{:S(2)}) collective-permute-start(f32[128,256]{1,0:T(8,128)S(1)} %collective-permute-done.9.refs_7_), channel_id=1, source_target_pairs={{0,4},{4,0},{8,12},{12,8},{16,20},{20,16},{24,28},{28,24},{1,5},{5... | collective-permute-start | bytes 393224 | tf_op jit(solution)/shard_map/ppermute | solution.py:328
  42.4 2.9 %collective-permute-start.19 = (f32[256,256]{1,0:T(8,128)S(1)}, f32[256,256]{1,0:T(8,128)S(1)}, u32[]{:S(2)}, u32[]{:S(2)}) collective-permute-start(f32[256,256]{1,0:T(8,128)S(1)} %get-tuple-element.41.refs_0_.refs_5_), channel_id=1, source_target_pairs={{0,4},{4,0},{8,12},{12,8},{16,20},{20,16},{24,28},{28,24},{1,5},{5... | collective-permute-start | bytes 786440 | tf_op jit(solution)/shard_map/ppermute | solution.py:328
  42.5 7.8 %collective-permute-start.22 = (f32[2,2,8,8,128]{4,3,2,1,0:T(8,128)S(1)}, f32[2,2,8,8,128]{4,3,2,1,0:T(8,128)S(1)}, u32[]{:S(2)}, u32[]{:S(2)}) collective-permute-start(f32[2,2,8,8,128]{4,3,2,1,0:T(8,128)S(1)} %get-tuple-element.44), channel_id=1, source_target_pairs={{0,3},{1,2},{2,1},{3,0},{4,7},{5,6},{6,5},{7,4},{8,11},{9,10},{10,... | collective-permute-start | bytes 393224 | tf_op jit(solution)/shard_map/ppermute | solution.py:328
  45.7 8.2 %collective-permute-start.23 = (f32[128,256]{1,0:T(8,128)S(1)}, f32[128,256]{1,0:T(8,128)S(1)}, u32[]{:S(2)}, u32[]{:S(2)}) collective-permute-start(f32[128,256]{1,0:T(8,128)S(1)} %get-tuple-element.43), channel_id=1, source_target_pairs={{0,16},{4,20},{8,24},{12,28},{16,0},{20,4},{24,8},{28,12},{1,17},{... | collective-permute-start | bytes 393224 | tf_op jit(solution)/shard_map/ppermute | solution.py:328
  47.8 7.3 %collective-permute-start.25 = (f32[128,256]{1,0:T(8,128)S(1)}, f32[128,256]{1,0:T(8,128)S(1)}, u32[]{:S(2)}, u32[]{:S(2)}) collective-permute-start(f32[128,256]{1,0:T(8,128)S(1)} %get-tuple-element.43), channel_id=1, source_target_pairs={{0,24},{4,28},{8,16},{12,20},{16,8},{20,12},{24,0},{28,4},{1,25},{... | collective-permute-start | bytes 393224 | tf_op jit(solution)/shard_map/ppermute | solution.py:328
  49.0 6.8 %collective-permute-start.20 = (f32[128,256]{1,0:T(8,128)S(1)}, f32[128,256]{1,0:T(8,128)S(1)}, u32[]{:S(2)}, u32[]{:S(2)}) collective-permute-start(f32[128,256]{1,0:T(8,128)S(1)} %get-tuple-element.43), channel_id=1, source_target_pairs={{0,8},{4,12},{8,0},{12,4},{16,24},{20,28},{24,16},{28,20},{1,9},{5... | collective-permute-start | bytes 393224 | tf_op jit(solution)/shard_map/ppermute | solution.py:328
  49.4 8.0 %collective-permute-start.18 = (f32[2,2,8,8,128]{4,3,2,1,0:T(8,128)S(1)}, f32[2,2,8,8,128]{4,3,2,1,0:T(8,128)S(1)}, u32[]{:S(2)}, u32[]{:S(2)}) collective-permute-start(f32[2,2,8,8,128]{4,3,2,1,0:T(8,128)S(1)} %get-tuple-element.39), channel_id=1, source_target_pairs={{0,2},{1,3},{2,0},{3,1},{4,6},{5,7},{6,4},{7,5},{8,10},{9,11},{10,... | collective-permute-start | bytes 393224 | tf_op jit(solution)/shard_map/ppermute | solution.py:328
  53.8 3.5 %collective-permute-start.24 = (f32[128,256]{1,0:T(8,128)S(1)}, f32[128,256]{1,0:T(8,128)S(1)}, u32[]{:S(2)}, u32[]{:S(2)}) collective-permute-start(f32[128,256]{1,0:T(8,128)S(1)} %hold.3.refs_10_), channel_id=1, source_target_pairs={{0,4},{4,0},{8,12},{12,8},{16,20},{20,16},{24,28},{28,24},{1,5},{5... | collective-permute-start | bytes 393224 | tf_op jit(solution)/shard_map/ppermute | solution.py:328
  55.1 2.2 %collective-permute-start.26 = (f32[128,256]{1,0:T(8,128)S(1)}, f32[128,256]{1,0:T(8,128)S(1)}, u32[]{:S(2)}, u32[]{:S(2)}) collective-permute-start(f32[128,256]{1,0:T(8,128)S(1)} %collective-permute-done.25.refs_12_), channel_id=1, source_target_pairs={{0,4},{4,0},{8,12},{12,8},{16,20},{20,16},{24,28},{28,24},{1,5},{5... | collective-permute-start | bytes 393224 | tf_op jit(solution)/shard_map/ppermute | solution.py:328
  55.8 1.6 %collective-permute-start.21 = (f32[128,256]{1,0:T(8,128)S(1)}, f32[128,256]{1,0:T(8,128)S(1)}, u32[]{:S(2)}, u32[]{:S(2)}) collective-permute-start(f32[128,256]{1,0:T(8,128)S(1)} %collective-permute-done.20.refs_8_), channel_id=1, source_target_pairs={{0,4},{4,0},{8,12},{12,8},{16,20},{20,16},{24,28},{28,24},{1,5},{5... | collective-permute-start | bytes 393224 | tf_op jit(solution)/shard_map/ppermute | solution.py:328
  58.8 14.2 %collective-permute-start.27 = (f32[2,2,2,8,8,128]{5,4,3,2,1,0:T(8,128)S(1)}, f32[2,2,2,8,8,128]{5,4,3,2,1,0:T(8,128)S(1)}, u32[]{:S(2)}, u32[]{:S(2)}) collective-permute-start(f32[2,2,2,8,8,128]{5,4,3,2,1,0:T(8,128)S(1)} %get-tuple-element.47), channel_id=1, source_target_pairs={{0,1},{1,0},{2,3},{3,2},{4,5},{5,4},{6,7},{7,6},{8,9},{9,8},{10,11... | collective-permute-start | bytes 786440 | tf_op jit(solution)/shard_map/ppermute | solution.py:328
  58.9 9.5 %collective-permute-start.28 = (f32[2,2,8,8,128]{4,3,2,1,0:T(8,128)S(1)}, f32[2,2,8,8,128]{4,3,2,1,0:T(8,128)S(1)}, u32[]{:S(2)}, u32[]{:S(2)}) collective-permute-start(f32[2,2,8,8,128]{4,3,2,1,0:T(8,128)S(1)} %get-tuple-element.48), channel_id=1, source_target_pairs={{0,2},{1,3},{2,0},{3,1},{4,6},{5,7},{6,4},{7,5},{8,10},{9,11},{10,... | collective-permute-start | bytes 393224 | tf_op jit(solution)/shard_map/ppermute | solution.py:328
  61.4 11.7 %collective-permute-start.29 = (f32[2,2,8,8,128]{4,3,2,1,0:T(8,128)S(1)}, f32[2,2,8,8,128]{4,3,2,1,0:T(8,128)S(1)}, u32[]{:S(2)}, u32[]{:S(2)}) collective-permute-start(f32[2,2,8,8,128]{4,3,2,1,0:T(8,128)S(1)} %get-tuple-element.49), channel_id=1, source_target_pairs={{0,3},{1,2},{2,1},{3,0},{4,7},{5,6},{6,5},{7,4},{8,11},{9,10},{10,... | collective-permute-start | bytes 393224 | tf_op jit(solution)/shard_map/ppermute | solution.py:328

commit v4 on v3

--- a/solution.py
+++ b/solution.py
@@ -55,22 +55,19 @@
 
 def pick(value, state, picked, offsets, coils, row):
     taps, lines = picked.shape[1] // 2 // coils, state.shape[1] // 2 // coils
+    line = [jnp.sum(offsets[row : row + 1, tap : tap + 1]) for tap in range(taps)]
     chunks = value.shape[1] // LANES
     for i in range(chunks):
         state[i] = value[:, i * LANES : (i + 1) * LANES]
         for part in range(2):
             for tap in range(taps):
-                source = pl.ds(part * coils * lines + offsets[row, tap], coils, stride=lines)
+                source = pl.ds(part * coils * lines + line[tap], coils, stride=lines)
                 picked[i, pl.ds(part * coils * taps + tap, coils, stride=taps), :] = state[i, source, :]
     return jnp.concatenate([picked[i] for i in range(chunks)], axis=1)
 
 
 def pick_scratch(lanes, state, size):
     return [pltpu.VMEM((lanes // LANES, state, LANES), F32), pltpu.VMEM((lanes // LANES, size, LANES), F32)]
-
-
-def offset_scratch(offsets):
-    return [pltpu.SMEM(offsets.shape, jnp.int32), pltpu.SemaphoreType.DMA]
 
 
 def visits(segs, backward):
@@ -176,11 +173,8 @@
     segs, _, coils, _, width = measured.shape
     lanes = size // 2 + width
 
-    def body(off_ref, hi_ref, lo_ref, m_ref, e_ref, state, picked, off, sem):
-        fetch = pltpu.make_async_copy(off_ref, off, sem)
-        fetch.start()
-        fetch.wait()
-        choose = functools.partial(pick, state=state, picked=picked, offsets=off, coils=coils)
+    def body(off_ref, hi_ref, lo_ref, m_ref, e_ref, state, picked):
+        choose = functools.partial(pick, state=state, picked=picked, offsets=off_ref, coils=coils)
         e_ref[...] = response(hi_ref, lo_ref, [m_ref[s].reshape(rows, width) for s in range(segs)], choose, False)
 
     return call(
@@ -188,7 +182,7 @@
         "summary",
         [((size, lanes), F32)],
         [VMEM] * 4,
-        pick_scratch(lanes, rows, size) + offset_scratch(offsets),
+        pick_scratch(lanes, rows, size),
     )(offsets, high, low, measured)[0]
 
 
@@ -255,14 +249,11 @@
         outs, refs = refs[:n], refs[n:]
         if following:
             e_ref, refs = refs[0], refs[1:]
-        whole, table, carried, state, picked, off, sem = refs
-        fetch = pltpu.make_async_copy(off_ref, off, sem)
-        fetch.start()
-        choose = functools.partial(pick, state=state, picked=picked, offsets=off, coils=coils)
+        whole, table, carried, state, picked = refs
+        choose = functools.partial(pick, state=state, picked=picked, offsets=off_ref, coils=coils)
         value = incoming(own, rest, table, carried, backward)
         moved = product(halves(real_form(b_ref[:, :cols])), value) + b_ref[:, cols:]
         value = jnp.where(my_chip()[1] == (1 if backward else 0), value, moved)
-        fetch.wait()
         source = [m_ref[s].reshape(rows, width) for s in range(segs)]
         states, _ = walk(lambda s: (hi_ref[s], lo_ref[s]), value, source, choose, backward)
         if following:
@@ -290,8 +281,7 @@
         [VMEM] * (6 + len(blocks) + len(extra)),
         scratch
         + incoming_scratch(chips, size, lanes)
-        + pick_scratch(lanes if following else width, rows, size)
-        + offset_scratch(offsets),
+        + pick_scratch(lanes if following else width, rows, size),
         after=after,
     )(offsets, high, low, sources, mine, other, *blocks, *extra)
 

time: 74.3 us -> 73.7 us (level)
  no operation moved by 1% of the time
where the time goes in v4:
time: 73.7 us; the launch traced here: 73.5 us
  starting transfers between devices  34.8 us (47%)
  waiting for transfers between devices  29.8 us (40%)
  Pallas kernels  6.97 us (9%)
  local copies, waits for them, and re-layouts  1.07 us (1%)
  between operations  0.84 us (1%)
    ppermute x28, starting transfers between devices, swap(): lax.ppermute(block, axis, [(i, i ^ distance) for i in range(lax.axis_size...  29.6 us
    ppermute x28, waiting for transfers between devices, swap(): lax.ppermute(block, axis, [(i, i ^ distance) for i in range(lax.axis_size...  27.2 us
    ppermute x1, starting transfers between devices, shards(): lax.ppermute(last, 'seg', [(i, i + 1) for i in range(places - 1)])[None]  3.97 us
    pallas_call x2, Pallas kernels, finish(): call(body, 'finish_backward' if backward else 'finish_forward', out_shape...  3.86 us
    ppermute x1, waiting for transfers between devices, shards(): lax.ppermute(first, 'seg', [(i + 1, i) for i in range(places - 1)])[None]  1.72 us
  transfers between devices with their start and end apart: 30, of which 15 were waited for; matrix products, arithmetic and copies ran while one was open for 0% of the time, Pallas kernels for 2%

profile of v4, /device:TPU:0, one launch (start us, length us, event | category | flops | bytes accessed | tf_op | source)
XLA Modules:
  0.0 73.5 jit_solution(8620547460083302078)
XLA Ops:
  0.6 4.1 %collective-permute-start.3 = (f32[2,2,32,256]{3,2,1,0:T(8,128)}, f32[2,2,32,256]{3,2,1,0:T(8,128)S(1)}, u32[]{:S(2)}, u32[]{:S(2)}) collective-permute-start(f32[2,2,32,256]{3,2,1,0:T(8,128)} %bitcast.10), channel_id=1, source_target_pairs={{0,2},{1,3},{2,0},{3,1},{4,6},{5,7},{6,4},{7,5},{8,10},{9,11},{10,... | collective-permute-start | bytes 393224 | tf_op jit(solution)/shard_map/ppermute | solution.py:318
  4.7 1.6 %collective-permute-start = (f32[2,2,32,256]{3,2,1,0:T(8,128)}, f32[2,2,32,256]{3,2,1,0:T(8,128)S(1)}, u32[]{:S(2)}, u32[]{:S(2)}) collective-permute-start(f32[2,2,32,256]{3,2,1,0:T(8,128)} %bitcast.11), channel_id=1, source_target_pairs={{0,1},{1,0},{2,3},{3,2},{4,5},{5,4},{6,7},{7,6},{8,9},{9,8},{10,11... | collective-permute-start | bytes 393224 | tf_op jit(solution)/shard_map/ppermute | solution.py:318
  6.3 1.0 %copy-done = f32[2,2,8,8,512]{4,3,2,1,0:T(8,128)S(1)} copy-done((f32[2,2,8,8,512]{4,3,2,1,0:T(8,128)S(1)}, f32[2,2,8,8,512]{4,3,2,1,0:T(8,128)}, u32[]{:S(2)}) %copy-start) | copy-done | bytes 524312
  7.4 0.1 pack.1
  7.5 0.0 copy-start.1
  7.5 0.5 collective-permute-start.5
  8.0 0.1 collective-permute-start.6
  8.1 3.9 %collective-permute-start.7 = (f32[2,2,8,8,128]{4,3,2,1,0:T(8,128)S(1)}, f32[2,2,8,8,128]{4,3,2,1,0:T(8,128)S(1)}, u32[]{:S(2)}, u32[]{:S(2)}) collective-permute-start(f32[2,2,8,8,128]{4,3,2,1,0:T(8,128)S(1)} %get-tuple-element.33), channel_id=1, source_target_pairs={{0,3},{1,2},{2,1},{3,0},{4,7},{5,6},{6,5},{7,4},{8,11},{9,10},{10,... | collective-permute-start | bytes 393224 | tf_op jit(solution)/shard_map/ppermute | solution.py:318
  11.9 0.0 collective-permute-done.3.refs_2_
  12.0 0.3 collective-permute-start.4
  12.2 2.6 %collective-permute-done.refs_0_.refs_1_ = f32[2,2,32,256]{3,2,1,0:T(8,128)S(1)} collective-permute-done((f32[2,2,32,256]{3,2,1,0:T(8,128)}, f32[2,2,32,256]{3,2,1,0:T(8,128)S(1)}, u32[]{:S(2)}, u32[]{:S(2)}) %collective-permute-start) | collective-permute-done | bytes 131104 | tf_op jit(solution)/shard_map/ppermute | solution.py:318
  14.9 1.3 %collective-permute-start.1 = (s32[4]{0:T(128)S(1)}, s32[4]{0:T(128)S(1)}, u32[]{:S(2)}, u32[]{:S(2)}) collective-permute-start(s32[4]{0:T(128)S(1)} %get-tuple-element.26), channel_id=1, source_target_pairs={{4,0},{8,4},{12,8},{16,12},{20,16},{24,20},{28,24},{5,1},{9,5},{13... | collective-permute-start | bytes 56 | tf_op jit(solution)/shard_map/ppermute | solution.py:363
  16.2 1.7 %collective-permute-done.1 = s32[4]{0:T(128)S(1)} collective-permute-done((s32[4]{0:T(128)S(1)}, s32[4]{0:T(128)S(1)}, u32[]{:S(2)}, u32[]{:S(2)}) %collective-permute-start.1) | collective-permute-done | bytes 48 | tf_op jit(solution)/shard_map/ppermute | solution.py:363
  17.9 4.0 %collective-permute-start.2 = (s32[4]{0:T(128)S(1)}, s32[4]{0:T(128)S(1)}, u32[]{:S(2)}, u32[]{:S(2)}) collective-permute-start(s32[4]{0:T(128)S(1)} %get-tuple-element.27), channel_id=1, source_target_pairs={{0,4},{4,8},{8,12},{12,16},{16,20},{20,24},{24,28},{1,5},{5,9},{9,... | collective-permute-start | bytes 56 | tf_op jit(solution)/shard_map/ppermute | solution.py:364
  21.8 0.8 %collective-permute-done.2 = s32[4]{0:T(128)S(1)} collective-permute-done((s32[4]{0:T(128)S(1)}, s32[4]{0:T(128)S(1)}, u32[]{:S(2)}, u32[]{:S(2)}) %collective-permute-start.2) | collective-permute-done | bytes 48 | tf_op jit(solution)/shard_map/ppermute | solution.py:364
  22.7 0.1 collective-permute-done.4.refs_3_
  22.8 0.3 prepare_forward.1
  23.1 0.0 collective-permute-done.5.refs_2_
  23.1 0.0 copy-start.2
  23.2 0.7 summary.1.refs_0_.refs_4_
  23.8 0.3 collective-permute-start.8
  24.1 2.0 %collective-permute-start.16 = (f32[2,2,32,256]{3,2,1,0:T(8,128)S(1)}, f32[2,2,32,256]{3,2,1,0:T(8,128)S(1)}, u32[]{:S(2)}, u32[]{:S(2)}) collective-permute-start(f32[2,2,32,256]{3,2,1,0:T(8,128)S(1)} %bitcast.13), channel_id=1, source_target_pairs={{0,2},{1,3},{2,0},{3,1},{4,6},{5,7},{6,4},{7,5},{8,10},{9,11},{10,... | collective-permute-start | bytes 393224 | tf_op jit(solution)/shard_map/ppermute | solution.py:318
  26.1 0.4 compose_forward.1
  26.5 2.5 %collective-permute-start.13 = (f32[128,256]{1,0:T(8,128)S(1)}, f32[128,256]{1,0:T(8,128)S(1)}, u32[]{:S(2)}, u32[]{:S(2)}) collective-permute-start(f32[128,256]{1,0:T(8,128)S(1)} %get-tuple-element.35), channel_id=1, source_target_pairs={{0,24},{4,28},{8,16},{12,20},{16,8},{20,12},{24,0},{28,4},{1,25},{... | collective-permute-start | bytes 393224 | tf_op jit(solution)/shard_map/ppermute | solution.py:318
  29.0 0.5 collective-permute-start.11
  29.5 0.7 collective-permute-start.9
  30.2 2.0 %collective-permute-start.15 = (f32[2,2,32,256]{3,2,1,0:T(8,128)S(1)}, f32[2,2,32,256]{3,2,1,0:T(8,128)S(1)}, u32[]{:S(2)}, u32[]{:S(2)}) collective-permute-start(f32[2,2,32,256]{3,2,1,0:T(8,128)S(1)} %bitcast.14), channel_id=1, source_target_pairs={{0,1},{1,0},{2,3},{3,2},{4,5},{5,4},{6,7},{7,6},{8,9},{9,8},{10,11... | collective-permute-start | bytes 393224 | tf_op jit(solution)/shard_map/ppermute | solution.py:318
  32.2 1.4 %collective-permute-done.16.refs_2_ = f32[2,2,32,256]{3,2,1,0:T(8,128)S(1)} collective-permute-done((f32[2,2,32,256]{3,2,1,0:T(8,128)S(1)}, f32[2,2,32,256]{3,2,1,0:T(8,128)S(1)}, u32[]{:S(2)}, u32[]{:S(2)}) %collective-permute-start.16) | collective-permute-done | bytes 131104 | tf_op jit(solution)/shard_map/ppermute | solution.py:318
  33.6 0.0 collective-permute-done.13.refs_11_
  33.6 0.0 collective-permute-start.14
  33.6 2.1 %collective-permute-done.11.refs_9_ = f32[128,256]{1,0:T(8,128)S(1)} collective-permute-done((f32[128,256]{1,0:T(8,128)S(1)}, f32[128,256]{1,0:T(8,128)S(1)}, u32[]{:S(2)}, u32[]{:S(2)}) %collective-permute-start.11) | collective-permute-done | bytes 131104 | tf_op jit(solution)/shard_map/ppermute | solution.py:318
  35.8 0.0 collective-permute-start.12
  35.8 0.8 %collective-permute-done.9.refs_7_ = f32[128,256]{1,0:T(8,128)S(1)} collective-permute-done((f32[128,256]{1,0:T(8,128)S(1)}, f32[128,256]{1,0:T(8,128)S(1)}, u32[]{:S(2)}, u32[]{:S(2)}) %collective-permute-start.9) | collective-permute-done | bytes 131104 | tf_op jit(solution)/shard_map/ppermute | solution.py:318
  36.6 0.0 collective-permute-start.10
  36.6 0.0 collective-permute-done.15.refs_1_
  36.6 2.6 %collective-permute-done.17.refs_3_ = f32[2,2,32,256]{3,2,1,0:T(8,128)S(1)} collective-permute-done((f32[2,2,32,256]{3,2,1,0:T(8,128)S(1)}, f32[2,2,32,256]{3,2,1,0:T(8,128)S(1)}, u32[]{:S(2)}, u32[]{:S(2)}) %collective-permute-start.17) | collective-permute-done | bytes 131104 | tf_op jit(solution)/shard_map/ppermute | solution.py:318
  39.1 0.3 prepare_backward.1
  39.4 0.0 collective-permute-done.12.refs_10_
  39.4 0.0 collective-permute-done.10.refs_8_
  39.4 2.4 %finish_forward.1 = (f32[2,2,8,8,128]{4,3,2,1,0:T(8,128)S(1)}, f32[2,2,8,8,128]{4,3,2,1,0:T(8,128)S(1)}, f32[2,2,8,8,128]{4,3,2,1,0:T(8,128)S(1)}, f32[2,2,8,8,1...) custom-call(s32[8,128]{1,0:T(8,128)S(1)} %pad.4.refs_0_.refs_1_, ...), custom_call_target="tpu_custom_call" | custom-call | tf_op jit(solution)/shard_map/finish_forward/pallas_call | solution.py:277
  41.9 0.1 collective-permute-start.19
  41.9 2.8 %collective-permute-start.22 = (f32[2,2,8,8,128]{4,3,2,1,0:T(8,128)S(1)}, f32[2,2,8,8,128]{4,3,2,1,0:T(8,128)S(1)}, u32[]{:S(2)}, u32[]{:S(2)}) collective-permute-start(f32[2,2,8,8,128]{4,3,2,1,0:T(8,128)S(1)} %get-tuple-element.44), channel_id=1, source_target_pairs={{0,3},{1,2},{2,1},{3,0},{4,7},{5,6},{6,5},{7,4},{8,11},{9,10},{10,... | collective-permute-start | bytes 393224 | tf_op jit(solution)/shard_map/ppermute | solution.py:318
  44.7 0.0 collective-permute-done.19.refs_1_.refs_6_
  44.7 0.4 compose_backward.1
  45.1 2.2 %collective-permute-start.23 = (f32[128,256]{1,0:T(8,128)S(1)}, f32[128,256]{1,0:T(8,128)S(1)}, u32[]{:S(2)}, u32[]{:S(2)}) collective-permute-start(f32[128,256]{1,0:T(8,128)S(1)} %get-tuple-element.43), channel_id=1, source_target_pairs={{0,16},{4,20},{8,24},{12,28},{16,0},{20,4},{24,8},{28,12},{1,17},{... | collective-permute-start | bytes 393224 | tf_op jit(solution)/shard_map/ppermute | solution.py:318
  47.2 1.1 %collective-permute-start.25 = (f32[128,256]{1,0:T(8,128)S(1)}, f32[128,256]{1,0:T(8,128)S(1)}, u32[]{:S(2)}, u32[]{:S(2)}) collective-permute-start(f32[128,256]{1,0:T(8,128)S(1)} %get-tuple-element.43), channel_id=1, source_target_pairs={{0,24},{4,28},{8,16},{12,20},{16,8},{20,12},{24,0},{28,4},{1,25},{... | collective-permute-start | bytes 393224 | tf_op jit(solution)/shard_map/ppermute | solution.py:318
  48.4 0.4 collective-permute-start.20
  48.8 0.1 collective-permute-start.18
  48.9 0.9 %collective-permute-done.22.refs_0_.refs_5_ = f32[2,2,8,8,128]{4,3,2,1,0:T(8,128)S(1)} collective-permute-done((f32[2,2,8,8,128]{4,3,2,1,0:T(8,128)S(1)}, f32[2,2,8,8,128]{4,3,2,1,0:T(8,128)S(1)}, u32[]{:S(2)}, u32[]{:S(2)}) %collective-permute-start.22) | collective-permute-done | bytes 131104 | tf_op jit(solution)/shard_map/ppermute | solution.py:318
  49.7 3.5 %collective-permute-done.23.refs_1_ = f32[128,256]{1,0:T(8,128)S(1)} collective-permute-done((f32[128,256]{1,0:T(8,128)S(1)}, f32[128,256]{1,0:T(8,128)S(1)}, u32[]{:S(2)}, u32[]{:S(2)}) %collective-permute-start.23) | collective-permute-done | bytes 131104 | tf_op jit(solution)/shard_map/ppermute | solution.py:318
  53.3 0.1 collective-permute-start.24
  53.3 1.2 %collective-permute-done.25.refs_12_ = f32[128,256]{1,0:T(8,128)S(1)} collective-permute-done((f32[128,256]{1,0:T(8,128)S(1)}, f32[128,256]{1,0:T(8,128)S(1)}, u32[]{:S(2)}, u32[]{:S(2)}) %collective-permute-start.25) | collective-permute-done | bytes 131104 | tf_op jit(solution)/shard_map/ppermute | solution.py:318
  54.5 0.0 collective-permute-start.26
  54.5 0.7 collective-permute-done.20.refs_8_
  55.2 0.0 collective-permute-start.21
  55.2 1.6 %collective-permute-done.18.refs_0_.refs_3_ = f32[2,2,8,8,128]{4,3,2,1,0:T(8,128)S(1)} collective-permute-done((f32[2,2,8,8,128]{4,3,2,1,0:T(8,128)S(1)}, f32[2,2,8,8,128]{4,3,2,1,0:T(8,128)S(1)}, u32[]{:S(2)}, u32[]{:S(2)}) %collective-permute-start.18) | collective-permute-done | bytes 131104 | tf_op jit(solution)/shard_map/ppermute | solution.py:318
  56.8 0.0 collective-permute-done.24.refs_11_
  56.8 1.4 %finish_backward.1 = (f32[2,2,8,8,128]{4,3,2,1,0:T(8,128)S(1)}, f32[2,2,2,8,8,128]{5,4,3,2,1,0:T(8,128)S(1)}, f32[2,2,8,8,128]{4,3,2,1,0:T(8,128)S(1)}, f32[2,2,8,8,128]{4,3,2,1,0:T(8,128)S(1)}) custom-call(f32[2,2,8,8,128]{4,3,2,1,0:T(8,128)S(1)} %collective-permute-done.18.refs_0_.refs_3_, s32[8,128]{1,0:T(8,128)S(1)} %pad.4.refs_0_.refs_1_, ...), custom_call_target="tpu_custom_call" | custom-call | tf_op jit(solution)/shard_map/finish_backward/pallas_call | solution.py:277
  58.2 0.1 collective-permute-start.27
  58.3 2.5 %collective-permute-start.28 = (f32[2,2,8,8,128]{4,3,2,1,0:T(8,128)S(1)}, f32[2,2,8,8,128]{4,3,2,1,0:T(8,128)S(1)}, u32[]{:S(2)}, u32[]{:S(2)}) collective-permute-start(f32[2,2,8,8,128]{4,3,2,1,0:T(8,128)S(1)} %get-tuple-element.48), channel_id=1, source_target_pairs={{0,2},{1,3},{2,0},{3,1},{4,6},{5,7},{6,4},{7,5},{8,10},{9,11},{10,... | collective-permute-start | bytes 393224 | tf_op jit(solution)/shard_map/ppermute | solution.py:318
  60.8 1.9 %collective-permute-start.29 = (f32[2,2,8,8,128]{4,3,2,1,0:T(8,128)S(1)}, f32[2,2,8,8,128]{4,3,2,1,0:T(8,128)S(1)}, u32[]{:S(2)}, u32[]{:S(2)}) collective-permute-start(f32[2,2,8,8,128]{4,3,2,1,0:T(8,128)S(1)} %get-tuple-element.49), channel_id=1, source_target_pairs={{0,3},{1,2},{2,1},{3,0},{4,7},{5,6},{6,5},{7,4},{8,11},{9,10},{10,... | collective-permute-start | bytes 393224 | tf_op jit(solution)/shard_map/ppermute | solution.py:318
  62.7 5.1 %collective-permute-done.28.refs_4_ = f32[2,2,8,8,128]{4,3,2,1,0:T(8,128)S(1)} collective-permute-done((f32[2,2,8,8,128]{4,3,2,1,0:T(8,128)S(1)}, f32[2,2,8,8,128]{4,3,2,1,0:T(8,128)S(1)}, u32[]{:S(2)}, u32[]{:S(2)}) %collective-permute-start.28) | collective-permute-done | bytes 131104 | tf_op jit(solution)/shard_map/ppermute | solution.py:318
  67.8 4.6 %collective-permute-done.29.refs_6_ = f32[2,2,8,8,128]{4,3,2,1,0:T(8,128)S(1)} collective-permute-done((f32[2,2,8,8,128]{4,3,2,1,0:T(8,128)S(1)}, f32[2,2,8,8,128]{4,3,2,1,0:T(8,128)S(1)}, u32[]{:S(2)}, u32[]{:S(2)}) %collective-permute-start.29) | collective-permute-done | bytes 131104 | tf_op jit(solution)/shard_map/ppermute | solution.py:318
  72.4 1.0 %unpack.1 = (f32[2,2,8,8,512]{4,3,2,1,0:T(8,128)}, f32[2,2,8,8,512]{4,3,2,1,0:T(8,128)}) custom-call(f32[2,2,8,8,128]{4,3,2,1,0:T(8,128)S(1)} %get-tuple-element.38.refs_0_, f32[2,2,8,8,128]{4,3,2,1,0:T(8,128)S(1)} %get-tuple-element.46.refs_1_, f32[2,2,2,8,8,128]{5,4,3,2,1,0:T(8,128)S(1)} %collective-permute-done.27.refs_2_, ...), custom_call_target="tpu_custom_call" | custom-call | tf_op jit(solution)/shard_map/unpack/pallas_call | solution.py:307
  (20 shorter events, 0.1 us)
Async XLA Ops:
  0.6 11.3 %collective-permute-start.3 = (f32[2,2,32,256]{3,2,1,0:T(8,128)}, f32[2,2,32,256]{3,2,1,0:T(8,128)S(1)}, u32[]{:S(2)}, u32[]{:S(2)}) collective-permute-start(f32[2,2,32,256]{3,2,1,0:T(8,128)} %bitcast.10), channel_id=1, source_target_pairs={{0,2},{1,3},{2,0},{3,1},{4,6},{5,7},{6,4},{7,5},{8,10},{9,11},{10,... | collective-permute-start | bytes 393224 | tf_op jit(solution)/shard_map/ppermute | solution.py:318
  4.7 10.1 %collective-permute-start = (f32[2,2,32,256]{3,2,1,0:T(8,128)}, f32[2,2,32,256]{3,2,1,0:T(8,128)S(1)}, u32[]{:S(2)}, u32[]{:S(2)}) collective-permute-start(f32[2,2,32,256]{3,2,1,0:T(8,128)} %bitcast.11), channel_id=1, source_target_pairs={{0,1},{1,0},{2,3},{3,2},{4,5},{5,4},{6,7},{7,6},{8,9},{9,8},{10,11... | collective-permute-start | bytes 393224 | tf_op jit(solution)/shard_map/ppermute | solution.py:318
  6.3 1.0 %copy-start = (f32[2,2,8,8,512]{4,3,2,1,0:T(8,128)S(1)}, f32[2,2,8,8,512]{4,3,2,1,0:T(8,128)}, u32[]{:S(2)}) copy-start(f32[2,2,8,8,512]{4,3,2,1,0:T(8,128)} %refs_0_.1) | copy-start | bytes 1572868
  7.3 4.6 %copy-start.3 = (s32[2,2,4]{2,1,0:T(2,128)S(1)}, s32[2,2,4]{2,1,0:T(2,128)}, u32[]{:S(2)}) copy-start(s32[2,2,4]{2,1,0:T(2,128)} %param.7) | copy-start | bytes 196
  7.5 15.3 %copy-start.1 = (f32[2,2,256,32]{2,3,1,0:T(8,128)S(1)}, f32[2,2,256,32]{2,3,1,0:T(8,128)}, u32[]{:S(2)}) copy-start(f32[2,2,256,32]{2,3,1,0:T(8,128)} %param.5) | copy-start | bytes 393220
  7.5 15.6 %collective-permute-start.5 = (f32[2,2,8,8,128]{4,3,2,1,0:T(8,128)S(1)}, f32[2,2,8,8,128]{4,3,2,1,0:T(8,128)S(1)}, u32[]{:S(2)}, u32[]{:S(2)}) collective-permute-start(f32[2,2,8,8,128]{4,3,2,1,0:T(8,128)S(1)} %get-tuple-element.31), channel_id=1, source_target_pairs={{0,1},{1,0},{2,3},{3,2},{4,5},{5,4},{6,7},{7,6},{8,9},{9,8},{10,11... | collective-permute-start | bytes 393224 | tf_op jit(solution)/shard_map/ppermute | solution.py:318
  8.0 15.1 %collective-permute-start.6 = (f32[2,2,8,8,128]{4,3,2,1,0:T(8,128)S(1)}, f32[2,2,8,8,128]{4,3,2,1,0:T(8,128)S(1)}, u32[]{:S(2)}, u32[]{:S(2)}) collective-permute-start(f32[2,2,8,8,128]{4,3,2,1,0:T(8,128)S(1)} %get-tuple-element.32), channel_id=1, source_target_pairs={{0,2},{1,3},{2,0},{3,1},{4,6},{5,7},{6,4},{7,5},{8,10},{9,11},{10,... | collective-permute-start | bytes 393224 | tf_op jit(solution)/shard_map/ppermute | solution.py:318
  8.1 15.0 %collective-permute-start.7 = (f32[2,2,8,8,128]{4,3,2,1,0:T(8,128)S(1)}, f32[2,2,8,8,128]{4,3,2,1,0:T(8,128)S(1)}, u32[]{:S(2)}, u32[]{:S(2)}) collective-permute-start(f32[2,2,8,8,128]{4,3,2,1,0:T(8,128)S(1)} %get-tuple-element.33), channel_id=1, source_target_pairs={{0,3},{1,2},{2,1},{3,0},{4,7},{5,6},{6,5},{7,4},{8,11},{9,10},{10,... | collective-permute-start | bytes 393224 | tf_op jit(solution)/shard_map/ppermute | solution.py:318
  12.0 10.8 %collective-permute-start.4 = (f32[2,2,32,256]{3,2,1,0:T(8,128)S(1)}, f32[2,2,32,256]{3,2,1,0:T(8,128)S(1)}, u32[]{:S(2)}, u32[]{:S(2)}) collective-permute-start(f32[2,2,32,256]{3,2,1,0:T(8,128)S(1)} %collective-permute-done.3.refs_2_), channel_id=1, source_target_pairs={{0,1},{1,0},{2,3},{3,2},{4,5},{5,4},{6,7},{7,6},{8,9},{9,8},{10,11... | collective-permute-start | bytes 393224 | tf_op jit(solution)/shard_map/ppermute | solution.py:318
  14.9 3.0 %collective-permute-start.1 = (s32[4]{0:T(128)S(1)}, s32[4]{0:T(128)S(1)}, u32[]{:S(2)}, u32[]{:S(2)}) collective-permute-start(s32[4]{0:T(128)S(1)} %get-tuple-element.26), channel_id=1, source_target_pairs={{4,0},{8,4},{12,8},{16,12},{20,16},{24,20},{28,24},{5,1},{9,5},{13... | collective-permute-start | bytes 56 | tf_op jit(solution)/shard_map/ppermute | solution.py:363
  17.9 4.8 %collective-permute-start.2 = (s32[4]{0:T(128)S(1)}, s32[4]{0:T(128)S(1)}, u32[]{:S(2)}, u32[]{:S(2)}) collective-permute-start(s32[4]{0:T(128)S(1)} %get-tuple-element.27), channel_id=1, source_target_pairs={{0,4},{4,8},{8,12},{12,16},{16,20},{20,24},{24,28},{1,5},{5,9},{9,... | collective-permute-start | bytes 56 | tf_op jit(solution)/shard_map/ppermute | solution.py:364
  23.1 1.0 %copy-start.2 = (f32[2,2,256,32]{2,3,1,0:T(8,128)S(1)}, f32[2,2,256,32]{2,3,1,0:T(8,128)}, u32[]{:S(2)}) copy-start(f32[2,2,256,32]{2,3,1,0:T(8,128)} %param.6) | copy-start | bytes 393220
  23.8 2.3 %collective-permute-start.8 = (f32[256,256]{1,0:T(8,128)S(1)}, f32[256,256]{1,0:T(8,128)S(1)}, u32[]{:S(2)}, u32[]{:S(2)}) collective-permute-start(f32[256,256]{1,0:T(8,128)S(1)} %summary.1.refs_0_.refs_4_), channel_id=1, source_target_pairs={{0,4},{4,0},{8,12},{12,8},{16,20},{20,16},{24,28},{28,24},{1,5},{5... | collective-permute-start | bytes 786440 | tf_op jit(solution)/shard_map/ppermute | solution.py:318
  24.1 9.5 %collective-permute-start.16 = (f32[2,2,32,256]{3,2,1,0:T(8,128)S(1)}, f32[2,2,32,256]{3,2,1,0:T(8,128)S(1)}, u32[]{:S(2)}, u32[]{:S(2)}) collective-permute-start(f32[2,2,32,256]{3,2,1,0:T(8,128)S(1)} %bitcast.13), channel_id=1, source_target_pairs={{0,2},{1,3},{2,0},{3,1},{4,6},{5,7},{6,4},{7,5},{8,10},{9,11},{10,... | collective-permute-start | bytes 393224 | tf_op jit(solution)/shard_map/ppermute | solution.py:318
  26.5 7.1 %collective-permute-start.13 = (f32[128,256]{1,0:T(8,128)S(1)}, f32[128,256]{1,0:T(8,128)S(1)}, u32[]{:S(2)}, u32[]{:S(2)}) collective-permute-start(f32[128,256]{1,0:T(8,128)S(1)} %get-tuple-element.35), channel_id=1, source_target_pairs={{0,24},{4,28},{8,16},{12,20},{16,8},{20,12},{24,0},{28,4},{1,25},{... | collective-permute-start | bytes 393224 | tf_op jit(solution)/shard_map/ppermute | solution.py:318
  29.0 6.7 %collective-permute-start.11 = (f32[128,256]{1,0:T(8,128)S(1)}, f32[128,256]{1,0:T(8,128)S(1)}, u32[]{:S(2)}, u32[]{:S(2)}) collective-permute-start(f32[128,256]{1,0:T(8,128)S(1)} %get-tuple-element.35), channel_id=1, source_target_pairs={{0,16},{4,20},{8,24},{12,28},{16,0},{20,4},{24,8},{28,12},{1,17},{... | collective-permute-start | bytes 393224 | tf_op jit(solution)/shard_map/ppermute | solution.py:318
  29.5 7.0 %collective-permute-start.9 = (f32[128,256]{1,0:T(8,128)S(1)}, f32[128,256]{1,0:T(8,128)S(1)}, u32[]{:S(2)}, u32[]{:S(2)}) collective-permute-start(f32[128,256]{1,0:T(8,128)S(1)} %get-tuple-element.35), channel_id=1, source_target_pairs={{0,8},{4,12},{8,0},{12,4},{16,24},{20,28},{24,16},{28,20},{1,9},{5... | collective-permute-start | bytes 393224 | tf_op jit(solution)/shard_map/ppermute | solution.py:318
  30.2 6.4 %collective-permute-start.15 = (f32[2,2,32,256]{3,2,1,0:T(8,128)S(1)}, f32[2,2,32,256]{3,2,1,0:T(8,128)S(1)}, u32[]{:S(2)}, u32[]{:S(2)}) collective-permute-start(f32[2,2,32,256]{3,2,1,0:T(8,128)S(1)} %bitcast.14), channel_id=1, source_target_pairs={{0,1},{1,0},{2,3},{3,2},{4,5},{5,4},{6,7},{7,6},{8,9},{9,8},{10,11... | collective-permute-start | bytes 393224 | tf_op jit(solution)/shard_map/ppermute | solution.py:318
  33.6 5.5 %collective-permute-start.17 = (f32[2,2,32,256]{3,2,1,0:T(8,128)S(1)}, f32[2,2,32,256]{3,2,1,0:T(8,128)S(1)}, u32[]{:S(2)}, u32[]{:S(2)}) collective-permute-start(f32[2,2,32,256]{3,2,1,0:T(8,128)S(1)} %collective-permute-done.16.refs_2_), channel_id=1, source_target_pairs={{0,1},{1,0},{2,3},{3,2},{4,5},{5,4},{6,7},{7,6},{8,9},{9,8},{10,11... | collective-permute-start | bytes 393224 | tf_op jit(solution)/shard_map/ppermute | solution.py:318
  33.6 5.8 %collective-permute-start.14 = (f32[128,256]{1,0:T(8,128)S(1)}, f32[128,256]{1,0:T(8,128)S(1)}, u32[]{:S(2)}, u32[]{:S(2)}) collective-permute-start(f32[128,256]{1,0:T(8,128)S(1)} %collective-permute-done.13.refs_11_), channel_id=1, source_target_pairs={{0,4},{4,0},{8,12},{12,8},{16,20},{20,16},{24,28},{28,24},{1,5},{5... | collective-permute-start | bytes 393224 | tf_op jit(solution)/shard_map/ppermute | solution.py:318
  35.8 3.6 %collective-permute-start.12 = (f32[128,256]{1,0:T(8,128)S(1)}, f32[128,256]{1,0:T(8,128)S(1)}, u32[]{:S(2)}, u32[]{:S(2)}) collective-permute-start(f32[128,256]{1,0:T(8,128)S(1)} %collective-permute-done.11.refs_9_), channel_id=1, source_target_pairs={{0,4},{4,0},{8,12},{12,8},{16,20},{20,16},{24,28},{28,24},{1,5},{5... | collective-permute-start | bytes 393224 | tf_op jit(solution)/shard_map/ppermute | solution.py:318
  36.6 2.8 %collective-permute-start.10 = (f32[128,256]{1,0:T(8,128)S(1)}, f32[128,256]{1,0:T(8,128)S(1)}, u32[]{:S(2)}, u32[]{:S(2)}) collective-permute-start(f32[128,256]{1,0:T(8,128)S(1)} %collective-permute-done.9.refs_7_), channel_id=1, source_target_pairs={{0,4},{4,0},{8,12},{12,8},{16,20},{20,16},{24,28},{28,24},{1,5},{5... | collective-permute-start | bytes 393224 | tf_op jit(solution)/shard_map/ppermute | solution.py:318
  41.9 2.9 %collective-permute-start.19 = (f32[256,256]{1,0:T(8,128)S(1)}, f32[256,256]{1,0:T(8,128)S(1)}, u32[]{:S(2)}, u32[]{:S(2)}) collective-permute-start(f32[256,256]{1,0:T(8,128)S(1)} %get-tuple-element.41.refs_0_.refs_5_), channel_id=1, source_target_pairs={{0,4},{4,0},{8,12},{12,8},{16,20},{20,16},{24,28},{28,24},{1,5},{5... | collective-permute-start | bytes 786440 | tf_op jit(solution)/shard_map/ppermute | solution.py:318
  41.9 7.8 %collective-permute-start.22 = (f32[2,2,8,8,128]{4,3,2,1,0:T(8,128)S(1)}, f32[2,2,8,8,128]{4,3,2,1,0:T(8,128)S(1)}, u32[]{:S(2)}, u32[]{:S(2)}) collective-permute-start(f32[2,2,8,8,128]{4,3,2,1,0:T(8,128)S(1)} %get-tuple-element.44), channel_id=1, source_target_pairs={{0,3},{1,2},{2,1},{3,0},{4,7},{5,6},{6,5},{7,4},{8,11},{9,10},{10,... | collective-permute-start | bytes 393224 | tf_op jit(solution)/shard_map/ppermute | solution.py:318
  45.1 8.2 %collective-permute-start.23 = (f32[128,256]{1,0:T(8,128)S(1)}, f32[128,256]{1,0:T(8,128)S(1)}, u32[]{:S(2)}, u32[]{:S(2)}) collective-permute-start(f32[128,256]{1,0:T(8,128)S(1)} %get-tuple-element.43), channel_id=1, source_target_pairs={{0,16},{4,20},{8,24},{12,28},{16,0},{20,4},{24,8},{28,12},{1,17},{... | collective-permute-start | bytes 393224 | tf_op jit(solution)/shard_map/ppermute | solution.py:318
  47.2 7.3 %collective-permute-start.25 = (f32[128,256]{1,0:T(8,128)S(1)}, f32[128,256]{1,0:T(8,128)S(1)}, u32[]{:S(2)}, u32[]{:S(2)}) collective-permute-start(f32[128,256]{1,0:T(8,128)S(1)} %get-tuple-element.43), channel_id=1, source_target_pairs={{0,24},{4,28},{8,16},{12,20},{16,8},{20,12},{24,0},{28,4},{1,25},{... | collective-permute-start | bytes 393224 | tf_op jit(solution)/shard_map/ppermute | solution.py:318
  48.4 6.8 %collective-permute-start.20 = (f32[128,256]{1,0:T(8,128)S(1)}, f32[128,256]{1,0:T(8,128)S(1)}, u32[]{:S(2)}, u32[]{:S(2)}) collective-permute-start(f32[128,256]{1,0:T(8,128)S(1)} %get-tuple-element.43), channel_id=1, source_target_pairs={{0,8},{4,12},{8,0},{12,4},{16,24},{20,28},{24,16},{28,20},{1,9},{5... | collective-permute-start | bytes 393224 | tf_op jit(solution)/shard_map/ppermute | solution.py:318
  48.8 8.0 %collective-permute-start.18 = (f32[2,2,8,8,128]{4,3,2,1,0:T(8,128)S(1)}, f32[2,2,8,8,128]{4,3,2,1,0:T(8,128)S(1)}, u32[]{:S(2)}, u32[]{:S(2)}) collective-permute-start(f32[2,2,8,8,128]{4,3,2,1,0:T(8,128)S(1)} %get-tuple-element.39), channel_id=1, source_target_pairs={{0,2},{1,3},{2,0},{3,1},{4,6},{5,7},{6,4},{7,5},{8,10},{9,11},{10,... | collective-permute-start | bytes 393224 | tf_op jit(solution)/shard_map/ppermute | solution.py:318
  53.3 3.5 %collective-permute-start.24 = (f32[128,256]{1,0:T(8,128)S(1)}, f32[128,256]{1,0:T(8,128)S(1)}, u32[]{:S(2)}, u32[]{:S(2)}) collective-permute-start(f32[128,256]{1,0:T(8,128)S(1)} %hold.3.refs_10_), channel_id=1, source_target_pairs={{0,4},{4,0},{8,12},{12,8},{16,20},{20,16},{24,28},{28,24},{1,5},{5... | collective-permute-start | bytes 393224 | tf_op jit(solution)/shard_map/ppermute | solution.py:318
  54.5 2.2 %collective-permute-start.26 = (f32[128,256]{1,0:T(8,128)S(1)}, f32[128,256]{1,0:T(8,128)S(1)}, u32[]{:S(2)}, u32[]{:S(2)}) collective-permute-start(f32[128,256]{1,0:T(8,128)S(1)} %collective-permute-done.25.refs_12_), channel_id=1, source_target_pairs={{0,4},{4,0},{8,12},{12,8},{16,20},{20,16},{24,28},{28,24},{1,5},{5... | collective-permute-start | bytes 393224 | tf_op jit(solution)/shard_map/ppermute | solution.py:318
  55.2 1.6 %collective-permute-start.21 = (f32[128,256]{1,0:T(8,128)S(1)}, f32[128,256]{1,0:T(8,128)S(1)}, u32[]{:S(2)}, u32[]{:S(2)}) collective-permute-start(f32[128,256]{1,0:T(8,128)S(1)} %collective-permute-done.20.refs_8_), channel_id=1, source_target_pairs={{0,4},{4,0},{8,12},{12,8},{16,20},{20,16},{24,28},{28,24},{1,5},{5... | collective-permute-start | bytes 393224 | tf_op jit(solution)/shard_map/ppermute | solution.py:318
  58.2 14.2 %collective-permute-start.27 = (f32[2,2,2,8,8,128]{5,4,3,2,1,0:T(8,128)S(1)}, f32[2,2,2,8,8,128]{5,4,3,2,1,0:T(8,128)S(1)}, u32[]{:S(2)}, u32[]{:S(2)}) collective-permute-start(f32[2,2,2,8,8,128]{5,4,3,2,1,0:T(8,128)S(1)} %get-tuple-element.47), channel_id=1, source_target_pairs={{0,1},{1,0},{2,3},{3,2},{4,5},{5,4},{6,7},{7,6},{8,9},{9,8},{10,11... | collective-permute-start | bytes 786440 | tf_op jit(solution)/shard_map/ppermute | solution.py:318
  58.3 9.5 %collective-permute-start.28 = (f32[2,2,8,8,128]{4,3,2,1,0:T(8,128)S(1)}, f32[2,2,8,8,128]{4,3,2,1,0:T(8,128)S(1)}, u32[]{:S(2)}, u32[]{:S(2)}) collective-permute-start(f32[2,2,8,8,128]{4,3,2,1,0:T(8,128)S(1)} %get-tuple-element.48), channel_id=1, source_target_pairs={{0,2},{1,3},{2,0},{3,1},{4,6},{5,7},{6,4},{7,5},{8,10},{9,11},{10,... | collective-permute-start | bytes 393224 | tf_op jit(solution)/shard_map/ppermute | solution.py:318
  60.8 11.6 %collective-permute-start.29 = (f32[2,2,8,8,128]{4,3,2,1,0:T(8,128)S(1)}, f32[2,2,8,8,128]{4,3,2,1,0:T(8,128)S(1)}, u32[]{:S(2)}, u32[]{:S(2)}) collective-permute-start(f32[2,2,8,8,128]{4,3,2,1,0:T(8,128)S(1)} %get-tuple-element.49), channel_id=1, source_target_pairs={{0,3},{1,2},{2,1},{3,0},{4,7},{5,6},{6,5},{7,4},{8,11},{9,10},{10,... | collective-permute-start | bytes 393224 | tf_op jit(solution)/shard_map/ppermute | solution.py:318

commit v5 on v4

--- a/solution.py
+++ b/solution.py
@@ -76,13 +76,15 @@
     return [(s, s + 1 if s < segs - 1 else 2 * segs) for s in range(segs)]
 
 
-def walk(maps, carried, sources, choose, backward):
+def walk(maps, carried, sources, choose, backward, sends):
     states = list(sources)
-    for s, row in visits(len(sources), backward):
+    order = visits(len(sources), backward)
+    for s, row in order:
         if carried is not None:
             states[s] = product(maps(s), carried) + sources[s]
-        carried = choose(states[s], row=row)
-    return states, carried
+        if sends or s != order[-1][0]:
+            carried = choose(states[s], row=row)
+    return carried if sends else states
 
 
 def response(high, low, states, choose, backward):
@@ -91,7 +93,7 @@
     columns = high[first, :, : size // 2].astype(F32) + low[first, :, : size // 2].astype(F32)
     blank = jnp.zeros_like(columns)
     sources = [jnp.concatenate([columns if s == first else blank, state], axis=1) for s, state in enumerate(states)]
-    return walk(lambda s: (high[s], low[s]), None, sources, choose, backward)[1]
+    return walk(lambda s: (high[s], low[s]), None, sources, choose, backward, True)
 
 
 def spot(near, i):
@@ -167,23 +169,23 @@
     )(*blocks)
 
 
-def summary(offsets, maps, measured):
+def summary(offsets, maps, sources, backward):
     high, low = maps
     _, rows, size = high.shape
-    segs, _, coils, _, width = measured.shape
+    segs, _, coils, _, width = sources.shape
     lanes = size // 2 + width
 
     def body(off_ref, hi_ref, lo_ref, m_ref, e_ref, state, picked):
         choose = functools.partial(pick, state=state, picked=picked, offsets=off_ref, coils=coils)
-        e_ref[...] = response(hi_ref, lo_ref, [m_ref[s].reshape(rows, width) for s in range(segs)], choose, False)
+        e_ref[...] = response(hi_ref, lo_ref, [m_ref[s].reshape(rows, width) for s in range(segs)], choose, backward)
 
     return call(
         body,
-        "summary",
+        "summary_backward" if backward else "summary_forward",
         [((size, lanes), F32)],
         [VMEM] * 4,
         pick_scratch(lanes, rows, size),
-    )(offsets, high, low, measured)[0]
+    )(offsets, high, low, sources)[0]
 
 
 def compose(mine, other, cols, backward):
@@ -233,7 +235,7 @@
     return [pltpu.VMEM((chips, 2, size // 2, lanes), F32), pltpu.VMEM((chips, size, lanes - size // 2), F32)]
 
 
-def finish(near, offsets, maps, sources, mine, other, blocks, backward, following=(), joined=None, after=()):
+def finish(near, offsets, maps, sources, mine, other, blocks, backward, joined=None, after=()):
     high, low = maps
     segs, _, coils, lines, width = sources.shape
     _, rows, size = high.shape
@@ -241,26 +243,23 @@
     chips = (len(blocks) + 1) // 2
     n = lax.axis_size("coil")
     own_coils = coils // n
-    extra = list(following) + ([] if joined is None else [joined])
+    extra = [] if joined is None else [joined]
 
     def body(off_ref, hi_ref, lo_ref, m_ref, a_ref, b_ref, own, *refs):
         at = 2 * chips - 2
         rest, extra_refs, refs = refs[:at], refs[at : at + len(extra)], refs[at + len(extra) :]
-        outs, refs = refs[:n], refs[n:]
-        if following:
-            e_ref, refs = refs[0], refs[1:]
+        pieces = n if backward else 0
+        outs, refs = refs[:pieces], refs[pieces:]
         whole, table, carried, state, picked = refs
         choose = functools.partial(pick, state=state, picked=picked, offsets=off_ref, coils=coils)
         value = incoming(own, rest, table, carried, backward)
         moved = product(halves(real_form(b_ref[:, :cols])), value) + b_ref[:, cols:]
         value = jnp.where(my_chip()[1] == (1 if backward else 0), value, moved)
         source = [m_ref[s].reshape(rows, width) for s in range(segs)]
-        states, _ = walk(lambda s: (hi_ref[s], lo_ref[s]), value, source, choose, backward)
-        if following:
-            e_ref[...] = response(extra_refs[0], extra_refs[1], states, choose, not backward)
+        states = walk(lambda s: (hi_ref[s], lo_ref[s]), value, source, choose, backward, False)
         for s in range(segs):
             whole[s] = states[s].reshape(2, coils, lines, width)
-        for i in range(n):
+        for i in range(len(outs)):
             cut = whole[:, :, pl.ds(spot(near, i) * own_coils, own_coils)]
             if joined is not None and i == 1:
                 outs[i][0] = extra_refs[-1][...]
@@ -271,19 +270,29 @@
     block = (segs, 2, own_coils, lines, width)
     out_shape = [((2, *block) if joined is not None and i == 1 else block, F32) for i in range(n)]
     scratch = [pltpu.VMEM(sources.shape, F32)]
-    if following:
-        out_shape += [((size, lanes), F32), (sources.shape, F32)]
+    if not backward:
+        out_shape = [(sources.shape, F32)]
         scratch = []
     return call(
         body,
         "finish_backward" if backward else "finish_forward",
         out_shape,
         [VMEM] * (6 + len(blocks) + len(extra)),
-        scratch
-        + incoming_scratch(chips, size, lanes)
-        + pick_scratch(lanes if following else width, rows, size),
+        scratch + incoming_scratch(chips, size, lanes) + pick_scratch(width, rows, size),
         after=after,
     )(offsets, high, low, sources, mine, other, *blocks, *extra)
+
+
+def cut(near, states, n, after):
+    segs, parts, coils, lines, width = states.shape
+    own_coils = coils // n
+
+    def body(s_ref, *outs):
+        for i in range(n):
+            outs[i][...] = s_ref[:, :, pl.ds(spot(near, i) * own_coils, own_coils)]
+
+    out = ((segs, parts, own_coils, lines, width), F32)
+    return call(body, "cut", [out] * n, [VMEM], after=after)(states)
 
 
 def unpack(forward, result, joined):
@@ -345,7 +354,6 @@
     taps = line_offsets.shape[2]
     width = measured.shape[4] // n
     cols = forward_kernel.shape[3] * n
-    first, last = line_offsets[0, 0], line_offsets[-1, 1]
     kernels_f, kernels_b = (jnp.swapaxes(k, 2, 3) for k in (forward_kernel, backward_kernel))
     aligned = width % LANES == 0 and (cols // taps // n) % 8 == 0
     if aligned:
@@ -353,25 +361,26 @@
         backward_blocks = spread_kernels(kernels_b)
         pieces = pack(measured)
         lines_blocks = [pieces[0]] + [swap(pieces[i], "coil", i) for i in range(1, n)]
-        first, last = hold(forward_blocks[1], first, last)
     else:
         forward_blocks = list(lax.all_gather(kernels_f, "coil"))
         backward_blocks = list(lax.all_gather(kernels_b, "coil"))
         split = lax.all_to_all(measured, "coil", split_axis=4, concat_axis=2, tiled=True)
         split = jnp.pad(split, [(0, 0)] * 4 + [(0, -width % LANES)])
         lines_blocks = jnp.split(split, n, axis=2)
-    after = lax.ppermute(first, "seg", [(i + 1, i) for i in range(places - 1)])[None]
-    before = lax.ppermute(last, "seg", [(i, i + 1) for i in range(places - 1)])[None]
+    after = lax.ppermute(line_offsets[0, 0], "seg", [((i + 1) % places, i) for i in range(places)])[None]
+    before = lax.ppermute(line_offsets[-1, 1], "seg", [(i, (i + 1) % places) for i in range(places)])[None]
     offsets = jnp.concatenate([line_offsets[:, 0], line_offsets[:, 1], after, before])
     offsets = jnp.pad(offsets, [(0, -offsets.shape[0] % 8), (0, LANES - taps)])
 
     forward_maps = prepare(aligned, forward_blocks, False)
     lines = gather(aligned, lines_blocks, forward_maps[:1])
     backward_maps = prepare(aligned, backward_blocks, True)
-    mine = summary(offsets, forward_maps, lines)
+    mine = summary(offsets, forward_maps, lines, False)
     other = swap(mine, "seg", 1)
     blocks = exchange(*compose(mine, other, cols, False))
-    *forward_out, mine, forward = finish(aligned, offsets, forward_maps, lines, mine, other, blocks, False, backward_maps)
+    (forward,) = finish(aligned, offsets, forward_maps, lines, mine, other, blocks, False)
+    forward_out = cut(aligned, forward, n, backward_maps[:1])
+    mine = summary(offsets, backward_maps, forward, True)
     other = swap(mine, "seg", 1)
     whole, half = compose(mine, other, cols, True)
     if aligned:

time: 73.7 us -> 72.7 us (0.986)
  starting transfers between devices: 34.8 us -> 28.3 us
  waiting for transfers between devices: 29.8 us -> 35.5 us
    ppermute x28, waiting for transfers between devices: 27.2 us -> 30.9 us  [swap(): lax.ppermute(block, axis, [(i, i ^ distance) for i in range(lax.axis_size...]
    ppermute x2, starting transfers between devices: 5.25 us -> 1.83 us  [the longest x1 1.03 us: shards(): lax.ppermute(line_offsets[0, 0], 'seg', [((i + 1) % places, i) for i in r...]
    ppermute x28, starting transfers between devices: 29.6 us -> 26.5 us  [swap(): lax.ppermute(block, axis, [(i, i ^ distance) for i in range(lax.axis_size...]
    ppermute x2, waiting for transfers between devices: 2.52 us -> 4.58 us  [the longest x1 3.29 us: shards(): lax.ppermute(line_offsets[-1, 1], 'seg', [(i, (i + 1) % places) for i in...]
    pallas_call x2, Pallas kernels: 3.86 us -> 2.76 us  [finish(): call(body, 'finish_backward' if backward else 'finish_forward', out_shape...]
  transfers between devices with their start and end apart: 30 -> 30, of which waited for: 15 -> 16; matrix products, arithmetic and copies ran while one was open for 0% -> 0% of each run, Pallas kernels for 2% -> 2%
where the time goes in v5:
time: 72.7 us; the launch traced here: 72.5 us
  waiting for transfers between devices  35.5 us (49%)
  starting transfers between devices  28.3 us (39%)
  Pallas kernels  6.59 us (9%)
  local copies, waits for them, and re-layouts  1.21 us (2%)
  between operations  0.86 us (1%)
    ppermute x28, waiting for transfers between devices, swap(): lax.ppermute(block, axis, [(i, i ^ distance) for i in range(lax.axis_size...  30.9 us
    ppermute x28, starting transfers between devices, swap(): lax.ppermute(block, axis, [(i, i ^ distance) for i in range(lax.axis_size...  26.5 us
    ppermute x1, waiting for transfers between devices, shards(): lax.ppermute(line_offsets[-1, 1], 'seg', [(i, (i + 1) % places) for i in...  3.29 us
    pallas_call x2, Pallas kernels, finish(): call(body, 'finish_backward' if backward else 'finish_forward', out_shape...  2.76 us
  transfers between devices with their start and end apart: 30, of which 16 were waited for; matrix products, arithmetic and copies ran while one was open for 0% of the time, Pallas kernels for 2%

profile of v5, /device:TPU:0, one launch (start us, length us, event | category | flops | bytes accessed | tf_op | source)
XLA Modules:
  0.0 72.5 jit_solution(14191782303137558559)
XLA Ops:
  0.6 4.1 %collective-permute-start.6 = (f32[2,2,32,256]{3,2,1,0:T(8,128)}, f32[2,2,32,256]{3,2,1,0:T(8,128)S(1)}, u32[]{:S(2)}, u32[]{:S(2)}) collective-permute-start(f32[2,2,32,256]{3,2,1,0:T(8,128)} %bitcast.10), channel_id=1, source_target_pairs={{0,2},{1,3},{2,0},{3,1},{4,6},{5,7},{6,4},{7,5},{8,10},{9,11},{10,... | collective-permute-start | bytes 393224 | tf_op jit(solution)/shard_map/ppermute | solution.py:327
  4.7 1.6 %collective-permute-start.5 = (f32[2,2,32,256]{3,2,1,0:T(8,128)}, f32[2,2,32,256]{3,2,1,0:T(8,128)S(1)}, u32[]{:S(2)}, u32[]{:S(2)}) collective-permute-start(f32[2,2,32,256]{3,2,1,0:T(8,128)} %bitcast.11), channel_id=1, source_target_pairs={{0,1},{1,0},{2,3},{3,2},{4,5},{5,4},{6,7},{7,6},{8,9},{9,8},{10,11... | collective-permute-start | bytes 393224 | tf_op jit(solution)/shard_map/ppermute | solution.py:327
  6.3 1.0 %copy-done = f32[2,2,8,8,512]{4,3,2,1,0:T(8,128)S(1)} copy-done((f32[2,2,8,8,512]{4,3,2,1,0:T(8,128)S(1)}, f32[2,2,8,8,512]{4,3,2,1,0:T(8,128)}, u32[]{:S(2)}) %copy-start) | copy-done | bytes 524312
  7.4 0.1 pack.1
  7.5 0.0 copy-start.3
  7.5 0.1 collective-permute-start.10
  7.6 0.9 %collective-permute-start.8 = (f32[2,2,8,8,128]{4,3,2,1,0:T(8,128)S(1)}, f32[2,2,8,8,128]{4,3,2,1,0:T(8,128)S(1)}, u32[]{:S(2)}, u32[]{:S(2)}) collective-permute-start(f32[2,2,8,8,128]{4,3,2,1,0:T(8,128)S(1)} %get-tuple-element.26), channel_id=1, source_target_pairs={{0,1},{1,0},{2,3},{3,2},{4,5},{5,4},{6,7},{7,6},{8,9},{9,8},{10,11... | collective-permute-start | bytes 393224 | tf_op jit(solution)/shard_map/ppermute | solution.py:327
  8.5 1.0 %collective-permute-start.3 = (s32[4]{0:T(128)S(1)}, s32[4]{0:T(128)S(1)}, u32[]{:S(2)}, u32[]{:S(2)}) collective-permute-start(s32[4]{0:T(128)S(1)} %get-tuple-element.44), channel_id=1, source_target_pairs={{4,0},{8,4},{12,8},{16,12},{20,16},{24,20},{28,24},{0,28},{5,1},{9... | collective-permute-start | bytes 56 | tf_op jit(solution)/shard_map/ppermute | solution.py:370
  9.5 1.3 %collective-permute-done.3 = s32[4]{0:T(128)S(1)} collective-permute-done((s32[4]{0:T(128)S(1)}, s32[4]{0:T(128)S(1)}, u32[]{:S(2)}, u32[]{:S(2)}) %collective-permute-start.3) | collective-permute-done | bytes 48 | tf_op jit(solution)/shard_map/ppermute | solution.py:370
  10.8 0.8 %collective-permute-start.4 = (s32[4]{0:T(128)S(1)}, s32[4]{0:T(128)S(1)}, u32[]{:S(2)}, u32[]{:S(2)}) collective-permute-start(s32[4]{0:T(128)S(1)} %get-tuple-element.45), channel_id=1, source_target_pairs={{0,4},{4,8},{8,12},{12,16},{16,20},{20,24},{24,28},{28,0},{1,5},{5... | collective-permute-start | bytes 56 | tf_op jit(solution)/shard_map/ppermute | solution.py:371
  11.6 3.3 %collective-permute-done.4 = s32[4]{0:T(128)S(1)} collective-permute-done((s32[4]{0:T(128)S(1)}, s32[4]{0:T(128)S(1)}, u32[]{:S(2)}, u32[]{:S(2)}) %collective-permute-start.4) | collective-permute-done | bytes 48 | tf_op jit(solution)/shard_map/ppermute | solution.py:371
  14.9 3.0 %collective-permute-start.9 = (f32[2,2,8,8,128]{4,3,2,1,0:T(8,128)S(1)}, f32[2,2,8,8,128]{4,3,2,1,0:T(8,128)S(1)}, u32[]{:S(2)}, u32[]{:S(2)}) collective-permute-start(f32[2,2,8,8,128]{4,3,2,1,0:T(8,128)S(1)} %get-tuple-element.27), channel_id=1, source_target_pairs={{0,2},{1,3},{2,0},{3,1},{4,6},{5,7},{6,4},{7,5},{8,10},{9,11},{10,... | collective-permute-start | bytes 393224 | tf_op jit(solution)/shard_map/ppermute | solution.py:327
  17.9 0.0 collective-permute-done.6.refs_2_
  17.9 0.6 collective-permute-start.7
  18.5 0.0 collective-permute-done.5.refs_1_
  18.5 4.8 %collective-permute-done.7.refs_3_ = f32[2,2,32,256]{3,2,1,0:T(8,128)S(1)} collective-permute-done((f32[2,2,32,256]{3,2,1,0:T(8,128)S(1)}, f32[2,2,32,256]{3,2,1,0:T(8,128)S(1)}, u32[]{:S(2)}, u32[]{:S(2)}) %collective-permute-start.7) | collective-permute-done | bytes 131104 | tf_op jit(solution)/shard_map/ppermute | solution.py:327
  23.3 0.3 prepare_forward.1
  23.6 0.0 collective-permute-done.8.refs_2_
  23.6 0.0 collective-permute-done.9.refs_3_
  23.6 0.0 copy-start.2
  23.6 0.7 summary_forward.1.refs_0_.refs_4_
  24.3 0.1 collective-permute-start.11
  24.4 0.1 copy-done.2
  24.5 0.9 %collective-permute-start.1 = (f32[2,2,32,256]{3,2,1,0:T(8,128)S(1)}, f32[2,2,32,256]{3,2,1,0:T(8,128)S(1)}, u32[]{:S(2)}, u32[]{:S(2)}) collective-permute-start(f32[2,2,32,256]{3,2,1,0:T(8,128)S(1)} %bitcast.13), channel_id=1, source_target_pairs={{0,2},{1,3},{2,0},{3,1},{4,6},{5,7},{6,4},{7,5},{8,10},{9,11},{10,... | collective-permute-start | bytes 393224 | tf_op jit(solution)/shard_map/ppermute | solution.py:327
  25.4 0.5 collective-permute-done.11.refs_1_.refs_5_
  25.9 0.4 compose_forward.1
  26.3 1.5 %collective-permute-start.12 = (f32[128,256]{1,0:T(8,128)S(1)}, f32[128,256]{1,0:T(8,128)S(1)}, u32[]{:S(2)}, u32[]{:S(2)}) collective-permute-start(f32[128,256]{1,0:T(8,128)S(1)} %get-tuple-element.30), channel_id=1, source_target_pairs={{0,8},{4,12},{8,0},{12,4},{16,24},{20,28},{24,16},{28,20},{1,9},{5... | collective-permute-start | bytes 393224 | tf_op jit(solution)/shard_map/ppermute | solution.py:327
  27.8 1.4 %collective-permute-start.14 = (f32[128,256]{1,0:T(8,128)S(1)}, f32[128,256]{1,0:T(8,128)S(1)}, u32[]{:S(2)}, u32[]{:S(2)}) collective-permute-start(f32[128,256]{1,0:T(8,128)S(1)} %get-tuple-element.30), channel_id=1, source_target_pairs={{0,16},{4,20},{8,24},{12,28},{16,0},{20,4},{24,8},{28,12},{1,17},{... | collective-permute-start | bytes 393224 | tf_op jit(solution)/shard_map/ppermute | solution.py:327
  29.2 0.7 collective-permute-start.16
  29.9 1.7 %collective-permute-start = (f32[2,2,32,256]{3,2,1,0:T(8,128)S(1)}, f32[2,2,32,256]{3,2,1,0:T(8,128)S(1)}, u32[]{:S(2)}, u32[]{:S(2)}) collective-permute-start(f32[2,2,32,256]{3,2,1,0:T(8,128)S(1)} %bitcast.14), channel_id=1, source_target_pairs={{0,1},{1,0},{2,3},{3,2},{4,5},{5,4},{6,7},{7,6},{8,9},{9,8},{10,11... | collective-permute-start | bytes 393224 | tf_op jit(solution)/shard_map/ppermute | solution.py:327
  31.6 2.6 %collective-permute-done.1.refs_2_ = f32[2,2,32,256]{3,2,1,0:T(8,128)S(1)} collective-permute-done((f32[2,2,32,256]{3,2,1,0:T(8,128)S(1)}, f32[2,2,32,256]{3,2,1,0:T(8,128)S(1)}, u32[]{:S(2)}, u32[]{:S(2)}) %collective-permute-start.1) | collective-permute-done | bytes 131104 | tf_op jit(solution)/shard_map/ppermute | solution.py:327
  34.1 0.0 collective-permute-start.2
  34.1 0.0 collective-permute-done.12.refs_7_
  34.1 0.0 collective-permute-start.13
  34.1 0.6 collective-permute-done.14.refs_9_
  34.8 0.0 collective-permute-start.15
  34.8 1.1 %collective-permute-done.16.refs_11_ = f32[128,256]{1,0:T(8,128)S(1)} collective-permute-done((f32[128,256]{1,0:T(8,128)S(1)}, f32[128,256]{1,0:T(8,128)S(1)}, u32[]{:S(2)}, u32[]{:S(2)}) %collective-permute-start.16) | collective-permute-done | bytes 131104 | tf_op jit(solution)/shard_map/ppermute | solution.py:327
  35.9 1.1 %collective-permute-done.refs_1_ = f32[2,2,32,256]{3,2,1,0:T(8,128)S(1)} collective-permute-done((f32[2,2,32,256]{3,2,1,0:T(8,128)S(1)}, f32[2,2,32,256]{3,2,1,0:T(8,128)S(1)}, u32[]{:S(2)}, u32[]{:S(2)}) %collective-permute-start) | collective-permute-done | bytes 131104 | tf_op jit(solution)/shard_map/ppermute | solution.py:327
  36.9 2.7 %collective-permute-done.2.refs_3_ = f32[2,2,32,256]{3,2,1,0:T(8,128)S(1)} collective-permute-done((f32[2,2,32,256]{3,2,1,0:T(8,128)S(1)}, f32[2,2,32,256]{3,2,1,0:T(8,128)S(1)}, u32[]{:S(2)}, u32[]{:S(2)}) %collective-permute-start.2) | collective-permute-done | bytes 131104 | tf_op jit(solution)/shard_map/ppermute | solution.py:327
  39.6 0.3 prepare_backward.1
  39.9 0.0 collective-permute-done.15.refs_10_
  39.9 1.4 %finish_forward.1.refs_1_.refs_3_.refs_4_ = f32[2,2,32,8,128]{4,3,2,1,0:T(8,128)S(1)} custom-call(s32[8,128]{1,0:T(8,128)S(1)} %pad.4.refs_0_.refs_1_, bf16[2,512,256]{2,1,0:T(8,128)(2,1)S(1)} %get-tuple-element.23.refs_0_.refs_1_, bf16[2,512,256]{2,1,0:T(8,128)(2,1)S(1)} %get-tuple-element.24.refs_2_, f32[2,2,32,8,128]{4,3,2,1,0:T(8,128)S(1)} %gather.1.refs_3_, ...), custom_call_target="tpu_custom_call" | custom-call | tf_op jit(solution)/shard_map/finish_forward/pallas_call | solution.py:276
  41.3 0.7 summary_backward.1.refs_0_.refs_5_
  42.0 0.1 collective-permute-start.19
  42.1 1.9 %collective-permute-start.22 = (f32[2,2,8,8,128]{4,3,2,1,0:T(8,128)S(1)}, f32[2,2,8,8,128]{4,3,2,1,0:T(8,128)S(1)}, u32[]{:S(2)}, u32[]{:S(2)}) collective-permute-start(f32[2,2,8,8,128]{4,3,2,1,0:T(8,128)S(1)} %get-tuple-element.36), channel_id=1, source_target_pairs={{0,3},{1,2},{2,1},{3,0},{4,7},{5,6},{6,5},{7,4},{8,11},{9,10},{10,... | collective-permute-start | bytes 393224 | tf_op jit(solution)/shard_map/ppermute | solution.py:327
  43.9 0.0 collective-permute-done.19.refs_1_.refs_6_
  44.0 0.4 compose_backward.1
  44.3 1.6 %collective-permute-start.23 = (f32[128,256]{1,0:T(8,128)S(1)}, f32[128,256]{1,0:T(8,128)S(1)}, u32[]{:S(2)}, u32[]{:S(2)}) collective-permute-start(f32[128,256]{1,0:T(8,128)S(1)} %get-tuple-element.35), channel_id=1, source_target_pairs={{0,16},{4,20},{8,24},{12,28},{16,0},{20,4},{24,8},{28,12},{1,17},{... | collective-permute-start | bytes 393224 | tf_op jit(solution)/shard_map/ppermute | solution.py:327
  45.9 1.4 %collective-permute-start.20 = (f32[128,256]{1,0:T(8,128)S(1)}, f32[128,256]{1,0:T(8,128)S(1)}, u32[]{:S(2)}, u32[]{:S(2)}) collective-permute-start(f32[128,256]{1,0:T(8,128)S(1)} %get-tuple-element.35), channel_id=1, source_target_pairs={{0,8},{4,12},{8,0},{12,4},{16,24},{20,28},{24,16},{28,20},{1,9},{5... | collective-permute-start | bytes 393224 | tf_op jit(solution)/shard_map/ppermute | solution.py:327
  47.4 0.5 collective-permute-start.25
  47.9 0.1 collective-permute-start.18
  47.9 2.0 %collective-permute-done.22.refs_0_.refs_5_ = f32[2,2,8,8,128]{4,3,2,1,0:T(8,128)S(1)} collective-permute-done((f32[2,2,8,8,128]{4,3,2,1,0:T(8,128)S(1)}, f32[2,2,8,8,128]{4,3,2,1,0:T(8,128)S(1)}, u32[]{:S(2)}, u32[]{:S(2)}) %collective-permute-start.22) | collective-permute-done | bytes 131104 | tf_op jit(solution)/shard_map/ppermute | solution.py:327
  49.9 0.1 collective-permute-done.23.refs_1_
  50.0 0.1 collective-permute-start.24
  50.1 2.2 %collective-permute-done.20.refs_8_ = f32[128,256]{1,0:T(8,128)S(1)} collective-permute-done((f32[128,256]{1,0:T(8,128)S(1)}, f32[128,256]{1,0:T(8,128)S(1)}, u32[]{:S(2)}, u32[]{:S(2)}) %collective-permute-start.20) | collective-permute-done | bytes 131104 | tf_op jit(solution)/shard_map/ppermute | solution.py:327
  52.3 1.7 %collective-permute-done.25.refs_12_ = f32[128,256]{1,0:T(8,128)S(1)} collective-permute-done((f32[128,256]{1,0:T(8,128)S(1)}, f32[128,256]{1,0:T(8,128)S(1)}, u32[]{:S(2)}, u32[]{:S(2)}) %collective-permute-start.25) | collective-permute-done | bytes 131104 | tf_op jit(solution)/shard_map/ppermute | solution.py:327
  54.0 1.7 %collective-permute-done.18.refs_0_.refs_3_ = f32[2,2,8,8,128]{4,3,2,1,0:T(8,128)S(1)} collective-permute-done((f32[2,2,8,8,128]{4,3,2,1,0:T(8,128)S(1)}, f32[2,2,8,8,128]{4,3,2,1,0:T(8,128)S(1)}, u32[]{:S(2)}, u32[]{:S(2)}) %collective-permute-start.18) | collective-permute-done | bytes 131104 | tf_op jit(solution)/shard_map/ppermute | solution.py:327
  55.8 1.4 %finish_backward.1 = (f32[2,2,8,8,128]{4,3,2,1,0:T(8,128)S(1)}, f32[2,2,2,8,8,128]{5,4,3,2,1,0:T(8,128)S(1)}, f32[2,2,8,8,128]{4,3,2,1,0:T(8,128)S(1)}, f32[2,2,8,8,128]{4,3,2,1,0:T(8,128)S(1)}) custom-call(f32[2,2,8,8,128]{4,3,2,1,0:T(8,128)S(1)} %collective-permute-done.18.refs_0_.refs_3_, s32[8,128]{1,0:T(8,128)S(1)} %pad.4.refs_0_.refs_1_, ...), custom_call_target="tpu_custom_call" | custom-call | tf_op jit(solution)/shard_map/finish_backward/pallas_call | solution.py:276
  57.2 0.1 collective-permute-start.27
  57.2 2.6 %collective-permute-start.28 = (f32[2,2,8,8,128]{4,3,2,1,0:T(8,128)S(1)}, f32[2,2,8,8,128]{4,3,2,1,0:T(8,128)S(1)}, u32[]{:S(2)}, u32[]{:S(2)}) collective-permute-start(f32[2,2,8,8,128]{4,3,2,1,0:T(8,128)S(1)} %get-tuple-element.40), channel_id=1, source_target_pairs={{0,2},{1,3},{2,0},{3,1},{4,6},{5,7},{6,4},{7,5},{8,10},{9,11},{10,... | collective-permute-start | bytes 393224 | tf_op jit(solution)/shard_map/ppermute | solution.py:327
  59.9 1.7 %collective-permute-start.29 = (f32[2,2,8,8,128]{4,3,2,1,0:T(8,128)S(1)}, f32[2,2,8,8,128]{4,3,2,1,0:T(8,128)S(1)}, u32[]{:S(2)}, u32[]{:S(2)}) collective-permute-start(f32[2,2,8,8,128]{4,3,2,1,0:T(8,128)S(1)} %get-tuple-element.41), channel_id=1, source_target_pairs={{0,3},{1,2},{2,1},{3,0},{4,7},{5,6},{6,5},{7,4},{8,11},{9,10},{10,... | collective-permute-start | bytes 393224 | tf_op jit(solution)/shard_map/ppermute | solution.py:327
  61.6 5.1 %collective-permute-done.28.refs_4_ = f32[2,2,8,8,128]{4,3,2,1,0:T(8,128)S(1)} collective-permute-done((f32[2,2,8,8,128]{4,3,2,1,0:T(8,128)S(1)}, f32[2,2,8,8,128]{4,3,2,1,0:T(8,128)S(1)}, u32[]{:S(2)}, u32[]{:S(2)}) %collective-permute-start.28) | collective-permute-done | bytes 131104 | tf_op jit(solution)/shard_map/ppermute | solution.py:327
  66.7 4.7 %collective-permute-done.29.refs_6_ = f32[2,2,8,8,128]{4,3,2,1,0:T(8,128)S(1)} collective-permute-done((f32[2,2,8,8,128]{4,3,2,1,0:T(8,128)S(1)}, f32[2,2,8,8,128]{4,3,2,1,0:T(8,128)S(1)}, u32[]{:S(2)}, u32[]{:S(2)}) %collective-permute-start.29) | collective-permute-done | bytes 131104 | tf_op jit(solution)/shard_map/ppermute | solution.py:327
  71.5 1.0 %unpack.1 = (f32[2,2,8,8,512]{4,3,2,1,0:T(8,128)}, f32[2,2,8,8,512]{4,3,2,1,0:T(8,128)}) custom-call(f32[2,2,8,8,128]{4,3,2,1,0:T(8,128)S(1)} %get-tuple-element.31.refs_0_, f32[2,2,8,8,128]{4,3,2,1,0:T(8,128)S(1)} %get-tuple-element.38.refs_1_, f32[2,2,2,8,8,128]{5,4,3,2,1,0:T(8,128)S(1)} %collective-permute-done.27.refs_2_, ...), custom_call_target="tpu_custom_call" | custom-call | tf_op jit(solution)/shard_map/unpack/pallas_call | solution.py:316
  (21 shorter events, 0.2 us)
Async XLA Ops:
  0.6 17.2 %collective-permute-start.6 = (f32[2,2,32,256]{3,2,1,0:T(8,128)}, f32[2,2,32,256]{3,2,1,0:T(8,128)S(1)}, u32[]{:S(2)}, u32[]{:S(2)}) collective-permute-start(f32[2,2,32,256]{3,2,1,0:T(8,128)} %bitcast.10), channel_id=1, source_target_pairs={{0,2},{1,3},{2,0},{3,1},{4,6},{5,7},{6,4},{7,5},{8,10},{9,11},{10,... | collective-permute-start | bytes 393224 | tf_op jit(solution)/shard_map/ppermute | solution.py:327
  4.7 13.7 %collective-permute-start.5 = (f32[2,2,32,256]{3,2,1,0:T(8,128)}, f32[2,2,32,256]{3,2,1,0:T(8,128)S(1)}, u32[]{:S(2)}, u32[]{:S(2)}) collective-permute-start(f32[2,2,32,256]{3,2,1,0:T(8,128)} %bitcast.11), channel_id=1, source_target_pairs={{0,1},{1,0},{2,3},{3,2},{4,5},{5,4},{6,7},{7,6},{8,9},{9,8},{10,11... | collective-permute-start | bytes 393224 | tf_op jit(solution)/shard_map/ppermute | solution.py:327
  6.3 1.0 %copy-start = (f32[2,2,8,8,512]{4,3,2,1,0:T(8,128)S(1)}, f32[2,2,8,8,512]{4,3,2,1,0:T(8,128)}, u32[]{:S(2)}) copy-start(f32[2,2,8,8,512]{4,3,2,1,0:T(8,128)} %refs_0_.1) | copy-start | bytes 1572868
  7.3 15.9 %copy-start.1 = (f32[2,2,256,32]{2,3,1,0:T(8,128)S(1)}, f32[2,2,256,32]{2,3,1,0:T(8,128)}, u32[]{:S(2)}) copy-start(f32[2,2,256,32]{2,3,1,0:T(8,128)} %param.5) | copy-start | bytes 393220
  7.5 1.0 %copy-start.3 = (s32[2,2,4]{2,1,0:T(2,128)S(1)}, s32[2,2,4]{2,1,0:T(2,128)}, u32[]{:S(2)}) copy-start(s32[2,2,4]{2,1,0:T(2,128)} %param.7) | copy-start | bytes 196
  7.5 16.1 %collective-permute-start.10 = (f32[2,2,8,8,128]{4,3,2,1,0:T(8,128)S(1)}, f32[2,2,8,8,128]{4,3,2,1,0:T(8,128)S(1)}, u32[]{:S(2)}, u32[]{:S(2)}) collective-permute-start(f32[2,2,8,8,128]{4,3,2,1,0:T(8,128)S(1)} %get-tuple-element.28), channel_id=1, source_target_pairs={{0,3},{1,2},{2,1},{3,0},{4,7},{5,6},{6,5},{7,4},{8,11},{9,10},{10,... | collective-permute-start | bytes 393224 | tf_op jit(solution)/shard_map/ppermute | solution.py:327
  7.6 16.0 %collective-permute-start.8 = (f32[2,2,8,8,128]{4,3,2,1,0:T(8,128)S(1)}, f32[2,2,8,8,128]{4,3,2,1,0:T(8,128)S(1)}, u32[]{:S(2)}, u32[]{:S(2)}) collective-permute-start(f32[2,2,8,8,128]{4,3,2,1,0:T(8,128)S(1)} %get-tuple-element.26), channel_id=1, source_target_pairs={{0,1},{1,0},{2,3},{3,2},{4,5},{5,4},{6,7},{7,6},{8,9},{9,8},{10,11... | collective-permute-start | bytes 393224 | tf_op jit(solution)/shard_map/ppermute | solution.py:327
  8.5 2.3 %collective-permute-start.3 = (s32[4]{0:T(128)S(1)}, s32[4]{0:T(128)S(1)}, u32[]{:S(2)}, u32[]{:S(2)}) collective-permute-start(s32[4]{0:T(128)S(1)} %get-tuple-element.44), channel_id=1, source_target_pairs={{4,0},{8,4},{12,8},{16,12},{20,16},{24,20},{28,24},{0,28},{5,1},{9... | collective-permute-start | bytes 56 | tf_op jit(solution)/shard_map/ppermute | solution.py:370
  10.8 4.1 %collective-permute-start.4 = (s32[4]{0:T(128)S(1)}, s32[4]{0:T(128)S(1)}, u32[]{:S(2)}, u32[]{:S(2)}) collective-permute-start(s32[4]{0:T(128)S(1)} %get-tuple-element.45), channel_id=1, source_target_pairs={{0,4},{4,8},{8,12},{12,16},{16,20},{20,24},{24,28},{28,0},{1,5},{5... | collective-permute-start | bytes 56 | tf_op jit(solution)/shard_map/ppermute | solution.py:371
  14.9 8.7 %collective-permute-start.9 = (f32[2,2,8,8,128]{4,3,2,1,0:T(8,128)S(1)}, f32[2,2,8,8,128]{4,3,2,1,0:T(8,128)S(1)}, u32[]{:S(2)}, u32[]{:S(2)}) collective-permute-start(f32[2,2,8,8,128]{4,3,2,1,0:T(8,128)S(1)} %get-tuple-element.27), channel_id=1, source_target_pairs={{0,2},{1,3},{2,0},{3,1},{4,6},{5,7},{6,4},{7,5},{8,10},{9,11},{10,... | collective-permute-start | bytes 393224 | tf_op jit(solution)/shard_map/ppermute | solution.py:327
  17.9 5.4 %collective-permute-start.7 = (f32[2,2,32,256]{3,2,1,0:T(8,128)S(1)}, f32[2,2,32,256]{3,2,1,0:T(8,128)S(1)}, u32[]{:S(2)}, u32[]{:S(2)}) collective-permute-start(f32[2,2,32,256]{3,2,1,0:T(8,128)S(1)} %collective-permute-done.6.refs_2_), channel_id=1, source_target_pairs={{0,1},{1,0},{2,3},{3,2},{4,5},{5,4},{6,7},{7,6},{8,9},{9,8},{10,11... | collective-permute-start | bytes 393224 | tf_op jit(solution)/shard_map/ppermute | solution.py:327
  23.6 0.9 %copy-start.2 = (f32[2,2,256,32]{2,3,1,0:T(8,128)S(1)}, f32[2,2,256,32]{2,3,1,0:T(8,128)}, u32[]{:S(2)}) copy-start(f32[2,2,256,32]{2,3,1,0:T(8,128)} %param.6) | copy-start | bytes 393220
  24.3 1.6 %collective-permute-start.11 = (f32[256,256]{1,0:T(8,128)S(1)}, f32[256,256]{1,0:T(8,128)S(1)}, u32[]{:S(2)}, u32[]{:S(2)}) collective-permute-start(f32[256,256]{1,0:T(8,128)S(1)} %summary_forward.1.refs_0_.refs_4_), channel_id=1, source_target_pairs={{0,4},{4,0},{8,12},{12,8},{16,20},{20,16},{24,28},{28,24},{1,5},{5... | collective-permute-start | bytes 786440 | tf_op jit(solution)/shard_map/ppermute | solution.py:327
  24.5 9.6 %collective-permute-start.1 = (f32[2,2,32,256]{3,2,1,0:T(8,128)S(1)}, f32[2,2,32,256]{3,2,1,0:T(8,128)S(1)}, u32[]{:S(2)}, u32[]{:S(2)}) collective-permute-start(f32[2,2,32,256]{3,2,1,0:T(8,128)S(1)} %bitcast.13), channel_id=1, source_target_pairs={{0,2},{1,3},{2,0},{3,1},{4,6},{5,7},{6,4},{7,5},{8,10},{9,11},{10,... | collective-permute-start | bytes 393224 | tf_op jit(solution)/shard_map/ppermute | solution.py:327
  26.3 7.8 %collective-permute-start.12 = (f32[128,256]{1,0:T(8,128)S(1)}, f32[128,256]{1,0:T(8,128)S(1)}, u32[]{:S(2)}, u32[]{:S(2)}) collective-permute-start(f32[128,256]{1,0:T(8,128)S(1)} %get-tuple-element.30), channel_id=1, source_target_pairs={{0,8},{4,12},{8,0},{12,4},{16,24},{20,28},{24,16},{28,20},{1,9},{5... | collective-permute-start | bytes 393224 | tf_op jit(solution)/shard_map/ppermute | solution.py:327
  27.8 7.0 %collective-permute-start.14 = (f32[128,256]{1,0:T(8,128)S(1)}, f32[128,256]{1,0:T(8,128)S(1)}, u32[]{:S(2)}, u32[]{:S(2)}) collective-permute-start(f32[128,256]{1,0:T(8,128)S(1)} %get-tuple-element.30), channel_id=1, source_target_pairs={{0,16},{4,20},{8,24},{12,28},{16,0},{20,4},{24,8},{28,12},{1,17},{... | collective-permute-start | bytes 393224 | tf_op jit(solution)/shard_map/ppermute | solution.py:327
  29.2 6.7 %collective-permute-start.16 = (f32[128,256]{1,0:T(8,128)S(1)}, f32[128,256]{1,0:T(8,128)S(1)}, u32[]{:S(2)}, u32[]{:S(2)}) collective-permute-start(f32[128,256]{1,0:T(8,128)S(1)} %get-tuple-element.30), channel_id=1, source_target_pairs={{0,24},{4,28},{8,16},{12,20},{16,8},{20,12},{24,0},{28,4},{1,25},{... | collective-permute-start | bytes 393224 | tf_op jit(solution)/shard_map/ppermute | solution.py:327
  29.9 7.1 %collective-permute-start = (f32[2,2,32,256]{3,2,1,0:T(8,128)S(1)}, f32[2,2,32,256]{3,2,1,0:T(8,128)S(1)}, u32[]{:S(2)}, u32[]{:S(2)}) collective-permute-start(f32[2,2,32,256]{3,2,1,0:T(8,128)S(1)} %bitcast.14), channel_id=1, source_target_pairs={{0,1},{1,0},{2,3},{3,2},{4,5},{5,4},{6,7},{7,6},{8,9},{9,8},{10,11... | collective-permute-start | bytes 393224 | tf_op jit(solution)/shard_map/ppermute | solution.py:327
  34.1 5.5 %collective-permute-start.2 = (f32[2,2,32,256]{3,2,1,0:T(8,128)S(1)}, f32[2,2,32,256]{3,2,1,0:T(8,128)S(1)}, u32[]{:S(2)}, u32[]{:S(2)}) collective-permute-start(f32[2,2,32,256]{3,2,1,0:T(8,128)S(1)} %collective-permute-done.1.refs_2_), channel_id=1, source_target_pairs={{0,1},{1,0},{2,3},{3,2},{4,5},{5,4},{6,7},{7,6},{8,9},{9,8},{10,11... | collective-permute-start | bytes 393224 | tf_op jit(solution)/shard_map/ppermute | solution.py:327
  34.1 5.7 %collective-permute-start.13 = (f32[128,256]{1,0:T(8,128)S(1)}, f32[128,256]{1,0:T(8,128)S(1)}, u32[]{:S(2)}, u32[]{:S(2)}) collective-permute-start(f32[128,256]{1,0:T(8,128)S(1)} %collective-permute-done.12.refs_7_), channel_id=1, source_target_pairs={{0,4},{4,0},{8,12},{12,8},{16,20},{20,16},{24,28},{28,24},{1,5},{5... | collective-permute-start | bytes 393224 | tf_op jit(solution)/shard_map/ppermute | solution.py:327
  34.8 5.1 %collective-permute-start.15 = (f32[128,256]{1,0:T(8,128)S(1)}, f32[128,256]{1,0:T(8,128)S(1)}, u32[]{:S(2)}, u32[]{:S(2)}) collective-permute-start(f32[128,256]{1,0:T(8,128)S(1)} %collective-permute-done.14.refs_9_), channel_id=1, source_target_pairs={{0,4},{4,0},{8,12},{12,8},{16,20},{20,16},{24,28},{28,24},{1,5},{5... | collective-permute-start | bytes 393224 | tf_op jit(solution)/shard_map/ppermute | solution.py:327
  35.8 4.0 %collective-permute-start.17 = (f32[128,256]{1,0:T(8,128)S(1)}, f32[128,256]{1,0:T(8,128)S(1)}, u32[]{:S(2)}, u32[]{:S(2)}) collective-permute-start(f32[128,256]{1,0:T(8,128)S(1)} %collective-permute-done.16.refs_11_), channel_id=1, source_target_pairs={{0,4},{4,0},{8,12},{12,8},{16,20},{20,16},{24,28},{28,24},{1,5},{5... | collective-permute-start | bytes 393224 | tf_op jit(solution)/shard_map/ppermute | solution.py:327
  42.0 2.0 %collective-permute-start.19 = (f32[256,256]{1,0:T(8,128)S(1)}, f32[256,256]{1,0:T(8,128)S(1)}, u32[]{:S(2)}, u32[]{:S(2)}) collective-permute-start(f32[256,256]{1,0:T(8,128)S(1)} %summary_backward.1.refs_0_.refs_5_), channel_id=1, source_target_pairs={{0,4},{4,0},{8,12},{12,8},{16,20},{20,16},{24,28},{28,24},{1,5},{5... | collective-permute-start | bytes 786440 | tf_op jit(solution)/shard_map/ppermute | solution.py:327
  42.1 7.9 %collective-permute-start.22 = (f32[2,2,8,8,128]{4,3,2,1,0:T(8,128)S(1)}, f32[2,2,8,8,128]{4,3,2,1,0:T(8,128)S(1)}, u32[]{:S(2)}, u32[]{:S(2)}) collective-permute-start(f32[2,2,8,8,128]{4,3,2,1,0:T(8,128)S(1)} %get-tuple-element.36), channel_id=1, source_target_pairs={{0,3},{1,2},{2,1},{3,0},{4,7},{5,6},{6,5},{7,4},{8,11},{9,10},{10,... | collective-permute-start | bytes 393224 | tf_op jit(solution)/shard_map/ppermute | solution.py:327
  44.3 5.7 %collective-permute-start.23 = (f32[128,256]{1,0:T(8,128)S(1)}, f32[128,256]{1,0:T(8,128)S(1)}, u32[]{:S(2)}, u32[]{:S(2)}) collective-permute-start(f32[128,256]{1,0:T(8,128)S(1)} %get-tuple-element.35), channel_id=1, source_target_pairs={{0,16},{4,20},{8,24},{12,28},{16,0},{20,4},{24,8},{28,12},{1,17},{... | collective-permute-start | bytes 393224 | tf_op jit(solution)/shard_map/ppermute | solution.py:327
  45.9 6.4 %collective-permute-start.20 = (f32[128,256]{1,0:T(8,128)S(1)}, f32[128,256]{1,0:T(8,128)S(1)}, u32[]{:S(2)}, u32[]{:S(2)}) collective-permute-start(f32[128,256]{1,0:T(8,128)S(1)} %get-tuple-element.35), channel_id=1, source_target_pairs={{0,8},{4,12},{8,0},{12,4},{16,24},{20,28},{24,16},{28,20},{1,9},{5... | collective-permute-start | bytes 393224 | tf_op jit(solution)/shard_map/ppermute | solution.py:327
  47.4 6.6 %collective-permute-start.25 = (f32[128,256]{1,0:T(8,128)S(1)}, f32[128,256]{1,0:T(8,128)S(1)}, u32[]{:S(2)}, u32[]{:S(2)}) collective-permute-start(f32[128,256]{1,0:T(8,128)S(1)} %get-tuple-element.35), channel_id=1, source_target_pairs={{0,24},{4,28},{8,16},{12,20},{16,8},{20,12},{24,0},{28,4},{1,25},{... | collective-permute-start | bytes 393224 | tf_op jit(solution)/shard_map/ppermute | solution.py:327
  47.9 7.9 %collective-permute-start.18 = (f32[2,2,8,8,128]{4,3,2,1,0:T(8,128)S(1)}, f32[2,2,8,8,128]{4,3,2,1,0:T(8,128)S(1)}, u32[]{:S(2)}, u32[]{:S(2)}) collective-permute-start(f32[2,2,8,8,128]{4,3,2,1,0:T(8,128)S(1)} %get-tuple-element.32), channel_id=1, source_target_pairs={{0,2},{1,3},{2,0},{3,1},{4,6},{5,7},{6,4},{7,5},{8,10},{9,11},{10,... | collective-permute-start | bytes 393224 | tf_op jit(solution)/shard_map/ppermute | solution.py:327
  50.0 5.7 %collective-permute-start.24 = (f32[128,256]{1,0:T(8,128)S(1)}, f32[128,256]{1,0:T(8,128)S(1)}, u32[]{:S(2)}, u32[]{:S(2)}) collective-permute-start(f32[128,256]{1,0:T(8,128)S(1)} %hold.1.refs_10_), channel_id=1, source_target_pairs={{0,4},{4,0},{8,12},{12,8},{16,20},{20,16},{24,28},{28,24},{1,5},{5... | collective-permute-start | bytes 393224 | tf_op jit(solution)/shard_map/ppermute | solution.py:327
  52.3 3.4 %collective-permute-start.21 = (f32[128,256]{1,0:T(8,128)S(1)}, f32[128,256]{1,0:T(8,128)S(1)}, u32[]{:S(2)}, u32[]{:S(2)}) collective-permute-start(f32[128,256]{1,0:T(8,128)S(1)} %collective-permute-done.20.refs_8_), channel_id=1, source_target_pairs={{0,4},{4,0},{8,12},{12,8},{16,20},{20,16},{24,28},{28,24},{1,5},{5... | collective-permute-start | bytes 393224 | tf_op jit(solution)/shard_map/ppermute | solution.py:327
  54.0 1.8 %collective-permute-start.26 = (f32[128,256]{1,0:T(8,128)S(1)}, f32[128,256]{1,0:T(8,128)S(1)}, u32[]{:S(2)}, u32[]{:S(2)}) collective-permute-start(f32[128,256]{1,0:T(8,128)S(1)} %collective-permute-done.25.refs_12_), channel_id=1, source_target_pairs={{0,4},{4,0},{8,12},{12,8},{16,20},{20,16},{24,28},{28,24},{1,5},{5... | collective-permute-start | bytes 393224 | tf_op jit(solution)/shard_map/ppermute | solution.py:327
  57.2 14.3 %collective-permute-start.27 = (f32[2,2,2,8,8,128]{5,4,3,2,1,0:T(8,128)S(1)}, f32[2,2,2,8,8,128]{5,4,3,2,1,0:T(8,128)S(1)}, u32[]{:S(2)}, u32[]{:S(2)}) collective-permute-start(f32[2,2,2,8,8,128]{5,4,3,2,1,0:T(8,128)S(1)} %get-tuple-element.39), channel_id=1, source_target_pairs={{0,1},{1,0},{2,3},{3,2},{4,5},{5,4},{6,7},{7,6},{8,9},{9,8},{10,11... | collective-permute-start | bytes 786440 | tf_op jit(solution)/shard_map/ppermute | solution.py:327
  57.2 9.5 %collective-permute-start.28 = (f32[2,2,8,8,128]{4,3,2,1,0:T(8,128)S(1)}, f32[2,2,8,8,128]{4,3,2,1,0:T(8,128)S(1)}, u32[]{:S(2)}, u32[]{:S(2)}) collective-permute-start(f32[2,2,8,8,128]{4,3,2,1,0:T(8,128)S(1)} %get-tuple-element.40), channel_id=1, source_target_pairs={{0,2},{1,3},{2,0},{3,1},{4,6},{5,7},{6,4},{7,5},{8,10},{9,11},{10,... | collective-permute-start | bytes 393224 | tf_op jit(solution)/shard_map/ppermute | solution.py:327
  59.9 11.6 %collective-permute-start.29 = (f32[2,2,8,8,128]{4,3,2,1,0:T(8,128)S(1)}, f32[2,2,8,8,128]{4,3,2,1,0:T(8,128)S(1)}, u32[]{:S(2)}, u32[]{:S(2)}) collective-permute-start(f32[2,2,8,8,128]{4,3,2,1,0:T(8,128)S(1)} %get-tuple-element.41), channel_id=1, source_target_pairs={{0,3},{1,2},{2,1},{3,0},{4,7},{5,6},{6,5},{7,4},{8,11},{9,10},{10,... | collective-permute-start | bytes 393224 | tf_op jit(solution)/shard_map/ppermute | solution.py:327

commit v6 on v5

--- a/solution.py
+++ b/solution.py
@@ -16,7 +16,7 @@
 PARAMS = pltpu.CompilerParams(vmem_limit_bytes=40 * 2**20)
 
 
-def call(body, name, out_shape, in_specs, scratch=(), out_specs=None, after=()):
+def call(body, name, out_shape, in_specs, scratch=(), out_specs=None, after=(), aliases=None):
     def whole(*refs):
         body(*refs[len(after) :])
 
@@ -26,6 +26,7 @@
         in_specs=[ANY] * len(after) + in_specs,
         out_specs=out_specs or [VMEM] * len(out_shape),
         scratch_shapes=list(scratch),
+        input_output_aliases=aliases or {},
         compiler_params=PARAMS,
         name=name,
     )
@@ -295,19 +296,29 @@
     return call(body, "cut", [out] * n, [VMEM], after=after)(states)
 
 
-def unpack(forward, result, joined):
-    n = len(forward)
-    segs, parts, coils, lines, width = forward[0].shape
-    sent = [forward[0], result[0], joined] + [b for i in range(2, n) for b in (forward[i], result[i])]
+def unpack(blocks, begun=()):
+    n = lax.axis_size("coil")
+    arrays, places = [], []
+    for i, pair in blocks:
+        for o in range(2):
+            if isinstance(pair, tuple):
+                if pair[o] is None:
+                    continue
+                places.append((len(arrays), i, o, False))
+                arrays.append(pair[o])
+            else:
+                places.append((len(arrays), i, o, True))
+        if not isinstance(pair, tuple):
+            arrays.append(pair)
+    segs, parts, coils, lines, width = arrays[0].shape[-5:]
 
     def body(*refs):
-        ins, outs, sems = refs[: len(sent)], refs[len(sent) : len(sent) + 2], refs[len(sent) + 2]
+        ins, outs, sems = refs[len(begun) :], refs[len(begun) + len(arrays) :], refs[-1]
         copies = []
-        for i in range(n):
+        for k, (at, i, o, joined) in enumerate(places):
             start = pl.multiple_of(spot(True, i) * width, width)
-            for o in range(2):
-                source = ins[2].at[o] if i == 1 else ins[o if i == 0 else 2 * i - 1 + o]
-                copies.append(pltpu.make_async_copy(source, outs[o].at[:, :, :, :, pl.ds(start, width)], sems.at[i, o]))
+            source = ins[at].at[o] if joined else ins[at]
+            copies.append(pltpu.make_async_copy(source, outs[o].at[:, :, :, :, pl.ds(start, width)], sems.at[k]))
         for c in copies:
             c.start()
         for c in copies:
@@ -315,12 +326,13 @@
 
     return call(
         body,
-        "unpack",
+        "unpack_rest" if begun else "unpack",
         [((segs, parts, coils, lines, n * width), F32)] * 2,
-        [VMEM] * len(sent),
-        [pltpu.SemaphoreType.DMA((n, 2))],
+        [ANY] * len(begun) + [VMEM] * len(arrays),
+        [pltpu.SemaphoreType.DMA((len(places),))],
         [ANY] * 2,
-    )(*sent)
+        aliases={i: i for i in range(len(begun))},
+    )(*begun, *arrays)
 
 
 def swap(block, axis, distance):
@@ -399,7 +411,10 @@
             after=[home[i] for i in range(2, n - 1)],
         )
         result_home = [result_out[0]] + [swap(result_out[i], "coil", i) for i in range(1, n)]
-        return tuple(unpack(home, result_home, result_home[1]))
+        begun = unpack([(0, (home[0], result_out[0]))] + [(i, (home[i], None)) for i in range(2, n)])
+        for i in range(1, n):
+            begun = unpack([(i, (None, result_home[i]) if i > 1 else result_home[i])], begun)
+        return tuple(begun)
     blocks = exchange(whole, half)
     result_out = finish(aligned, offsets, backward_maps, forward, mine, other, blocks, True)
 

time: 72.7 us -> 72.3 us (level)
  waiting for transfers between devices: 35.5 us -> 33.2 us
  Pallas kernels: 6.59 us -> 8.42 us
    ppermute x28, waiting for transfers between devices: 30.9 us -> 28.7 us  [swap(): lax.ppermute(block, axis, [(i, i ^ distance) for i in range(lax.axis_size...]
    pallas_call x1 -> x4, Pallas kernels: 1.02 us -> 2.87 us  [unpack(): call(body, 'unpack_rest' if begun else 'unpack', [((segs, parts, coils, l...]
  transfers between devices with their start and end apart: 30 -> 30, of which waited for: 16 -> 16; matrix products, arithmetic and copies ran while one was open for 0% -> 0% of each run, Pallas kernels for 2% -> 5%
where the time goes in v6:
time: 72.3 us; the launch traced here: 72.1 us
  waiting for transfers between devices  33.2 us (46%)
  starting transfers between devices  28.3 us (39%)
  Pallas kernels  8.42 us (12%)
  local copies, waits for them, and re-layouts  1.21 us (2%)
  between operations  0.89 us (1%)
    ppermute x28, waiting for transfers between devices, swap(): lax.ppermute(block, axis, [(i, i ^ distance) for i in range(lax.axis_size...  28.7 us
    ppermute x28, starting transfers between devices, swap(): lax.ppermute(block, axis, [(i, i ^ distance) for i in range(lax.axis_size...  26.5 us
    ppermute x1, waiting for transfers between devices, shards(): lax.ppermute(line_offsets[-1, 1], 'seg', [(i, (i + 1) % places) for i in...  3.29 us
    pallas_call x4, Pallas kernels, unpack(): call(body, 'unpack_rest' if begun else 'unpack', [((segs, parts, coils, l...  2.87 us
    pallas_call x2, Pallas kernels, finish(): call(body, 'finish_backward' if backward else 'finish_forward', out_shape...  2.76 us
  transfers between devices with their start and end apart: 30, of which 16 were waited for; matrix products, arithmetic and copies ran while one was open for 0% of the time, Pallas kernels for 5%

profile of v6, /device:TPU:0, one launch (start us, length us, event | category | flops | bytes accessed | tf_op | source)
XLA Modules:
  0.0 72.1 jit_solution(13280905832586315157)
XLA Ops:
  0.6 4.1 %collective-permute-start.6 = (f32[2,2,32,256]{3,2,1,0:T(8,128)}, f32[2,2,32,256]{3,2,1,0:T(8,128)S(1)}, u32[]{:S(2)}, u32[]{:S(2)}) collective-permute-start(f32[2,2,32,256]{3,2,1,0:T(8,128)} %bitcast.10), channel_id=1, source_target_pairs={{0,2},{1,3},{2,0},{3,1},{4,6},{5,7},{6,4},{7,5},{8,10},{9,11},{10,... | collective-permute-start | bytes 393224 | tf_op jit(solution)/shard_map/ppermute | solution.py:339
  4.7 1.6 %collective-permute-start.5 = (f32[2,2,32,256]{3,2,1,0:T(8,128)}, f32[2,2,32,256]{3,2,1,0:T(8,128)S(1)}, u32[]{:S(2)}, u32[]{:S(2)}) collective-permute-start(f32[2,2,32,256]{3,2,1,0:T(8,128)} %bitcast.11), channel_id=1, source_target_pairs={{0,1},{1,0},{2,3},{3,2},{4,5},{5,4},{6,7},{7,6},{8,9},{9,8},{10,11... | collective-permute-start | bytes 393224 | tf_op jit(solution)/shard_map/ppermute | solution.py:339
  6.3 1.0 %copy-done = f32[2,2,8,8,512]{4,3,2,1,0:T(8,128)S(1)} copy-done((f32[2,2,8,8,512]{4,3,2,1,0:T(8,128)S(1)}, f32[2,2,8,8,512]{4,3,2,1,0:T(8,128)}, u32[]{:S(2)}) %copy-start) | copy-done | bytes 524312
  7.4 0.1 pack.1
  7.5 0.0 copy-start.3
  7.5 0.1 collective-permute-start.10
  7.6 0.9 %collective-permute-start.8 = (f32[2,2,8,8,128]{4,3,2,1,0:T(8,128)S(1)}, f32[2,2,8,8,128]{4,3,2,1,0:T(8,128)S(1)}, u32[]{:S(2)}, u32[]{:S(2)}) collective-permute-start(f32[2,2,8,8,128]{4,3,2,1,0:T(8,128)S(1)} %get-tuple-element.32), channel_id=1, source_target_pairs={{0,1},{1,0},{2,3},{3,2},{4,5},{5,4},{6,7},{7,6},{8,9},{9,8},{10,11... | collective-permute-start | bytes 393224 | tf_op jit(solution)/shard_map/ppermute | solution.py:339
  8.5 1.0 %collective-permute-start.3 = (s32[4]{0:T(128)S(1)}, s32[4]{0:T(128)S(1)}, u32[]{:S(2)}, u32[]{:S(2)}) collective-permute-start(s32[4]{0:T(128)S(1)} %get-tuple-element.56), channel_id=1, source_target_pairs={{4,0},{8,4},{12,8},{16,12},{20,16},{24,20},{28,24},{0,28},{5,1},{9... | collective-permute-start | bytes 56 | tf_op jit(solution)/shard_map/ppermute | solution.py:382
  9.5 1.3 %collective-permute-done.3 = s32[4]{0:T(128)S(1)} collective-permute-done((s32[4]{0:T(128)S(1)}, s32[4]{0:T(128)S(1)}, u32[]{:S(2)}, u32[]{:S(2)}) %collective-permute-start.3) | collective-permute-done | bytes 48 | tf_op jit(solution)/shard_map/ppermute | solution.py:382
  10.8 0.8 %collective-permute-start.4 = (s32[4]{0:T(128)S(1)}, s32[4]{0:T(128)S(1)}, u32[]{:S(2)}, u32[]{:S(2)}) collective-permute-start(s32[4]{0:T(128)S(1)} %get-tuple-element.57), channel_id=1, source_target_pairs={{0,4},{4,8},{8,12},{12,16},{16,20},{20,24},{24,28},{28,0},{1,5},{5... | collective-permute-start | bytes 56 | tf_op jit(solution)/shard_map/ppermute | solution.py:383
  11.6 3.3 %collective-permute-done.4 = s32[4]{0:T(128)S(1)} collective-permute-done((s32[4]{0:T(128)S(1)}, s32[4]{0:T(128)S(1)}, u32[]{:S(2)}, u32[]{:S(2)}) %collective-permute-start.4) | collective-permute-done | bytes 48 | tf_op jit(solution)/shard_map/ppermute | solution.py:383
  14.9 3.0 %collective-permute-start.9 = (f32[2,2,8,8,128]{4,3,2,1,0:T(8,128)S(1)}, f32[2,2,8,8,128]{4,3,2,1,0:T(8,128)S(1)}, u32[]{:S(2)}, u32[]{:S(2)}) collective-permute-start(f32[2,2,8,8,128]{4,3,2,1,0:T(8,128)S(1)} %get-tuple-element.33), channel_id=1, source_target_pairs={{0,2},{1,3},{2,0},{3,1},{4,6},{5,7},{6,4},{7,5},{8,10},{9,11},{10,... | collective-permute-start | bytes 393224 | tf_op jit(solution)/shard_map/ppermute | solution.py:339
  17.9 0.0 collective-permute-done.6.refs_2_
  17.9 0.6 collective-permute-start.7
  18.5 0.0 collective-permute-done.5.refs_1_
  18.5 4.8 %collective-permute-done.7.refs_3_ = f32[2,2,32,256]{3,2,1,0:T(8,128)S(1)} collective-permute-done((f32[2,2,32,256]{3,2,1,0:T(8,128)S(1)}, f32[2,2,32,256]{3,2,1,0:T(8,128)S(1)}, u32[]{:S(2)}, u32[]{:S(2)}) %collective-permute-start.7) | collective-permute-done | bytes 131104 | tf_op jit(solution)/shard_map/ppermute | solution.py:339
  23.3 0.3 prepare_forward.1
  23.6 0.0 collective-permute-done.10.refs_4_
  23.6 0.0 collective-permute-done.8.refs_2_
  23.6 0.0 copy-start.2
  23.6 0.7 summary_forward.1.refs_0_.refs_4_
  24.3 0.1 collective-permute-start.11
  24.4 0.1 copy-done.2
  24.5 0.9 %collective-permute-start.1 = (f32[2,2,32,256]{3,2,1,0:T(8,128)S(1)}, f32[2,2,32,256]{3,2,1,0:T(8,128)S(1)}, u32[]{:S(2)}, u32[]{:S(2)}) collective-permute-start(f32[2,2,32,256]{3,2,1,0:T(8,128)S(1)} %bitcast.13), channel_id=1, source_target_pairs={{0,2},{1,3},{2,0},{3,1},{4,6},{5,7},{6,4},{7,5},{8,10},{9,11},{10,... | collective-permute-start | bytes 393224 | tf_op jit(solution)/shard_map/ppermute | solution.py:339
  25.4 0.5 collective-permute-done.11.refs_1_.refs_5_
  25.9 0.4 compose_forward.1
  26.3 1.5 %collective-permute-start.12 = (f32[128,256]{1,0:T(8,128)S(1)}, f32[128,256]{1,0:T(8,128)S(1)}, u32[]{:S(2)}, u32[]{:S(2)}) collective-permute-start(f32[128,256]{1,0:T(8,128)S(1)} %get-tuple-element.36), channel_id=1, source_target_pairs={{0,8},{4,12},{8,0},{12,4},{16,24},{20,28},{24,16},{28,20},{1,9},{5... | collective-permute-start | bytes 393224 | tf_op jit(solution)/shard_map/ppermute | solution.py:339
  27.8 1.4 %collective-permute-start.14 = (f32[128,256]{1,0:T(8,128)S(1)}, f32[128,256]{1,0:T(8,128)S(1)}, u32[]{:S(2)}, u32[]{:S(2)}) collective-permute-start(f32[128,256]{1,0:T(8,128)S(1)} %get-tuple-element.36), channel_id=1, source_target_pairs={{0,16},{4,20},{8,24},{12,28},{16,0},{20,4},{24,8},{28,12},{1,17},{... | collective-permute-start | bytes 393224 | tf_op jit(solution)/shard_map/ppermute | solution.py:339
  29.2 0.7 collective-permute-start.16
  29.9 1.7 %collective-permute-start = (f32[2,2,32,256]{3,2,1,0:T(8,128)S(1)}, f32[2,2,32,256]{3,2,1,0:T(8,128)S(1)}, u32[]{:S(2)}, u32[]{:S(2)}) collective-permute-start(f32[2,2,32,256]{3,2,1,0:T(8,128)S(1)} %bitcast.14), channel_id=1, source_target_pairs={{0,1},{1,0},{2,3},{3,2},{4,5},{5,4},{6,7},{7,6},{8,9},{9,8},{10,11... | collective-permute-start | bytes 393224 | tf_op jit(solution)/shard_map/ppermute | solution.py:339
  31.6 2.6 %collective-permute-done.1.refs_2_ = f32[2,2,32,256]{3,2,1,0:T(8,128)S(1)} collective-permute-done((f32[2,2,32,256]{3,2,1,0:T(8,128)S(1)}, f32[2,2,32,256]{3,2,1,0:T(8,128)S(1)}, u32[]{:S(2)}, u32[]{:S(2)}) %collective-permute-start.1) | collective-permute-done | bytes 131104 | tf_op jit(solution)/shard_map/ppermute | solution.py:339
  34.1 0.0 collective-permute-start.2
  34.1 0.0 collective-permute-done.12.refs_7_
  34.1 0.0 collective-permute-start.13
  34.1 0.6 collective-permute-done.14.refs_9_
  34.8 1.1 %collective-permute-done.16.refs_11_ = f32[128,256]{1,0:T(8,128)S(1)} collective-permute-done((f32[128,256]{1,0:T(8,128)S(1)}, f32[128,256]{1,0:T(8,128)S(1)}, u32[]{:S(2)}, u32[]{:S(2)}) %collective-permute-start.16) | collective-permute-done | bytes 131104 | tf_op jit(solution)/shard_map/ppermute | solution.py:339
  35.9 1.1 %collective-permute-done.refs_1_ = f32[2,2,32,256]{3,2,1,0:T(8,128)S(1)} collective-permute-done((f32[2,2,32,256]{3,2,1,0:T(8,128)S(1)}, f32[2,2,32,256]{3,2,1,0:T(8,128)S(1)}, u32[]{:S(2)}, u32[]{:S(2)}) %collective-permute-start) | collective-permute-done | bytes 131104 | tf_op jit(solution)/shard_map/ppermute | solution.py:339
  36.9 2.7 %collective-permute-done.2.refs_3_ = f32[2,2,32,256]{3,2,1,0:T(8,128)S(1)} collective-permute-done((f32[2,2,32,256]{3,2,1,0:T(8,128)S(1)}, f32[2,2,32,256]{3,2,1,0:T(8,128)S(1)}, u32[]{:S(2)}, u32[]{:S(2)}) %collective-permute-start.2) | collective-permute-done | bytes 131104 | tf_op jit(solution)/shard_map/ppermute | solution.py:339
  39.6 0.3 prepare_backward.1
  39.9 1.4 %finish_forward.1.refs_1_.refs_3_.refs_4_ = f32[2,2,32,8,128]{4,3,2,1,0:T(8,128)S(1)} custom-call(s32[8,128]{1,0:T(8,128)S(1)} %pad.4.refs_0_.refs_1_, bf16[2,512,256]{2,1,0:T(8,128)(2,1)S(1)} %get-tuple-element.29.refs_0_.refs_1_, bf16[2,512,256]{2,1,0:T(8,128)(2,1)S(1)} %get-tuple-element.30.refs_2_, f32[2,2,32,8,128]{4,3,2,1,0:T(8,128)S(1)} %gather.1.refs_3_, ...), custom_call_target="tpu_custom_call" | custom-call | tf_op jit(solution)/shard_map/finish_forward/pallas_call | solution.py:277
  41.3 0.7 summary_backward.1.refs_0_.refs_5_
  42.0 0.1 collective-permute-start.19
  42.1 1.9 %collective-permute-start.22 = (f32[2,2,8,8,128]{4,3,2,1,0:T(8,128)S(1)}, f32[2,2,8,8,128]{4,3,2,1,0:T(8,128)S(1)}, u32[]{:S(2)}, u32[]{:S(2)}) collective-permute-start(f32[2,2,8,8,128]{4,3,2,1,0:T(8,128)S(1)} %get-tuple-element.42), channel_id=1, source_target_pairs={{0,3},{1,2},{2,1},{3,0},{4,7},{5,6},{6,5},{7,4},{8,11},{9,10},{10,... | collective-permute-start | bytes 393224 | tf_op jit(solution)/shard_map/ppermute | solution.py:339
  43.9 0.4 compose_backward.1
  44.3 1.6 %collective-permute-start.23 = (f32[128,256]{1,0:T(8,128)S(1)}, f32[128,256]{1,0:T(8,128)S(1)}, u32[]{:S(2)}, u32[]{:S(2)}) collective-permute-start(f32[128,256]{1,0:T(8,128)S(1)} %get-tuple-element.41), channel_id=1, source_target_pairs={{0,16},{4,20},{8,24},{12,28},{16,0},{20,4},{24,8},{28,12},{1,17},{... | collective-permute-start | bytes 393224 | tf_op jit(solution)/shard_map/ppermute | solution.py:339
  45.9 1.4 %collective-permute-start.20 = (f32[128,256]{1,0:T(8,128)S(1)}, f32[128,256]{1,0:T(8,128)S(1)}, u32[]{:S(2)}, u32[]{:S(2)}) collective-permute-start(f32[128,256]{1,0:T(8,128)S(1)} %get-tuple-element.41), channel_id=1, source_target_pairs={{0,8},{4,12},{8,0},{12,4},{16,24},{20,28},{24,16},{28,20},{1,9},{5... | collective-permute-start | bytes 393224 | tf_op jit(solution)/shard_map/ppermute | solution.py:339
  47.4 0.5 collective-permute-start.25
  47.9 0.1 collective-permute-start.18
  47.9 2.0 %collective-permute-done.22.refs_0_.refs_3_ = f32[2,2,8,8,128]{4,3,2,1,0:T(8,128)S(1)} collective-permute-done((f32[2,2,8,8,128]{4,3,2,1,0:T(8,128)S(1)}, f32[2,2,8,8,128]{4,3,2,1,0:T(8,128)S(1)}, u32[]{:S(2)}, u32[]{:S(2)}) %collective-permute-start.22) | collective-permute-done | bytes 131104 | tf_op jit(solution)/shard_map/ppermute | solution.py:339
  49.9 0.1 collective-permute-done.23.refs_1_
  50.0 0.1 collective-permute-start.24
  50.1 2.2 %collective-permute-done.20.refs_8_ = f32[128,256]{1,0:T(8,128)S(1)} collective-permute-done((f32[128,256]{1,0:T(8,128)S(1)}, f32[128,256]{1,0:T(8,128)S(1)}, u32[]{:S(2)}, u32[]{:S(2)}) %collective-permute-start.20) | collective-permute-done | bytes 131104 | tf_op jit(solution)/shard_map/ppermute | solution.py:339
  52.3 1.7 %collective-permute-done.25.refs_12_ = f32[128,256]{1,0:T(8,128)S(1)} collective-permute-done((f32[128,256]{1,0:T(8,128)S(1)}, f32[128,256]{1,0:T(8,128)S(1)}, u32[]{:S(2)}, u32[]{:S(2)}) %collective-permute-start.25) | collective-permute-done | bytes 131104 | tf_op jit(solution)/shard_map/ppermute | solution.py:339
  54.0 1.7 %collective-permute-done.18.refs_0_.refs_2_ = f32[2,2,8,8,128]{4,3,2,1,0:T(8,128)S(1)} collective-permute-done((f32[2,2,8,8,128]{4,3,2,1,0:T(8,128)S(1)}, f32[2,2,8,8,128]{4,3,2,1,0:T(8,128)S(1)}, u32[]{:S(2)}, u32[]{:S(2)}) %collective-permute-start.18) | collective-permute-done | bytes 131104 | tf_op jit(solution)/shard_map/ppermute | solution.py:339
  55.7 1.4 %finish_backward.1 = (f32[2,2,8,8,128]{4,3,2,1,0:T(8,128)S(1)}, f32[2,2,2,8,8,128]{5,4,3,2,1,0:T(8,128)S(1)}, f32[2,2,8,8,128]{4,3,2,1,0:T(8,128)S(1)}, f32[2,2,8,8,128]{4,3,2,1,0:T(8,128)S(1)}) custom-call(f32[2,2,8,8,128]{4,3,2,1,0:T(8,128)S(1)} %collective-permute-done.18.refs_0_.refs_2_, s32[8,128]{1,0:T(8,128)S(1)} %pad.4.refs_0_.refs_1_, ...), custom_call_target="tpu_custom_call" | custom-call | tf_op jit(solution)/shard_map/finish_backward/pallas_call | solution.py:277
  57.1 0.1 collective-permute-start.27
  57.2 2.6 %collective-permute-start.28 = (f32[2,2,8,8,128]{4,3,2,1,0:T(8,128)S(1)}, f32[2,2,8,8,128]{4,3,2,1,0:T(8,128)S(1)}, u32[]{:S(2)}, u32[]{:S(2)}) collective-permute-start(f32[2,2,8,8,128]{4,3,2,1,0:T(8,128)S(1)} %get-tuple-element.50), channel_id=1, source_target_pairs={{0,2},{1,3},{2,0},{3,1},{4,6},{5,7},{6,4},{7,5},{8,10},{9,11},{10,... | collective-permute-start | bytes 393224 | tf_op jit(solution)/shard_map/ppermute | solution.py:339
  59.9 1.7 %collective-permute-start.29 = (f32[2,2,8,8,128]{4,3,2,1,0:T(8,128)S(1)}, f32[2,2,8,8,128]{4,3,2,1,0:T(8,128)S(1)}, u32[]{:S(2)}, u32[]{:S(2)}) collective-permute-start(f32[2,2,8,8,128]{4,3,2,1,0:T(8,128)S(1)} %get-tuple-element.53), channel_id=1, source_target_pairs={{0,3},{1,2},{2,1},{3,0},{4,7},{5,6},{6,5},{7,4},{8,11},{9,10},{10,... | collective-permute-start | bytes 393224 | tf_op jit(solution)/shard_map/ppermute | solution.py:339
  61.6 0.8 %unpack.1 = (f32[2,2,8,8,512]{4,3,2,1,0:T(8,128)}, f32[2,2,8,8,512]{4,3,2,1,0:T(8,128)}) custom-call(f32[2,2,8,8,128]{4,3,2,1,0:T(8,128)S(1)} %get-tuple-element.37.refs_0_, f32[2,2,8,8,128]{4,3,2,1,0:T(8,128)S(1)} %get-tuple-element.44.refs_1_, f32[2,2,8,8,128]{4,3,2,1,0:T(8,128)S(1)} %collective-permute-done.18.refs_0_.refs_2_, ...), custom_call_target="tpu_custom_call" | custom-call | tf_op jit(solution)/shard_map/unpack/pallas_call | solution.py:327
  62.4 6.4 %collective-permute-done.27.refs_2_ = f32[2,2,2,8,8,128]{5,4,3,2,1,0:T(8,128)S(1)} collective-permute-done((f32[2,2,2,8,8,128]{5,4,3,2,1,0:T(8,128)S(1)}, f32[2,2,2,8,8,128]{5,4,3,2,1,0:T(8,128)S(1)}, u32[]{:S(2)}, u32[]{:S(2)}) %collective-permute-start.27) | collective-permute-done | bytes 262176 | tf_op jit(solution)/shard_map/ppermute | solution.py:339
  68.8 0.7 unpack_rest.3
  69.5 0.7 unpack_rest.4
  70.2 1.2 %collective-permute-done.29.refs_2_ = f32[2,2,8,8,128]{4,3,2,1,0:T(8,128)S(1)} collective-permute-done((f32[2,2,8,8,128]{4,3,2,1,0:T(8,128)S(1)}, f32[2,2,8,8,128]{4,3,2,1,0:T(8,128)S(1)}, u32[]{:S(2)}, u32[]{:S(2)}) %collective-permute-start.29) | collective-permute-done | bytes 131104 | tf_op jit(solution)/shard_map/ppermute | solution.py:339
  71.4 0.7 unpack_rest.5
  (24 shorter events, 0.2 us)
Async XLA Ops:
  0.6 17.2 %collective-permute-start.6 = (f32[2,2,32,256]{3,2,1,0:T(8,128)}, f32[2,2,32,256]{3,2,1,0:T(8,128)S(1)}, u32[]{:S(2)}, u32[]{:S(2)}) collective-permute-start(f32[2,2,32,256]{3,2,1,0:T(8,128)} %bitcast.10), channel_id=1, source_target_pairs={{0,2},{1,3},{2,0},{3,1},{4,6},{5,7},{6,4},{7,5},{8,10},{9,11},{10,... | collective-permute-start | bytes 393224 | tf_op jit(solution)/shard_map/ppermute | solution.py:339
  4.7 13.7 %collective-permute-start.5 = (f32[2,2,32,256]{3,2,1,0:T(8,128)}, f32[2,2,32,256]{3,2,1,0:T(8,128)S(1)}, u32[]{:S(2)}, u32[]{:S(2)}) collective-permute-start(f32[2,2,32,256]{3,2,1,0:T(8,128)} %bitcast.11), channel_id=1, source_target_pairs={{0,1},{1,0},{2,3},{3,2},{4,5},{5,4},{6,7},{7,6},{8,9},{9,8},{10,11... | collective-permute-start | bytes 393224 | tf_op jit(solution)/shard_map/ppermute | solution.py:339
  6.3 1.0 %copy-start = (f32[2,2,8,8,512]{4,3,2,1,0:T(8,128)S(1)}, f32[2,2,8,8,512]{4,3,2,1,0:T(8,128)}, u32[]{:S(2)}) copy-start(f32[2,2,8,8,512]{4,3,2,1,0:T(8,128)} %refs_0_.1) | copy-start | bytes 1572868
  7.3 15.9 %copy-start.1 = (f32[2,2,256,32]{2,3,1,0:T(8,128)S(1)}, f32[2,2,256,32]{2,3,1,0:T(8,128)}, u32[]{:S(2)}) copy-start(f32[2,2,256,32]{2,3,1,0:T(8,128)} %param.5) | copy-start | bytes 393220
  7.5 1.0 %copy-start.3 = (s32[2,2,4]{2,1,0:T(2,128)S(1)}, s32[2,2,4]{2,1,0:T(2,128)}, u32[]{:S(2)}) copy-start(s32[2,2,4]{2,1,0:T(2,128)} %param.7) | copy-start | bytes 196
  7.5 16.1 %collective-permute-start.10 = (f32[2,2,8,8,128]{4,3,2,1,0:T(8,128)S(1)}, f32[2,2,8,8,128]{4,3,2,1,0:T(8,128)S(1)}, u32[]{:S(2)}, u32[]{:S(2)}) collective-permute-start(f32[2,2,8,8,128]{4,3,2,1,0:T(8,128)S(1)} %get-tuple-element.34), channel_id=1, source_target_pairs={{0,3},{1,2},{2,1},{3,0},{4,7},{5,6},{6,5},{7,4},{8,11},{9,10},{10,... | collective-permute-start | bytes 393224 | tf_op jit(solution)/shard_map/ppermute | solution.py:339
  7.6 16.0 %collective-permute-start.8 = (f32[2,2,8,8,128]{4,3,2,1,0:T(8,128)S(1)}, f32[2,2,8,8,128]{4,3,2,1,0:T(8,128)S(1)}, u32[]{:S(2)}, u32[]{:S(2)}) collective-permute-start(f32[2,2,8,8,128]{4,3,2,1,0:T(8,128)S(1)} %get-tuple-element.32), channel_id=1, source_target_pairs={{0,1},{1,0},{2,3},{3,2},{4,5},{5,4},{6,7},{7,6},{8,9},{9,8},{10,11... | collective-permute-start | bytes 393224 | tf_op jit(solution)/shard_map/ppermute | solution.py:339
  8.5 2.3 %collective-permute-start.3 = (s32[4]{0:T(128)S(1)}, s32[4]{0:T(128)S(1)}, u32[]{:S(2)}, u32[]{:S(2)}) collective-permute-start(s32[4]{0:T(128)S(1)} %get-tuple-element.56), channel_id=1, source_target_pairs={{4,0},{8,4},{12,8},{16,12},{20,16},{24,20},{28,24},{0,28},{5,1},{9... | collective-permute-start | bytes 56 | tf_op jit(solution)/shard_map/ppermute | solution.py:382
  10.8 4.1 %collective-permute-start.4 = (s32[4]{0:T(128)S(1)}, s32[4]{0:T(128)S(1)}, u32[]{:S(2)}, u32[]{:S(2)}) collective-permute-start(s32[4]{0:T(128)S(1)} %get-tuple-element.57), channel_id=1, source_target_pairs={{0,4},{4,8},{8,12},{12,16},{16,20},{20,24},{24,28},{28,0},{1,5},{5... | collective-permute-start | bytes 56 | tf_op jit(solution)/shard_map/ppermute | solution.py:383
  14.9 8.7 %collective-permute-start.9 = (f32[2,2,8,8,128]{4,3,2,1,0:T(8,128)S(1)}, f32[2,2,8,8,128]{4,3,2,1,0:T(8,128)S(1)}, u32[]{:S(2)}, u32[]{:S(2)}) collective-permute-start(f32[2,2,8,8,128]{4,3,2,1,0:T(8,128)S(1)} %get-tuple-element.33), channel_id=1, source_target_pairs={{0,2},{1,3},{2,0},{3,1},{4,6},{5,7},{6,4},{7,5},{8,10},{9,11},{10,... | collective-permute-start | bytes 393224 | tf_op jit(solution)/shard_map/ppermute | solution.py:339
  17.9 5.4 %collective-permute-start.7 = (f32[2,2,32,256]{3,2,1,0:T(8,128)S(1)}, f32[2,2,32,256]{3,2,1,0:T(8,128)S(1)}, u32[]{:S(2)}, u32[]{:S(2)}) collective-permute-start(f32[2,2,32,256]{3,2,1,0:T(8,128)S(1)} %collective-permute-done.6.refs_2_), channel_id=1, source_target_pairs={{0,1},{1,0},{2,3},{3,2},{4,5},{5,4},{6,7},{7,6},{8,9},{9,8},{10,11... | collective-permute-start | bytes 393224 | tf_op jit(solution)/shard_map/ppermute | solution.py:339
  23.6 0.9 %copy-start.2 = (f32[2,2,256,32]{2,3,1,0:T(8,128)S(1)}, f32[2,2,256,32]{2,3,1,0:T(8,128)}, u32[]{:S(2)}) copy-start(f32[2,2,256,32]{2,3,1,0:T(8,128)} %param.6) | copy-start | bytes 393220
  24.3 1.6 %collective-permute-start.11 = (f32[256,256]{1,0:T(8,128)S(1)}, f32[256,256]{1,0:T(8,128)S(1)}, u32[]{:S(2)}, u32[]{:S(2)}) collective-permute-start(f32[256,256]{1,0:T(8,128)S(1)} %summary_forward.1.refs_0_.refs_4_), channel_id=1, source_target_pairs={{0,4},{4,0},{8,12},{12,8},{16,20},{20,16},{24,28},{28,24},{1,5},{5... | collective-permute-start | bytes 786440 | tf_op jit(solution)/shard_map/ppermute | solution.py:339
  24.5 9.6 %collective-permute-start.1 = (f32[2,2,32,256]{3,2,1,0:T(8,128)S(1)}, f32[2,2,32,256]{3,2,1,0:T(8,128)S(1)}, u32[]{:S(2)}, u32[]{:S(2)}) collective-permute-start(f32[2,2,32,256]{3,2,1,0:T(8,128)S(1)} %bitcast.13), channel_id=1, source_target_pairs={{0,2},{1,3},{2,0},{3,1},{4,6},{5,7},{6,4},{7,5},{8,10},{9,11},{10,... | collective-permute-start | bytes 393224 | tf_op jit(solution)/shard_map/ppermute | solution.py:339
  26.3 7.8 %collective-permute-start.12 = (f32[128,256]{1,0:T(8,128)S(1)}, f32[128,256]{1,0:T(8,128)S(1)}, u32[]{:S(2)}, u32[]{:S(2)}) collective-permute-start(f32[128,256]{1,0:T(8,128)S(1)} %get-tuple-element.36), channel_id=1, source_target_pairs={{0,8},{4,12},{8,0},{12,4},{16,24},{20,28},{24,16},{28,20},{1,9},{5... | collective-permute-start | bytes 393224 | tf_op jit(solution)/shard_map/ppermute | solution.py:339
  27.8 7.0 %collective-permute-start.14 = (f32[128,256]{1,0:T(8,128)S(1)}, f32[128,256]{1,0:T(8,128)S(1)}, u32[]{:S(2)}, u32[]{:S(2)}) collective-permute-start(f32[128,256]{1,0:T(8,128)S(1)} %get-tuple-element.36), channel_id=1, source_target_pairs={{0,16},{4,20},{8,24},{12,28},{16,0},{20,4},{24,8},{28,12},{1,17},{... | collective-permute-start | bytes 393224 | tf_op jit(solution)/shard_map/ppermute | solution.py:339
  29.2 6.7 %collective-permute-start.16 = (f32[128,256]{1,0:T(8,128)S(1)}, f32[128,256]{1,0:T(8,128)S(1)}, u32[]{:S(2)}, u32[]{:S(2)}) collective-permute-start(f32[128,256]{1,0:T(8,128)S(1)} %get-tuple-element.36), channel_id=1, source_target_pairs={{0,24},{4,28},{8,16},{12,20},{16,8},{20,12},{24,0},{28,4},{1,25},{... | collective-permute-start | bytes 393224 | tf_op jit(solution)/shard_map/ppermute | solution.py:339
  29.9 7.1 %collective-permute-start = (f32[2,2,32,256]{3,2,1,0:T(8,128)S(1)}, f32[2,2,32,256]{3,2,1,0:T(8,128)S(1)}, u32[]{:S(2)}, u32[]{:S(2)}) collective-permute-start(f32[2,2,32,256]{3,2,1,0:T(8,128)S(1)} %bitcast.14), channel_id=1, source_target_pairs={{0,1},{1,0},{2,3},{3,2},{4,5},{5,4},{6,7},{7,6},{8,9},{9,8},{10,11... | collective-permute-start | bytes 393224 | tf_op jit(solution)/shard_map/ppermute | solution.py:339
  34.1 5.5 %collective-permute-start.2 = (f32[2,2,32,256]{3,2,1,0:T(8,128)S(1)}, f32[2,2,32,256]{3,2,1,0:T(8,128)S(1)}, u32[]{:S(2)}, u32[]{:S(2)}) collective-permute-start(f32[2,2,32,256]{3,2,1,0:T(8,128)S(1)} %collective-permute-done.1.refs_2_), channel_id=1, source_target_pairs={{0,1},{1,0},{2,3},{3,2},{4,5},{5,4},{6,7},{7,6},{8,9},{9,8},{10,11... | collective-permute-start | bytes 393224 | tf_op jit(solution)/shard_map/ppermute | solution.py:339
  34.1 5.7 %collective-permute-start.13 = (f32[128,256]{1,0:T(8,128)S(1)}, f32[128,256]{1,0:T(8,128)S(1)}, u32[]{:S(2)}, u32[]{:S(2)}) collective-permute-start(f32[128,256]{1,0:T(8,128)S(1)} %collective-permute-done.12.refs_7_), channel_id=1, source_target_pairs={{0,4},{4,0},{8,12},{12,8},{16,20},{20,16},{24,28},{28,24},{1,5},{5... | collective-permute-start | bytes 393224 | tf_op jit(solution)/shard_map/ppermute | solution.py:339
  34.8 5.1 %collective-permute-start.15 = (f32[128,256]{1,0:T(8,128)S(1)}, f32[128,256]{1,0:T(8,128)S(1)}, u32[]{:S(2)}, u32[]{:S(2)}) collective-permute-start(f32[128,256]{1,0:T(8,128)S(1)} %collective-permute-done.14.refs_9_), channel_id=1, source_target_pairs={{0,4},{4,0},{8,12},{12,8},{16,20},{20,16},{24,28},{28,24},{1,5},{5... | collective-permute-start | bytes 393224 | tf_op jit(solution)/shard_map/ppermute | solution.py:339
  35.8 4.0 %collective-permute-start.17 = (f32[128,256]{1,0:T(8,128)S(1)}, f32[128,256]{1,0:T(8,128)S(1)}, u32[]{:S(2)}, u32[]{:S(2)}) collective-permute-start(f32[128,256]{1,0:T(8,128)S(1)} %collective-permute-done.16.refs_11_), channel_id=1, source_target_pairs={{0,4},{4,0},{8,12},{12,8},{16,20},{20,16},{24,28},{28,24},{1,5},{5... | collective-permute-start | bytes 393224 | tf_op jit(solution)/shard_map/ppermute | solution.py:339
  42.0 2.0 %collective-permute-start.19 = (f32[256,256]{1,0:T(8,128)S(1)}, f32[256,256]{1,0:T(8,128)S(1)}, u32[]{:S(2)}, u32[]{:S(2)}) collective-permute-start(f32[256,256]{1,0:T(8,128)S(1)} %summary_backward.1.refs_0_.refs_5_), channel_id=1, source_target_pairs={{0,4},{4,0},{8,12},{12,8},{16,20},{20,16},{24,28},{28,24},{1,5},{5... | collective-permute-start | bytes 786440 | tf_op jit(solution)/shard_map/ppermute | solution.py:339
  42.1 7.9 %collective-permute-start.22 = (f32[2,2,8,8,128]{4,3,2,1,0:T(8,128)S(1)}, f32[2,2,8,8,128]{4,3,2,1,0:T(8,128)S(1)}, u32[]{:S(2)}, u32[]{:S(2)}) collective-permute-start(f32[2,2,8,8,128]{4,3,2,1,0:T(8,128)S(1)} %get-tuple-element.42), channel_id=1, source_target_pairs={{0,3},{1,2},{2,1},{3,0},{4,7},{5,6},{6,5},{7,4},{8,11},{9,10},{10,... | collective-permute-start | bytes 393224 | tf_op jit(solution)/shard_map/ppermute | solution.py:339
  44.3 5.7 %collective-permute-start.23 = (f32[128,256]{1,0:T(8,128)S(1)}, f32[128,256]{1,0:T(8,128)S(1)}, u32[]{:S(2)}, u32[]{:S(2)}) collective-permute-start(f32[128,256]{1,0:T(8,128)S(1)} %get-tuple-element.41), channel_id=1, source_target_pairs={{0,16},{4,20},{8,24},{12,28},{16,0},{20,4},{24,8},{28,12},{1,17},{... | collective-permute-start | bytes 393224 | tf_op jit(solution)/shard_map/ppermute | solution.py:339
  45.9 6.4 %collective-permute-start.20 = (f32[128,256]{1,0:T(8,128)S(1)}, f32[128,256]{1,0:T(8,128)S(1)}, u32[]{:S(2)}, u32[]{:S(2)}) collective-permute-start(f32[128,256]{1,0:T(8,128)S(1)} %get-tuple-element.41), channel_id=1, source_target_pairs={{0,8},{4,12},{8,0},{12,4},{16,24},{20,28},{24,16},{28,20},{1,9},{5... | collective-permute-start | bytes 393224 | tf_op jit(solution)/shard_map/ppermute | solution.py:339
  47.4 6.6 %collective-permute-start.25 = (f32[128,256]{1,0:T(8,128)S(1)}, f32[128,256]{1,0:T(8,128)S(1)}, u32[]{:S(2)}, u32[]{:S(2)}) collective-permute-start(f32[128,256]{1,0:T(8,128)S(1)} %get-tuple-element.41), channel_id=1, source_target_pairs={{0,24},{4,28},{8,16},{12,20},{16,8},{20,12},{24,0},{28,4},{1,25},{... | collective-permute-start | bytes 393224 | tf_op jit(solution)/shard_map/ppermute | solution.py:339
  47.9 7.9 %collective-permute-start.18 = (f32[2,2,8,8,128]{4,3,2,1,0:T(8,128)S(1)}, f32[2,2,8,8,128]{4,3,2,1,0:T(8,128)S(1)}, u32[]{:S(2)}, u32[]{:S(2)}) collective-permute-start(f32[2,2,8,8,128]{4,3,2,1,0:T(8,128)S(1)} %get-tuple-element.38), channel_id=1, source_target_pairs={{0,2},{1,3},{2,0},{3,1},{4,6},{5,7},{6,4},{7,5},{8,10},{9,11},{10,... | collective-permute-start | bytes 393224 | tf_op jit(solution)/shard_map/ppermute | solution.py:339
  50.0 5.7 %collective-permute-start.24 = (f32[128,256]{1,0:T(8,128)S(1)}, f32[128,256]{1,0:T(8,128)S(1)}, u32[]{:S(2)}, u32[]{:S(2)}) collective-permute-start(f32[128,256]{1,0:T(8,128)S(1)} %hold.1.refs_10_), channel_id=1, source_target_pairs={{0,4},{4,0},{8,12},{12,8},{16,20},{20,16},{24,28},{28,24},{1,5},{5... | collective-permute-start | bytes 393224 | tf_op jit(solution)/shard_map/ppermute | solution.py:339
  52.3 3.4 %collective-permute-start.21 = (f32[128,256]{1,0:T(8,128)S(1)}, f32[128,256]{1,0:T(8,128)S(1)}, u32[]{:S(2)}, u32[]{:S(2)}) collective-permute-start(f32[128,256]{1,0:T(8,128)S(1)} %collective-permute-done.20.refs_8_), channel_id=1, source_target_pairs={{0,4},{4,0},{8,12},{12,8},{16,20},{20,16},{24,28},{28,24},{1,5},{5... | collective-permute-start | bytes 393224 | tf_op jit(solution)/shard_map/ppermute | solution.py:339
  54.0 1.8 %collective-permute-start.26 = (f32[128,256]{1,0:T(8,128)S(1)}, f32[128,256]{1,0:T(8,128)S(1)}, u32[]{:S(2)}, u32[]{:S(2)}) collective-permute-start(f32[128,256]{1,0:T(8,128)S(1)} %collective-permute-done.25.refs_12_), channel_id=1, source_target_pairs={{0,4},{4,0},{8,12},{12,8},{16,20},{20,16},{24,28},{28,24},{1,5},{5... | collective-permute-start | bytes 393224 | tf_op jit(solution)/shard_map/ppermute | solution.py:339
  57.1 11.6 %collective-permute-start.27 = (f32[2,2,2,8,8,128]{5,4,3,2,1,0:T(8,128)S(1)}, f32[2,2,2,8,8,128]{5,4,3,2,1,0:T(8,128)S(1)}, u32[]{:S(2)}, u32[]{:S(2)}) collective-permute-start(f32[2,2,2,8,8,128]{5,4,3,2,1,0:T(8,128)S(1)} %get-tuple-element.47), channel_id=1, source_target_pairs={{0,1},{1,0},{2,3},{3,2},{4,5},{5,4},{6,7},{7,6},{8,9},{9,8},{10,11... | collective-permute-start | bytes 786440 | tf_op jit(solution)/shard_map/ppermute | solution.py:339
  57.2 12.3 %collective-permute-start.28 = (f32[2,2,8,8,128]{4,3,2,1,0:T(8,128)S(1)}, f32[2,2,8,8,128]{4,3,2,1,0:T(8,128)S(1)}, u32[]{:S(2)}, u32[]{:S(2)}) collective-permute-start(f32[2,2,8,8,128]{4,3,2,1,0:T(8,128)S(1)} %get-tuple-element.50), channel_id=1, source_target_pairs={{0,2},{1,3},{2,0},{3,1},{4,6},{5,7},{6,4},{7,5},{8,10},{9,11},{10,... | collective-permute-start | bytes 393224 | tf_op jit(solution)/shard_map/ppermute | solution.py:339
  59.9 11.6 %collective-permute-start.29 = (f32[2,2,8,8,128]{4,3,2,1,0:T(8,128)S(1)}, f32[2,2,8,8,128]{4,3,2,1,0:T(8,128)S(1)}, u32[]{:S(2)}, u32[]{:S(2)}) collective-permute-start(f32[2,2,8,8,128]{4,3,2,1,0:T(8,128)S(1)} %get-tuple-element.53), channel_id=1, source_target_pairs={{0,3},{1,2},{2,1},{3,0},{4,7},{5,6},{6,5},{7,4},{8,11},{9,10},{10,... | collective-permute-start | bytes 393224 | tf_op jit(solution)/shard_map/ppermute | solution.py:339

commit v7 on v6

--- a/solution.py
+++ b/solution.py
@@ -192,11 +192,11 @@
 def compose(mine, other, cols, backward):
     size, lanes = mine.shape
 
-    def body(a_ref, b_ref, whole, out_ref, pair):
+    def body(a_ref, b_ref, whole, out_ref):
         _, core = my_chip()
-        pair[pl.ds(core, 1)] = a_ref[...][None]
-        pair[pl.ds(1 - core, 1)] = b_ref[...][None]
-        near, far = (pair[1], pair[0]) if backward else (pair[0], pair[1])
+        leads = core == (1 if backward else 0)
+        near = jnp.where(leads, a_ref[...], b_ref[...])
+        far = jnp.where(leads, b_ref[...], a_ref[...])
         both = product(halves(real_form(far[:, :cols])), near)
         whole[:, :cols] = both[:, :cols]
         whole[:, cols:] = both[:, cols:] + far[:, cols:]
@@ -207,7 +207,6 @@
         "compose_backward" if backward else "compose_forward",
         [((size, lanes), F32), ((size // 2, lanes), F32)],
         [VMEM, VMEM],
-        [pltpu.VMEM((2, size, lanes), F32)],
     )(mine, other)
 
 

time: 72.3 us -> 72.2 us (level)
  no operation moved by 1% of the time
where the time goes in v7:
time: 72.2 us; the launch traced here: 72.1 us
  waiting for transfers between devices  33.2 us (46%)
  starting transfers between devices  28.4 us (39%)
  Pallas kernels  8.32 us (12%)
  local copies, waits for them, and re-layouts  1.21 us (2%)
  between operations  0.89 us (1%)
    ppermute x28, waiting for transfers between devices, swap(): lax.ppermute(block, axis, [(i, i ^ distance) for i in range(lax.axis_size...  28.7 us
    ppermute x28, starting transfers between devices, swap(): lax.ppermute(block, axis, [(i, i ^ distance) for i in range(lax.axis_size...  26.6 us
    ppermute x1, waiting for transfers between devices, shards(): lax.ppermute(line_offsets[-1, 1], 'seg', [(i, (i + 1) % places) for i in...  3.29 us
    pallas_call x4, Pallas kernels, unpack(): call(body, 'unpack_rest' if begun else 'unpack', [((segs, parts, coils, l...  2.87 us
    pallas_call x2, Pallas kernels, finish(): call(body, 'finish_backward' if backward else 'finish_forward', out_shape...  2.76 us
  transfers between devices with their start and end apart: 30, of which 16 were waited for; matrix products, arithmetic and copies ran while one was open for 0% of the time, Pallas kernels for 5%

profile of v7, /device:TPU:0, one launch (start us, length us, event | category | flops | bytes accessed | tf_op | source)
XLA Modules:
  0.0 72.1 jit_solution(15404483602614031969)
XLA Ops:
  0.6 4.1 %collective-permute-start.6 = (f32[2,2,32,256]{3,2,1,0:T(8,128)}, f32[2,2,32,256]{3,2,1,0:T(8,128)S(1)}, u32[]{:S(2)}, u32[]{:S(2)}) collective-permute-start(f32[2,2,32,256]{3,2,1,0:T(8,128)} %bitcast.10), channel_id=1, source_target_pairs={{0,2},{1,3},{2,0},{3,1},{4,6},{5,7},{6,4},{7,5},{8,10},{9,11},{10,... | collective-permute-start | bytes 393224 | tf_op jit(solution)/shard_map/ppermute | solution.py:338
  4.7 1.6 %collective-permute-start.5 = (f32[2,2,32,256]{3,2,1,0:T(8,128)}, f32[2,2,32,256]{3,2,1,0:T(8,128)S(1)}, u32[]{:S(2)}, u32[]{:S(2)}) collective-permute-start(f32[2,2,32,256]{3,2,1,0:T(8,128)} %bitcast.11), channel_id=1, source_target_pairs={{0,1},{1,0},{2,3},{3,2},{4,5},{5,4},{6,7},{7,6},{8,9},{9,8},{10,11... | collective-permute-start | bytes 393224 | tf_op jit(solution)/shard_map/ppermute | solution.py:338
  6.3 1.0 %copy-done = f32[2,2,8,8,512]{4,3,2,1,0:T(8,128)S(1)} copy-done((f32[2,2,8,8,512]{4,3,2,1,0:T(8,128)S(1)}, f32[2,2,8,8,512]{4,3,2,1,0:T(8,128)}, u32[]{:S(2)}) %copy-start) | copy-done | bytes 524312
  7.4 0.1 pack.1
  7.5 0.0 copy-start.3
  7.5 0.1 collective-permute-start.10
  7.6 0.9 %collective-permute-start.8 = (f32[2,2,8,8,128]{4,3,2,1,0:T(8,128)S(1)}, f32[2,2,8,8,128]{4,3,2,1,0:T(8,128)S(1)}, u32[]{:S(2)}, u32[]{:S(2)}) collective-permute-start(f32[2,2,8,8,128]{4,3,2,1,0:T(8,128)S(1)} %get-tuple-element.32), channel_id=1, source_target_pairs={{0,1},{1,0},{2,3},{3,2},{4,5},{5,4},{6,7},{7,6},{8,9},{9,8},{10,11... | collective-permute-start | bytes 393224 | tf_op jit(solution)/shard_map/ppermute | solution.py:338
  8.5 1.0 %collective-permute-start.3 = (s32[4]{0:T(128)S(1)}, s32[4]{0:T(128)S(1)}, u32[]{:S(2)}, u32[]{:S(2)}) collective-permute-start(s32[4]{0:T(128)S(1)} %get-tuple-element.56), channel_id=1, source_target_pairs={{4,0},{8,4},{12,8},{16,12},{20,16},{24,20},{28,24},{0,28},{5,1},{9... | collective-permute-start | bytes 56 | tf_op jit(solution)/shard_map/ppermute | solution.py:381
  9.5 1.3 %collective-permute-done.3 = s32[4]{0:T(128)S(1)} collective-permute-done((s32[4]{0:T(128)S(1)}, s32[4]{0:T(128)S(1)}, u32[]{:S(2)}, u32[]{:S(2)}) %collective-permute-start.3) | collective-permute-done | bytes 48 | tf_op jit(solution)/shard_map/ppermute | solution.py:381
  10.8 0.8 %collective-permute-start.4 = (s32[4]{0:T(128)S(1)}, s32[4]{0:T(128)S(1)}, u32[]{:S(2)}, u32[]{:S(2)}) collective-permute-start(s32[4]{0:T(128)S(1)} %get-tuple-element.57), channel_id=1, source_target_pairs={{0,4},{4,8},{8,12},{12,16},{16,20},{20,24},{24,28},{28,0},{1,5},{5... | collective-permute-start | bytes 56 | tf_op jit(solution)/shard_map/ppermute | solution.py:382
  11.6 3.3 %collective-permute-done.4 = s32[4]{0:T(128)S(1)} collective-permute-done((s32[4]{0:T(128)S(1)}, s32[4]{0:T(128)S(1)}, u32[]{:S(2)}, u32[]{:S(2)}) %collective-permute-start.4) | collective-permute-done | bytes 48 | tf_op jit(solution)/shard_map/ppermute | solution.py:382
  14.9 3.0 %collective-permute-start.9 = (f32[2,2,8,8,128]{4,3,2,1,0:T(8,128)S(1)}, f32[2,2,8,8,128]{4,3,2,1,0:T(8,128)S(1)}, u32[]{:S(2)}, u32[]{:S(2)}) collective-permute-start(f32[2,2,8,8,128]{4,3,2,1,0:T(8,128)S(1)} %get-tuple-element.33), channel_id=1, source_target_pairs={{0,2},{1,3},{2,0},{3,1},{4,6},{5,7},{6,4},{7,5},{8,10},{9,11},{10,... | collective-permute-start | bytes 393224 | tf_op jit(solution)/shard_map/ppermute | solution.py:338
  17.9 0.0 collective-permute-done.6.refs_2_
  17.9 0.6 collective-permute-start.7
  18.5 4.8 %collective-permute-done.7.refs_3_ = f32[2,2,32,256]{3,2,1,0:T(8,128)S(1)} collective-permute-done((f32[2,2,32,256]{3,2,1,0:T(8,128)S(1)}, f32[2,2,32,256]{3,2,1,0:T(8,128)S(1)}, u32[]{:S(2)}, u32[]{:S(2)}) %collective-permute-start.7) | collective-permute-done | bytes 131104 | tf_op jit(solution)/shard_map/ppermute | solution.py:338
  23.3 0.3 prepare_forward.1
  23.6 0.0 collective-permute-done.10.refs_4_
  23.6 0.0 copy-start.2
  23.6 0.7 summary_forward.1.refs_0_.refs_4_
  24.3 0.1 collective-permute-start.11
  24.4 0.1 copy-done.2
  24.5 0.9 %collective-permute-start.1 = (f32[2,2,32,256]{3,2,1,0:T(8,128)S(1)}, f32[2,2,32,256]{3,2,1,0:T(8,128)S(1)}, u32[]{:S(2)}, u32[]{:S(2)}) collective-permute-start(f32[2,2,32,256]{3,2,1,0:T(8,128)S(1)} %bitcast.13), channel_id=1, source_target_pairs={{0,2},{1,3},{2,0},{3,1},{4,6},{5,7},{6,4},{7,5},{8,10},{9,11},{10,... | collective-permute-start | bytes 393224 | tf_op jit(solution)/shard_map/ppermute | solution.py:338
  25.4 0.5 collective-permute-done.11.refs_1_.refs_5_
  25.9 0.3 compose_forward.1
  26.2 1.5 %collective-permute-start.12 = (f32[128,256]{1,0:T(8,128)S(1)}, f32[128,256]{1,0:T(8,128)S(1)}, u32[]{:S(2)}, u32[]{:S(2)}) collective-permute-start(f32[128,256]{1,0:T(8,128)S(1)} %get-tuple-element.36), channel_id=1, source_target_pairs={{0,8},{4,12},{8,0},{12,4},{16,24},{20,28},{24,16},{28,20},{1,9},{5... | collective-permute-start | bytes 393224 | tf_op jit(solution)/shard_map/ppermute | solution.py:338
  27.7 1.4 %collective-permute-start.14 = (f32[128,256]{1,0:T(8,128)S(1)}, f32[128,256]{1,0:T(8,128)S(1)}, u32[]{:S(2)}, u32[]{:S(2)}) collective-permute-start(f32[128,256]{1,0:T(8,128)S(1)} %get-tuple-element.36), channel_id=1, source_target_pairs={{0,16},{4,20},{8,24},{12,28},{16,0},{20,4},{24,8},{28,12},{1,17},{... | collective-permute-start | bytes 393224 | tf_op jit(solution)/shard_map/ppermute | solution.py:338
  29.1 0.7 collective-permute-start.16
  29.8 1.7 %collective-permute-start = (f32[2,2,32,256]{3,2,1,0:T(8,128)S(1)}, f32[2,2,32,256]{3,2,1,0:T(8,128)S(1)}, u32[]{:S(2)}, u32[]{:S(2)}) collective-permute-start(f32[2,2,32,256]{3,2,1,0:T(8,128)S(1)} %bitcast.14), channel_id=1, source_target_pairs={{0,1},{1,0},{2,3},{3,2},{4,5},{5,4},{6,7},{7,6},{8,9},{9,8},{10,11... | collective-permute-start | bytes 393224 | tf_op jit(solution)/shard_map/ppermute | solution.py:338
  31.5 2.6 %collective-permute-done.1.refs_2_ = f32[2,2,32,256]{3,2,1,0:T(8,128)S(1)} collective-permute-done((f32[2,2,32,256]{3,2,1,0:T(8,128)S(1)}, f32[2,2,32,256]{3,2,1,0:T(8,128)S(1)}, u32[]{:S(2)}, u32[]{:S(2)}) %collective-permute-start.1) | collective-permute-done | bytes 131104 | tf_op jit(solution)/shard_map/ppermute | solution.py:338
  34.1 0.0 collective-permute-start.2
  34.1 0.0 collective-permute-done.12.refs_7_
  34.1 0.0 collective-permute-start.13
  34.1 0.6 collective-permute-done.14.refs_9_
  34.7 0.0 collective-permute-start.15
  34.7 1.1 %collective-permute-done.16.refs_11_ = f32[128,256]{1,0:T(8,128)S(1)} collective-permute-done((f32[128,256]{1,0:T(8,128)S(1)}, f32[128,256]{1,0:T(8,128)S(1)}, u32[]{:S(2)}, u32[]{:S(2)}) %collective-permute-start.16) | collective-permute-done | bytes 131104 | tf_op jit(solution)/shard_map/ppermute | solution.py:338
  35.8 0.0 collective-permute-start.17
  35.8 1.1 %collective-permute-done.refs_1_ = f32[2,2,32,256]{3,2,1,0:T(8,128)S(1)} collective-permute-done((f32[2,2,32,256]{3,2,1,0:T(8,128)S(1)}, f32[2,2,32,256]{3,2,1,0:T(8,128)S(1)}, u32[]{:S(2)}, u32[]{:S(2)}) %collective-permute-start) | collective-permute-done | bytes 131104 | tf_op jit(solution)/shard_map/ppermute | solution.py:338
  36.9 2.6 %collective-permute-done.2.refs_3_ = f32[2,2,32,256]{3,2,1,0:T(8,128)S(1)} collective-permute-done((f32[2,2,32,256]{3,2,1,0:T(8,128)S(1)}, f32[2,2,32,256]{3,2,1,0:T(8,128)S(1)}, u32[]{:S(2)}, u32[]{:S(2)}) %collective-permute-start.2) | collective-permute-done | bytes 131104 | tf_op jit(solution)/shard_map/ppermute | solution.py:338
  39.6 0.3 prepare_backward.1
  39.8 1.4 %finish_forward.1.refs_1_.refs_3_.refs_4_ = f32[2,2,32,8,128]{4,3,2,1,0:T(8,128)S(1)} custom-call(s32[8,128]{1,0:T(8,128)S(1)} %pad.4.refs_0_.refs_1_, bf16[2,512,256]{2,1,0:T(8,128)(2,1)S(1)} %get-tuple-element.29.refs_0_.refs_1_, bf16[2,512,256]{2,1,0:T(8,128)(2,1)S(1)} %get-tuple-element.30.refs_2_, f32[2,2,32,8,128]{4,3,2,1,0:T(8,128)S(1)} %gather.1.refs_3_, ...), custom_call_target="tpu_custom_call" | custom-call | tf_op jit(solution)/shard_map/finish_forward/pallas_call | solution.py:276
  41.2 0.7 summary_backward.1.refs_0_.refs_5_
  41.9 0.1 collective-permute-start.19
  42.0 1.9 %collective-permute-start.22 = (f32[2,2,8,8,128]{4,3,2,1,0:T(8,128)S(1)}, f32[2,2,8,8,128]{4,3,2,1,0:T(8,128)S(1)}, u32[]{:S(2)}, u32[]{:S(2)}) collective-permute-start(f32[2,2,8,8,128]{4,3,2,1,0:T(8,128)S(1)} %get-tuple-element.42), channel_id=1, source_target_pairs={{0,3},{1,2},{2,1},{3,0},{4,7},{5,6},{6,5},{7,4},{8,11},{9,10},{10,... | collective-permute-start | bytes 393224 | tf_op jit(solution)/shard_map/ppermute | solution.py:338
  44.0 0.3 compose_backward.1
  44.3 1.6 %collective-permute-start.23 = (f32[128,256]{1,0:T(8,128)S(1)}, f32[128,256]{1,0:T(8,128)S(1)}, u32[]{:S(2)}, u32[]{:S(2)}) collective-permute-start(f32[128,256]{1,0:T(8,128)S(1)} %get-tuple-element.41), channel_id=1, source_target_pairs={{0,16},{4,20},{8,24},{12,28},{16,0},{20,4},{24,8},{28,12},{1,17},{... | collective-permute-start | bytes 393224 | tf_op jit(solution)/shard_map/ppermute | solution.py:338
  45.9 1.5 %collective-permute-start.20 = (f32[128,256]{1,0:T(8,128)S(1)}, f32[128,256]{1,0:T(8,128)S(1)}, u32[]{:S(2)}, u32[]{:S(2)}) collective-permute-start(f32[128,256]{1,0:T(8,128)S(1)} %get-tuple-element.41), channel_id=1, source_target_pairs={{0,8},{4,12},{8,0},{12,4},{16,24},{20,28},{24,16},{28,20},{1,9},{5... | collective-permute-start | bytes 393224 | tf_op jit(solution)/shard_map/ppermute | solution.py:338
  47.3 0.5 collective-permute-start.25
  47.8 0.1 collective-permute-start.18
  47.9 2.0 %collective-permute-done.22.refs_0_.refs_3_ = f32[2,2,8,8,128]{4,3,2,1,0:T(8,128)S(1)} collective-permute-done((f32[2,2,8,8,128]{4,3,2,1,0:T(8,128)S(1)}, f32[2,2,8,8,128]{4,3,2,1,0:T(8,128)S(1)}, u32[]{:S(2)}, u32[]{:S(2)}) %collective-permute-start.22) | collective-permute-done | bytes 131104 | tf_op jit(solution)/shard_map/ppermute | solution.py:338
  49.9 0.1 collective-permute-done.23.refs_1_
  50.0 0.1 collective-permute-start.24
  50.0 2.2 %collective-permute-done.20.refs_8_ = f32[128,256]{1,0:T(8,128)S(1)} collective-permute-done((f32[128,256]{1,0:T(8,128)S(1)}, f32[128,256]{1,0:T(8,128)S(1)}, u32[]{:S(2)}, u32[]{:S(2)}) %collective-permute-start.20) | collective-permute-done | bytes 131104 | tf_op jit(solution)/shard_map/ppermute | solution.py:338
  52.3 1.7 %collective-permute-done.25.refs_12_ = f32[128,256]{1,0:T(8,128)S(1)} collective-permute-done((f32[128,256]{1,0:T(8,128)S(1)}, f32[128,256]{1,0:T(8,128)S(1)}, u32[]{:S(2)}, u32[]{:S(2)}) %collective-permute-start.25) | collective-permute-done | bytes 131104 | tf_op jit(solution)/shard_map/ppermute | solution.py:338
  53.9 1.7 %collective-permute-done.18.refs_0_.refs_2_ = f32[2,2,8,8,128]{4,3,2,1,0:T(8,128)S(1)} collective-permute-done((f32[2,2,8,8,128]{4,3,2,1,0:T(8,128)S(1)}, f32[2,2,8,8,128]{4,3,2,1,0:T(8,128)S(1)}, u32[]{:S(2)}, u32[]{:S(2)}) %collective-permute-start.18) | collective-permute-done | bytes 131104 | tf_op jit(solution)/shard_map/ppermute | solution.py:338
  55.7 1.4 %finish_backward.1 = (f32[2,2,8,8,128]{4,3,2,1,0:T(8,128)S(1)}, f32[2,2,2,8,8,128]{5,4,3,2,1,0:T(8,128)S(1)}, f32[2,2,8,8,128]{4,3,2,1,0:T(8,128)S(1)}, f32[2,2,8,8,128]{4,3,2,1,0:T(8,128)S(1)}) custom-call(f32[2,2,8,8,128]{4,3,2,1,0:T(8,128)S(1)} %collective-permute-done.18.refs_0_.refs_2_, s32[8,128]{1,0:T(8,128)S(1)} %pad.4.refs_0_.refs_1_, ...), custom_call_target="tpu_custom_call" | custom-call | tf_op jit(solution)/shard_map/finish_backward/pallas_call | solution.py:276
  57.1 0.1 collective-permute-start.27
  57.2 2.7 %collective-permute-start.28 = (f32[2,2,8,8,128]{4,3,2,1,0:T(8,128)S(1)}, f32[2,2,8,8,128]{4,3,2,1,0:T(8,128)S(1)}, u32[]{:S(2)}, u32[]{:S(2)}) collective-permute-start(f32[2,2,8,8,128]{4,3,2,1,0:T(8,128)S(1)} %get-tuple-element.50), channel_id=1, source_target_pairs={{0,2},{1,3},{2,0},{3,1},{4,6},{5,7},{6,4},{7,5},{8,10},{9,11},{10,... | collective-permute-start | bytes 393224 | tf_op jit(solution)/shard_map/ppermute | solution.py:338
  59.9 1.7 %collective-permute-start.29 = (f32[2,2,8,8,128]{4,3,2,1,0:T(8,128)S(1)}, f32[2,2,8,8,128]{4,3,2,1,0:T(8,128)S(1)}, u32[]{:S(2)}, u32[]{:S(2)}) collective-permute-start(f32[2,2,8,8,128]{4,3,2,1,0:T(8,128)S(1)} %get-tuple-element.53), channel_id=1, source_target_pairs={{0,3},{1,2},{2,1},{3,0},{4,7},{5,6},{6,5},{7,4},{8,11},{9,10},{10,... | collective-permute-start | bytes 393224 | tf_op jit(solution)/shard_map/ppermute | solution.py:338
  61.5 0.8 %unpack.1 = (f32[2,2,8,8,512]{4,3,2,1,0:T(8,128)}, f32[2,2,8,8,512]{4,3,2,1,0:T(8,128)}) custom-call(f32[2,2,8,8,128]{4,3,2,1,0:T(8,128)S(1)} %get-tuple-element.37.refs_0_, f32[2,2,8,8,128]{4,3,2,1,0:T(8,128)S(1)} %get-tuple-element.44.refs_1_, f32[2,2,8,8,128]{4,3,2,1,0:T(8,128)S(1)} %collective-permute-done.18.refs_0_.refs_2_, ...), custom_call_target="tpu_custom_call" | custom-call | tf_op jit(solution)/shard_map/unpack/pallas_call | solution.py:326
  62.4 6.4 %collective-permute-done.27.refs_2_ = f32[2,2,2,8,8,128]{5,4,3,2,1,0:T(8,128)S(1)} collective-permute-done((f32[2,2,2,8,8,128]{5,4,3,2,1,0:T(8,128)S(1)}, f32[2,2,2,8,8,128]{5,4,3,2,1,0:T(8,128)S(1)}, u32[]{:S(2)}, u32[]{:S(2)}) %collective-permute-start.27) | collective-permute-done | bytes 262176 | tf_op jit(solution)/shard_map/ppermute | solution.py:338
  68.8 0.7 unpack_rest.3
  69.5 0.7 unpack_rest.4
  70.2 1.2 %collective-permute-done.29.refs_2_ = f32[2,2,8,8,128]{4,3,2,1,0:T(8,128)S(1)} collective-permute-done((f32[2,2,8,8,128]{4,3,2,1,0:T(8,128)S(1)}, f32[2,2,8,8,128]{4,3,2,1,0:T(8,128)S(1)}, u32[]{:S(2)}, u32[]{:S(2)}) %collective-permute-start.29) | collective-permute-done | bytes 131104 | tf_op jit(solution)/shard_map/ppermute | solution.py:338
  71.4 0.7 unpack_rest.5
  (24 shorter events, 0.2 us)
Async XLA Ops:
  0.6 17.2 %collective-permute-start.6 = (f32[2,2,32,256]{3,2,1,0:T(8,128)}, f32[2,2,32,256]{3,2,1,0:T(8,128)S(1)}, u32[]{:S(2)}, u32[]{:S(2)}) collective-permute-start(f32[2,2,32,256]{3,2,1,0:T(8,128)} %bitcast.10), channel_id=1, source_target_pairs={{0,2},{1,3},{2,0},{3,1},{4,6},{5,7},{6,4},{7,5},{8,10},{9,11},{10,... | collective-permute-start | bytes 393224 | tf_op jit(solution)/shard_map/ppermute | solution.py:338
  4.7 13.7 %collective-permute-start.5 = (f32[2,2,32,256]{3,2,1,0:T(8,128)}, f32[2,2,32,256]{3,2,1,0:T(8,128)S(1)}, u32[]{:S(2)}, u32[]{:S(2)}) collective-permute-start(f32[2,2,32,256]{3,2,1,0:T(8,128)} %bitcast.11), channel_id=1, source_target_pairs={{0,1},{1,0},{2,3},{3,2},{4,5},{5,4},{6,7},{7,6},{8,9},{9,8},{10,11... | collective-permute-start | bytes 393224 | tf_op jit(solution)/shard_map/ppermute | solution.py:338
  6.3 1.0 %copy-start = (f32[2,2,8,8,512]{4,3,2,1,0:T(8,128)S(1)}, f32[2,2,8,8,512]{4,3,2,1,0:T(8,128)}, u32[]{:S(2)}) copy-start(f32[2,2,8,8,512]{4,3,2,1,0:T(8,128)} %refs_0_.1) | copy-start | bytes 1572868
  7.3 15.9 %copy-start.1 = (f32[2,2,256,32]{2,3,1,0:T(8,128)S(1)}, f32[2,2,256,32]{2,3,1,0:T(8,128)}, u32[]{:S(2)}) copy-start(f32[2,2,256,32]{2,3,1,0:T(8,128)} %param.5) | copy-start | bytes 393220
  7.5 1.0 %copy-start.3 = (s32[2,2,4]{2,1,0:T(2,128)S(1)}, s32[2,2,4]{2,1,0:T(2,128)}, u32[]{:S(2)}) copy-start(s32[2,2,4]{2,1,0:T(2,128)} %param.7) | copy-start | bytes 196
  7.5 16.1 %collective-permute-start.10 = (f32[2,2,8,8,128]{4,3,2,1,0:T(8,128)S(1)}, f32[2,2,8,8,128]{4,3,2,1,0:T(8,128)S(1)}, u32[]{:S(2)}, u32[]{:S(2)}) collective-permute-start(f32[2,2,8,8,128]{4,3,2,1,0:T(8,128)S(1)} %get-tuple-element.34), channel_id=1, source_target_pairs={{0,3},{1,2},{2,1},{3,0},{4,7},{5,6},{6,5},{7,4},{8,11},{9,10},{10,... | collective-permute-start | bytes 393224 | tf_op jit(solution)/shard_map/ppermute | solution.py:338
  7.6 16.0 %collective-permute-start.8 = (f32[2,2,8,8,128]{4,3,2,1,0:T(8,128)S(1)}, f32[2,2,8,8,128]{4,3,2,1,0:T(8,128)S(1)}, u32[]{:S(2)}, u32[]{:S(2)}) collective-permute-start(f32[2,2,8,8,128]{4,3,2,1,0:T(8,128)S(1)} %get-tuple-element.32), channel_id=1, source_target_pairs={{0,1},{1,0},{2,3},{3,2},{4,5},{5,4},{6,7},{7,6},{8,9},{9,8},{10,11... | collective-permute-start | bytes 393224 | tf_op jit(solution)/shard_map/ppermute | solution.py:338
  8.5 2.3 %collective-permute-start.3 = (s32[4]{0:T(128)S(1)}, s32[4]{0:T(128)S(1)}, u32[]{:S(2)}, u32[]{:S(2)}) collective-permute-start(s32[4]{0:T(128)S(1)} %get-tuple-element.56), channel_id=1, source_target_pairs={{4,0},{8,4},{12,8},{16,12},{20,16},{24,20},{28,24},{0,28},{5,1},{9... | collective-permute-start | bytes 56 | tf_op jit(solution)/shard_map/ppermute | solution.py:381
  10.8 4.1 %collective-permute-start.4 = (s32[4]{0:T(128)S(1)}, s32[4]{0:T(128)S(1)}, u32[]{:S(2)}, u32[]{:S(2)}) collective-permute-start(s32[4]{0:T(128)S(1)} %get-tuple-element.57), channel_id=1, source_target_pairs={{0,4},{4,8},{8,12},{12,16},{16,20},{20,24},{24,28},{28,0},{1,5},{5... | collective-permute-start | bytes 56 | tf_op jit(solution)/shard_map/ppermute | solution.py:382
  14.9 8.7 %collective-permute-start.9 = (f32[2,2,8,8,128]{4,3,2,1,0:T(8,128)S(1)}, f32[2,2,8,8,128]{4,3,2,1,0:T(8,128)S(1)}, u32[]{:S(2)}, u32[]{:S(2)}) collective-permute-start(f32[2,2,8,8,128]{4,3,2,1,0:T(8,128)S(1)} %get-tuple-element.33), channel_id=1, source_target_pairs={{0,2},{1,3},{2,0},{3,1},{4,6},{5,7},{6,4},{7,5},{8,10},{9,11},{10,... | collective-permute-start | bytes 393224 | tf_op jit(solution)/shard_map/ppermute | solution.py:338
  17.9 5.4 %collective-permute-start.7 = (f32[2,2,32,256]{3,2,1,0:T(8,128)S(1)}, f32[2,2,32,256]{3,2,1,0:T(8,128)S(1)}, u32[]{:S(2)}, u32[]{:S(2)}) collective-permute-start(f32[2,2,32,256]{3,2,1,0:T(8,128)S(1)} %collective-permute-done.6.refs_2_), channel_id=1, source_target_pairs={{0,1},{1,0},{2,3},{3,2},{4,5},{5,4},{6,7},{7,6},{8,9},{9,8},{10,11... | collective-permute-start | bytes 393224 | tf_op jit(solution)/shard_map/ppermute | solution.py:338
  23.6 0.9 %copy-start.2 = (f32[2,2,256,32]{2,3,1,0:T(8,128)S(1)}, f32[2,2,256,32]{2,3,1,0:T(8,128)}, u32[]{:S(2)}) copy-start(f32[2,2,256,32]{2,3,1,0:T(8,128)} %param.6) | copy-start | bytes 393220
  24.3 1.6 %collective-permute-start.11 = (f32[256,256]{1,0:T(8,128)S(1)}, f32[256,256]{1,0:T(8,128)S(1)}, u32[]{:S(2)}, u32[]{:S(2)}) collective-permute-start(f32[256,256]{1,0:T(8,128)S(1)} %summary_forward.1.refs_0_.refs_4_), channel_id=1, source_target_pairs={{0,4},{4,0},{8,12},{12,8},{16,20},{20,16},{24,28},{28,24},{1,5},{5... | collective-permute-start | bytes 786440 | tf_op jit(solution)/shard_map/ppermute | solution.py:338
  24.5 9.6 %collective-permute-start.1 = (f32[2,2,32,256]{3,2,1,0:T(8,128)S(1)}, f32[2,2,32,256]{3,2,1,0:T(8,128)S(1)}, u32[]{:S(2)}, u32[]{:S(2)}) collective-permute-start(f32[2,2,32,256]{3,2,1,0:T(8,128)S(1)} %bitcast.13), channel_id=1, source_target_pairs={{0,2},{1,3},{2,0},{3,1},{4,6},{5,7},{6,4},{7,5},{8,10},{9,11},{10,... | collective-permute-start | bytes 393224 | tf_op jit(solution)/shard_map/ppermute | solution.py:338
  26.2 7.9 %collective-permute-start.12 = (f32[128,256]{1,0:T(8,128)S(1)}, f32[128,256]{1,0:T(8,128)S(1)}, u32[]{:S(2)}, u32[]{:S(2)}) collective-permute-start(f32[128,256]{1,0:T(8,128)S(1)} %get-tuple-element.36), channel_id=1, source_target_pairs={{0,8},{4,12},{8,0},{12,4},{16,24},{20,28},{24,16},{28,20},{1,9},{5... | collective-permute-start | bytes 393224 | tf_op jit(solution)/shard_map/ppermute | solution.py:338
  27.7 7.0 %collective-permute-start.14 = (f32[128,256]{1,0:T(8,128)S(1)}, f32[128,256]{1,0:T(8,128)S(1)}, u32[]{:S(2)}, u32[]{:S(2)}) collective-permute-start(f32[128,256]{1,0:T(8,128)S(1)} %get-tuple-element.36), channel_id=1, source_target_pairs={{0,16},{4,20},{8,24},{12,28},{16,0},{20,4},{24,8},{28,12},{1,17},{... | collective-permute-start | bytes 393224 | tf_op jit(solution)/shard_map/ppermute | solution.py:338
  29.1 6.7 %collective-permute-start.16 = (f32[128,256]{1,0:T(8,128)S(1)}, f32[128,256]{1,0:T(8,128)S(1)}, u32[]{:S(2)}, u32[]{:S(2)}) collective-permute-start(f32[128,256]{1,0:T(8,128)S(1)} %get-tuple-element.36), channel_id=1, source_target_pairs={{0,24},{4,28},{8,16},{12,20},{16,8},{20,12},{24,0},{28,4},{1,25},{... | collective-permute-start | bytes 393224 | tf_op jit(solution)/shard_map/ppermute | solution.py:338
  29.8 7.1 %collective-permute-start = (f32[2,2,32,256]{3,2,1,0:T(8,128)S(1)}, f32[2,2,32,256]{3,2,1,0:T(8,128)S(1)}, u32[]{:S(2)}, u32[]{:S(2)}) collective-permute-start(f32[2,2,32,256]{3,2,1,0:T(8,128)S(1)} %bitcast.14), channel_id=1, source_target_pairs={{0,1},{1,0},{2,3},{3,2},{4,5},{5,4},{6,7},{7,6},{8,9},{9,8},{10,11... | collective-permute-start | bytes 393224 | tf_op jit(solution)/shard_map/ppermute | solution.py:338
  34.1 5.4 %collective-permute-start.2 = (f32[2,2,32,256]{3,2,1,0:T(8,128)S(1)}, f32[2,2,32,256]{3,2,1,0:T(8,128)S(1)}, u32[]{:S(2)}, u32[]{:S(2)}) collective-permute-start(f32[2,2,32,256]{3,2,1,0:T(8,128)S(1)} %collective-permute-done.1.refs_2_), channel_id=1, source_target_pairs={{0,1},{1,0},{2,3},{3,2},{4,5},{5,4},{6,7},{7,6},{8,9},{9,8},{10,11... | collective-permute-start | bytes 393224 | tf_op jit(solution)/shard_map/ppermute | solution.py:338
  34.1 5.7 %collective-permute-start.13 = (f32[128,256]{1,0:T(8,128)S(1)}, f32[128,256]{1,0:T(8,128)S(1)}, u32[]{:S(2)}, u32[]{:S(2)}) collective-permute-start(f32[128,256]{1,0:T(8,128)S(1)} %collective-permute-done.12.refs_7_), channel_id=1, source_target_pairs={{0,4},{4,0},{8,12},{12,8},{16,20},{20,16},{24,28},{28,24},{1,5},{5... | collective-permute-start | bytes 393224 | tf_op jit(solution)/shard_map/ppermute | solution.py:338
  34.7 5.1 %collective-permute-start.15 = (f32[128,256]{1,0:T(8,128)S(1)}, f32[128,256]{1,0:T(8,128)S(1)}, u32[]{:S(2)}, u32[]{:S(2)}) collective-permute-start(f32[128,256]{1,0:T(8,128)S(1)} %collective-permute-done.14.refs_9_), channel_id=1, source_target_pairs={{0,4},{4,0},{8,12},{12,8},{16,20},{20,16},{24,28},{28,24},{1,5},{5... | collective-permute-start | bytes 393224 | tf_op jit(solution)/shard_map/ppermute | solution.py:338
  35.8 4.0 %collective-permute-start.17 = (f32[128,256]{1,0:T(8,128)S(1)}, f32[128,256]{1,0:T(8,128)S(1)}, u32[]{:S(2)}, u32[]{:S(2)}) collective-permute-start(f32[128,256]{1,0:T(8,128)S(1)} %collective-permute-done.16.refs_11_), channel_id=1, source_target_pairs={{0,4},{4,0},{8,12},{12,8},{16,20},{20,16},{24,28},{28,24},{1,5},{5... | collective-permute-start | bytes 393224 | tf_op jit(solution)/shard_map/ppermute | solution.py:338
  41.9 2.1 %collective-permute-start.19 = (f32[256,256]{1,0:T(8,128)S(1)}, f32[256,256]{1,0:T(8,128)S(1)}, u32[]{:S(2)}, u32[]{:S(2)}) collective-permute-start(f32[256,256]{1,0:T(8,128)S(1)} %summary_backward.1.refs_0_.refs_5_), channel_id=1, source_target_pairs={{0,4},{4,0},{8,12},{12,8},{16,20},{20,16},{24,28},{28,24},{1,5},{5... | collective-permute-start | bytes 786440 | tf_op jit(solution)/shard_map/ppermute | solution.py:338
  42.0 7.9 %collective-permute-start.22 = (f32[2,2,8,8,128]{4,3,2,1,0:T(8,128)S(1)}, f32[2,2,8,8,128]{4,3,2,1,0:T(8,128)S(1)}, u32[]{:S(2)}, u32[]{:S(2)}) collective-permute-start(f32[2,2,8,8,128]{4,3,2,1,0:T(8,128)S(1)} %get-tuple-element.42), channel_id=1, source_target_pairs={{0,3},{1,2},{2,1},{3,0},{4,7},{5,6},{6,5},{7,4},{8,11},{9,10},{10,... | collective-permute-start | bytes 393224 | tf_op jit(solution)/shard_map/ppermute | solution.py:338
  44.3 5.7 %collective-permute-start.23 = (f32[128,256]{1,0:T(8,128)S(1)}, f32[128,256]{1,0:T(8,128)S(1)}, u32[]{:S(2)}, u32[]{:S(2)}) collective-permute-start(f32[128,256]{1,0:T(8,128)S(1)} %get-tuple-element.41), channel_id=1, source_target_pairs={{0,16},{4,20},{8,24},{12,28},{16,0},{20,4},{24,8},{28,12},{1,17},{... | collective-permute-start | bytes 393224 | tf_op jit(solution)/shard_map/ppermute | solution.py:338
  45.9 6.4 %collective-permute-start.20 = (f32[128,256]{1,0:T(8,128)S(1)}, f32[128,256]{1,0:T(8,128)S(1)}, u32[]{:S(2)}, u32[]{:S(2)}) collective-permute-start(f32[128,256]{1,0:T(8,128)S(1)} %get-tuple-element.41), channel_id=1, source_target_pairs={{0,8},{4,12},{8,0},{12,4},{16,24},{20,28},{24,16},{28,20},{1,9},{5... | collective-permute-start | bytes 393224 | tf_op jit(solution)/shard_map/ppermute | solution.py:338
  47.3 6.6 %collective-permute-start.25 = (f32[128,256]{1,0:T(8,128)S(1)}, f32[128,256]{1,0:T(8,128)S(1)}, u32[]{:S(2)}, u32[]{:S(2)}) collective-permute-start(f32[128,256]{1,0:T(8,128)S(1)} %get-tuple-element.41), channel_id=1, source_target_pairs={{0,24},{4,28},{8,16},{12,20},{16,8},{20,12},{24,0},{28,4},{1,25},{... | collective-permute-start | bytes 393224 | tf_op jit(solution)/shard_map/ppermute | solution.py:338
  47.8 7.9 %collective-permute-start.18 = (f32[2,2,8,8,128]{4,3,2,1,0:T(8,128)S(1)}, f32[2,2,8,8,128]{4,3,2,1,0:T(8,128)S(1)}, u32[]{:S(2)}, u32[]{:S(2)}) collective-permute-start(f32[2,2,8,8,128]{4,3,2,1,0:T(8,128)S(1)} %get-tuple-element.38), channel_id=1, source_target_pairs={{0,2},{1,3},{2,0},{3,1},{4,6},{5,7},{6,4},{7,5},{8,10},{9,11},{10,... | collective-permute-start | bytes 393224 | tf_op jit(solution)/shard_map/ppermute | solution.py:338
  50.0 5.7 %collective-permute-start.24 = (f32[128,256]{1,0:T(8,128)S(1)}, f32[128,256]{1,0:T(8,128)S(1)}, u32[]{:S(2)}, u32[]{:S(2)}) collective-permute-start(f32[128,256]{1,0:T(8,128)S(1)} %hold.1.refs_10_), channel_id=1, source_target_pairs={{0,4},{4,0},{8,12},{12,8},{16,20},{20,16},{24,28},{28,24},{1,5},{5... | collective-permute-start | bytes 393224 | tf_op jit(solution)/shard_map/ppermute | solution.py:338
  52.3 3.4 %collective-permute-start.21 = (f32[128,256]{1,0:T(8,128)S(1)}, f32[128,256]{1,0:T(8,128)S(1)}, u32[]{:S(2)}, u32[]{:S(2)}) collective-permute-start(f32[128,256]{1,0:T(8,128)S(1)} %collective-permute-done.20.refs_8_), channel_id=1, source_target_pairs={{0,4},{4,0},{8,12},{12,8},{16,20},{20,16},{24,28},{28,24},{1,5},{5... | collective-permute-start | bytes 393224 | tf_op jit(solution)/shard_map/ppermute | solution.py:338
  53.9 1.8 %collective-permute-start.26 = (f32[128,256]{1,0:T(8,128)S(1)}, f32[128,256]{1,0:T(8,128)S(1)}, u32[]{:S(2)}, u32[]{:S(2)}) collective-permute-start(f32[128,256]{1,0:T(8,128)S(1)} %collective-permute-done.25.refs_12_), channel_id=1, source_target_pairs={{0,4},{4,0},{8,12},{12,8},{16,20},{20,16},{24,28},{28,24},{1,5},{5... | collective-permute-start | bytes 393224 | tf_op jit(solution)/shard_map/ppermute | solution.py:338
  57.1 11.7 %collective-permute-start.27 = (f32[2,2,2,8,8,128]{5,4,3,2,1,0:T(8,128)S(1)}, f32[2,2,2,8,8,128]{5,4,3,2,1,0:T(8,128)S(1)}, u32[]{:S(2)}, u32[]{:S(2)}) collective-permute-start(f32[2,2,2,8,8,128]{5,4,3,2,1,0:T(8,128)S(1)} %get-tuple-element.47), channel_id=1, source_target_pairs={{0,1},{1,0},{2,3},{3,2},{4,5},{5,4},{6,7},{7,6},{8,9},{9,8},{10,11... | collective-permute-start | bytes 786440 | tf_op jit(solution)/shard_map/ppermute | solution.py:338
  57.2 12.3 %collective-permute-start.28 = (f32[2,2,8,8,128]{4,3,2,1,0:T(8,128)S(1)}, f32[2,2,8,8,128]{4,3,2,1,0:T(8,128)S(1)}, u32[]{:S(2)}, u32[]{:S(2)}) collective-permute-start(f32[2,2,8,8,128]{4,3,2,1,0:T(8,128)S(1)} %get-tuple-element.50), channel_id=1, source_target_pairs={{0,2},{1,3},{2,0},{3,1},{4,6},{5,7},{6,4},{7,5},{8,10},{9,11},{10,... | collective-permute-start | bytes 393224 | tf_op jit(solution)/shard_map/ppermute | solution.py:338
  59.9 11.5 %collective-permute-start.29 = (f32[2,2,8,8,128]{4,3,2,1,0:T(8,128)S(1)}, f32[2,2,8,8,128]{4,3,2,1,0:T(8,128)S(1)}, u32[]{:S(2)}, u32[]{:S(2)}) collective-permute-start(f32[2,2,8,8,128]{4,3,2,1,0:T(8,128)S(1)} %get-tuple-element.53), channel_id=1, source_target_pairs={{0,3},{1,2},{2,1},{3,0},{4,7},{5,6},{6,5},{7,4},{8,11},{9,10},{10,... | collective-permute-start | bytes 393224 | tf_op jit(solution)/shard_map/ppermute | solution.py:338

commit v8 on v7

--- a/solution.py
+++ b/solution.py
@@ -353,7 +353,7 @@
     blocks = [whole]
     for i in range(1, chips):
         block = swap(half, "seg", 2 * i)
-        if i == min(2, chips - 1) and first is not None:
+        if i == min(3, chips - 1) and first is not None:
             (block,) = hold(first, block)
         blocks += [block, swap(block, "seg", 1)]
     return blocks

time: 72.2 us -> 72.3 us (level)
  transfers between devices with their start and end apart: 30 -> 30, of which waited for: 16 -> 15; matrix products, arithmetic and copies ran while one was open for 0% -> 0% of each run, Pallas kernels for 5% -> 5%
where the time goes in v8:
time: 72.3 us; the launch traced here: 72.1 us
  waiting for transfers between devices  32.8 us (45%)
  starting transfers between devices  28.9 us (40%)
  Pallas kernels  8.32 us (12%)
  local copies, waits for them, and re-layouts  1.21 us (2%)
  between operations  0.89 us (1%)
    ppermute x28, waiting for transfers between devices, swap(): lax.ppermute(block, axis, [(i, i ^ distance) for i in range(lax.axis_size...  28.2 us
    ppermute x28, starting transfers between devices, swap(): lax.ppermute(block, axis, [(i, i ^ distance) for i in range(lax.axis_size...  27.1 us
    ppermute x1, waiting for transfers between devices, shards(): lax.ppermute(line_offsets[-1, 1], 'seg', [(i, (i + 1) % places) for i in...  3.29 us
    pallas_call x4, Pallas kernels, unpack(): call(body, 'unpack_rest' if begun else 'unpack', [((segs, parts, coils, l...  2.87 us
    pallas_call x2, Pallas kernels, finish(): call(body, 'finish_backward' if backward else 'finish_forward', out_shape...  2.76 us
  transfers between devices with their start and end apart: 30, of which 15 were waited for; matrix products, arithmetic and copies ran while one was open for 0% of the time, Pallas kernels for 5%

profile of v8, /device:TPU:0, one launch (start us, length us, event | category | flops | bytes accessed | tf_op | source)
XLA Modules:
  0.0 72.1 jit_solution(12305162407489078947)
XLA Ops:
  0.6 4.1 %collective-permute-start.6 = (f32[2,2,32,256]{3,2,1,0:T(8,128)}, f32[2,2,32,256]{3,2,1,0:T(8,128)S(1)}, u32[]{:S(2)}, u32[]{:S(2)}) collective-permute-start(f32[2,2,32,256]{3,2,1,0:T(8,128)} %bitcast.10), channel_id=1, source_target_pairs={{0,2},{1,3},{2,0},{3,1},{4,6},{5,7},{6,4},{7,5},{8,10},{9,11},{10,... | collective-permute-start | bytes 393224 | tf_op jit(solution)/shard_map/ppermute | solution.py:338
  4.7 1.6 %collective-permute-start.5 = (f32[2,2,32,256]{3,2,1,0:T(8,128)}, f32[2,2,32,256]{3,2,1,0:T(8,128)S(1)}, u32[]{:S(2)}, u32[]{:S(2)}) collective-permute-start(f32[2,2,32,256]{3,2,1,0:T(8,128)} %bitcast.11), channel_id=1, source_target_pairs={{0,1},{1,0},{2,3},{3,2},{4,5},{5,4},{6,7},{7,6},{8,9},{9,8},{10,11... | collective-permute-start | bytes 393224 | tf_op jit(solution)/shard_map/ppermute | solution.py:338
  6.3 1.0 %copy-done = f32[2,2,8,8,512]{4,3,2,1,0:T(8,128)S(1)} copy-done((f32[2,2,8,8,512]{4,3,2,1,0:T(8,128)S(1)}, f32[2,2,8,8,512]{4,3,2,1,0:T(8,128)}, u32[]{:S(2)}) %copy-start) | copy-done | bytes 524312
  7.4 0.1 pack.1
  7.5 0.0 copy-start.3
  7.5 0.1 collective-permute-start.10
  7.6 0.9 %collective-permute-start.8 = (f32[2,2,8,8,128]{4,3,2,1,0:T(8,128)S(1)}, f32[2,2,8,8,128]{4,3,2,1,0:T(8,128)S(1)}, u32[]{:S(2)}, u32[]{:S(2)}) collective-permute-start(f32[2,2,8,8,128]{4,3,2,1,0:T(8,128)S(1)} %get-tuple-element.32), channel_id=1, source_target_pairs={{0,1},{1,0},{2,3},{3,2},{4,5},{5,4},{6,7},{7,6},{8,9},{9,8},{10,11... | collective-permute-start | bytes 393224 | tf_op jit(solution)/shard_map/ppermute | solution.py:338
  8.5 1.0 %collective-permute-start.3 = (s32[4]{0:T(128)S(1)}, s32[4]{0:T(128)S(1)}, u32[]{:S(2)}, u32[]{:S(2)}) collective-permute-start(s32[4]{0:T(128)S(1)} %get-tuple-element.56), channel_id=1, source_target_pairs={{4,0},{8,4},{12,8},{16,12},{20,16},{24,20},{28,24},{0,28},{5,1},{9... | collective-permute-start | bytes 56 | tf_op jit(solution)/shard_map/ppermute | solution.py:381
  9.5 1.3 %collective-permute-done.3 = s32[4]{0:T(128)S(1)} collective-permute-done((s32[4]{0:T(128)S(1)}, s32[4]{0:T(128)S(1)}, u32[]{:S(2)}, u32[]{:S(2)}) %collective-permute-start.3) | collective-permute-done | bytes 48 | tf_op jit(solution)/shard_map/ppermute | solution.py:381
  10.8 0.8 %collective-permute-start.4 = (s32[4]{0:T(128)S(1)}, s32[4]{0:T(128)S(1)}, u32[]{:S(2)}, u32[]{:S(2)}) collective-permute-start(s32[4]{0:T(128)S(1)} %get-tuple-element.57), channel_id=1, source_target_pairs={{0,4},{4,8},{8,12},{12,16},{16,20},{20,24},{24,28},{28,0},{1,5},{5... | collective-permute-start | bytes 56 | tf_op jit(solution)/shard_map/ppermute | solution.py:382
  11.6 3.3 %collective-permute-done.4 = s32[4]{0:T(128)S(1)} collective-permute-done((s32[4]{0:T(128)S(1)}, s32[4]{0:T(128)S(1)}, u32[]{:S(2)}, u32[]{:S(2)}) %collective-permute-start.4) | collective-permute-done | bytes 48 | tf_op jit(solution)/shard_map/ppermute | solution.py:382
  14.9 3.0 %collective-permute-start.9 = (f32[2,2,8,8,128]{4,3,2,1,0:T(8,128)S(1)}, f32[2,2,8,8,128]{4,3,2,1,0:T(8,128)S(1)}, u32[]{:S(2)}, u32[]{:S(2)}) collective-permute-start(f32[2,2,8,8,128]{4,3,2,1,0:T(8,128)S(1)} %get-tuple-element.33), channel_id=1, source_target_pairs={{0,2},{1,3},{2,0},{3,1},{4,6},{5,7},{6,4},{7,5},{8,10},{9,11},{10,... | collective-permute-start | bytes 393224 | tf_op jit(solution)/shard_map/ppermute | solution.py:338
  17.9 0.6 collective-permute-start.7
  18.5 0.0 collective-permute-done.5.refs_1_
  18.5 4.8 %collective-permute-done.7.refs_3_ = f32[2,2,32,256]{3,2,1,0:T(8,128)S(1)} collective-permute-done((f32[2,2,32,256]{3,2,1,0:T(8,128)S(1)}, f32[2,2,32,256]{3,2,1,0:T(8,128)S(1)}, u32[]{:S(2)}, u32[]{:S(2)}) %collective-permute-start.7) | collective-permute-done | bytes 131104 | tf_op jit(solution)/shard_map/ppermute | solution.py:338
  23.3 0.3 prepare_forward.1
  23.6 0.0 collective-permute-done.8.refs_2_
  23.6 0.0 collective-permute-done.9.refs_3_
  23.6 0.0 copy-start.2
  23.6 0.7 summary_forward.1.refs_0_.refs_4_
  24.3 0.1 collective-permute-start.11
  24.4 0.1 copy-done.2
  24.5 0.9 %collective-permute-start.1 = (f32[2,2,32,256]{3,2,1,0:T(8,128)S(1)}, f32[2,2,32,256]{3,2,1,0:T(8,128)S(1)}, u32[]{:S(2)}, u32[]{:S(2)}) collective-permute-start(f32[2,2,32,256]{3,2,1,0:T(8,128)S(1)} %bitcast.13), channel_id=1, source_target_pairs={{0,2},{1,3},{2,0},{3,1},{4,6},{5,7},{6,4},{7,5},{8,10},{9,11},{10,... | collective-permute-start | bytes 393224 | tf_op jit(solution)/shard_map/ppermute | solution.py:338
  25.4 0.5 collective-permute-done.11.refs_1_.refs_5_
  25.9 0.3 compose_forward.1
  26.2 1.5 %collective-permute-start.12 = (f32[128,256]{1,0:T(8,128)S(1)}, f32[128,256]{1,0:T(8,128)S(1)}, u32[]{:S(2)}, u32[]{:S(2)}) collective-permute-start(f32[128,256]{1,0:T(8,128)S(1)} %get-tuple-element.36), channel_id=1, source_target_pairs={{0,8},{4,12},{8,0},{12,4},{16,24},{20,28},{24,16},{28,20},{1,9},{5... | collective-permute-start | bytes 393224 | tf_op jit(solution)/shard_map/ppermute | solution.py:338
  27.7 1.4 %collective-permute-start.14 = (f32[128,256]{1,0:T(8,128)S(1)}, f32[128,256]{1,0:T(8,128)S(1)}, u32[]{:S(2)}, u32[]{:S(2)}) collective-permute-start(f32[128,256]{1,0:T(8,128)S(1)} %get-tuple-element.36), channel_id=1, source_target_pairs={{0,16},{4,20},{8,24},{12,28},{16,0},{20,4},{24,8},{28,12},{1,17},{... | collective-permute-start | bytes 393224 | tf_op jit(solution)/shard_map/ppermute | solution.py:338
  29.1 0.7 collective-permute-start.16
  29.8 1.7 %collective-permute-start = (f32[2,2,32,256]{3,2,1,0:T(8,128)S(1)}, f32[2,2,32,256]{3,2,1,0:T(8,128)S(1)}, u32[]{:S(2)}, u32[]{:S(2)}) collective-permute-start(f32[2,2,32,256]{3,2,1,0:T(8,128)S(1)} %bitcast.14), channel_id=1, source_target_pairs={{0,1},{1,0},{2,3},{3,2},{4,5},{5,4},{6,7},{7,6},{8,9},{9,8},{10,11... | collective-permute-start | bytes 393224 | tf_op jit(solution)/shard_map/ppermute | solution.py:338
  31.5 2.6 %collective-permute-done.1.refs_2_ = f32[2,2,32,256]{3,2,1,0:T(8,128)S(1)} collective-permute-done((f32[2,2,32,256]{3,2,1,0:T(8,128)S(1)}, f32[2,2,32,256]{3,2,1,0:T(8,128)S(1)}, u32[]{:S(2)}, u32[]{:S(2)}) %collective-permute-start.1) | collective-permute-done | bytes 131104 | tf_op jit(solution)/shard_map/ppermute | solution.py:338
  34.1 0.0 collective-permute-start.2
  34.1 0.0 collective-permute-done.12.refs_7_
  34.1 0.0 collective-permute-start.13
  34.1 0.6 collective-permute-done.14.refs_9_
  34.7 0.0 collective-permute-start.15
  34.7 1.1 %collective-permute-done.16.refs_11_ = f32[128,256]{1,0:T(8,128)S(1)} collective-permute-done((f32[128,256]{1,0:T(8,128)S(1)}, f32[128,256]{1,0:T(8,128)S(1)}, u32[]{:S(2)}, u32[]{:S(2)}) %collective-permute-start.16) | collective-permute-done | bytes 131104 | tf_op jit(solution)/shard_map/ppermute | solution.py:338
  35.8 1.1 %collective-permute-done.refs_1_ = f32[2,2,32,256]{3,2,1,0:T(8,128)S(1)} collective-permute-done((f32[2,2,32,256]{3,2,1,0:T(8,128)S(1)}, f32[2,2,32,256]{3,2,1,0:T(8,128)S(1)}, u32[]{:S(2)}, u32[]{:S(2)}) %collective-permute-start) | collective-permute-done | bytes 131104 | tf_op jit(solution)/shard_map/ppermute | solution.py:338
  36.9 2.6 %collective-permute-done.2.refs_3_ = f32[2,2,32,256]{3,2,1,0:T(8,128)S(1)} collective-permute-done((f32[2,2,32,256]{3,2,1,0:T(8,128)S(1)}, f32[2,2,32,256]{3,2,1,0:T(8,128)S(1)}, u32[]{:S(2)}, u32[]{:S(2)}) %collective-permute-start.2) | collective-permute-done | bytes 131104 | tf_op jit(solution)/shard_map/ppermute | solution.py:338
  39.5 0.3 prepare_backward.1
  39.8 1.4 %finish_forward.1.refs_1_.refs_3_.refs_4_ = f32[2,2,32,8,128]{4,3,2,1,0:T(8,128)S(1)} custom-call(s32[8,128]{1,0:T(8,128)S(1)} %pad.4.refs_0_.refs_1_, bf16[2,512,256]{2,1,0:T(8,128)(2,1)S(1)} %get-tuple-element.29.refs_0_.refs_1_, bf16[2,512,256]{2,1,0:T(8,128)(2,1)S(1)} %get-tuple-element.30.refs_2_, f32[2,2,32,8,128]{4,3,2,1,0:T(8,128)S(1)} %gather.1.refs_3_, ...), custom_call_target="tpu_custom_call" | custom-call | tf_op jit(solution)/shard_map/finish_forward/pallas_call | solution.py:276
  41.2 0.7 summary_backward.1.refs_0_.refs_5_
  41.9 0.1 collective-permute-start.19
  42.0 1.9 %collective-permute-start.24 = (f32[2,2,8,8,128]{4,3,2,1,0:T(8,128)S(1)}, f32[2,2,8,8,128]{4,3,2,1,0:T(8,128)S(1)}, u32[]{:S(2)}, u32[]{:S(2)}) collective-permute-start(f32[2,2,8,8,128]{4,3,2,1,0:T(8,128)S(1)} %get-tuple-element.42), channel_id=1, source_target_pairs={{0,3},{1,2},{2,1},{3,0},{4,7},{5,6},{6,5},{7,4},{8,11},{9,10},{10,... | collective-permute-start | bytes 393224 | tf_op jit(solution)/shard_map/ppermute | solution.py:338
  43.9 0.3 compose_backward.1
  44.3 2.5 %collective-permute-start.25 = (f32[128,256]{1,0:T(8,128)S(1)}, f32[128,256]{1,0:T(8,128)S(1)}, u32[]{:S(2)}, u32[]{:S(2)}) collective-permute-start(f32[128,256]{1,0:T(8,128)S(1)} %get-tuple-element.41), channel_id=1, source_target_pairs={{0,24},{4,28},{8,16},{12,20},{16,8},{20,12},{24,0},{28,4},{1,25},{... | collective-permute-start | bytes 393224 | tf_op jit(solution)/shard_map/ppermute | solution.py:338
  46.8 0.6 collective-permute-start.20
  47.4 0.5 collective-permute-start.22
  47.8 0.1 collective-permute-start.18
  47.9 2.0 %collective-permute-done.24.refs_0_.refs_3_ = f32[2,2,8,8,128]{4,3,2,1,0:T(8,128)S(1)} collective-permute-done((f32[2,2,8,8,128]{4,3,2,1,0:T(8,128)S(1)}, f32[2,2,8,8,128]{4,3,2,1,0:T(8,128)S(1)}, u32[]{:S(2)}, u32[]{:S(2)}) %collective-permute-start.24) | collective-permute-done | bytes 131104 | tf_op jit(solution)/shard_map/ppermute | solution.py:338
  49.9 1.7 %collective-permute-done.25.refs_1_ = f32[128,256]{1,0:T(8,128)S(1)} collective-permute-done((f32[128,256]{1,0:T(8,128)S(1)}, f32[128,256]{1,0:T(8,128)S(1)}, u32[]{:S(2)}, u32[]{:S(2)}) %collective-permute-start.25) | collective-permute-done | bytes 131104 | tf_op jit(solution)/shard_map/ppermute | solution.py:338
  51.6 0.1 collective-permute-start.26
  51.7 2.1 %collective-permute-done.20.refs_8_ = f32[128,256]{1,0:T(8,128)S(1)} collective-permute-done((f32[128,256]{1,0:T(8,128)S(1)}, f32[128,256]{1,0:T(8,128)S(1)}, u32[]{:S(2)}, u32[]{:S(2)}) %collective-permute-start.20) | collective-permute-done | bytes 131104 | tf_op jit(solution)/shard_map/ppermute | solution.py:338
  53.8 0.5 collective-permute-start.23
  54.3 1.4 %collective-permute-done.18.refs_0_.refs_2_ = f32[2,2,8,8,128]{4,3,2,1,0:T(8,128)S(1)} collective-permute-done((f32[2,2,8,8,128]{4,3,2,1,0:T(8,128)S(1)}, f32[2,2,8,8,128]{4,3,2,1,0:T(8,128)S(1)}, u32[]{:S(2)}, u32[]{:S(2)}) %collective-permute-start.18) | collective-permute-done | bytes 131104 | tf_op jit(solution)/shard_map/ppermute | solution.py:338
  55.7 1.4 %finish_backward.1 = (f32[2,2,8,8,128]{4,3,2,1,0:T(8,128)S(1)}, f32[2,2,2,8,8,128]{5,4,3,2,1,0:T(8,128)S(1)}, f32[2,2,8,8,128]{4,3,2,1,0:T(8,128)S(1)}, f32[2,2,8,8,128]{4,3,2,1,0:T(8,128)S(1)}) custom-call(f32[2,2,8,8,128]{4,3,2,1,0:T(8,128)S(1)} %collective-permute-done.18.refs_0_.refs_2_, s32[8,128]{1,0:T(8,128)S(1)} %pad.4.refs_0_.refs_1_, ...), custom_call_target="tpu_custom_call" | custom-call | tf_op jit(solution)/shard_map/finish_backward/pallas_call | solution.py:276
  57.1 0.1 collective-permute-start.27
  57.1 2.7 %collective-permute-start.28 = (f32[2,2,8,8,128]{4,3,2,1,0:T(8,128)S(1)}, f32[2,2,8,8,128]{4,3,2,1,0:T(8,128)S(1)}, u32[]{:S(2)}, u32[]{:S(2)}) collective-permute-start(f32[2,2,8,8,128]{4,3,2,1,0:T(8,128)S(1)} %get-tuple-element.50), channel_id=1, source_target_pairs={{0,2},{1,3},{2,0},{3,1},{4,6},{5,7},{6,4},{7,5},{8,10},{9,11},{10,... | collective-permute-start | bytes 393224 | tf_op jit(solution)/shard_map/ppermute | solution.py:338
  59.9 1.6 %collective-permute-start.29 = (f32[2,2,8,8,128]{4,3,2,1,0:T(8,128)S(1)}, f32[2,2,8,8,128]{4,3,2,1,0:T(8,128)S(1)}, u32[]{:S(2)}, u32[]{:S(2)}) collective-permute-start(f32[2,2,8,8,128]{4,3,2,1,0:T(8,128)S(1)} %get-tuple-element.53), channel_id=1, source_target_pairs={{0,3},{1,2},{2,1},{3,0},{4,7},{5,6},{6,5},{7,4},{8,11},{9,10},{10,... | collective-permute-start | bytes 393224 | tf_op jit(solution)/shard_map/ppermute | solution.py:338
  61.5 0.8 %unpack.1 = (f32[2,2,8,8,512]{4,3,2,1,0:T(8,128)}, f32[2,2,8,8,512]{4,3,2,1,0:T(8,128)}) custom-call(f32[2,2,8,8,128]{4,3,2,1,0:T(8,128)S(1)} %get-tuple-element.37.refs_0_, f32[2,2,8,8,128]{4,3,2,1,0:T(8,128)S(1)} %get-tuple-element.44.refs_1_, f32[2,2,8,8,128]{4,3,2,1,0:T(8,128)S(1)} %collective-permute-done.18.refs_0_.refs_2_, ...), custom_call_target="tpu_custom_call" | custom-call | tf_op jit(solution)/shard_map/unpack/pallas_call | solution.py:326
  62.3 6.3 %collective-permute-done.27.refs_2_ = f32[2,2,2,8,8,128]{5,4,3,2,1,0:T(8,128)S(1)} collective-permute-done((f32[2,2,2,8,8,128]{5,4,3,2,1,0:T(8,128)S(1)}, f32[2,2,2,8,8,128]{5,4,3,2,1,0:T(8,128)S(1)}, u32[]{:S(2)}, u32[]{:S(2)}) %collective-permute-start.27) | collective-permute-done | bytes 262176 | tf_op jit(solution)/shard_map/ppermute | solution.py:338
  68.6 0.7 unpack_rest.3
  69.3 0.7 unpack_rest.4
  70.0 1.4 %collective-permute-done.29.refs_2_ = f32[2,2,8,8,128]{4,3,2,1,0:T(8,128)S(1)} collective-permute-done((f32[2,2,8,8,128]{4,3,2,1,0:T(8,128)S(1)}, f32[2,2,8,8,128]{4,3,2,1,0:T(8,128)S(1)}, u32[]{:S(2)}, u32[]{:S(2)}) %collective-permute-start.29) | collective-permute-done | bytes 131104 | tf_op jit(solution)/shard_map/ppermute | solution.py:338
  71.4 0.7 unpack_rest.5
  (24 shorter events, 0.2 us)
Async XLA Ops:
  0.6 17.2 %collective-permute-start.6 = (f32[2,2,32,256]{3,2,1,0:T(8,128)}, f32[2,2,32,256]{3,2,1,0:T(8,128)S(1)}, u32[]{:S(2)}, u32[]{:S(2)}) collective-permute-start(f32[2,2,32,256]{3,2,1,0:T(8,128)} %bitcast.10), channel_id=1, source_target_pairs={{0,2},{1,3},{2,0},{3,1},{4,6},{5,7},{6,4},{7,5},{8,10},{9,11},{10,... | collective-permute-start | bytes 393224 | tf_op jit(solution)/shard_map/ppermute | solution.py:338
  4.7 13.7 %collective-permute-start.5 = (f32[2,2,32,256]{3,2,1,0:T(8,128)}, f32[2,2,32,256]{3,2,1,0:T(8,128)S(1)}, u32[]{:S(2)}, u32[]{:S(2)}) collective-permute-start(f32[2,2,32,256]{3,2,1,0:T(8,128)} %bitcast.11), channel_id=1, source_target_pairs={{0,1},{1,0},{2,3},{3,2},{4,5},{5,4},{6,7},{7,6},{8,9},{9,8},{10,11... | collective-permute-start | bytes 393224 | tf_op jit(solution)/shard_map/ppermute | solution.py:338
  6.3 1.0 %copy-start = (f32[2,2,8,8,512]{4,3,2,1,0:T(8,128)S(1)}, f32[2,2,8,8,512]{4,3,2,1,0:T(8,128)}, u32[]{:S(2)}) copy-start(f32[2,2,8,8,512]{4,3,2,1,0:T(8,128)} %refs_0_.1) | copy-start | bytes 1572868
  7.3 15.9 %copy-start.1 = (f32[2,2,256,32]{2,3,1,0:T(8,128)S(1)}, f32[2,2,256,32]{2,3,1,0:T(8,128)}, u32[]{:S(2)}) copy-start(f32[2,2,256,32]{2,3,1,0:T(8,128)} %param.5) | copy-start | bytes 393220
  7.5 1.0 %copy-start.3 = (s32[2,2,4]{2,1,0:T(2,128)S(1)}, s32[2,2,4]{2,1,0:T(2,128)}, u32[]{:S(2)}) copy-start(s32[2,2,4]{2,1,0:T(2,128)} %param.7) | copy-start | bytes 196
  7.5 16.1 %collective-permute-start.10 = (f32[2,2,8,8,128]{4,3,2,1,0:T(8,128)S(1)}, f32[2,2,8,8,128]{4,3,2,1,0:T(8,128)S(1)}, u32[]{:S(2)}, u32[]{:S(2)}) collective-permute-start(f32[2,2,8,8,128]{4,3,2,1,0:T(8,128)S(1)} %get-tuple-element.34), channel_id=1, source_target_pairs={{0,3},{1,2},{2,1},{3,0},{4,7},{5,6},{6,5},{7,4},{8,11},{9,10},{10,... | collective-permute-start | bytes 393224 | tf_op jit(solution)/shard_map/ppermute | solution.py:338
  7.6 16.0 %collective-permute-start.8 = (f32[2,2,8,8,128]{4,3,2,1,0:T(8,128)S(1)}, f32[2,2,8,8,128]{4,3,2,1,0:T(8,128)S(1)}, u32[]{:S(2)}, u32[]{:S(2)}) collective-permute-start(f32[2,2,8,8,128]{4,3,2,1,0:T(8,128)S(1)} %get-tuple-element.32), channel_id=1, source_target_pairs={{0,1},{1,0},{2,3},{3,2},{4,5},{5,4},{6,7},{7,6},{8,9},{9,8},{10,11... | collective-permute-start | bytes 393224 | tf_op jit(solution)/shard_map/ppermute | solution.py:338
  8.5 2.3 %collective-permute-start.3 = (s32[4]{0:T(128)S(1)}, s32[4]{0:T(128)S(1)}, u32[]{:S(2)}, u32[]{:S(2)}) collective-permute-start(s32[4]{0:T(128)S(1)} %get-tuple-element.56), channel_id=1, source_target_pairs={{4,0},{8,4},{12,8},{16,12},{20,16},{24,20},{28,24},{0,28},{5,1},{9... | collective-permute-start | bytes 56 | tf_op jit(solution)/shard_map/ppermute | solution.py:381
  10.8 4.1 %collective-permute-start.4 = (s32[4]{0:T(128)S(1)}, s32[4]{0:T(128)S(1)}, u32[]{:S(2)}, u32[]{:S(2)}) collective-permute-start(s32[4]{0:T(128)S(1)} %get-tuple-element.57), channel_id=1, source_target_pairs={{0,4},{4,8},{8,12},{12,16},{16,20},{20,24},{24,28},{28,0},{1,5},{5... | collective-permute-start | bytes 56 | tf_op jit(solution)/shard_map/ppermute | solution.py:382
  14.9 8.7 %collective-permute-start.9 = (f32[2,2,8,8,128]{4,3,2,1,0:T(8,128)S(1)}, f32[2,2,8,8,128]{4,3,2,1,0:T(8,128)S(1)}, u32[]{:S(2)}, u32[]{:S(2)}) collective-permute-start(f32[2,2,8,8,128]{4,3,2,1,0:T(8,128)S(1)} %get-tuple-element.33), channel_id=1, source_target_pairs={{0,2},{1,3},{2,0},{3,1},{4,6},{5,7},{6,4},{7,5},{8,10},{9,11},{10,... | collective-permute-start | bytes 393224 | tf_op jit(solution)/shard_map/ppermute | solution.py:338
  17.9 5.4 %collective-permute-start.7 = (f32[2,2,32,256]{3,2,1,0:T(8,128)S(1)}, f32[2,2,32,256]{3,2,1,0:T(8,128)S(1)}, u32[]{:S(2)}, u32[]{:S(2)}) collective-permute-start(f32[2,2,32,256]{3,2,1,0:T(8,128)S(1)} %collective-permute-done.6.refs_2_), channel_id=1, source_target_pairs={{0,1},{1,0},{2,3},{3,2},{4,5},{5,4},{6,7},{7,6},{8,9},{9,8},{10,11... | collective-permute-start | bytes 393224 | tf_op jit(solution)/shard_map/ppermute | solution.py:338
  23.6 0.9 %copy-start.2 = (f32[2,2,256,32]{2,3,1,0:T(8,128)S(1)}, f32[2,2,256,32]{2,3,1,0:T(8,128)}, u32[]{:S(2)}) copy-start(f32[2,2,256,32]{2,3,1,0:T(8,128)} %param.6) | copy-start | bytes 393220
  24.3 1.6 %collective-permute-start.11 = (f32[256,256]{1,0:T(8,128)S(1)}, f32[256,256]{1,0:T(8,128)S(1)}, u32[]{:S(2)}, u32[]{:S(2)}) collective-permute-start(f32[256,256]{1,0:T(8,128)S(1)} %summary_forward.1.refs_0_.refs_4_), channel_id=1, source_target_pairs={{0,4},{4,0},{8,12},{12,8},{16,20},{20,16},{24,28},{28,24},{1,5},{5... | collective-permute-start | bytes 786440 | tf_op jit(solution)/shard_map/ppermute | solution.py:338
  24.5 9.6 %collective-permute-start.1 = (f32[2,2,32,256]{3,2,1,0:T(8,128)S(1)}, f32[2,2,32,256]{3,2,1,0:T(8,128)S(1)}, u32[]{:S(2)}, u32[]{:S(2)}) collective-permute-start(f32[2,2,32,256]{3,2,1,0:T(8,128)S(1)} %bitcast.13), channel_id=1, source_target_pairs={{0,2},{1,3},{2,0},{3,1},{4,6},{5,7},{6,4},{7,5},{8,10},{9,11},{10,... | collective-permute-start | bytes 393224 | tf_op jit(solution)/shard_map/ppermute | solution.py:338
  26.2 7.9 %collective-permute-start.12 = (f32[128,256]{1,0:T(8,128)S(1)}, f32[128,256]{1,0:T(8,128)S(1)}, u32[]{:S(2)}, u32[]{:S(2)}) collective-permute-start(f32[128,256]{1,0:T(8,128)S(1)} %get-tuple-element.36), channel_id=1, source_target_pairs={{0,8},{4,12},{8,0},{12,4},{16,24},{20,28},{24,16},{28,20},{1,9},{5... | collective-permute-start | bytes 393224 | tf_op jit(solution)/shard_map/ppermute | solution.py:338
  27.7 7.0 %collective-permute-start.14 = (f32[128,256]{1,0:T(8,128)S(1)}, f32[128,256]{1,0:T(8,128)S(1)}, u32[]{:S(2)}, u32[]{:S(2)}) collective-permute-start(f32[128,256]{1,0:T(8,128)S(1)} %get-tuple-element.36), channel_id=1, source_target_pairs={{0,16},{4,20},{8,24},{12,28},{16,0},{20,4},{24,8},{28,12},{1,17},{... | collective-permute-start | bytes 393224 | tf_op jit(solution)/shard_map/ppermute | solution.py:338
  29.1 6.7 %collective-permute-start.16 = (f32[128,256]{1,0:T(8,128)S(1)}, f32[128,256]{1,0:T(8,128)S(1)}, u32[]{:S(2)}, u32[]{:S(2)}) collective-permute-start(f32[128,256]{1,0:T(8,128)S(1)} %get-tuple-element.36), channel_id=1, source_target_pairs={{0,24},{4,28},{8,16},{12,20},{16,8},{20,12},{24,0},{28,4},{1,25},{... | collective-permute-start | bytes 393224 | tf_op jit(solution)/shard_map/ppermute | solution.py:338
  29.8 7.1 %collective-permute-start = (f32[2,2,32,256]{3,2,1,0:T(8,128)S(1)}, f32[2,2,32,256]{3,2,1,0:T(8,128)S(1)}, u32[]{:S(2)}, u32[]{:S(2)}) collective-permute-start(f32[2,2,32,256]{3,2,1,0:T(8,128)S(1)} %bitcast.14), channel_id=1, source_target_pairs={{0,1},{1,0},{2,3},{3,2},{4,5},{5,4},{6,7},{7,6},{8,9},{9,8},{10,11... | collective-permute-start | bytes 393224 | tf_op jit(solution)/shard_map/ppermute | solution.py:338
  34.1 5.4 %collective-permute-start.2 = (f32[2,2,32,256]{3,2,1,0:T(8,128)S(1)}, f32[2,2,32,256]{3,2,1,0:T(8,128)S(1)}, u32[]{:S(2)}, u32[]{:S(2)}) collective-permute-start(f32[2,2,32,256]{3,2,1,0:T(8,128)S(1)} %collective-permute-done.1.refs_2_), channel_id=1, source_target_pairs={{0,1},{1,0},{2,3},{3,2},{4,5},{5,4},{6,7},{7,6},{8,9},{9,8},{10,11... | collective-permute-start | bytes 393224 | tf_op jit(solution)/shard_map/ppermute | solution.py:338
  34.1 5.7 %collective-permute-start.13 = (f32[128,256]{1,0:T(8,128)S(1)}, f32[128,256]{1,0:T(8,128)S(1)}, u32[]{:S(2)}, u32[]{:S(2)}) collective-permute-start(f32[128,256]{1,0:T(8,128)S(1)} %collective-permute-done.12.refs_7_), channel_id=1, source_target_pairs={{0,4},{4,0},{8,12},{12,8},{16,20},{20,16},{24,28},{28,24},{1,5},{5... | collective-permute-start | bytes 393224 | tf_op jit(solution)/shard_map/ppermute | solution.py:338
  34.7 5.1 %collective-permute-start.15 = (f32[128,256]{1,0:T(8,128)S(1)}, f32[128,256]{1,0:T(8,128)S(1)}, u32[]{:S(2)}, u32[]{:S(2)}) collective-permute-start(f32[128,256]{1,0:T(8,128)S(1)} %collective-permute-done.14.refs_9_), channel_id=1, source_target_pairs={{0,4},{4,0},{8,12},{12,8},{16,20},{20,16},{24,28},{28,24},{1,5},{5... | collective-permute-start | bytes 393224 | tf_op jit(solution)/shard_map/ppermute | solution.py:338
  35.8 4.0 %collective-permute-start.17 = (f32[128,256]{1,0:T(8,128)S(1)}, f32[128,256]{1,0:T(8,128)S(1)}, u32[]{:S(2)}, u32[]{:S(2)}) collective-permute-start(f32[128,256]{1,0:T(8,128)S(1)} %collective-permute-done.16.refs_11_), channel_id=1, source_target_pairs={{0,4},{4,0},{8,12},{12,8},{16,20},{20,16},{24,28},{28,24},{1,5},{5... | collective-permute-start | bytes 393224 | tf_op jit(solution)/shard_map/ppermute | solution.py:338
  41.9 2.1 %collective-permute-start.19 = (f32[256,256]{1,0:T(8,128)S(1)}, f32[256,256]{1,0:T(8,128)S(1)}, u32[]{:S(2)}, u32[]{:S(2)}) collective-permute-start(f32[256,256]{1,0:T(8,128)S(1)} %summary_backward.1.refs_0_.refs_5_), channel_id=1, source_target_pairs={{0,4},{4,0},{8,12},{12,8},{16,20},{20,16},{24,28},{28,24},{1,5},{5... | collective-permute-start | bytes 786440 | tf_op jit(solution)/shard_map/ppermute | solution.py:338
  42.0 7.9 %collective-permute-start.24 = (f32[2,2,8,8,128]{4,3,2,1,0:T(8,128)S(1)}, f32[2,2,8,8,128]{4,3,2,1,0:T(8,128)S(1)}, u32[]{:S(2)}, u32[]{:S(2)}) collective-permute-start(f32[2,2,8,8,128]{4,3,2,1,0:T(8,128)S(1)} %get-tuple-element.42), channel_id=1, source_target_pairs={{0,3},{1,2},{2,1},{3,0},{4,7},{5,6},{6,5},{7,4},{8,11},{9,10},{10,... | collective-permute-start | bytes 393224 | tf_op jit(solution)/shard_map/ppermute | solution.py:338
  44.3 7.3 %collective-permute-start.25 = (f32[128,256]{1,0:T(8,128)S(1)}, f32[128,256]{1,0:T(8,128)S(1)}, u32[]{:S(2)}, u32[]{:S(2)}) collective-permute-start(f32[128,256]{1,0:T(8,128)S(1)} %get-tuple-element.41), channel_id=1, source_target_pairs={{0,24},{4,28},{8,16},{12,20},{16,8},{20,12},{24,0},{28,4},{1,25},{... | collective-permute-start | bytes 393224 | tf_op jit(solution)/shard_map/ppermute | solution.py:338
  46.8 7.0 %collective-permute-start.20 = (f32[128,256]{1,0:T(8,128)S(1)}, f32[128,256]{1,0:T(8,128)S(1)}, u32[]{:S(2)}, u32[]{:S(2)}) collective-permute-start(f32[128,256]{1,0:T(8,128)S(1)} %get-tuple-element.41), channel_id=1, source_target_pairs={{0,8},{4,12},{8,0},{12,4},{16,24},{20,28},{24,16},{28,20},{1,9},{5... | collective-permute-start | bytes 393224 | tf_op jit(solution)/shard_map/ppermute | solution.py:338
  47.4 6.4 %collective-permute-start.22 = (f32[128,256]{1,0:T(8,128)S(1)}, f32[128,256]{1,0:T(8,128)S(1)}, u32[]{:S(2)}, u32[]{:S(2)}) collective-permute-start(f32[128,256]{1,0:T(8,128)S(1)} %get-tuple-element.41), channel_id=1, source_target_pairs={{0,16},{4,20},{8,24},{12,28},{16,0},{20,4},{24,8},{28,12},{1,17},{... | collective-permute-start | bytes 393224 | tf_op jit(solution)/shard_map/ppermute | solution.py:338
  47.8 7.8 %collective-permute-start.18 = (f32[2,2,8,8,128]{4,3,2,1,0:T(8,128)S(1)}, f32[2,2,8,8,128]{4,3,2,1,0:T(8,128)S(1)}, u32[]{:S(2)}, u32[]{:S(2)}) collective-permute-start(f32[2,2,8,8,128]{4,3,2,1,0:T(8,128)S(1)} %get-tuple-element.38), channel_id=1, source_target_pairs={{0,2},{1,3},{2,0},{3,1},{4,6},{5,7},{6,4},{7,5},{8,10},{9,11},{10,... | collective-permute-start | bytes 393224 | tf_op jit(solution)/shard_map/ppermute | solution.py:338
  51.6 4.1 %collective-permute-start.26 = (f32[128,256]{1,0:T(8,128)S(1)}, f32[128,256]{1,0:T(8,128)S(1)}, u32[]{:S(2)}, u32[]{:S(2)}) collective-permute-start(f32[128,256]{1,0:T(8,128)S(1)} %hold.1.refs_12_), channel_id=1, source_target_pairs={{0,4},{4,0},{8,12},{12,8},{16,20},{20,16},{24,28},{28,24},{1,5},{5... | collective-permute-start | bytes 393224 | tf_op jit(solution)/shard_map/ppermute | solution.py:338
  53.8 1.9 %collective-permute-start.21 = (f32[128,256]{1,0:T(8,128)S(1)}, f32[128,256]{1,0:T(8,128)S(1)}, u32[]{:S(2)}, u32[]{:S(2)}) collective-permute-start(f32[128,256]{1,0:T(8,128)S(1)} %collective-permute-done.20.refs_8_), channel_id=1, source_target_pairs={{0,4},{4,0},{8,12},{12,8},{16,20},{20,16},{24,28},{28,24},{1,5},{5... | collective-permute-start | bytes 393224 | tf_op jit(solution)/shard_map/ppermute | solution.py:338
  53.8 1.9 %collective-permute-start.23 = (f32[128,256]{1,0:T(8,128)S(1)}, f32[128,256]{1,0:T(8,128)S(1)}, u32[]{:S(2)}, u32[]{:S(2)}) collective-permute-start(f32[128,256]{1,0:T(8,128)S(1)} %collective-permute-done.22.refs_10_), channel_id=1, source_target_pairs={{0,4},{4,0},{8,12},{12,8},{16,20},{20,16},{24,28},{28,24},{1,5},{5... | collective-permute-start | bytes 393224 | tf_op jit(solution)/shard_map/ppermute | solution.py:338
  57.1 11.5 %collective-permute-start.27 = (f32[2,2,2,8,8,128]{5,4,3,2,1,0:T(8,128)S(1)}, f32[2,2,2,8,8,128]{5,4,3,2,1,0:T(8,128)S(1)}, u32[]{:S(2)}, u32[]{:S(2)}) collective-permute-start(f32[2,2,2,8,8,128]{5,4,3,2,1,0:T(8,128)S(1)} %get-tuple-element.47), channel_id=1, source_target_pairs={{0,1},{1,0},{2,3},{3,2},{4,5},{5,4},{6,7},{7,6},{8,9},{9,8},{10,11... | collective-permute-start | bytes 786440 | tf_op jit(solution)/shard_map/ppermute | solution.py:338
  57.1 12.2 %collective-permute-start.28 = (f32[2,2,8,8,128]{4,3,2,1,0:T(8,128)S(1)}, f32[2,2,8,8,128]{4,3,2,1,0:T(8,128)S(1)}, u32[]{:S(2)}, u32[]{:S(2)}) collective-permute-start(f32[2,2,8,8,128]{4,3,2,1,0:T(8,128)S(1)} %get-tuple-element.50), channel_id=1, source_target_pairs={{0,2},{1,3},{2,0},{3,1},{4,6},{5,7},{6,4},{7,5},{8,10},{9,11},{10,... | collective-permute-start | bytes 393224 | tf_op jit(solution)/shard_map/ppermute | solution.py:338
  59.9 11.6 %collective-permute-start.29 = (f32[2,2,8,8,128]{4,3,2,1,0:T(8,128)S(1)}, f32[2,2,8,8,128]{4,3,2,1,0:T(8,128)S(1)}, u32[]{:S(2)}, u32[]{:S(2)}) collective-permute-start(f32[2,2,8,8,128]{4,3,2,1,0:T(8,128)S(1)} %get-tuple-element.53), channel_id=1, source_target_pairs={{0,3},{1,2},{2,1},{3,0},{4,7},{5,6},{6,5},{7,4},{8,11},{9,10},{10,... | collective-permute-start | bytes 393224 | tf_op jit(solution)/shard_map/ppermute | solution.py:338
